TPU v7x, 32 devices: a whole 2x2x4 slice. The times are simulated.
32 devices in a mesh: dp: 8 (over z, core), ctx: 4 (over y, x).
Axes of the slice: x: 2, y: 2, z: 4, core: 2. Of those that a mesh axis runs over, the one named last changes fastest.
Arguments:
- hidden_in: bfloat16 [8192, 2048], P(('dp', 'ctx')), may hold values from -6 to 6
- segments: int32 [8192], P('dp'), may hold values from 0 to 4, as said below
- routes: int32 [8192, 6], P(('dp', 'ctx')), may hold values from 0 to 15, all different within a row; in each aligned block of 256 rows (0 to 255, 256 to 511, ...) at most 192 rows name the same one
- gates: float32 [8192, 6], P(('dp', 'ctx')), may hold values from 0.25 to 0.75
- cotangent: bfloat16 [8192, 2048], P(('dp', 'ctx')), may hold values from -6 to 6
- norm_attn: bfloat16 [2048], P(('dp', 'ctx')), may hold values from 0.25 to 1.75
- w_query: bfloat16 [2048, 3072], P(('dp', 'ctx')), may hold values from -0.125 to 0.125
- w_kv_down: bfloat16 [2048, 576], P(('dp', 'ctx')), may hold values from -0.125 to 0.125
- norm_latent: bfloat16 [512], P(('dp', 'ctx')), may hold values from 0.25 to 1.75
- w_kv_up: bfloat16 [512, 4096], P(('dp', 'ctx')), may hold values from -0.25 to 0.25
- w_out: bfloat16 [2048, 2048], P(('dp', 'ctx')), may hold values from -0.75 to 0.75
- norm_ffn: bfloat16 [2048], P(('dp', 'ctx')), may hold values from 0.25 to 1.75
- w_shared_in: bfloat16 [2048, 5632], P(('dp', 'ctx')), may hold values from -0.125 to 0.125
- w_shared_out: bfloat16 [2816, 2048], P(('dp', 'ctx')), may hold values from -0.109375 to 0.109375
- w_expert_in: bfloat16 [32, 2048, 1408], P(('dp', 'ctx')), may hold values from -0.125 to 0.125
- w_expert_out: bfloat16 [32, 704, 2048], P(('dp', 'ctx')), may hold values from -0.15625 to 0.15625
Outputs:
- mixed: bfloat16 [8192, 2048], P(('dp', 'ctx'))
- grad_in: float32 [8192, 2048], P(('dp', 'ctx'))
- grad_norm_attn: float32 [2048], P(('dp', 'ctx'))
- grad_w_query: float32 [2048, 3072], P(('dp', 'ctx'))
- grad_w_kv_down: float32 [2048, 576], P(('dp', 'ctx'))
- grad_norm_latent: float32 [512], P(('dp', 'ctx'))
- grad_w_kv_up: float32 [512, 4096], P(('dp', 'ctx'))
- grad_w_out: float32 [2048, 2048], P(('dp', 'ctx'))
- grad_norm_ffn: float32 [2048], P(('dp', 'ctx'))
- grad_w_shared_in: float32 [2048, 5632], P(('dp', 'ctx'))
- grad_w_shared_out: float32 [2816, 2048], P(('dp', 'ctx'))
- grad_w_expert_in: float32 [32, 2048, 1408], P(('dp', 'ctx'))
- grad_w_expert_out: float32 [32, 704, 2048], P(('dp', 'ctx'))
Inputs may be any that keep to these rules, and one draw needn't show every extreme that they name: `routes`: in each aligned block of 256 rows (the rows of one device) no expert is named by more than 192 rows. `segments`: segment numbers never fall along a packed row of 1024 tokens; in every row one document begins within the first 256 positions and ends within the last 256.
All inputs are finite; a program needn't handle non-finite values.
Results may differ from a plain program's by a relative error of at most 0.018.
Values may be sent and summed in bfloat16 or wider, within the bound.
No kernel may reach another device: no remote copies, remote signals or barrier semaphores. Data moves between devices by JAX's collectives and lax.ppermute only.
A program may use at most 576 MiB of HBM per device.

v0:
```python
import math

import jax
import jax.numpy as jnp
from jax import lax
from jax.sharding import PartitionSpec as P

D = 2048
HEADS = 16
NOPE = 128
ROPE = 64
VDIM = 128
LATENT = 512
EXPERT_FF = 1408
SHARED_FF = 2816
TOP = 6


epsilon = 1e-06


def matmul(left, right):
    return jnp.dot(left, right, preferred_element_type=jnp.float32)


def matmul_left_t(left, right):
    return lax.dot_general(
        left, right, (((0,), (0,)), ((), ())), preferred_element_type=jnp.float32
    )


def matmul_right_t(left, right):
    return lax.dot_general(
        left, right, (((1,), (1,)), ((), ())), preferred_element_type=jnp.float32
    )


def rope_tables(positions, rope_width):
    half_width = rope_width // 2
    frequency = jnp.exp(
        -math.log(10000.0) * jnp.arange(half_width).astype(jnp.float32) / half_width
    )
    angles = positions.astype(jnp.float32)[:, None] * frequency[None, :]
    return (jnp.cos(angles), jnp.sin(angles))


def rotate(operand, cosine, sine_part):
    half_width = operand.shape[-1] // 2
    first_half = operand[..., :half_width]
    second_half = operand[..., half_width:]
    return jnp.concatenate(
        [
            first_half * cosine - second_half * sine_part,
            second_half * cosine + first_half * sine_part,
        ],
        axis=-1,
    )


def unrotate(operand, cosine, sine_part):
    half_width = operand.shape[-1] // 2
    first_half = operand[..., :half_width]
    second_half = operand[..., half_width:]
    return jnp.concatenate(
        [
            first_half * cosine + second_half * sine_part,
            second_half * cosine - first_half * sine_part,
        ],
        axis=-1,
    )


def swish(operand):
    return operand * jax.nn.sigmoid(operand)


def swish_slope(operand):
    sigma = jax.nn.sigmoid(operand)
    return sigma * (1.0 + operand * (1.0 - sigma))


def swiglu_backward(pre_act, grad_act, half_width):
    gate_part = pre_act[:, :half_width]
    up_part = pre_act[:, half_width:]
    return jnp.concatenate(
        [grad_act * up_part * swish_slope(gate_part), grad_act * swish(gate_part)], axis=1
    ).astype(jnp.bfloat16)


def rms_forward(operand, gain_vec):
    inverse = lax.rsqrt(jnp.mean(operand * operand, axis=-1, keepdims=True) + epsilon)
    return (operand * inverse * gain_vec, inverse)


def rms_backward(operand, inverse, gain_vec, grad_out):
    scaled = grad_out * gain_vec
    grad_gain = jnp.sum(grad_out * operand * inverse, axis=0)
    grad_operand = inverse * scaled - operand * inverse * inverse * inverse * jnp.mean(
        scaled * operand, axis=-1, keepdims=True
    )
    return (grad_operand, grad_gain)


def shards(
    hidden_in,
    segments,
    routes,
    gates,
    cotangent,
    norm_attn,
    w_query,
    w_kv_down,
    norm_latent,
    w_kv_up,
    w_out,
    norm_ffn,
    w_shared_in,
    w_shared_out,
    w_expert_in,
    w_expert_out,
):
    tok_rows = hidden_in.shape[0]
    seq_length = segments.shape[0]
    devices = lax.axis_size(("dp", "ctx"))
    experts = devices // 2
    capacity = 2 * tok_rows * TOP // experts
    half_ff = EXPERT_FF // 2
    scale = 1.0 / math.sqrt(NOPE + ROPE)
    place = lax.axis_index("ctx")
    positions = place * tok_rows + jnp.arange(tok_rows, dtype=jnp.int32)
    key_positions = jnp.arange(seq_length, dtype=jnp.int32)
    cosine, sine_part = rope_tables(positions, ROPE)
    own_segments = lax.dynamic_slice_in_dim(segments, place * tok_rows, tok_rows)
    allowed = (key_positions[None, :] <= positions[:, None]) & (
        segments[None, :] == own_segments[:, None]
    )
    gathered = (
        lax.all_gather(norm_attn, ("dp", "ctx"), axis=0, tiled=True),
        lax.all_gather(w_query, ("dp", "ctx"), axis=0, tiled=True),
        lax.all_gather(w_kv_down, ("dp", "ctx"), axis=0, tiled=True),
        lax.all_gather(norm_latent, ("dp", "ctx"), axis=0, tiled=True),
        lax.all_gather(w_kv_up, ("dp", "ctx"), axis=0, tiled=True),
        lax.all_gather(w_out, ("dp", "ctx"), axis=0, tiled=True),
        lax.all_gather(norm_ffn, ("dp", "ctx"), axis=0, tiled=True),
        lax.all_gather(w_shared_in, ("dp", "ctx"), axis=0, tiled=True),
        lax.all_gather(w_shared_out, ("dp", "ctx"), axis=0, tiled=True),
    )
    gain_attn, query_w, down_w, gain_latent, up_w, out_w, gain_ffn, shared_in_w, shared_out_w = (
        gathered
    )
    inputs = hidden_in.astype(jnp.float32)
    normed_f, inverse_attn = rms_forward(inputs, gain_attn.astype(jnp.float32))
    normed = normed_f.astype(jnp.bfloat16)
    query_raw = matmul(normed, query_w).reshape(tok_rows, HEADS, NOPE + ROPE)
    query_nope = query_raw[..., :NOPE].astype(jnp.bfloat16)
    query_rope = rotate(query_raw[..., NOPE:], cosine[:, None, :], sine_part[:, None, :]).astype(
        jnp.bfloat16
    )
    compressed = matmul(normed, down_w)
    latent_f, inverse_latent = rms_forward(compressed[:, :LATENT], gain_latent.astype(jnp.float32))
    latent = latent_f.astype(jnp.bfloat16)
    key_rope = rotate(compressed[:, LATENT:], cosine, sine_part).astype(jnp.bfloat16)
    local_keyval = matmul(latent, up_w).astype(jnp.bfloat16)
    keyval_all, rope_all = (
        lax.all_gather(local_keyval, "ctx", axis=0, tiled=True),
        lax.all_gather(key_rope, "ctx", axis=0, tiled=True),
    )
    keyval_all = keyval_all.reshape(seq_length, HEADS, NOPE + VDIM)
    key_nope = keyval_all[..., :NOPE]
    key_values = keyval_all[..., NOPE:]

    def masked_scores():
        raw_scores = jnp.einsum(
            "qhd,khd->hqk", query_nope, key_nope, preferred_element_type=jnp.float32
        )
        raw_scores = raw_scores + jnp.einsum(
            "qhd,kd->hqk", query_rope, rope_all, preferred_element_type=jnp.float32
        )
        return jnp.where(allowed[None], raw_scores * scale, -1e30)

    scores = masked_scores()
    row_max = jnp.max(scores, axis=-1, keepdims=True)
    exponent = jnp.exp(scores - row_max)
    row_total = jnp.sum(exponent, axis=-1, keepdims=True)
    log_total = row_max + jnp.log(row_total)
    probs = (exponent / row_total).astype(jnp.bfloat16)
    heads_out = jnp.einsum("hqk,khd->qhd", probs, key_values, preferred_element_type=jnp.float32)
    heads_out = heads_out.astype(jnp.bfloat16).reshape(tok_rows, HEADS * VDIM)
    middle = inputs + matmul(heads_out, out_w)
    ffn_f, inverse_ffn = rms_forward(middle, gain_ffn.astype(jnp.float32))
    ffn_in = ffn_f.astype(jnp.bfloat16)
    shared_pre = matmul(ffn_in, shared_in_w)
    shared_act = (swish(shared_pre[:, :SHARED_FF]) * shared_pre[:, SHARED_FF:]).astype(jnp.bfloat16)
    shared_out = matmul(shared_act, shared_out_w)
    route_count = tok_rows * TOP
    flat_experts = routes.reshape(-1)
    chosen = (flat_experts[:, None] == jnp.arange(experts, dtype=jnp.int32)[None, :]).astype(
        jnp.int32
    )
    ranking = jnp.sum((jnp.cumsum(chosen, axis=0) - chosen) * chosen, axis=1)
    slot_of_route = flat_experts * capacity + ranking
    route_of_slot = (
        jnp.full((experts * capacity,), route_count, jnp.int32)
        .at[slot_of_route]
        .set(jnp.arange(route_count, dtype=jnp.int32))
    )
    token_of_slot = route_of_slot // TOP
    gate_of_slot = jnp.concatenate([gates.reshape(-1), jnp.zeros((1,), jnp.float32)])[route_of_slot]

    def to_halves(slot_rows):
        paired = jnp.broadcast_to(
            slot_rows.reshape(experts, 1, capacity, D), (experts, 2, capacity, D)
        )
        return paired.reshape(devices, capacity, D)

    def from_halves(returned):
        paired = returned.reshape(experts, 2, capacity, D).astype(jnp.float32)
        summed = (paired[:, 0] + paired[:, 1]).reshape(experts * capacity, D)
        return summed[slot_of_route].reshape(tok_rows, TOP, D)

    send_rows = jnp.concatenate([ffn_in, jnp.zeros((1, D), jnp.bfloat16)])[token_of_slot]
    received = lax.all_to_all(
        to_halves(send_rows), ("dp", "ctx"), split_axis=0, concat_axis=0, tiled=True
    ).reshape(devices * capacity, D)
    expert_pre = matmul(received, w_expert_in[0])
    expert_act = (swish(expert_pre[:, :half_ff]) * expert_pre[:, half_ff:]).astype(jnp.bfloat16)
    expert_part = (
        matmul(expert_act, w_expert_out[0]).astype(jnp.bfloat16).reshape(devices, capacity, D)
    )
    returned = lax.all_to_all(expert_part, ("dp", "ctx"), split_axis=0, concat_axis=0, tiled=True)
    routed = jnp.sum(gates[:, :, None] * from_halves(returned), axis=1)
    mixed = (middle + shared_out + routed).astype(jnp.bfloat16)
    grad_out = cotangent.astype(jnp.float32)
    again = (
        lax.all_gather(norm_attn, ("dp", "ctx"), axis=0, tiled=True),
        lax.all_gather(w_query, ("dp", "ctx"), axis=0, tiled=True),
        lax.all_gather(w_kv_down, ("dp", "ctx"), axis=0, tiled=True),
        lax.all_gather(norm_latent, ("dp", "ctx"), axis=0, tiled=True),
        lax.all_gather(w_kv_up, ("dp", "ctx"), axis=0, tiled=True),
        lax.all_gather(w_out, ("dp", "ctx"), axis=0, tiled=True),
        lax.all_gather(norm_ffn, ("dp", "ctx"), axis=0, tiled=True),
        lax.all_gather(w_shared_in, ("dp", "ctx"), axis=0, tiled=True),
        lax.all_gather(w_shared_out, ("dp", "ctx"), axis=0, tiled=True),
    )
    gain_attn, query_w, down_w, gain_latent, up_w, out_w, gain_ffn, shared_in_w, shared_out_w = (
        again
    )
    slot_grads = (
        jnp.concatenate([grad_out, jnp.zeros((1, D), jnp.float32)])[token_of_slot]
        * gate_of_slot[:, None]
    )
    grad_received = lax.all_to_all(
        to_halves(slot_grads.astype(jnp.bfloat16)),
        ("dp", "ctx"),
        split_axis=0,
        concat_axis=0,
        tiled=True,
    ).reshape(devices * capacity, D)
    grad_expert_act = matmul_right_t(grad_received, w_expert_out[0])
    grad_w_expert_out = matmul_left_t(expert_act, grad_received)
    grad_expert_pre = swiglu_backward(expert_pre, grad_expert_act, half_ff)
    grad_w_expert_in = matmul_left_t(received, grad_expert_pre)
    grad_rows = (
        matmul_right_t(grad_expert_pre, w_expert_in[0])
        .astype(jnp.bfloat16)
        .reshape(devices, capacity, D)
    )
    grad_back = lax.all_to_all(grad_rows, ("dp", "ctx"), split_axis=0, concat_axis=0, tiled=True)
    grad_ffn_routed = jnp.sum(from_halves(grad_back), axis=1)
    grad_shared = grad_out.astype(jnp.bfloat16)
    grad_shared_act = matmul_right_t(grad_shared, shared_out_w)
    grad_w_shared_out = matmul_left_t(shared_act, grad_shared)
    grad_shared_pre = swiglu_backward(shared_pre, grad_shared_act, SHARED_FF)
    grad_w_shared_in = matmul_left_t(ffn_in, grad_shared_pre)
    grad_ffn = matmul_right_t(grad_shared_pre, shared_in_w) + grad_ffn_routed
    grad_middle_part, grad_norm_ffn = rms_backward(
        middle, inverse_ffn, gain_ffn.astype(jnp.float32), grad_ffn
    )
    grad_middle = grad_out + grad_middle_part
    grad_attended = grad_middle.astype(jnp.bfloat16)
    grad_w_out = matmul_left_t(heads_out, grad_attended)
    grad_heads = (
        matmul_right_t(grad_attended, out_w).astype(jnp.bfloat16).reshape(tok_rows, HEADS, VDIM)
    )
    soft_probs = jnp.exp(masked_scores() - log_total)
    grad_values = jnp.einsum(
        "hqk,qhd->khd",
        soft_probs.astype(jnp.bfloat16),
        grad_heads,
        preferred_element_type=jnp.float32,
    )
    grad_probs = jnp.einsum(
        "qhd,khd->hqk", grad_heads, key_values, preferred_element_type=jnp.float32
    )
    row_delta = jnp.sum(soft_probs * grad_probs, axis=-1, keepdims=True)
    grad_raw = (soft_probs * (grad_probs - row_delta) * scale).astype(jnp.bfloat16)
    grad_query_nope = jnp.einsum(
        "hqk,khd->qhd", grad_raw, key_nope, preferred_element_type=jnp.float32
    )
    grad_query_rope = jnp.einsum(
        "hqk,kd->qhd", grad_raw, rope_all, preferred_element_type=jnp.float32
    )
    grad_key_nope = jnp.einsum(
        "hqk,qhd->khd", grad_raw, query_nope, preferred_element_type=jnp.float32
    )
    grad_rope_terms = jnp.einsum(
        "hqk,qhd->kd", grad_raw, query_rope, preferred_element_type=jnp.float32
    )
    grad_kv_terms = jnp.concatenate([grad_key_nope, grad_values], axis=-1).reshape(
        seq_length, HEADS * (NOPE + VDIM)
    )
    grad_keyval, grad_key_rope = (
        lax.psum_scatter(
            grad_kv_terms.astype(jnp.bfloat16), "ctx", scatter_dimension=0, tiled=True
        ).astype(jnp.float32),
        lax.psum_scatter(
            grad_rope_terms.astype(jnp.bfloat16), "ctx", scatter_dimension=0, tiled=True
        ).astype(jnp.float32),
    )
    grad_keyval_low = grad_keyval.astype(jnp.bfloat16)
    grad_w_kv_up = matmul_left_t(latent, grad_keyval_low)
    grad_latent = matmul_right_t(grad_keyval_low, up_w)
    grad_compressed_latent, grad_norm_latent = rms_backward(
        compressed[:, :LATENT], inverse_latent, gain_latent.astype(jnp.float32), grad_latent
    )
    grad_compressed_rope = unrotate(grad_key_rope, cosine, sine_part)
    grad_compressed = jnp.concatenate(
        [grad_compressed_latent, grad_compressed_rope], axis=1
    ).astype(jnp.bfloat16)
    grad_w_kv_down = matmul_left_t(normed, grad_compressed)
    grad_normed = matmul_right_t(grad_compressed, down_w)
    grad_query_raw = jnp.concatenate(
        [grad_query_nope, unrotate(grad_query_rope, cosine[:, None, :], sine_part[:, None, :])],
        axis=-1,
    )
    grad_query_raw = grad_query_raw.reshape(tok_rows, HEADS * (NOPE + ROPE)).astype(jnp.bfloat16)
    grad_w_query = matmul_left_t(normed, grad_query_raw)
    grad_normed = grad_normed + matmul_right_t(grad_query_raw, query_w)
    grad_input_part, grad_norm_attn = rms_backward(
        inputs, inverse_attn, gain_attn.astype(jnp.float32), grad_normed
    )
    grad_in = grad_middle + grad_input_part
    owned = (
        lax.psum_scatter(grad_norm_attn, ("dp", "ctx"), scatter_dimension=0, tiled=True),
        lax.psum_scatter(grad_w_query, ("dp", "ctx"), scatter_dimension=0, tiled=True),
        lax.psum_scatter(grad_w_kv_down, ("dp", "ctx"), scatter_dimension=0, tiled=True),
        lax.psum_scatter(grad_norm_latent, ("dp", "ctx"), scatter_dimension=0, tiled=True),
        lax.psum_scatter(grad_w_kv_up, ("dp", "ctx"), scatter_dimension=0, tiled=True),
        lax.psum_scatter(grad_w_out, ("dp", "ctx"), scatter_dimension=0, tiled=True),
        lax.psum_scatter(grad_norm_ffn, ("dp", "ctx"), scatter_dimension=0, tiled=True),
        lax.psum_scatter(grad_w_shared_in, ("dp", "ctx"), scatter_dimension=0, tiled=True),
        lax.psum_scatter(grad_w_shared_out, ("dp", "ctx"), scatter_dimension=0, tiled=True),
    )
    return (
        mixed,
        grad_in,
        owned[0],
        owned[1],
        owned[2],
        owned[3],
        owned[4],
        owned[5],
        owned[6],
        owned[7],
        owned[8],
        grad_w_expert_in[None],
        grad_w_expert_out[None],
    )


def solution(mesh):
    return jax.shard_map(
        shards,
        mesh=mesh,
        in_specs=(
            P(("dp", "ctx"), None),
            P("dp"),
            P(("dp", "ctx"), None),
            P(("dp", "ctx"), None),
            P(("dp", "ctx"), None),
            P(("dp", "ctx")),
            P(("dp", "ctx"), None),
            P(("dp", "ctx"), None),
            P(("dp", "ctx")),
            P(("dp", "ctx"), None),
            P(("dp", "ctx"), None),
            P(("dp", "ctx")),
            P(("dp", "ctx"), None),
            P(("dp", "ctx"), None),
            P(("dp", "ctx"), None, None),
            P(("dp", "ctx"), None, None),
        ),
        out_specs=(
            P(("dp", "ctx"), None),
            P(("dp", "ctx"), None),
            P(("dp", "ctx")),
            P(("dp", "ctx"), None),
            P(("dp", "ctx"), None),
            P(("dp", "ctx")),
            P(("dp", "ctx"), None),
            P(("dp", "ctx"), None),
            P(("dp", "ctx")),
            P(("dp", "ctx"), None),
            P(("dp", "ctx"), None),
            P(("dp", "ctx"), None, None),
            P(("dp", "ctx"), None, None),
        ),
        check_vma=False,
    )
```

profile of v0, /device:TPU:0, one launch (start us, length us, event | category | flops | bytes accessed | tf_op | source)
XLA Modules:
  0.0 5556.3 jit_solution(6595942313458458563)
XLA Ops:
  11.3 42.2 all-reduce.9
  55.1 16.7 all-gather.8.cloned.1.call-done
  75.1 60.5 %all-gather.10.cloned.1.call-done = bf16[512,4096]{1,0:T(8,128)(2,1)} async-done(((bf16[16,4096]{1,0:T(8,128)(2,1)}), bf16[512,4096]{1,0:T(8,128)(2,1)}) %all-gather.10.cloned.1.call-update) | async-done | bytes 4194320 | tf_op jit(solution)/shard_map/all_gather | solution.py:142
  147.2 9.5 reduce-window.6
  167.5 10.4 all_gather.48
  177.8 49.7 all-gather.12.cloned.1.call-done
  227.5 9.9 copy.122
  244.1 6.7 copy.115
  250.8 75.5 %all-gather.14.cloned.1.call-done = bf16[2048,3072]{1,0:T(8,128)(2,1)} async-done(((bf16[64,3072]{1,0:T(8,128)(2,1)}), bf16[2048,3072]{1,0:T(8,128)(2,1)}) %all-gather.14.cloned.1.call-update) | async-done | bytes 12582928 | tf_op jit(solution)/shard_map/all_gather | solution.py:139
  326.3 8.3 fusion.132
  334.9 8.2 fusion.81
  343.1 14.3 fusion.137
  357.4 8.0 fusion.9
  366.0 8.7 fusion.62
  374.7 30.2 all-gather.16.cloned.1.call-done
  414.9 25.2 gather_fusion
  440.1 15.4 broadcast_in_dim.37
  460.6 17.4 gather_fusion.3
  480.9 25.5 gather_fusion.2
  506.5 13.2 multiply_convert_fusion
  519.7 518.8 %all-to-all-done = bf16[32,192,2048]{2,1,0:T(8,128)(2,1)} async-done(((bf16[32,192,2048]{2,1,0:T(8,128)(2,1)}), bf16[32,192,2048]{2,1,0:T(8,128)(2,1)}, u32[]{:S(2)}, u32[]{:S(2)}) %all-to-all-start) | async-done | bytes 25165856 | tf_op jit(solution)/shard_map/all_to_all | solution.py:222
  1038.4 15.3 broadcast_in_dim.39
  1058.5 43.8 fusion.19
  1102.3 637.4 %all-to-all-done.2 = bf16[32,192,2048]{2,1,0:T(8,128)(2,1)} async-done(((bf16[32,192,2048]{2,1,0:T(8,128)(2,1)}), bf16[32,192,2048]{2,1,0:T(8,128)(2,1)}, u32[]{:S(2)}, u32[]{:S(2)}) %all-to-all-start.2) | async-done | bytes 25165856 | tf_op jit(solution)/shard_map/all_to_all | solution.py:252
  1739.6 57.2 %multiply_convert_fusion.2 = (bf16[6144,704]{0,1:T(8,128)(2,1)}, bf16[6144,704]{0,1:T(8,128)(2,1)}, bf16[6144,704]{0,1:T(8,128)(2,1)}) fusion(f32[6144,1408]{0,1:T(8,128)} %fusion.19, bf16[6144,2048]{1,0:T(8,128)(2,1)} %bitcast.17, bf16[1,704,2048]{2,1,0:T(8,128)(2,1)S(1)} %copy-done), kind=kOutput, calls=%fused_computation.18 | convolution fusion | flops 17781620736 | bytes 88604672 | tf_op jit(solution)/shard_map/dot_general | solution.py:33
  1796.8 46.1 convolution_convert_fusion
  1848.0 12.8 fusion.138
  1860.8 245.5 %all-gather.20.cloned.1.call-done = bf16[2816,2048]{1,0:T(8,128)(2,1)} async-done(((bf16[88,2048]{1,0:T(8,128)(2,1)}), bf16[2816,2048]{1,0:T(8,128)(2,1)}) %all-gather.20.cloned.1.call-update) | async-done | bytes 11534352 | tf_op jit(solution)/shard_map/all_gather | solution.py:146
  2106.3 12.3 multiply_convert_fusion.6
  2118.7 359.2 %all-to-all-done.3 = bf16[32,192,2048]{2,1,0:T(8,128)(2,1)} async-done(((bf16[32,192,2048]{2,1,0:T(8,128)(2,1)}), bf16[32,192,2048]{2,1,0:T(8,128)(2,1)}, u32[]{:S(2)}, u32[]{:S(2)}) %all-to-all-start.3) | async-done | bytes 25165856 | tf_op jit(solution)/shard_map/all_to_all | solution.py:268
  2477.9 27.4 convert.74
  2505.3 25.2 fusion.1
  2530.5 20.7 gather_fusion.4
  2551.2 15.0 reshape.316
  2566.2 9.8 reduce_sum.135
  2576.1 14.8 multiply_reduce_fusion.2
  2604.4 10.7 fusion.139
  2615.1 8.8 convert_bitcast_fusion
  2623.9 37.9 fusion.74
  2661.8 32.4 convert_bitcast_fusion.1
  2694.3 8.1 pad_maximum_fusion.5
  2702.4 12.6 fusion.141
  2715.2 21.2 fusion.56
  2737.8 66.1 %reduce-scatter.9.cloned.1.call-done = bf16[256,4096]{0,1:T(8,128)(2,1)} async-done(((bf16[1024,4096]{0,1:T(8,128)(2,1)}), bf16[256,4096]{0,1:T(8,128)(2,1)}) %reduce-scatter.9.cloned.1.call-update) | async-done | bytes 2097168 | tf_op jit(solution)/shard_map/reduce_scatter | solution.py:313
  2819.3 10.1 fusion.78
  2829.5 27.0 convolution_convert_fusion.1
  2862.0 37.8 fusion.68
  2901.1 35.8 fusion.63
  2939.4 11.5 fusion.130
  2951.0 25.1 convolution_bitcast_fusion
  2976.1 48.5 fusion.12
  3024.5 497.8 %all-to-all-done.1 = bf16[32,192,2048]{2,1,0:T(8,128)(2,1)} async-done(((bf16[32,192,2048]{2,1,0:T(8,128)(2,1)}), bf16[32,192,2048]{2,1,0:T(8,128)(2,1)}, u32[]{:S(2)}, u32[]{:S(2)}) %all-to-all-start.1) | async-done | bytes 25165856 | tf_op jit(solution)/shard_map/all_to_all | solution.py:230
  3522.3 27.4 convert.73
  3549.7 25.7 fusion.2
  3575.5 21.1 gather_fusion.1
  3596.5 15.0 reshape.311
  3611.5 9.3 multiply_reduce_fusion.1
  3627.7 8.6 fusion.44
  3639.1 47.9 all-reduce.8
  3693.3 908.4 %reduce-scatter.21.cloned.1.call-done = f32[64,5632]{1,0:T(8,128)} async-done(((f32[2048,5632]{1,0:T(8,128)}), f32[64,5632]{1,0:T(8,128)}) %reduce-scatter.21.cloned.1.call-update) | async-done | bytes 1441808 | tf_op jit(solution)/shard_map/reduce_scatter | solution.py:351
  4601.7 148.9 %reduce-scatter.15.cloned.1.call-done = f32[64,576]{1,0:T(8,128)} async-done(((f32[2048,576]{1,0:T(8,128)}), f32[64,576]{1,0:T(8,128)}) %reduce-scatter.15.cloned.1.call-update) | async-done | bytes 147472 | tf_op jit(solution)/shard_map/reduce_scatter | solution.py:346
  4750.6 183.9 %reduce-scatter.17.cloned.1.call-done = f32[16,4096]{1,0:T(8,128)} async-done(((f32[512,4096]{1,0:T(8,128)}), f32[16,4096]{1,0:T(8,128)}) %reduce-scatter.17.cloned.1.call-update) | async-done | bytes 262160 | tf_op jit(solution)/shard_map/reduce_scatter | solution.py:348
  4934.5 361.4 %reduce-scatter.19.cloned.1.call-done = f32[64,2048]{1,0:T(8,128)} async-done(((f32[2048,2048]{1,0:T(8,128)}), f32[64,2048]{1,0:T(8,128)}) %reduce-scatter.19.cloned.1.call-update) | async-done | bytes 524304 | tf_op jit(solution)/shard_map/reduce_scatter | solution.py:349
  5295.9 253.7 %reduce-scatter.13.cloned.1.call-done = f32[64,3072]{1,0:T(8,128)} async-done(((f32[2048,3072]{1,0:T(8,128)}), f32[64,3072]{1,0:T(8,128)}) %reduce-scatter.13.cloned.1.call-update) | async-done | bytes 786448 | tf_op jit(solution)/shard_map/reduce_scatter | solution.py:345
  (252 shorter events, 121.8 us)
Async XLA Ops:
  7.2 1732.4 %copy-start = (bf16[1,704,2048]{2,1,0:T(8,128)(2,1)S(1)}, bf16[1,704,2048]{2,1,0:T(8,128)(2,1)}, u32[]{:S(2)}) copy-start(bf16[1,704,2048]{2,1,0:T(8,128)(2,1)} %param.31) | copy-start | bytes 8650756
  7.2 134.5 %copy-start.54 = (s32[256,6]{0,1:T(8,128)S(1)}, s32[256,6]{0,1:T(8,128)}, u32[]{:S(2)}) copy-start(s32[256,6]{0,1:T(8,128)} %param.18) | copy-start | bytes 18436
  7.2 64.6 %all-gather.8.cloned.1.call-start = ((), (), s32[]{:S(2)}) async-start(), calls=%async_computation.12 | async-start | bytes 2703360 | tf_op jit(solution)/shard_map/all_gather | solution.py:140
  7.9 127.7 %all-gather.10.cloned.1.call-start = ((), (), s32[]{:S(2)}) async-start(), calls=%async_computation.13 | async-start | bytes 4325376 | tf_op jit(solution)/shard_map/all_gather | solution.py:142
  8.7 218.8 %all-gather.12.cloned.1.call-start = ((), (), s32[]{:S(2)}) async-start(), calls=%async_computation.14 | async-start | bytes 10485760 | tf_op jit(solution)/shard_map/all_gather | solution.py:165
  53.6 93.6 %copy-start.41 = (f32[512]{0:T(512)}, f32[512]{0:T(512)S(1)}, u32[]{:S(2)}) copy-start(f32[512]{0:T(512)S(1)} %convert_element_type.132) | copy-start | bytes 6148
  53.6 272.8 %copy-start.27 = (f32[2048]{0:T(1024)}, f32[2048]{0:T(1024)S(1)}, u32[]{:S(2)}) copy-start(f32[2048]{0:T(1024)S(1)} %convert_element_type.130) | copy-start | bytes 24580
  53.6 104.6 %copy-start.63 = (s32[1024]{0:T(1024)S(1)}, s32[1024]{0:T(1024)}, u32[]{:S(2)}) copy-start(s32[1024]{0:T(1024)} %param.17) | copy-start | bytes 12292
  55.1 111.1 %copy-start.49 = (f32[256]{0:T(256)}, f32[256]{0:T(256)S(1)}, u32[]{:S(2)}) copy-start(f32[256]{0:T(256)S(1)} %add_rsqrt_fusion.2) | copy-start | bytes 3076
  75.0 162.4 %copy-start.9 = (f32[256,576]{0,1:T(8,128)}, f32[256,576]{0,1:T(8,128)S(1)}, u32[]{:S(2)}) copy-start(f32[256,576]{0,1:T(8,128)S(1)} %fusion.134) | copy-start | bytes 1769476
  75.1 67.4 %copy-start.57 = (f32[256]{0:T(256)}, f32[256]{0:T(256)S(1)}, u32[]{:S(2)}) copy-start(f32[256]{0:T(256)S(1)} %add_rsqrt_fusion.1) | copy-start | bytes 3076
  140.5 185.8 %all-gather.14.cloned.1.call-start = ((), (), s32[]{:S(2)}) async-start(), calls=%async_computation.15 | async-start | bytes 12976128 | tf_op jit(solution)/shard_map/all_gather | solution.py:139
  141.1 263.8 %all-gather.16.cloned.1.call-start = ((), (), s32[]{:S(2)}) async-start(), calls=%async_computation.16 | async-start | bytes 8650752 | tf_op jit(solution)/shard_map/all_gather | solution.py:143
  144.6 266.7 %copy-start.45 = (f32[2048]{0:T(1024)}, f32[2048]{0:T(1024)S(1)}, u32[]{:S(2)}) copy-start(f32[2048]{0:T(1024)S(1)} %convert_element_type.140) | copy-start | bytes 24580
  167.4 167.3 %copy-start.30 = (f32[256,32]{0,1:T(8,128)}, f32[256,32]{0,1:T(8,128)S(1)}, u32[]{:S(2)}) copy-start(f32[256,32]{0,1:T(8,128)S(1)} %get-tuple-element.43) | copy-start | bytes 98308
  167.4 167.3 %copy-start.32 = (f32[256,32]{0,1:T(8,128)}, f32[256,32]{0,1:T(8,128)S(1)}, u32[]{:S(2)}) copy-start(f32[256,32]{0,1:T(8,128)S(1)} %get-tuple-element.44) | copy-start | bytes 98308
  244.1 82.3 %copy-start.50 = (f32[256]{0:T(256)S(1)}, f32[256]{0:T(256)}, u32[]{:S(2)}) copy-start(f32[256]{0:T(256)} %copy-done.49) | copy-start | bytes 3076
  250.8 84.1 %copy-start.25 = (bf16[1024,64]{0,1:T(8,128)(2,1)S(1)}, bf16[1024,64]{0,1:T(8,128)(2,1)}, u32[]{:S(2)}) copy-start(bf16[1024,64]{0,1:T(8,128)(2,1)} %all_gather.48) | copy-start | bytes 393220
  404.9 10.0 copy-start.40
  411.3 28.8 copy-start.59
  455.4 583.0 %all-to-all-start = ((bf16[32,192,2048]{2,1,0:T(8,128)(2,1)}), bf16[32,192,2048]{2,1,0:T(8,128)(2,1)}, u32[]{:S(2)}, u32[]{:S(2)}) async-start(bf16[32,192,2048]{2,1,0:T(8,128)(2,1)} %bitcast.135), calls=%async_computation | async-start | bytes 50331648 | tf_op jit(solution)/shard_map/all_to_all | solution.py:222
  1053.8 685.8 %all-to-all-start.2 = ((bf16[32,192,2048]{2,1,0:T(8,128)(2,1)}), bf16[32,192,2048]{2,1,0:T(8,128)(2,1)}, u32[]{:S(2)}, u32[]{:S(2)}) async-start(bf16[32,192,2048]{2,1,0:T(8,128)(2,1)} %bitcast.136), calls=%async_computation.2 | async-start | bytes 50331648 | tf_op jit(solution)/shard_map/all_to_all | solution.py:252
  1057.9 790.1 %all-gather.18.cloned.1.call-start = ((), (), s32[]{:S(2)}) async-start(), calls=%async_computation.17 | async-start | bytes 23789568 | tf_op jit(solution)/shard_map/all_gather | solution.py:145
  1842.9 635.0 %all-to-all-start.3 = ((bf16[32,192,2048]{2,1,0:T(8,128)(2,1)}), bf16[32,192,2048]{2,1,0:T(8,128)(2,1)}, u32[]{:S(2)}, u32[]{:S(2)}) async-start(bf16[32,192,2048]{2,1,0:T(8,128)(2,1)} %bitcast.142), calls=%async_computation.3 | async-start | bytes 50331648 | tf_op jit(solution)/shard_map/all_to_all | solution.py:268
  1847.1 259.2 %all-gather.20.cloned.1.call-start = ((), (), s32[]{:S(2)}) async-start(), calls=%async_computation.18 | async-start | bytes 11894784 | tf_op jit(solution)/shard_map/all_gather | solution.py:146
  1847.9 888.9 %reduce-scatter.11.cloned.1.call-start = ((), (), s32[]{:S(2)}) async-start(), calls=%async_computation.20 | async-start | bytes 163840 | tf_op jit(solution)/shard_map/reduce_scatter | solution.py:316
  1848.0 682.5 %copy-start.43 = (s32[2048]{0:T(1024)}, s32[2048]{0:T(1024)S(1)}, u32[]{:S(2)}) copy-start(s32[2048]{0:T(1024)S(1)} %pad_clamp_fusion) | copy-start | bytes 24580
  2566.2 9.8 copy-start.46
  2566.2 9.8 copy-start.60
  2604.4 10.7 copy-start.7
  2615.1 8.8 copy-start.21
  2615.1 8.8 copy-start.23
  2694.2 109.6 %reduce-scatter.9.cloned.1.call-start = ((), (), s32[]{:S(2)}) async-start(), calls=%async_computation.19 | async-start | bytes 10485760 | tf_op jit(solution)/shard_map/reduce_scatter | solution.py:313
  2702.4 990.9 %reduce-scatter.23.cloned.1.call-start = ((), (), s32[]{:S(2)}) async-start(), calls=%async_computation.26 | async-start | bytes 23789568 | tf_op jit(solution)/shard_map/reduce_scatter | solution.py:352
  2715.1 1886.6 %reduce-scatter.21.cloned.1.call-start = ((), (), s32[]{:S(2)}) async-start(), calls=%async_computation.25 | async-start | bytes 47579136 | tf_op jit(solution)/shard_map/reduce_scatter | solution.py:351
  2736.4 67.5 %copy-start.10 = (f32[256,576]{0,1:T(8,128)S(1)}, f32[256,576]{0,1:T(8,128)}, u32[]{:S(2)}) copy-start(f32[256,576]{0,1:T(8,128)} %copy-done.9) | copy-start | bytes 1769476
  2736.4 67.5 %copy-start.42 = (f32[512]{0:T(512)S(1)}, f32[512]{0:T(512)}, u32[]{:S(2)}) copy-start(f32[512]{0:T(512)} %copy-done.41) | copy-start | bytes 6148
  2736.4 67.5 %copy-start.58 = (f32[256]{0:T(256)S(1)}, f32[256]{0:T(256)}, u32[]{:S(2)}) copy-start(f32[256]{0:T(256)} %copy-done.57) | copy-start | bytes 3076
  2736.5 73.1 %copy-start.28 = (f32[2048]{0:T(1024)S(1)}, f32[2048]{0:T(1024)}, u32[]{:S(2)}) copy-start(f32[2048]{0:T(1024)} %copy-done.27) | copy-start | bytes 24580
  2736.5 73.1 %copy-start.51 = (f32[256]{0:T(256)S(1)}, f32[256]{0:T(256)}, u32[]{:S(2)}) copy-start(f32[256]{0:T(256)} %copy-done.49) | copy-start | bytes 3076
  2736.5 2014.1 %reduce-scatter.15.cloned.1.call-start = ((), (), s32[]{:S(2)}) async-start(), calls=%async_computation.22 | async-start | bytes 5406720 | tf_op jit(solution)/shard_map/reduce_scatter | solution.py:346
  2737.7 75.2 %copy-start.34 = (bf16[256,32]{0,1:T(8,128)(2,1)}, bf16[256,32]{0,1:T(8,128)(2,1)S(1)}, u32[]{:S(2)}) copy-start(bf16[256,32]{0,1:T(8,128)(2,1)S(1)} %get-tuple-element.39) | copy-start | bytes 49156
  2737.7 75.2 %copy-start.36 = (bf16[256,32]{0,1:T(8,128)(2,1)}, bf16[256,32]{0,1:T(8,128)(2,1)S(1)}, u32[]{:S(2)}) copy-start(bf16[256,32]{0,1:T(8,128)(2,1)S(1)} %get-tuple-element.40) | copy-start | bytes 49156
  2813.0 2121.5 %reduce-scatter.17.cloned.1.call-start = ((), (), s32[]{:S(2)}) async-start(), calls=%async_computation.23 | async-start | bytes 8650752 | tf_op jit(solution)/shard_map/reduce_scatter | solution.py:348
  2819.2 2476.6 %reduce-scatter.19.cloned.1.call-start = ((), (), s32[]{:S(2)}) async-start(), calls=%async_computation.24 | async-start | bytes 17301504 | tf_op jit(solution)/shard_map/reduce_scatter | solution.py:349
  2856.4 665.9 %all-to-all-start.1 = ((bf16[32,192,2048]{2,1,0:T(8,128)(2,1)}), bf16[32,192,2048]{2,1,0:T(8,128)(2,1)}, u32[]{:S(2)}, u32[]{:S(2)}) async-start(bf16[32,192,2048]{2,1,0:T(8,128)(2,1)} %bitcast.141), calls=%async_computation.1 | async-start | bytes 50331648 | tf_op jit(solution)/shard_map/all_to_all | solution.py:230
  2861.5 38.3 copy-start.31
  2861.5 38.3 copy-start.33
  2861.5 2688.1 %reduce-scatter.13.cloned.1.call-start = ((), (), s32[]{:S(2)}) async-start(), calls=%async_computation.21 | async-start | bytes 25952256 | tf_op jit(solution)/shard_map/reduce_scatter | solution.py:345
  2950.9 25.1 slice-start
  2951.0 25.1 slice-start.1
  2951.0 25.1 slice-start.2
  3549.7 25.7 copy-start.44
  3596.5 15.0 copy-start.19
  3611.5 9.3 copy-start.12
  3627.6 8.7 copy-start.2
  3627.6 8.7 copy-start.15
  3627.6 8.7 copy-start.17
  3627.6 8.6 copy-start.29
  3627.6 8.6 copy-start.35
  3627.6 8.6 copy-start.37
  3627.6 8.6 copy-start.52
  3627.6 11.4 copy-start.62
  3627.7 11.4 copy-start.68
  (27 other events, 118.7 us)
Sparse Core Ops, SparseCore 0:
  10.9 60.8 all-gather.7
  74.6 60.9 all-gather.9
  140.6 86.8 all-gather.11
  230.3 96.0 all-gather.13
  329.0 75.8 all-gather.15
  1061.3 397.8 all-gather.17
  1850.8 255.4 all-gather.19
  2694.3 19.7 reduce-scatter.10
  2717.5 86.3 reduce-scatter.8
  2806.6 793.8 reduce-scatter.22
  3603.4 998.2 reduce-scatter.20
  4604.4 146.1 reduce-scatter.14
  4753.4 181.0 reduce-scatter.16
  4937.2 358.6 reduce-scatter.18
  5302.7 246.7 reduce-scatter.12
where the time goes:
time: 5570 us; the launch traced here: 5560 us
  waiting for transfers between devices  4420 us (79%)
  matrix products  599 us (11%)
  local copies, waits for them, and re-layouts  224 us (4%)
  other arithmetic  181 us (3%)
  blocking collectives  100 us (2%)
    reduce_scatter x1, waiting for transfers between devices, shards(): lax.psum_scatter(grad_w_shared_in, ('dp', 'ctx'), scatter_dimension=0, ti...  908 us
    all_to_all x1, waiting for transfers between devices, shards(): lax.all_to_all(to_halves(slot_grads.astype(jnp.bfloat16)), ('dp', 'ctx'),...  637 us
    all_to_all x1, waiting for transfers between devices, shards(): lax.all_to_all(to_halves(send_rows), ('dp', 'ctx'), split_axis=0, concat_...  519 us
    all_to_all x1, waiting for transfers between devices, shards(): lax.all_to_all(expert_part, ('dp', 'ctx'), split_axis=0, concat_axis=0, t...  498 us
    reduce_scatter x1, waiting for transfers between devices, shards(): lax.psum_scatter(grad_w_out, ('dp', 'ctx'), scatter_dimension=0, tiled=True)  361 us
    all_to_all x1, waiting for transfers between devices, shards(): lax.all_to_all(grad_rows, ('dp', 'ctx'), split_axis=0, concat_axis=0, til...  359 us
    reduce_scatter x1, waiting for transfers between devices, shards(): lax.psum_scatter(grad_w_query, ('dp', 'ctx'), scatter_dimension=0, tiled=...  254 us
    all_gather x1, waiting for transfers between devices, shards(): lax.all_gather(w_shared_out, ('dp', 'ctx'), axis=0, tiled=True)  246 us
  transfers between devices with their start and end apart: 19, of which 16 were waited for; matrix products, arithmetic and copies ran while one was open for 13% of the time, Pallas kernels for 0%

commit v1 on v0

v1 whole, which is shorter than its diff:
```python
import math

import jax
import jax.numpy as jnp
from jax import lax
from jax.experimental import pallas as pl
from jax.experimental.pallas import tpu as pltpu
from jax.sharding import PartitionSpec as P

D = 2048
HEADS = 16
NOPE = 128
ROPE = 64
VDIM = 128
LATENT = 512
EXPERT_FF = 1408
SHARED_FF = 2816
TOP = 6

BOTH = ("dp", "ctx")
epsilon = 1e-06
f32 = jnp.float32
bf16 = jnp.bfloat16


def matmul(left, right):
    return jnp.dot(left, right, preferred_element_type=f32)


def matmul_left_t(left, right):
    return lax.dot_general(left, right, (((0,), (0,)), ((), ())), preferred_element_type=f32)


def matmul_right_t(left, right):
    return lax.dot_general(left, right, (((1,), (1,)), ((), ())), preferred_element_type=f32)


def rope_tables(positions, rope_width):
    half_width = rope_width // 2
    frequency = jnp.exp(
        -math.log(10000.0) * jnp.arange(half_width).astype(f32) / half_width
    )
    angles = positions.astype(f32)[:, None] * frequency[None, :]
    return (jnp.cos(angles), jnp.sin(angles))


def rotate(operand, cosine, sine_part):
    half_width = operand.shape[-1] // 2
    first_half = operand[..., :half_width]
    second_half = operand[..., half_width:]
    return jnp.concatenate(
        [
            first_half * cosine - second_half * sine_part,
            second_half * cosine + first_half * sine_part,
        ],
        axis=-1,
    )


def unrotate(operand, cosine, sine_part):
    return rotate(operand, cosine, -sine_part)


def swish(operand):
    return operand * jax.nn.sigmoid(operand)


def swish_slope(operand):
    sigma = jax.nn.sigmoid(operand)
    return sigma * (1.0 + operand * (1.0 - sigma))


def rms_inverse(operand):
    return lax.rsqrt(jnp.mean(operand * operand, axis=-1, keepdims=True) + epsilon)


def rms_backward(operand, inverse, gain_vec, grad_out):
    scaled = grad_out * gain_vec
    grad_gain = jnp.sum(grad_out * operand * inverse, axis=0)
    grad_operand = inverse * scaled - operand * inverse * inverse * inverse * jnp.mean(
        scaled * operand, axis=-1, keepdims=True
    )
    return (grad_operand, grad_gain)


class Links:
    def __init__(self):
        self.dp = lax.axis_size("dp")
        self.ctx = lax.axis_size("ctx")
        self.size = {"z": self.dp // 2, "c": 2, "y": self.ctx // 2, "x": 2}
        dp, ctx = lax.axis_index("dp"), lax.axis_index("ctx")
        self.own = {"z": dp // 2, "c": dp % 2, "y": ctx // 2, "x": ctx % 2}

    def shift(self, value, axis, by):
        if axis in "zc":
            name, count = "dp", self.dp
        else:
            name, count = "ctx", self.ctx
        if axis in "zy":
            pairs = [(i, (i + 2 * by) % count) for i in range(count)]
        else:
            pairs = [(i, i ^ 1) for i in range(count)]
        return lax.ppermute(value, name, pairs)

    def shift_ctx(self, value, ky, kx):
        pairs = [
            (i, ((i // 2 - ky) % (self.ctx // 2)) * 2 + (i + kx) % 2) for i in range(self.ctx)
        ]
        return lax.ppermute(value, "ctx", pairs)

    def ring(self, block, axis):
        held = [block]
        for _ in range(self.size[axis] - 1):
            held.append(self.shift(held[-1], axis, 1))
        return held

    def gather(self, block, order):
        for axis in order:
            block = jnp.concatenate(self.ring(block, axis), axis=0)
        return block

    def reduce(self, parts, axis):
        total = parts[-1]
        for part in parts[-2::-1]:
            moved = self.shift(total, axis, -1)
            total = (moved.astype(f32) + part.astype(f32)).astype(bf16)
        return total

    def scatter_sum(self, block, order):
        for axis in order[::-1]:
            count = self.size[axis]
            rows = block.shape[0] // count
            block = self.reduce([block[k * rows : (k + 1) * rows] for k in range(count)], axis)
        return block

    def device_of(self, order):
        place = dict(self.own)
        depth = len(order)
        for i, axis in enumerate(order):
            shape = [1] * depth
            shape[depth - 1 - i] = self.size[axis]
            offsets = jnp.arange(self.size[axis], dtype=jnp.int32).reshape(shape)
            place[axis] = (self.own[axis] - offsets) % self.size[axis]
        number = ((place["z"] * 2 + place["c"]) * self.size["y"] + place["y"]) * 2 + place["x"]
        return number.reshape(-1)

    def place_of(self, order):
        count = self.dp * self.ctx
        number = jnp.arange(count, dtype=jnp.int32)
        coordinate = {
            "x": number % 2,
            "y": (number // 2) % self.size["y"],
            "c": (number // self.ctx) % 2,
            "z": number // (2 * self.ctx),
        }
        place = jnp.zeros_like(number)
        for axis in order[::-1]:
            steps = (self.own[axis] - coordinate[axis]) % self.size[axis]
            place = place * self.size[axis] + steps
        return place

    def ctx_relative(self):
        y = (self.own["y"] - jnp.arange(self.size["y"], dtype=jnp.int32)) % self.size["y"]
        x = (self.own["x"] - jnp.arange(2, dtype=jnp.int32)) % 2
        return (y[:, None] * 2 + x[None, :]).reshape(-1)

    def ctx_exchange(self, pieces):
        ny = self.size["y"]
        result = [pieces[0]] + [None] * (self.ctx - 1)
        for k in range(1, self.ctx):
            ky, kx = k // 2, k % 2
            result[((-ky) % ny) * 2 + kx] = self.shift_ctx(pieces[k], ky, kx)
        return result

    def ctx_gather(self, block):
        half = block.shape[0] // 2
        ny = self.size["y"]
        first = self.ring(block[:half], "x")
        first = self.ring(jnp.concatenate(first, axis=0), "y")
        second = self.ring(block[half:], "y")
        second = self.ring(jnp.concatenate(second, axis=0), "x")
        pieces = []
        for ky in range(ny):
            for kx in range(2):
                pieces.append(first[ky][kx * half : (kx + 1) * half])
                pieces.append(second[kx][ky * half : (ky + 1) * half])
        return jnp.concatenate(pieces, axis=0)


def after(value, *others):
    return lax.optimization_barrier((value,) + others)[0]


GROUP = 4


def ffn_kernel(half_ff, adds, devices_ref, x_ref, *refs):
    g_refs, (m_ref, w_in, w_out) = refs[:GROUP], refs[GROUP : GROUP + 3]
    refs = refs[GROUP + 3 :]
    if adds:
        add_out, add_grad = refs[:2]
    x_all, g_all, act, grad_pre, out, row_grad = refs[-6:]
    half_all = act.shape[1]
    count = x_ref.shape[0] // GROUP
    x_all[...] = x_ref[...]
    for i, g_ref in enumerate(g_refs):
        g_all[i * count : (i + 1) * count] = g_ref[0]
    pre = matmul(x_ref[...], w_in[...])
    gate, up = pre[:, :half_all], pre[:, half_all:]
    column = lax.broadcasted_iota(jnp.int32, (1, half_all), 1)
    weight = jnp.where(column < half_ff, m_ref[...], 1.0)
    sigma = jax.nn.sigmoid(gate)
    swished = gate * sigma
    act[...] = (swished * up * weight).astype(bf16)
    grad_act = matmul_right_t(g_all[...], w_out[...]) * weight
    slope = sigma * (1.0 + gate * (1.0 - sigma))
    grad_pre[:, :half_all] = (grad_act * up * slope).astype(bf16)
    grad_pre[:, half_all:] = (grad_act * swished).astype(bf16)
    out_part = matmul(act[...], w_out[...])
    grad_part = matmul_right_t(grad_pre[...], w_in[...])
    if adds:
        out_part = out_part + add_out[...].astype(f32)
        grad_part = grad_part + add_grad[...].astype(f32)
    out[...] = out_part.astype(bf16)
    row_grad[...] = grad_part.astype(bf16)


def ffn_chunk(x, g_blocks, m, w_in, w_out, half_ff, source, place, kept, start, tokens, adds):
    half_all = w_out.shape[0]
    count = x.shape[0] // source.shape[0]
    tile = GROUP * count
    steps = x.shape[0] // tile
    base = start // tile

    def rows(width, first=0):
        return pl.BlockSpec((tile, width), lambda i, _: (first + i, 0))

    def whole(value):
        return pl.BlockSpec(value.shape, lambda i, _: (0, 0), pipeline_mode=pl.Buffered(1))

    def g_spec(j):
        return pl.BlockSpec((1, count, D), lambda i, s: (s[GROUP * i + j], place, 0))

    operands = [source, x] + [g_blocks] * GROUP + [m, w_in, w_out]
    in_specs = [rows(D)] + [g_spec(j) for j in range(GROUP)]
    in_specs += [rows(1), whole(w_in), whole(w_out)]
    if adds is not None:
        operands += adds
        in_specs += [rows(D)] * 2
    aliases = {}
    if kept is not None:
        aliases = {len(operands) + i: i for i in range(4)}
        operands += kept
        in_specs += [pl.BlockSpec(memory_space=pl.ANY)] * 4
    widths = (D, D, half_all, 2 * half_all)
    out_shape = [jax.ShapeDtypeStruct((tokens, w), bf16) for w in widths]
    out_shape += [jax.ShapeDtypeStruct(x.shape, bf16)] * 2
    flops = 2 * x.shape[0] * D * 6 * half_all
    result = pl.pallas_call(
        lambda *refs: ffn_kernel(half_ff, adds is not None, *refs),
        grid_spec=pltpu.PrefetchScalarGridSpec(
            num_scalar_prefetch=1,
            grid=(steps,),
            in_specs=in_specs,
            out_specs=[rows(w, base) for w in widths] + [rows(D)] * 2,
        ),
        out_shape=out_shape,
        input_output_aliases=aliases,
        compiler_params=pltpu.CompilerParams(vmem_limit_bytes=60 * 2**20),
        cost_estimate=pl.CostEstimate(
            flops=flops, bytes_accessed=x.shape[0] * D * 16, transcendentals=0
        ),
        name="ffn_chunk",
    )(*operands)
    return result[:4], result[4], result[5]


def shards(
    hidden_in,
    segments,
    routes,
    gates,
    cotangent,
    norm_attn,
    w_query,
    w_kv_down,
    norm_latent,
    w_kv_up,
    w_out,
    norm_ffn,
    w_shared_in,
    w_shared_out,
    w_expert_in,
    w_expert_out,
):
    links = Links()
    tok = hidden_in.shape[0]
    row = segments.shape[0]
    ctx = links.ctx
    devices = links.dp * ctx
    me = lax.axis_index("dp") * ctx + lax.axis_index("ctx")
    half_ff = EXPERT_FF // 2
    half_sh = w_shared_out.shape[0]
    half_all = -(-(half_ff + half_sh) // 128) * 128
    heads = HEADS // ctx
    q_cols = heads * (NOPE + ROPE)
    v_cols = heads * VDIM
    kv_cols = heads * (NOPE + VDIM)
    dn_cols = (LATENT + ROPE) // ctx
    rows_d = w_query.shape[0]
    rows_l = w_kv_up.shape[0]
    up_fold = rows_l * kv_cols // rows_d
    up_parts = rows_d // rows_l
    scale = 1.0 / math.sqrt(NOPE + ROPE)
    rel_ctx = links.ctx_relative()
    ctx_number = jnp.arange(ctx, dtype=jnp.int32)
    ctx_place = ((links.own["y"] - ctx_number // 2) % links.size["y"]) * 2 + (
        links.own["x"] - ctx_number
    ) % 2

    def columns(value, k, width):
        return lax.dynamic_slice_in_dim(value, rel_ctx[k] * width, width, 1)

    hidden_row = links.ctx_gather(hidden_in)
    latent_gain = jnp.zeros((rows_d,), bf16).at[:rows_l].set(norm_latent)
    small = jnp.concatenate(
        [w_kv_down, norm_attn[:, None], norm_ffn[:, None], latent_gain[:, None]], axis=1
    )
    small = jnp.pad(small, ((0, 0), (0, -small.shape[1] % 128)))
    small_order = ("z", "x", "y", "c")
    small_all = links.gather(small, small_order).reshape(devices, rows_d, small.shape[1])
    small_all = small_all[links.place_of(small_order)]
    down_w = small_all[:, :, : LATENT + ROPE].reshape(D, LATENT + ROPE)
    gain_attn = small_all[:, :, LATENT + ROPE].reshape(D).astype(f32)
    gain_ffn = small_all[:, :, LATENT + ROPE + 1].reshape(D).astype(f32)
    gain_latent = small_all[:, :rows_l, LATENT + ROPE + 2].reshape(LATENT).astype(f32)

    pieces = []
    for k in range(ctx):
        folded = columns(w_kv_up, k, kv_cols).reshape(rows_l, up_parts, up_fold)
        folded = folded.transpose(1, 0, 2).reshape(rows_d, up_fold)
        pieces.append(jnp.concatenate([columns(w_query, k, q_cols), folded], axis=1))
    heads_w = jnp.concatenate(links.ctx_exchange(pieces), axis=0)
    heads_w = links.gather(heads_w, ("z", "c")).reshape(devices, rows_d, q_cols + up_fold)
    heads_place = links.place_of(("x", "y", "z", "c"))
    heads_w = heads_w[heads_place]
    query_w = heads_w[:, :, :q_cols].reshape(D, q_cols)
    up_w = heads_w[:, :, q_cols:].reshape(devices, up_parts, rows_l, up_fold)
    up_w = up_w.transpose(0, 2, 1, 3).reshape(LATENT, kv_cols)

    experts = devices // 2
    expert_number = jnp.arange(experts, dtype=jnp.int32)[:, None, None]
    gate_matrix = jnp.sum(
        jnp.where(routes.T[None] == expert_number, gates.T[None], 0.0), axis=1
    )
    m_all = lax.all_to_all(
        jnp.repeat(gate_matrix, 2, axis=0), BOTH, split_axis=0, concat_axis=0, tiled=True
    )
    out_w = lax.all_gather(after(w_out, heads_w, hidden_row), BOTH, axis=0, tiled=True)
    g_all = lax.all_gather(after(cotangent, out_w), BOTH, axis=0, tiled=True)
    g_blocks = g_all.reshape(devices, tok, D)

    inputs_row = hidden_row.astype(f32)
    inverse_row = rms_inverse(inputs_row)
    normed_row = (inputs_row * inverse_row * gain_attn).astype(bf16)
    positions = (rel_ctx[:, None] * tok + jnp.arange(tok, dtype=jnp.int32)[None, :]).reshape(-1)
    row_segments = segments.reshape(ctx, tok)[rel_ctx].reshape(-1)
    allowed = (positions[None, :] <= positions[:, None]) & (
        row_segments[None, :] == row_segments[:, None]
    )
    cosine, sine_part = rope_tables(positions, ROPE)
    query_raw = matmul(normed_row, query_w).reshape(row, heads, NOPE + ROPE)
    query = jnp.concatenate(
        [
            query_raw[..., :NOPE],
            rotate(query_raw[..., NOPE:], cosine[:, None, :], sine_part[:, None, :]),
        ],
        axis=-1,
    ).astype(bf16)
    query = query.transpose(1, 0, 2)
    compressed = matmul(normed_row, down_w)
    raw_latent = compressed[:, :LATENT]
    inverse_latent = rms_inverse(raw_latent)
    latent = (raw_latent * inverse_latent * gain_latent).astype(bf16)
    key_rope = rotate(compressed[:, LATENT:], cosine, sine_part).astype(bf16)
    keyval = matmul(latent, up_w).astype(bf16).reshape(row, heads, NOPE + VDIM)
    keyval = keyval.transpose(1, 0, 2)
    key = jnp.concatenate(
        [keyval[..., :NOPE], jnp.broadcast_to(key_rope[None], (heads, row, ROPE))], axis=-1
    )
    value = keyval[..., NOPE:]

    def masked_scores():
        raw = jnp.einsum("hqd,hkd->hqk", query, key, preferred_element_type=f32)
        return jnp.where(allowed[None], raw * scale, -1e30)

    scores = masked_scores()
    row_max = jnp.max(scores, axis=-1, keepdims=True)
    exponent = jnp.exp(scores - row_max)
    row_total = jnp.sum(exponent, axis=-1, keepdims=True)
    log_total = row_max + jnp.log(row_total)
    probs = (exponent / row_total).astype(bf16)
    heads_part = jnp.einsum("hqk,hkd->qhd", probs, value, preferred_element_type=f32)
    heads_part = heads_part.astype(bf16).reshape(ctx, tok, v_cols)
    returned = jnp.stack(links.ctx_exchange([heads_part[k] for k in range(ctx)]))
    heads_out = returned[ctx_place].transpose(1, 0, 2).reshape(tok, HEADS * VDIM)
    inputs = hidden_in.astype(f32)
    middle = inputs + matmul(heads_out, out_w)
    inverse_ffn = rms_inverse(middle)
    ffn_in = (middle * inverse_ffn * gain_ffn).astype(bf16)

    shared_pieces = jnp.concatenate(
        [
            w_shared_in[:, :SHARED_FF].reshape(rows_d, devices, half_sh),
            w_shared_in[:, SHARED_FF:].reshape(rows_d, devices, half_sh),
        ],
        axis=2,
    ).transpose(1, 0, 2)
    shared_w = lax.all_to_all(shared_pieces, BOTH, split_axis=0, concat_axis=0, tiled=True)
    shared_w = shared_w.reshape(D, 2 * half_sh)
    pad = half_all - half_ff - half_sh
    w_in = jnp.concatenate(
        [
            w_expert_in[0][:, :half_ff],
            jnp.pad(shared_w[:, :half_sh], ((0, 0), (0, pad))),
            w_expert_in[0][:, half_ff:],
            jnp.pad(shared_w[:, half_sh:], ((0, 0), (0, pad))),
        ],
        axis=1,
    )
    w_back = jnp.concatenate(
        [w_expert_out[0], jnp.pad(w_shared_out, ((0, pad), (0, 0)))], axis=0
    )

    most_rows = 3 * tok // 8
    paths = (
        (("y", "z", "x"), 0, most_rows),
        (("z", "x", "y"), most_rows, most_rows),
        (("x", "y", "z"), 2 * most_rows, tok - 2 * most_rows),
    )
    tokens = devices * tok
    x_own, x_sib = [], []
    for order, start, count in paths:
        x_own.append(links.gather(ffn_in[start : start + count], order))
    for x in x_own:
        x_sib.append(links.shift(x, "c", 1))
    region = [0] * 6
    for i in range(1, 6):
        region[i] = region[i - 1] + x_own[(i - 1) // 2].shape[0]
    kept = None
    moved, outs, row_grads = [None] * 3, [None] * 3, [None] * 3

    def ffn(i, side, kept, adds):
        order, start, count = paths[i]
        source = links.device_of(order + ("c",)).reshape(2, -1)[side]
        m = m_all[source][:, start : start + count].reshape(-1, 1)
        return ffn_chunk(
            (x_own, x_sib)[side][i],
            g_blocks,
            m,
            w_in,
            w_back,
            half_ff,
            source,
            start // count,
            kept,
            region[2 * i + side],
            tokens,
            adds,
        )

    for i, side in ((0, 1), (1, 1), (0, 0), (2, 1), (1, 0), (2, 0)):
        if side == 1:
            kept, out, grad = ffn(i, 1, kept, None)
            moved[i] = [links.shift(out, "c", -1), links.shift(grad, "c", -1)]
        else:
            kept, out, grad = ffn(i, 0, kept, moved[i])
            row_grads[i] = links.scatter_sum(grad, paths[i][0])
            outs[i] = links.scatter_sum(out, paths[i][0])
    ffn_out = jnp.concatenate(outs, axis=0).astype(f32)
    grad_ffn = jnp.concatenate(row_grads, axis=0).astype(f32)
    mixed = (middle + ffn_out).astype(bf16)
    x_all, g_kept, act_all, grad_pre_all = kept
    query_w_all = lax.all_gather(after(w_query, moved[2][0]), BOTH, axis=0, tiled=True)
    grad_w_in = matmul_left_t(x_all, grad_pre_all)
    grad_w_back = matmul_left_t(act_all, g_kept)
    grad_w_expert_in = jnp.concatenate(
        [grad_w_in[:, :half_ff], grad_w_in[:, half_all : half_all + half_ff]], axis=1
    )
    grad_w_expert_out = grad_w_back[:half_ff]
    grad_w_shared_out = grad_w_back[half_ff : half_ff + half_sh]
    grad_shared = jnp.concatenate(
        [
            grad_w_in[:, half_ff : half_ff + half_sh],
            grad_w_in[:, half_all + half_ff : half_all + half_ff + half_sh],
        ],
        axis=1,
    ).reshape(devices, rows_d, 2 * half_sh)
    grad_shared = lax.all_to_all(grad_shared, BOTH, split_axis=0, concat_axis=0, tiled=True)
    grad_shared = grad_shared.transpose(1, 0, 2)
    grad_w_shared_in = jnp.concatenate(
        [
            grad_shared[:, :, :half_sh].reshape(rows_d, SHARED_FF),
            grad_shared[:, :, half_sh:].reshape(rows_d, SHARED_FF),
        ],
        axis=1,
    )

    grad_out = cotangent.astype(f32)
    grad_middle_part, grad_norm_ffn = rms_backward(middle, inverse_ffn, gain_ffn, grad_ffn)
    grad_middle = grad_out + grad_middle_part
    grad_attended = grad_middle.astype(bf16)
    grad_heads_all = matmul_right_t(grad_attended, out_w).astype(bf16)
    pieces = [
        jnp.concatenate(
            [columns(grad_heads_all, k, v_cols), columns(grad_attended, k, D // ctx)], axis=1
        )
        for k in range(ctx)
    ]
    arrived = jnp.concatenate(links.ctx_exchange(pieces), axis=0)
    grad_heads = arrived[:, :v_cols].reshape(row, heads, VDIM).transpose(1, 0, 2)
    grad_attended_cols = arrived[:, v_cols:]
    heads_out_row = links.ctx_gather(heads_out)

    soft = jnp.exp(masked_scores() - log_total)
    grad_values = jnp.einsum(
        "hqk,hqd->hkd", soft.astype(bf16), grad_heads, preferred_element_type=f32
    )
    grad_probs = jnp.einsum("hqd,hkd->hqk", grad_heads, value, preferred_element_type=f32)
    row_delta = jnp.sum(soft * grad_probs, axis=-1, keepdims=True)
    grad_raw = (soft * (grad_probs - row_delta) * scale).astype(bf16)
    grad_query = jnp.einsum("hqk,hkd->qhd", grad_raw, key, preferred_element_type=f32)
    grad_key = jnp.einsum("hqk,hqd->khd", grad_raw, query, preferred_element_type=f32)
    grad_key_rope = jnp.sum(grad_key[..., NOPE:], axis=1)
    grad_keyval = jnp.concatenate(
        [grad_key[..., :NOPE], grad_values.transpose(1, 0, 2)], axis=-1
    )
    grad_keyval = grad_keyval.astype(bf16).reshape(row, kv_cols)
    grad_w_up = matmul_left_t(latent, grad_keyval)
    grad_latent = matmul_right_t(grad_keyval, up_w)
    grad_low = jnp.concatenate([grad_latent, grad_key_rope], axis=1).astype(bf16)
    grad_low = links.scatter_sum(grad_low, ("x", "y")).astype(f32)
    grad_query_raw = jnp.concatenate(
        [
            grad_query[..., :NOPE],
            unrotate(grad_query[..., NOPE:], cosine[:, None, :], sine_part[:, None, :]),
        ],
        axis=-1,
    )
    grad_query_raw = grad_query_raw.astype(bf16).reshape(ctx, tok, q_cols)
    query_back = jnp.stack(links.ctx_exchange([grad_query_raw[k] for k in range(ctx)]))
    query_back = query_back[ctx_place].transpose(1, 0, 2).reshape(tok, ctx * q_cols)
    grad_compressed_latent, grad_norm_latent = rms_backward(
        raw_latent[:tok], inverse_latent[:tok], gain_latent, grad_low[:, :LATENT]
    )
    grad_compressed = jnp.concatenate(
        [
            grad_compressed_latent,
            unrotate(grad_low[:, LATENT:], cosine[:tok], sine_part[:tok]),
        ],
        axis=1,
    ).astype(bf16)
    grad_normed = matmul_right_t(grad_compressed, down_w) + matmul_right_t(
        query_back, query_w_all
    )
    grad_input_part, grad_norm_attn = rms_backward(
        inputs, inverse_row[:tok], gain_attn, grad_normed
    )
    grad_in = grad_middle + grad_input_part

    z_rel = (links.own["z"] - jnp.arange(links.size["z"], dtype=jnp.int32)) % links.size["z"]
    c_rel = (links.own["c"] - jnp.arange(2, dtype=jnp.int32)) % 2
    dp_rel = (c_rel[:, None] + 2 * z_rel[None, :]).reshape(-1)

    def to_owners(value):
        count = value.shape[1]
        value = value.astype(bf16).reshape(links.dp, ctx * count, -1)[dp_rel]
        value = links.scatter_sum(value.reshape(devices * count, -1), ("z", "c"))
        value = value.reshape(ctx, count, -1)[rel_ctx]
        value = jnp.stack(links.ctx_exchange([value[k] for k in range(ctx)]))[ctx_place]
        return value.astype(f32)

    def joined(value):
        return value.transpose(1, 0, 2).reshape(value.shape[1], -1)

    grad_out_cols = matmul_left_t(heads_out_row, grad_attended_cols)
    grad_w_out = joined(to_owners(grad_out_cols.reshape(devices, rows_d, D // ctx)))
    grad_w_q = matmul_left_t(normed_row, grad_query_raw.reshape(row, q_cols))
    grad_w_up = grad_w_up.astype(bf16).reshape(devices, rows_l, up_parts, up_fold)
    grad_w_up = grad_w_up.transpose(0, 2, 1, 3).reshape(devices, rows_d, up_fold)
    heads_grads = to_owners(
        jnp.concatenate(
            [grad_w_q.astype(bf16).reshape(devices, rows_d, q_cols), grad_w_up], axis=2
        )
    )
    grad_w_query = joined(heads_grads[:, :, :q_cols])
    grad_w_kv_up = heads_grads[:, :, q_cols:].reshape(ctx, up_parts, rows_l, up_fold)
    grad_w_kv_up = grad_w_kv_up.transpose(2, 0, 1, 3).reshape(rows_l, ctx * kv_cols)

    compressed_cols = jnp.concatenate(
        links.ctx_exchange([columns(grad_compressed, k, dn_cols) for k in range(ctx)]), axis=0
    )
    grad_w_down = matmul_left_t(normed_row, compressed_cols).astype(bf16)
    vectors = jnp.stack(
        [
            jnp.pad(v.reshape(devices, -1), ((0, 0), (0, dn_cols - v.size // devices)))
            for v in (grad_norm_attn, grad_norm_ffn, grad_norm_latent)
        ],
        axis=1,
    )
    vectors = jnp.pad(vectors, ((0, 0), (0, 13), (0, 0))).astype(bf16)
    last_grads = to_owners(
        jnp.concatenate([grad_w_down.reshape(devices, rows_d, dn_cols), vectors], axis=1)
    )
    grad_w_kv_down = joined(last_grads[:, :rows_d])
    vector_sums = jnp.sum(last_grads[:, rows_d : rows_d + 3], axis=0)
    return (
        mixed,
        grad_in,
        vector_sums[0, :rows_d],
        grad_w_query,
        grad_w_kv_down,
        vector_sums[2, :rows_l],
        grad_w_kv_up,
        grad_w_out,
        vector_sums[1, :rows_d],
        grad_w_shared_in,
        grad_w_shared_out,
        grad_w_expert_in[None],
        grad_w_expert_out[None],
    )


def solution(mesh):
    rows = P(BOTH, None)
    vector = P(BOTH)
    experts = P(BOTH, None, None)
    return jax.shard_map(
        shards,
        mesh=mesh,
        in_specs=(
            rows,
            P("dp"),
            rows,
            rows,
            rows,
            vector,
            rows,
            rows,
            vector,
            rows,
            rows,
            vector,
            rows,
            rows,
            experts,
            experts,
        ),
        out_specs=(
            rows,
            rows,
            vector,
            rows,
            rows,
            vector,
            rows,
            rows,
            vector,
            rows,
            rows,
            experts,
            experts,
        ),
        check_vma=False,
    )
```

time: 5570 us -> 1990 us (0.36)
  waiting for transfers between devices: 4420 us -> 874 us
  matrix products: 599 us -> 260 us
  Pallas kernels: 0 us -> 259 us
  starting transfers between devices: 18.8 us -> 142 us
  blocking collectives: 100 us -> 0 us
    all_to_all x4 -> x3, waiting for transfers between devices: 2010 us -> 0.01 us  [the longest x1 0.01 us: shards(): lax.all_to_all(shared_pieces, BOTH, split_axis=0, concat_axis=0, tiled=True)]
    reduce_scatter x8 -> x0, waiting for transfers between devices: 1920 us -> none  [the longest x1 908 us: shards(): lax.psum_scatter(grad_w_shared_in, ('dp', 'ctx'), scatter_dimension=0, ti...]
    ppermute x0 -> x110, waiting for transfers between devices: none -> 797 us  [the longest x86 744 us: shift(): return lax.ppermute(value, name, pairs)]
    all_gather x7 -> x3, waiting for transfers between devices: 478 us -> 77.6 us  [the longest x1 77.5 us: shards(): lax.all_gather(after(w_out, heads_w, hidden_row), BOTH, axis=0, tiled=True)]
    pallas_call x0 -> x6, Pallas kernels: none -> 259 us  [ffn_chunk(): pl.pallas_call(lambda *refs: ffn_kernel(half_ff, adds is not None, *refs)...]
    dot_general x17 -> x10, matrix products: 310 us -> 113 us  [the longest x1 28.8 us: shards(): jnp.einsum('hqk,hqd->khd', grad_raw, query, preferred_element_type=f32)]
    dot_general x8 -> x4, matrix products: 151 us -> 19.2 us  [matmul_right_t(): lax.dot_general(left, right, (((1,), (1,)), ((), ())), preferred_element_...]
    ppermute x0 -> x110, starting transfers between devices: none -> 131 us  [the longest x86 102 us: shift(): return lax.ppermute(value, name, pairs)]
  transfers between devices with their start and end apart: 19 -> 116, of which waited for: 16 -> 47; matrix products, arithmetic and copies ran while one was open for 13% -> 32% of each run, Pallas kernels for 0% -> 13%
where the time goes in v1:
time: 1990 us; the launch traced here: 1980 us
  waiting for transfers between devices  874 us (44%)
  local copies, waits for them, and re-layouts  274 us (14%)
  matrix products  260 us (13%)
  Pallas kernels  259 us (13%)
  other arithmetic  143 us (7%)
  starting transfers between devices  142 us (7%)
  between operations  26.3 us (1%)
    ppermute x86, waiting for transfers between devices, shift(): return lax.ppermute(value, name, pairs)  744 us
    pallas_call x6, Pallas kernels, ffn_chunk(): pl.pallas_call(lambda *refs: ffn_kernel(half_ff, adds is not None, *refs)...  259 us
    dot_general x6, matrix products, matmul_left_t(): lax.dot_general(left, right, (((0,), (0,)), ((), ())), preferred_element_...  128 us
    ppermute x86, starting transfers between devices, shift(): return lax.ppermute(value, name, pairs)  102 us
    all_gather x1, waiting for transfers between devices, shards(): lax.all_gather(after(w_out, heads_w, hidden_row), BOTH, axis=0, tiled=True)  77.5 us
    unnamed x270, local copies, waits for them, and re-layouts  62.7 us
    convert_element_type x43, other arithmetic, reduce(): total = (moved.astype(f32) + part.astype(f32)).astype(bf16)  57.2 us
    ppermute x24, waiting for transfers between devices, shift_ctx(): return lax.ppermute(value, 'ctx', pairs)  52.9 us
  transfers between devices with their start and end apart: 116, of which 47 were waited for; matrix products, arithmetic and copies ran while one was open for 32% of the time, Pallas kernels for 13%

profile of v1, /device:TPU:0, one launch (start us, length us, event | category | flops | bytes accessed | tf_op | source)
XLA Modules:
  0.0 1979.9 jit_solution(16033673780374858826)
XLA Ops:
  35.0 9.1 collective-permute-done.13
  48.3 7.9 collective-permute-done.14
  60.1 7.1 collective-permute-done.15
  68.9 6.9 collective-permute-done.3
  80.7 5.1 gather_fusion.1
  85.9 77.5 %all-gather.4.cloned.1.call-done = bf16[2048,2048]{1,0:T(8,128)(2,1)} async-done(((bf16[64,2048]{1,0:T(8,128)(2,1)}), bf16[2048,2048]{1,0:T(8,128)(2,1)}) %all-gather.4.cloned.1.call-update) | async-done | bytes 8388624 | tf_op jit(solution)/shard_map/all_gather | solution.py:359
  166.1 4.9 collective-permute-done.4
  171.0 6.2 collective-permute-done.5
  177.8 7.9 collective-permute-done.6
  195.3 11.5 collective-permute-done.8
  233.1 6.7 fusion.22
  245.8 7.9 fusion.146
  253.7 8.0 fusion.4
  261.7 11.7 fusion.52
  277.3 11.2 collective-permute-done.17
  290.5 10.2 collective-permute-done.19
  303.1 6.2 multiply_reduce_fusion.1
  311.8 19.7 collective-permute-done.20
  333.0 29.6 %collective-permute-done.21 = bf16[192,2048]{1,0:T(8,128)(2,1)S(1)} collective-permute-done((bf16[192,2048]{1,0:T(8,128)(2,1)S(1)}, bf16[192,2048]{1,0:T(8,128)(2,1)S(1)}, u32[]{:S(2)}, u32[]{:S(2)}) %collective-permute-start.21) | collective-permute-done | bytes 786464 | tf_op jit(solution)/shard_map/ppermute | solution.py:103
  362.6 5.1 collective-permute-start.22
  367.7 34.2 %collective-permute-done.22 = bf16[192,2048]{1,0:T(8,128)(2,1)S(1)} collective-permute-done((bf16[192,2048]{1,0:T(8,128)(2,1)S(1)}, bf16[192,2048]{1,0:T(8,128)(2,1)S(1)}, u32[]{:S(2)}, u32[]{:S(2)}) %collective-permute-start.22) | collective-permute-done | bytes 786464 | tf_op jit(solution)/shard_map/ppermute | solution.py:103
  405.7 15.0 collective-permute-done.23
  433.0 10.0 collective-permute-done.28
  443.1 12.3 collective-permute-done.29
  455.7 11.5 collective-permute-done.30
  469.9 25.7 %collective-permute-done.24 = bf16[768,2048]{1,0:T(8,128)(2,1)} collective-permute-done((bf16[768,2048]{1,0:T(8,128)(2,1)}, bf16[768,2048]{1,0:T(8,128)(2,1)}, u32[]{:S(2)}, u32[]{:S(2)}) %collective-permute-start.24) | collective-permute-done | bytes 3145760 | tf_op jit(solution)/shard_map/ppermute | solution.py:103
  509.3 17.4 collective-permute-done.31
  546.5 73.2 %collective-permute-done.42 = bf16[128,2048]{1,0:T(8,128)(2,1)S(1)} collective-permute-done((bf16[128,2048]{1,0:T(8,128)(2,1)S(1)}, bf16[128,2048]{1,0:T(8,128)(2,1)S(1)}, u32[]{:S(2)}, u32[]{:S(2)}) %collective-permute-start.42) | collective-permute-done | bytes 524320 | tf_op jit(solution)/shard_map/ppermute | solution.py:103
  624.7 6.3 fusion.127
  637.0 11.8 concatenate.199.refs_7_
  649.7 47.4 %ffn_chunk.6 = (bf16[8192,2048]{1,0:T(8,128)(2,1)}, bf16[8192,2048]{1,0:T(8,128)(2,1)}, bf16[8192,896]{1,0:T(8,128)(2,1)}, bf16[8192,1792]{1,0:T(8,128)(2,1)}, b...) custom-call(s32[16]{0:T(128)} %squeeze.118.refs_0_, bf16[1536,2048]{1,0:T(8,128)(2,1)} %collective-permute-done.25.refs_1_, ...), custom_call_target="tpu_custom_call" | custom-call | flops 33822867456 | bytes 50331648 | tf_op jit(solution)/shard_map/ffn_chunk/pallas_call | solution.py:259
  708.1 19.4 collective-permute-done.45
  730.2 47.4 %ffn_chunk.7 = (bf16[8192,2048]{1,0:T(8,128)(2,1)}, bf16[8192,2048]{1,0:T(8,128)(2,1)}, bf16[8192,896]{1,0:T(8,128)(2,1)}, bf16[8192,1792]{1,0:T(8,128)(2,1)}, b...) custom-call(s32[16]{0:T(128)} %squeeze.120.refs_0_, ...), custom_call_target="tpu_custom_call", output_to_operand_aliasing={{0}: (9, {}), {1}: (10, {}), {2}: (11, {}), {3}: (12, {})} | custom-call | flops 33822867456 | bytes 50331648 | tf_op jit(solution)/shard_map/ffn_chunk/pallas_call | solution.py:259
  802.7 48.6 %ffn_chunk.8 = (bf16[8192,2048]{1,0:T(8,128)(2,1)}, bf16[8192,2048]{1,0:T(8,128)(2,1)}, bf16[8192,896]{1,0:T(8,128)(2,1)}, bf16[8192,1792]{1,0:T(8,128)(2,1)}, b...) custom-call(s32[16]{0:T(128)} %squeeze.114.refs_0_, ...), custom_call_target="tpu_custom_call", output_to_operand_aliasing={{0}: (11, {}), {1}: (12, {}), {2}: (13, {}), {3}: (14, {})} | custom-call | flops 33822867456 | bytes 50331648 | tf_op jit(solution)/shard_map/ffn_chunk/pallas_call | solution.py:259
  856.0 33.0 %ffn_chunk.9 = (bf16[8192,2048]{1,0:T(8,128)(2,1)}, bf16[8192,2048]{1,0:T(8,128)(2,1)}, bf16[8192,896]{1,0:T(8,128)(2,1)}, bf16[8192,1792]{1,0:T(8,128)(2,1)}, b...) custom-call(s32[16]{0:T(128)} %squeeze.124.refs_0_, ...), custom_call_target="tpu_custom_call", output_to_operand_aliasing={{0}: (9, {}), {1}: (10, {}), {2}: (11, {}), {3}: (12, {})} | custom-call | flops 22548578304 | bytes 33554432 | tf_op jit(solution)/shard_map/ffn_chunk/pallas_call | solution.py:259
  889.0 49.0 %ffn_chunk.10 = (bf16[8192,2048]{1,0:T(8,128)(2,1)}, bf16[8192,2048]{1,0:T(8,128)(2,1)}, bf16[8192,896]{1,0:T(8,128)(2,1)}, bf16[8192,1792]{1,0:T(8,128)(2,1)}, ...) custom-call(s32[16]{0:T(128)} %squeeze.122.refs_0_, ...), custom_call_target="tpu_custom_call", output_to_operand_aliasing={{0}: (11, {}), {1}: (12, {}), {2}: (13, {}), {3}: (14, {})} | custom-call | flops 33822867456 | bytes 50331648 | tf_op jit(solution)/shard_map/ffn_chunk/pallas_call | solution.py:259
  962.6 49.0 %collective-permute-done.64 = bf16[768,2048]{1,0:T(8,128)(2,1)} collective-permute-done((bf16[768,2048]{1,0:T(8,128)(2,1)S(1)}, bf16[768,2048]{1,0:T(8,128)(2,1)}, u32[]{:S(2)}, u32[]{:S(2)}) %collective-permute-start.64) | collective-permute-done | bytes 3145760 | tf_op jit(solution)/shard_map/ppermute | solution.py:103
  1023.7 53.7 %collective-permute-done.47 = bf16[768,2048]{1,0:T(8,128)(2,1)} collective-permute-done((bf16[768,2048]{1,0:T(8,128)(2,1)}, bf16[768,2048]{1,0:T(8,128)(2,1)}, u32[]{:S(2)}, u32[]{:S(2)}) %collective-permute-start.47) | collective-permute-done | bytes 3145760 | tf_op jit(solution)/shard_map/ppermute | solution.py:103
  1086.4 9.0 collective-permute-done.35
  1100.2 33.9 %ffn_chunk.11 = (bf16[8192,2048]{1,0:T(8,128)(2,1)}, bf16[8192,2048]{1,0:T(8,128)(2,1)}, bf16[8192,896]{1,0:T(8,128)(2,1)}, bf16[8192,1792]{1,0:T(8,128)(2,1)}, ...) custom-call(s32[16]{0:T(128)} %squeeze.126.refs_0_, ...), custom_call_target="tpu_custom_call", output_to_operand_aliasing={{0}: (11, {}), {1}: (12, {}), {2}: (13, {}), {3}: (14, {})} | custom-call | flops 22548578304 | bytes 33554432 | tf_op jit(solution)/shard_map/ffn_chunk/pallas_call | solution.py:259
  1134.1 70.5 %fusion.147 = f32[2048,1792]{0,1:T(8,128)} fusion(bf16[8192,2048]{1,0:T(8,128)(2,1)} %get-tuple-element.99, bf16[8192,1792]{1,0:T(8,128)(2,1)} %get-tuple-element.100), kind=kOutput, calls=%fused_computation.495 | convolution fusion | flops 60129542144 | bytes 77594624 | tf_op jit(solution)/shard_map/dot_general | solution.py:31
  1204.5 10.7 fusion.125
  1215.2 10.5 maximum_bitcast_fusion
  1225.7 38.1 %fusion.148 = f32[896,2048]{1,0:T(8,128)S(1)} fusion(bf16[8192,896]{1,0:T(8,128)(2,1)} %get-tuple-element.101, bf16[8192,2048]{1,0:T(8,128)(2,1)} %get-tuple-element.102), kind=kOutput, calls=%fused_computation.496 | convolution fusion | flops 30064771072 | bytes 55574528 | tf_op jit(solution)/shard_map/dot_general | solution.py:31
  1269.1 11.9 copy.249
  1307.8 128.5 %collective-permute-done.66 = bf16[96,2048]{1,0:T(8,128)(2,1)S(1)} collective-permute-done((bf16[96,2048]{1,0:T(8,128)(2,1)S(1)}, bf16[96,2048]{1,0:T(8,128)(2,1)S(1)}, u32[]{:S(2)}, u32[]{:S(2)}) %collective-permute-start.66) | collective-permute-done | bytes 393248 | tf_op jit(solution)/shard_map/ppermute | solution.py:103
  1438.6 19.3 collective-permute-done.49
  1467.4 19.4 collective-permute-done.67
  1488.6 12.3 collective-permute-done.50
  1502.2 63.2 %collective-permute-done.68 = bf16[96,2048]{1,0:T(8,128)(2,1)S(1)} collective-permute-done((bf16[96,2048]{1,0:T(8,128)(2,1)S(1)}, bf16[96,2048]{1,0:T(8,128)(2,1)S(1)}, u32[]{:S(2)}, u32[]{:S(2)}) %collective-permute-start.68) | collective-permute-done | bytes 393248 | tf_op jit(solution)/shard_map/ppermute | solution.py:103
  1580.3 16.2 collective-permute-done.71
  1600.0 16.9 collective-permute-done.56
  1623.6 7.6 collective-permute-done.57
  1647.3 7.2 collective-permute-done.74
  1654.5 8.5 collective-permute-done.75
  1675.3 8.3 fusion.54
  1683.6 27.5 %fusion.45 = f32[1024,4,192]{0,2,1:T(8,128)} fusion(f32[4,1024,1024]{1,2,0:T(8,128)} %fusion.54, f32[4,1024,1024]{1,2,0:T(8,128)} %get-tuple-element.337, f32[4,1024]{1,0:T(4,128)} %log_add_fusion, bf16[4,1024,64]{1,2,0:T(8,128)(2,1)} %copy-done.67, bf16[4,1024,128]{1,2,0:T(8,128)(2,1)S(1)} %copy-done.63), kind=kOutput, calls=%fused_computation.104 | convolution fusion | flops 1643123712 | bytes 38289408 | tf_op jit(solution)/shard_map/hqk,hkd->qhd/dot_general | solution.py:532
  1712.9 28.8 %fusion.42 = f32[1024,4,192]{0,2,1:T(8,128)} fusion(f32[4,1024,1024]{1,2,0:T(8,128)} %fusion.54, f32[4,1024,1024]{1,2,0:T(8,128)} %get-tuple-element.337, f32[4,1024]{1,0:T(4,128)} %log_add_fusion, bf16[1024,4,32]{0,2,1:T(8,128)(2,1)} %copy-done.70, bf16[1024,4,32]{0,2,1:T(8,128)(2,1)} %copy-done.69, bf16[1024,4,128]{0,2,1:T(8,128)(2,1)} %copy-done.61), kind=kOutput, calls=%fused_computation.103 | convolution fusion | flops 1644696576 | bytes 38289408 | tf_op jit(solution)/shard_map/hqk,hqd->khd/dot_general | solution.py:533
  1746.5 9.9 fusion.48
  1763.5 8.4 convolution_convert_fusion
  1781.2 5.2 gather_fusion.14
  1800.1 8.7 collective-permute-done.80
  1852.5 6.4 collective-permute-done.93
  1883.1 11.4 fusion.40
  (791 shorter events, 530.0 us)
Async XLA Ops:
  7.2 156.2 %all-gather.4.cloned.1.call-start = ((), (), s32[]{:S(2)}) async-start(), calls=%async_computation.3 | async-start | bytes 8650752 | tf_op jit(solution)/shard_map/all_gather | solution.py:359
  23.2 23.0 %collective-permute-start.1 = (bf16[128,2048]{1,0:T(8,128)(2,1)S(1)}, bf16[128,2048]{1,0:T(8,128)(2,1)S(1)}, u32[]{:S(2)}, u32[]{:S(2)}) collective-permute-start(bf16[128,2048]{1,0:T(8,128)(2,1)S(1)} %get-tuple-element.241), channel_id=1, source_target_pairs={{0,2},{1,3},{2,0},{3,1},{4,6},{5,7},{6,4},{7,5},{8,10},{9,11},{10,... | collective-permute-start | bytes 1572872 | tf_op jit(solution)/shard_map/ppermute | solution.py:103
  25.3 31.3 %collective-permute-start = (bf16[128,2048]{1,0:T(8,128)(2,1)S(1)}, bf16[128,2048]{1,0:T(8,128)(2,1)S(1)}, u32[]{:S(2)}, u32[]{:S(2)}) collective-permute-start(bf16[128,2048]{1,0:T(8,128)(2,1)S(1)} %get-tuple-element.242), channel_id=1, source_target_pairs={{0,1},{1,0},{2,3},{3,2},{4,5},{5,4},{6,7},{7,6},{8,9},{9,8},{10,11... | collective-permute-start | bytes 1572872 | tf_op jit(solution)/shard_map/ppermute | solution.py:103
  85.8 563.8 %all-gather.6.cloned.1.call-start = ((), (), s32[]{:S(2)}) async-start(), calls=%async_computation.4 | async-start | bytes 34603008 | tf_op jit(solution)/shard_map/all_gather | solution.py:360
  275.7 25.0 %collective-permute-start.19 = (bf16[256,512]{0,1:T(8,128)(2,1)S(1)}, bf16[256,512]{0,1:T(8,128)(2,1)S(1)}, u32[]{:S(2)}, u32[]{:S(2)}) collective-permute-start(bf16[256,512]{0,1:T(8,128)(2,1)S(1)} %bitcast.316), channel_id=1, source_target_pairs={{0,3},{1,2},{2,1},{3,0},{4,7},{5,6},{6,5},{7,4},{8,11},{9,10},{10,... | collective-permute-start | bytes 786440 | tf_op jit(solution)/shard_map/ppermute | solution.py:109
  331.5 31.1 %collective-permute-start.21 = (bf16[192,2048]{1,0:T(8,128)(2,1)S(1)}, bf16[192,2048]{1,0:T(8,128)(2,1)S(1)}, u32[]{:S(2)}, u32[]{:S(2)}) collective-permute-start(bf16[192,2048]{1,0:T(8,128)(2,1)S(1)} %pad_maximum_fusion.16), channel_id=1, source_target_pairs={{0,8},{4,12},{8,16},{12,20},{16,24},{20,28},{24,0},{28,4},{1,9},{5... | collective-permute-start | bytes 2359304 | tf_op jit(solution)/shard_map/ppermute | solution.py:103
  362.6 39.3 %collective-permute-start.22 = (bf16[192,2048]{1,0:T(8,128)(2,1)S(1)}, bf16[192,2048]{1,0:T(8,128)(2,1)S(1)}, u32[]{:S(2)}, u32[]{:S(2)}) collective-permute-start(bf16[192,2048]{1,0:T(8,128)(2,1)S(1)} %collective-permute-done.21), channel_id=1, source_target_pairs={{0,8},{4,12},{8,16},{12,20},{16,24},{20,28},{24,0},{28,4},{1,9},{5... | collective-permute-start | bytes 2359304 | tf_op jit(solution)/shard_map/ppermute | solution.py:103
  422.0 73.6 %collective-permute-start.24 = (bf16[768,2048]{1,0:T(8,128)(2,1)}, bf16[768,2048]{1,0:T(8,128)(2,1)}, u32[]{:S(2)}, u32[]{:S(2)}) collective-permute-start(bf16[768,2048]{1,0:T(8,128)(2,1)} %get-tuple-element.247), channel_id=1, source_target_pairs={{0,1},{1,0},{2,3},{3,2},{4,5},{5,4},{6,7},{7,6},{8,9},{9,8},{10,11... | collective-permute-start | bytes 9437192 | tf_op jit(solution)/shard_map/ppermute | solution.py:103
  426.7 115.0 %all-to-all-start = ((f32[32,1,256]{2,1,0:T(1,128)}), f32[32,1,256]{2,1,0:T(1,128)S(1)}, u32[]{:S(2)}, u32[]{:S(2)}) async-start(f32[32,1,256]{2,1,0:T(1,128)} %all_to_all.14), calls=%async_computation | async-start | bytes 65536 | tf_op jit(solution)/shard_map/all_to_all | solution.py:356
  468.4 58.3 %collective-permute-start.31 = (bf16[384,2048]{1,0:T(8,128)(2,1)}, bf16[384,2048]{1,0:T(8,128)(2,1)}, u32[]{:S(2)}, u32[]{:S(2)}) collective-permute-start(bf16[384,2048]{1,0:T(8,128)(2,1)} %pad_maximum_fusion.3), channel_id=1, source_target_pairs={{0,1},{1,0},{2,3},{3,2},{4,5},{5,4},{6,7},{7,6},{8,9},{9,8},{10,11... | collective-permute-start | bytes 4718600 | tf_op jit(solution)/shard_map/ppermute | solution.py:103
  499.5 150.1 %collective-permute-start.25 = (bf16[1536,2048]{1,0:T(8,128)(2,1)}, bf16[1536,2048]{1,0:T(8,128)(2,1)}, u32[]{:S(2)}, u32[]{:S(2)}) collective-permute-start(bf16[1536,2048]{1,0:T(8,128)(2,1)} %constant_dynamic-update-slice_fusion.41.refs_1_), channel_id=1, source_target_pairs={{0,4},{4,0},{8,12},{12,8},{16,20},{20,16},{24,28},{28,24},{1,5},{5... | collective-permute-start | bytes 18874376 | tf_op jit(solution)/shard_map/ppermute | solution.py:103
  530.3 90.5 %collective-permute-start.32 = (bf16[768,2048]{1,0:T(8,128)(2,1)}, bf16[768,2048]{1,0:T(8,128)(2,1)}, u32[]{:S(2)}, u32[]{:S(2)}) collective-permute-start(bf16[768,2048]{1,0:T(8,128)(2,1)} %get-tuple-element.215), channel_id=1, source_target_pairs={{0,2},{1,3},{2,0},{3,1},{4,6},{5,7},{6,4},{7,5},{8,10},{9,11},{10,... | collective-permute-start | bytes 9437192 | tf_op jit(solution)/shard_map/ppermute | solution.py:103
  541.0 78.7 %collective-permute-start.42 = (bf16[128,2048]{1,0:T(8,128)(2,1)S(1)}, bf16[128,2048]{1,0:T(8,128)(2,1)S(1)}, u32[]{:S(2)}, u32[]{:S(2)}) collective-permute-start(bf16[128,2048]{1,0:T(8,128)(2,1)S(1)} %pad_maximum_fusion.19), channel_id=1, source_target_pairs={{0,2},{1,3},{2,0},{3,1},{4,6},{5,7},{6,4},{7,5},{8,10},{9,11},{10,... | collective-permute-start | bytes 1572872 | tf_op jit(solution)/shard_map/ppermute | solution.py:103
  541.7 91.4 %all-to-all-start.1 = ((bf16[32,64,176]{2,1,0:T(8,128)(2,1)}), bf16[32,64,176]{2,1,0:T(8,128)(2,1)}, u32[]{:S(2)}, u32[]{:S(2)}) async-start(bf16[32,64,176]{2,1,0:T(8,128)(2,1)} %maximum_bitcast_fusion.2), calls=%async_computation.1 | async-start | bytes 2097152 | tf_op jit(solution)/shard_map/all_to_all | solution.py:419
  620.8 28.0 %collective-permute-start.43 = (bf16[256,2048]{1,0:T(8,128)(2,1)}, bf16[256,2048]{1,0:T(8,128)(2,1)}, u32[]{:S(2)}, u32[]{:S(2)}) collective-permute-start(bf16[256,2048]{1,0:T(8,128)(2,1)} %pad_maximum_fusion.12), channel_id=1, source_target_pairs={{0,8},{4,12},{8,16},{12,20},{16,24},{20,28},{24,0},{28,4},{1,9},{5... | collective-permute-start | bytes 3145736 | tf_op jit(solution)/shard_map/ppermute | solution.py:103
  624.7 105.4 %collective-permute-start.33 = (bf16[1536,2048]{1,0:T(8,128)(2,1)}, bf16[1536,2048]{1,0:T(8,128)(2,1)}, u32[]{:S(2)}, u32[]{:S(2)}) collective-permute-start(bf16[1536,2048]{1,0:T(8,128)(2,1)} %constant_dynamic-update-slice_fusion.52.refs_1_), channel_id=1, source_target_pairs={{0,4},{4,0},{8,12},{12,8},{16,20},{20,16},{24,28},{28,24},{1,5},{5... | collective-permute-start | bytes 18874376 | tf_op jit(solution)/shard_map/ppermute | solution.py:103
  648.7 51.2 %collective-permute-start.44 = (bf16[256,2048]{1,0:T(8,128)(2,1)}, bf16[256,2048]{1,0:T(8,128)(2,1)}, u32[]{:S(2)}, u32[]{:S(2)}) collective-permute-start(bf16[256,2048]{1,0:T(8,128)(2,1)} %collective-permute-done.43), channel_id=1, source_target_pairs={{0,8},{4,12},{8,16},{12,20},{16,24},{20,28},{24,0},{28,4},{1,9},{5... | collective-permute-start | bytes 3145736 | tf_op jit(solution)/shard_map/ppermute | solution.py:103
  697.1 103.8 %collective-permute-start.26 = (bf16[1536,2048]{1,0:T(8,128)(2,1)}, bf16[1536,2048]{1,0:T(8,128)(2,1)}, u32[]{:S(2)}, u32[]{:S(2)}) collective-permute-start(bf16[1536,2048]{1,0:T(8,128)(2,1)} %get-tuple-element.66), channel_id=1, source_target_pairs={{0,4},{4,0},{8,12},{12,8},{16,20},{20,16},{24,28},{28,24},{1,5},{5... | collective-permute-start | bytes 18874376 | tf_op jit(solution)/shard_map/ppermute | solution.py:103
  697.4 104.9 %collective-permute-start.27 = (bf16[1536,2048]{1,0:T(8,128)(2,1)}, bf16[1536,2048]{1,0:T(8,128)(2,1)}, u32[]{:S(2)}, u32[]{:S(2)}) collective-permute-start(bf16[1536,2048]{1,0:T(8,128)(2,1)} %get-tuple-element.67), channel_id=1, source_target_pairs={{0,4},{4,0},{8,12},{12,8},{16,20},{20,16},{24,28},{28,24},{1,5},{5... | collective-permute-start | bytes 18874376 | tf_op jit(solution)/shard_map/ppermute | solution.py:103
  699.9 27.6 %collective-permute-start.45 = (bf16[256,2048]{1,0:T(8,128)(2,1)}, bf16[256,2048]{1,0:T(8,128)(2,1)S(1)}, u32[]{:S(2)}, u32[]{:S(2)}) collective-permute-start(bf16[256,2048]{1,0:T(8,128)(2,1)} %collective-permute-done.44), channel_id=1, source_target_pairs={{0,8},{4,12},{8,16},{12,20},{16,24},{20,28},{24,0},{28,4},{1,9},{5... | collective-permute-start | bytes 3145736 | tf_op jit(solution)/shard_map/ppermute | solution.py:103
  700.4 77.2 %collective-permute-start.99 = (bf16[128,2048]{0,1:T(8,128)(2,1)S(1)}, bf16[128,2048]{0,1:T(8,128)(2,1)S(1)}, u32[]{:S(2)}, u32[]{:S(2)}) collective-permute-start(bf16[128,2048]{0,1:T(8,128)(2,1)S(1)} %bitcast.281), channel_id=1, source_target_pairs={{0,1},{1,0},{2,3},{3,2},{4,5},{5,4},{6,7},{7,6},{8,9},{9,8},{10,11... | collective-permute-start | bytes 1572872 | tf_op jit(solution)/shard_map/ppermute | solution.py:103
  727.5 50.8 %collective-permute-start.100 = (bf16[128,2048]{0,1:T(8,128)(2,1)S(1)}, bf16[128,2048]{0,1:T(8,128)(2,1)S(1)}, u32[]{:S(2)}, u32[]{:S(2)}) collective-permute-start(bf16[128,2048]{0,1:T(8,128)(2,1)S(1)} %bitcast.278), channel_id=1, source_target_pairs={{0,2},{1,3},{2,0},{3,1},{4,6},{5,7},{6,4},{7,5},{8,10},{9,11},{10,... | collective-permute-start | bytes 1572872 | tf_op jit(solution)/shard_map/ppermute | solution.py:103
  730.2 125.2 %collective-permute-start.46 = (bf16[1024,2048]{1,0:T(8,128)(2,1)}, bf16[1024,2048]{1,0:T(8,128)(2,1)}, u32[]{:S(2)}, u32[]{:S(2)}) collective-permute-start(bf16[1024,2048]{1,0:T(8,128)(2,1)} %constant_dynamic-update-slice_fusion.58.refs_1_), channel_id=1, source_target_pairs={{0,4},{4,0},{8,12},{12,8},{16,20},{20,16},{24,28},{28,24},{1,5},{5... | collective-permute-start | bytes 12582920 | tf_op jit(solution)/shard_map/ppermute | solution.py:103
  777.7 111.3 %collective-permute-start.39 = (bf16[1536,2048]{1,0:T(8,128)(2,1)}, bf16[1536,2048]{1,0:T(8,128)(2,1)}, u32[]{:S(2)}, u32[]{:S(2)}) collective-permute-start(bf16[1536,2048]{1,0:T(8,128)(2,1)} %get-tuple-element.77), channel_id=1, source_target_pairs={{0,4},{4,0},{8,12},{12,8},{16,20},{20,16},{24,28},{28,24},{1,5},{5... | collective-permute-start | bytes 18874376 | tf_op jit(solution)/shard_map/ppermute | solution.py:103
  778.2 110.8 %collective-permute-start.40 = (bf16[1536,2048]{1,0:T(8,128)(2,1)}, bf16[1536,2048]{1,0:T(8,128)(2,1)}, u32[]{:S(2)}, u32[]{:S(2)}) collective-permute-start(bf16[1536,2048]{1,0:T(8,128)(2,1)} %get-tuple-element.78), channel_id=1, source_target_pairs={{0,4},{4,0},{8,12},{12,8},{16,20},{20,16},{24,28},{28,24},{1,5},{5... | collective-permute-start | bytes 18874376 | tf_op jit(solution)/shard_map/ppermute | solution.py:103
  800.9 146.4 %collective-permute-start.101 = (bf16[256,2048]{0,1:T(8,128)(2,1)}, bf16[256,2048]{0,1:T(8,128)(2,1)}, u32[]{:S(2)}, u32[]{:S(2)}) collective-permute-start(bf16[256,2048]{0,1:T(8,128)(2,1)} %pad_maximum_fusion.14), channel_id=1, source_target_pairs={{0,1},{1,0},{2,3},{3,2},{4,5},{5,4},{6,7},{7,6},{8,9},{9,8},{10,11... | collective-permute-start | bytes 3145736 | tf_op jit(solution)/shard_map/ppermute | solution.py:103
  802.3 147.0 %collective-permute-start.102 = (bf16[256,2048]{0,1:T(8,128)(2,1)}, bf16[256,2048]{0,1:T(8,128)(2,1)}, u32[]{:S(2)}, u32[]{:S(2)}) collective-permute-start(bf16[256,2048]{0,1:T(8,128)(2,1)} %pad_maximum_fusion.15), channel_id=1, source_target_pairs={{0,2},{1,3},{2,0},{3,1},{4,6},{5,7},{6,4},{7,5},{8,10},{9,11},{10,... | collective-permute-start | bytes 3145736 | tf_op jit(solution)/shard_map/ppermute | solution.py:103
  855.4 101.0 %collective-permute-start.59 = (bf16[768,2048]{1,0:T(8,128)(2,1)}, bf16[768,2048]{1,0:T(8,128)(2,1)}, u32[]{:S(2)}, u32[]{:S(2)}) collective-permute-start(bf16[768,2048]{1,0:T(8,128)(2,1)} %slice.667), channel_id=1, source_target_pairs={{0,1},{1,0},{2,3},{3,2},{4,5},{5,4},{6,7},{7,6},{8,9},{9,8},{10,11... | collective-permute-start | bytes 9437192 | tf_op jit(solution)/shard_map/ppermute | solution.py:103
  940.4 71.2 %collective-permute-start.64 = (bf16[768,2048]{1,0:T(8,128)(2,1)S(1)}, bf16[768,2048]{1,0:T(8,128)(2,1)}, u32[]{:S(2)}, u32[]{:S(2)}) collective-permute-start(bf16[768,2048]{1,0:T(8,128)(2,1)S(1)} %slice.675), channel_id=1, source_target_pairs={{0,2},{1,3},{2,0},{3,1},{4,6},{5,7},{6,4},{7,5},{8,10},{9,11},{10,... | collective-permute-start | bytes 9437192 | tf_op jit(solution)/shard_map/ppermute | solution.py:103
  945.8 72.3 %collective-permute-start.34 = (bf16[768,2048]{1,0:T(8,128)(2,1)}, bf16[768,2048]{1,0:T(8,128)(2,1)}, u32[]{:S(2)}, u32[]{:S(2)}) collective-permute-start(bf16[768,2048]{1,0:T(8,128)(2,1)} %slice.636), channel_id=1, source_target_pairs={{0,1},{1,0},{2,3},{3,2},{4,5},{5,4},{6,7},{7,6},{8,9},{9,8},{10,11... | collective-permute-start | bytes 9437192 | tf_op jit(solution)/shard_map/ppermute | solution.py:103
  953.2 124.3 %collective-permute-start.47 = (bf16[768,2048]{1,0:T(8,128)(2,1)}, bf16[768,2048]{1,0:T(8,128)(2,1)}, u32[]{:S(2)}, u32[]{:S(2)}) collective-permute-start(bf16[768,2048]{1,0:T(8,128)(2,1)} %slice.649), channel_id=1, source_target_pairs={{0,2},{1,3},{2,0},{3,1},{4,6},{5,7},{6,4},{7,5},{8,10},{9,11},{10,... | collective-permute-start | bytes 9437192 | tf_op jit(solution)/shard_map/ppermute | solution.py:103
  956.4 143.8 %collective-permute-start.52 = (bf16[1024,2048]{1,0:T(8,128)(2,1)}, bf16[1024,2048]{1,0:T(8,128)(2,1)}, u32[]{:S(2)}, u32[]{:S(2)}) collective-permute-start(bf16[1024,2048]{1,0:T(8,128)(2,1)} %get-tuple-element.88), channel_id=1, source_target_pairs={{0,4},{4,0},{8,12},{12,8},{16,20},{20,16},{24,28},{28,24},{1,5},{5... | collective-permute-start | bytes 12582920 | tf_op jit(solution)/shard_map/ppermute | solution.py:103
  956.4 143.8 %collective-permute-start.53 = (bf16[1024,2048]{1,0:T(8,128)(2,1)}, bf16[1024,2048]{1,0:T(8,128)(2,1)}, u32[]{:S(2)}, u32[]{:S(2)}) collective-permute-start(bf16[1024,2048]{1,0:T(8,128)(2,1)} %get-tuple-element.89), channel_id=1, source_target_pairs={{0,4},{4,0},{8,12},{12,8},{16,20},{20,16},{24,28},{28,24},{1,5},{5... | collective-permute-start | bytes 12582920 | tf_op jit(solution)/shard_map/ppermute | solution.py:103
  1011.6 72.2 %collective-permute-start.60 = (bf16[192,2048]{1,0:T(8,128)(2,1)S(1)}, bf16[192,2048]{1,0:T(8,128)(2,1)S(1)}, u32[]{:S(2)}, u32[]{:S(2)}) collective-permute-start(bf16[192,2048]{1,0:T(8,128)(2,1)S(1)} %slice.868), channel_id=1, source_target_pairs={{0,24},{4,28},{8,0},{12,4},{16,8},{20,12},{24,16},{28,20},{1,25},{... | collective-permute-start | bytes 2359304 | tf_op jit(solution)/shard_map/ppermute | solution.py:103
  1018.9 280.1 %collective-permute-start.65 = (bf16[384,2048]{1,0:T(8,128)(2,1)}, bf16[384,2048]{1,0:T(8,128)(2,1)}, u32[]{:S(2)}, u32[]{:S(2)}) collective-permute-start(bf16[384,2048]{1,0:T(8,128)(2,1)} %slice.874), channel_id=1, source_target_pairs={{0,1},{1,0},{2,3},{3,2},{4,5},{5,4},{6,7},{7,6},{8,9},{9,8},{10,11... | collective-permute-start | bytes 4718600 | tf_op jit(solution)/shard_map/ppermute | solution.py:103
  1083.8 218.6 %collective-permute-start.48 = (bf16[384,2048]{1,0:T(8,128)(2,1)}, bf16[384,2048]{1,0:T(8,128)(2,1)}, u32[]{:S(2)}, u32[]{:S(2)}) collective-permute-start(bf16[384,2048]{1,0:T(8,128)(2,1)} %slice.856), channel_id=1, source_target_pairs={{0,1},{1,0},{2,3},{3,2},{4,5},{5,4},{6,7},{7,6},{8,9},{9,8},{10,11... | collective-permute-start | bytes 4718600 | tf_op jit(solution)/shard_map/ppermute | solution.py:103
  1095.5 199.5 %collective-permute-start.61 = (bf16[192,2048]{1,0:T(8,128)(2,1)}, bf16[192,2048]{1,0:T(8,128)(2,1)}, u32[]{:S(2)}, u32[]{:S(2)}) collective-permute-start(bf16[192,2048]{1,0:T(8,128)(2,1)} %add_convert_fusion.15), channel_id=1, source_target_pairs={{0,24},{4,28},{8,0},{12,4},{16,8},{20,12},{24,16},{28,20},{1,25},{... | collective-permute-start | bytes 2359304 | tf_op jit(solution)/shard_map/ppermute | solution.py:103
  1100.2 196.8 %collective-permute-start.36 = (bf16[192,2048]{1,0:T(8,128)(2,1)}, bf16[192,2048]{1,0:T(8,128)(2,1)}, u32[]{:S(2)}, u32[]{:S(2)}) collective-permute-start(bf16[192,2048]{1,0:T(8,128)(2,1)} %add_convert_fusion.18), channel_id=1, source_target_pairs={{0,24},{4,28},{8,0},{12,4},{16,8},{20,12},{24,16},{28,20},{1,25},{... | collective-permute-start | bytes 2359304 | tf_op jit(solution)/shard_map/ppermute | solution.py:103
  1283.0 291.8 %all-to-all-start.2 = ((f32[32,64,176]{2,1,0:T(8,128)}), f32[32,64,176]{2,1,0:T(8,128)}, u32[]{:S(2)}, u32[]{:S(2)}) async-start(f32[32,64,176]{2,1,0:T(8,128)} %bitcast.124), calls=%async_computation.2 | async-start | bytes 4194304 | tf_op jit(solution)/shard_map/all_to_all | solution.py:499
  1287.5 595.6 %all-gather.8.cloned.1.call-start = ((), (), s32[]{:S(2)}) async-start(), calls=%async_computation.5 | async-start | bytes 12976128 | tf_op jit(solution)/shard_map/all_gather | solution.py:484
  1290.0 168.0 %collective-permute-start.69 = (bf16[256,2048]{1,0:T(8,128)(2,1)}, bf16[256,2048]{1,0:T(8,128)(2,1)}, u32[]{:S(2)}, u32[]{:S(2)}) collective-permute-start(bf16[256,2048]{1,0:T(8,128)(2,1)} %slice.683), channel_id=1, source_target_pairs={{0,24},{4,28},{8,0},{12,4},{16,8},{20,12},{24,16},{28,20},{1,25},{... | collective-permute-start | bytes 3145736 | tf_op jit(solution)/shard_map/ppermute | solution.py:103
  1295.0 167.2 %collective-permute-start.54 = (bf16[256,2048]{1,0:T(8,128)(2,1)S(1)}, bf16[256,2048]{1,0:T(8,128)(2,1)S(1)}, u32[]{:S(2)}, u32[]{:S(2)}) collective-permute-start(bf16[256,2048]{1,0:T(8,128)(2,1)S(1)} %slice.659), channel_id=1, source_target_pairs={{0,24},{4,28},{8,0},{12,4},{16,8},{20,12},{24,16},{28,20},{1,25},{... | collective-permute-start | bytes 3145736 | tf_op jit(solution)/shard_map/ppermute | solution.py:103
  1297.0 168.1 %collective-permute-start.62 = (bf16[192,2048]{1,0:T(8,128)(2,1)S(1)}, bf16[192,2048]{1,0:T(8,128)(2,1)S(1)}, u32[]{:S(2)}, u32[]{:S(2)}) collective-permute-start(bf16[192,2048]{1,0:T(8,128)(2,1)S(1)} %add_convert_fusion.14), channel_id=1, source_target_pairs={{0,24},{4,28},{8,0},{12,4},{16,8},{20,12},{24,16},{28,20},{1,25},{... | collective-permute-start | bytes 2359304 | tf_op jit(solution)/shard_map/ppermute | solution.py:103
  1299.0 166.5 %collective-permute-start.37 = (bf16[192,2048]{1,0:T(8,128)(2,1)S(1)}, bf16[192,2048]{1,0:T(8,128)(2,1)S(1)}, u32[]{:S(2)}, u32[]{:S(2)}) collective-permute-start(bf16[192,2048]{1,0:T(8,128)(2,1)S(1)} %add_convert_fusion.17), channel_id=1, source_target_pairs={{0,24},{4,28},{8,0},{12,4},{16,8},{20,12},{24,16},{28,20},{1,25},{... | collective-permute-start | bytes 2359304 | tf_op jit(solution)/shard_map/ppermute | solution.py:103
  1302.4 133.8 %collective-permute-start.66 = (bf16[96,2048]{1,0:T(8,128)(2,1)S(1)}, bf16[96,2048]{1,0:T(8,128)(2,1)S(1)}, u32[]{:S(2)}, u32[]{:S(2)}) collective-permute-start(bf16[96,2048]{1,0:T(8,128)(2,1)S(1)} %slice.876), channel_id=1, source_target_pairs={{0,24},{4,28},{8,0},{12,4},{16,8},{20,12},{24,16},{28,20},{1,25},{... | collective-permute-start | bytes 1179656 | tf_op jit(solution)/shard_map/ppermute | solution.py:103
  1457.9 29.0 %collective-permute-start.67 = (bf16[96,2048]{1,0:T(8,128)(2,1)S(1)}, bf16[96,2048]{1,0:T(8,128)(2,1)S(1)}, u32[]{:S(2)}, u32[]{:S(2)}) collective-permute-start(bf16[96,2048]{1,0:T(8,128)(2,1)S(1)} %add_convert_fusion.27), channel_id=1, source_target_pairs={{0,24},{4,28},{8,0},{12,4},{16,8},{20,12},{24,16},{28,20},{1,25},{... | collective-permute-start | bytes 1179656 | tf_op jit(solution)/shard_map/ppermute | solution.py:103
  1458.0 42.8 %collective-permute-start.50 = (bf16[96,2048]{1,0:T(8,128)(2,1)S(1)}, bf16[96,2048]{1,0:T(8,128)(2,1)S(1)}, u32[]{:S(2)}, u32[]{:S(2)}) collective-permute-start(bf16[96,2048]{1,0:T(8,128)(2,1)S(1)} %add_convert_fusion.31), channel_id=1, source_target_pairs={{0,24},{4,28},{8,0},{12,4},{16,8},{20,12},{24,16},{28,20},{1,25},{... | collective-permute-start | bytes 1179656 | tf_op jit(solution)/shard_map/ppermute | solution.py:103
  1462.2 103.4 %collective-permute-start.70 = (bf16[256,2048]{1,0:T(8,128)(2,1)S(1)}, bf16[256,2048]{1,0:T(8,128)(2,1)S(1)}, u32[]{:S(2)}, u32[]{:S(2)}) collective-permute-start(bf16[256,2048]{1,0:T(8,128)(2,1)S(1)} %add_convert_fusion.8), channel_id=1, source_target_pairs={{0,24},{4,28},{8,0},{12,4},{16,8},{20,12},{24,16},{28,20},{1,25},{... | collective-permute-start | bytes 3145736 | tf_op jit(solution)/shard_map/ppermute | solution.py:103
  1465.1 103.7 %collective-permute-start.55 = (bf16[256,2048]{1,0:T(8,128)(2,1)S(1)}, bf16[256,2048]{1,0:T(8,128)(2,1)S(1)}, u32[]{:S(2)}, u32[]{:S(2)}) collective-permute-start(bf16[256,2048]{1,0:T(8,128)(2,1)S(1)} %add_convert_fusion.12), channel_id=1, source_target_pairs={{0,24},{4,28},{8,0},{12,4},{16,8},{20,12},{24,16},{28,20},{1,25},{... | collective-permute-start | bytes 3145736 | tf_op jit(solution)/shard_map/ppermute | solution.py:103
  1465.6 35.4 %collective-permute-start.63 = (bf16[96,2048]{1,0:T(8,128)(2,1)S(1)}, bf16[96,2048]{1,0:T(8,128)(2,1)S(1)}, u32[]{:S(2)}, u32[]{:S(2)}) collective-permute-start(bf16[96,2048]{1,0:T(8,128)(2,1)S(1)} %slice.872), channel_id=1, source_target_pairs={{0,2},{1,3},{2,0},{3,1},{4,6},{5,7},{6,4},{7,5},{8,10},{9,11},{10,... | collective-permute-start | bytes 1179656 | tf_op jit(solution)/shard_map/ppermute | solution.py:103
  1500.9 64.6 %collective-permute-start.68 = (bf16[96,2048]{1,0:T(8,128)(2,1)S(1)}, bf16[96,2048]{1,0:T(8,128)(2,1)S(1)}, u32[]{:S(2)}, u32[]{:S(2)}) collective-permute-start(bf16[96,2048]{1,0:T(8,128)(2,1)S(1)} %add_convert_fusion.26), channel_id=1, source_target_pairs={{0,24},{4,28},{8,0},{12,4},{16,8},{20,12},{24,16},{28,20},{1,25},{... | collective-permute-start | bytes 1179656 | tf_op jit(solution)/shard_map/ppermute | solution.py:103
  1501.0 72.9 %collective-permute-start.51 = (bf16[96,2048]{1,0:T(8,128)(2,1)S(1)}, bf16[96,2048]{1,0:T(8,128)(2,1)S(1)}, u32[]{:S(2)}, u32[]{:S(2)}) collective-permute-start(bf16[96,2048]{1,0:T(8,128)(2,1)S(1)} %add_convert_fusion.30), channel_id=1, source_target_pairs={{0,24},{4,28},{8,0},{12,4},{16,8},{20,12},{24,16},{28,20},{1,25},{... | collective-permute-start | bytes 1179656 | tf_op jit(solution)/shard_map/ppermute | solution.py:103
  1567.0 29.5 %collective-permute-start.71 = (bf16[256,2048]{1,0:T(8,128)(2,1)}, bf16[256,2048]{1,0:T(8,128)(2,1)}, u32[]{:S(2)}, u32[]{:S(2)}) collective-permute-start(bf16[256,2048]{1,0:T(8,128)(2,1)} %add_convert_fusion.7), channel_id=1, source_target_pairs={{0,24},{4,28},{8,0},{12,4},{16,8},{20,12},{24,16},{28,20},{1,25},{... | collective-permute-start | bytes 3145736 | tf_op jit(solution)/shard_map/ppermute | solution.py:103
  1570.3 46.7 %collective-permute-start.56 = (bf16[256,2048]{1,0:T(8,128)(2,1)}, bf16[256,2048]{1,0:T(8,128)(2,1)}, u32[]{:S(2)}, u32[]{:S(2)}) collective-permute-start(bf16[256,2048]{1,0:T(8,128)(2,1)} %add_convert_fusion.11), channel_id=1, source_target_pairs={{0,24},{4,28},{8,0},{12,4},{16,8},{20,12},{24,16},{28,20},{1,25},{... | collective-permute-start | bytes 3145736 | tf_op jit(solution)/shard_map/ppermute | solution.py:103
  1598.5 23.4 %collective-permute-start.72 = (bf16[128,2048]{1,0:T(8,128)(2,1)S(1)}, bf16[128,2048]{1,0:T(8,128)(2,1)S(1)}, u32[]{:S(2)}, u32[]{:S(2)}) collective-permute-start(bf16[128,2048]{1,0:T(8,128)(2,1)S(1)} %slice.880), channel_id=1, source_target_pairs={{0,2},{1,3},{2,0},{3,1},{4,6},{5,7},{6,4},{7,5},{8,10},{9,11},{10,... | collective-permute-start | bytes 1572872 | tf_op jit(solution)/shard_map/ppermute | solution.py:103
  1640.8 22.3 %collective-permute-start.75 = (bf16[256,1024]{1,0:T(8,128)(2,1)}, bf16[256,1024]{1,0:T(8,128)(2,1)}, u32[]{:S(2)}, u32[]{:S(2)}) collective-permute-start(bf16[256,1024]{1,0:T(8,128)(2,1)} %pad_maximum_fusion.21), channel_id=1, source_target_pairs={{0,2},{1,3},{2,0},{3,1},{4,6},{5,7},{6,4},{7,5},{8,10},{9,11},{10,... | collective-permute-start | bytes 1572872 | tf_op jit(solution)/shard_map/ppermute | solution.py:109
  1675.3 142.9 %collective-permute-start.103 = (bf16[1024,512]{1,0:T(8,128)(2,1)}, bf16[1024,512]{1,0:T(8,128)(2,1)}, u32[]{:S(2)}, u32[]{:S(2)}) collective-permute-start(bf16[1024,512]{1,0:T(8,128)(2,1)} %bitcast.114), channel_id=1, source_target_pairs={{0,4},{4,0},{8,12},{12,8},{16,20},{20,16},{24,28},{28,24},{1,5},{5... | collective-permute-start | bytes 3145736 | tf_op jit(solution)/shard_map/ppermute | solution.py:103
  1760.5 31.1 %collective-permute-start.77 = (bf16[512,576]{0,1:T(8,128)(2,1)}, bf16[512,576]{0,1:T(8,128)(2,1)}, u32[]{:S(2)}, u32[]{:S(2)}) collective-permute-start(bf16[512,576]{0,1:T(8,128)(2,1)} %fusion.60), channel_id=1, source_target_pairs={{0,2},{1,3},{2,0},{3,1},{4,6},{5,7},{6,4},{7,5},{8,10},{9,11},{10,... | collective-permute-start | bytes 1769480 | tf_op jit(solution)/shard_map/ppermute | solution.py:103
  1800.1 42.7 %collective-permute-start.92 = (bf16[1024,1024]{1,0:T(8,128)(2,1)}, bf16[1024,1024]{1,0:T(8,128)(2,1)}, u32[]{:S(2)}, u32[]{:S(2)}) collective-permute-start(bf16[1024,1024]{1,0:T(8,128)(2,1)} %bitcast.97), channel_id=1, source_target_pairs={{0,4},{4,0},{8,12},{12,8},{16,20},{20,16},{24,28},{28,24},{1,5},{5... | collective-permute-start | bytes 6291464 | tf_op jit(solution)/shard_map/ppermute | solution.py:103
  1825.4 36.1 %collective-permute-start.82 = (bf16[256,144]{0,1:T(8,128)(2,1)}, bf16[256,144]{0,1:T(8,128)(2,1)}, u32[]{:S(2)}, u32[]{:S(2)}) collective-permute-start(bf16[256,144]{0,1:T(8,128)(2,1)} %get-tuple-element.284), channel_id=1, source_target_pairs={{0,1},{1,0},{2,3},{3,2},{4,5},{5,4},{6,7},{7,6},{8,9},{9,8},{10,11... | collective-permute-start | bytes 221192 | tf_op jit(solution)/shard_map/ppermute | solution.py:109
  1826.7 37.1 %collective-permute-start.83 = (bf16[256,144]{0,1:T(8,128)(2,1)}, bf16[256,144]{0,1:T(8,128)(2,1)}, u32[]{:S(2)}, u32[]{:S(2)}) collective-permute-start(bf16[256,144]{0,1:T(8,128)(2,1)} %get-tuple-element.283), channel_id=1, source_target_pairs={{0,2},{1,3},{2,0},{3,1},{4,6},{5,7},{6,4},{7,5},{8,10},{9,11},{10,... | collective-permute-start | bytes 221192 | tf_op jit(solution)/shard_map/ppermute | solution.py:109
  1827.3 39.8 %collective-permute-start.84 = (bf16[256,144]{0,1:T(8,128)(2,1)}, bf16[256,144]{0,1:T(8,128)(2,1)}, u32[]{:S(2)}, u32[]{:S(2)}) collective-permute-start(bf16[256,144]{0,1:T(8,128)(2,1)} %get-tuple-element.285), channel_id=1, source_target_pairs={{0,3},{1,2},{2,1},{3,0},{4,7},{5,6},{6,5},{7,4},{8,11},{9,10},{10,... | collective-permute-start | bytes 221192 | tf_op jit(solution)/shard_map/ppermute | solution.py:109
  1851.2 23.6 %collective-permute-start.107 = (bf16[64,512]{1,0:T(8,128)(2,1)}, bf16[64,512]{1,0:T(8,128)(2,1)}, u32[]{:S(2)}, u32[]{:S(2)}) collective-permute-start(bf16[64,512]{1,0:T(8,128)(2,1)} %get-tuple-element.288), channel_id=1, source_target_pairs={{0,1},{1,0},{2,3},{3,2},{4,5},{5,4},{6,7},{7,6},{8,9},{9,8},{10,11... | collective-permute-start | bytes 196616 | tf_op jit(solution)/shard_map/ppermute | solution.py:109
  1882.9 33.9 %collective-permute-start.95 = (bf16[256,1024]{1,0:T(8,128)(2,1)}, bf16[256,1024]{1,0:T(8,128)(2,1)}, u32[]{:S(2)}, u32[]{:S(2)}) collective-permute-start(bf16[256,1024]{1,0:T(8,128)(2,1)} %add_convert_fusion.21), channel_id=1, source_target_pairs={{0,24},{4,28},{8,0},{12,4},{16,8},{20,12},{24,16},{28,20},{1,25},{... | collective-permute-start | bytes 1572872 | tf_op jit(solution)/shard_map/ppermute | solution.py:103
  (168 other events, 2992.7 us)
Sparse Core Ops, SparseCore 0:
  86.0 77.4 all-gather.3
  166.3 239.4 all-gather.5
  1293.7 233.6 all-gather.7

commit v2 on v1

--- a/solution.py
+++ b/solution.py
@@ -87,50 +87,52 @@
     def __init__(self):
         self.dp = lax.axis_size("dp")
         self.ctx = lax.axis_size("ctx")
-        self.size = {"z": self.dp // 2, "c": 2, "y": self.ctx // 2, "x": 2}
+        self.size = {"z": self.dp // 2, "c": 2, "w": self.ctx // 4, "y": 2, "x": 2}
         dp, ctx = lax.axis_index("dp"), lax.axis_index("ctx")
-        self.own = {"z": dp // 2, "c": dp % 2, "y": ctx // 2, "x": ctx % 2}
-
-    def shift(self, value, axis, by):
-        if axis in "zc":
-            name, count = "dp", self.dp
+        self.own = {
+            "z": dp // 2,
+            "c": dp % 2,
+            "w": ctx // 4,
+            "y": (ctx // 2) % 2,
+            "x": ctx % 2,
+        }
+
+    def shift(self, value, axis, by=1):
+        name, count = ("dp", self.dp) if axis in "zc" else ("ctx", self.ctx)
+        if axis == "z":
+            pairs = [(i, (i + 2 * by) % count) for i in range(count)]
+        elif axis == "w":
+            pairs = [(i, (i + 4 * by) % count) for i in range(count)]
         else:
-            name, count = "ctx", self.ctx
-        if axis in "zy":
-            pairs = [(i, (i + 2 * by) % count) for i in range(count)]
-        else:
-            pairs = [(i, i ^ 1) for i in range(count)]
+            pairs = [(i, i ^ (2 if axis == "y" else 1)) for i in range(count)]
         return lax.ppermute(value, name, pairs)
 
-    def shift_ctx(self, value, ky, kx):
+    def shift_ctx(self, value, k):
         pairs = [
-            (i, ((i // 2 - ky) % (self.ctx // 2)) * 2 + (i + kx) % 2) for i in range(self.ctx)
+            (i, (i // 4 - k // 4) % self.size["w"] * 4 + (i ^ k) % 4) for i in range(self.ctx)
         ]
         return lax.ppermute(value, "ctx", pairs)
 
     def ring(self, block, axis):
         held = [block]
         for _ in range(self.size[axis] - 1):
-            held.append(self.shift(held[-1], axis, 1))
+            held.append(self.shift(held[-1], axis))
         return held
 
     def gather(self, block, order):
         for axis in order:
-            block = jnp.concatenate(self.ring(block, axis), axis=0)
+            block = joined_rows(self.ring(block, axis))
         return block
 
     def reduce(self, parts, axis):
         total = parts[-1]
         for part in parts[-2::-1]:
-            moved = self.shift(total, axis, -1)
-            total = (moved.astype(f32) + part.astype(f32)).astype(bf16)
+            total = plus(self.shift(total, axis, -1), part)
         return total
 
     def scatter_sum(self, block, order):
         for axis in order[::-1]:
-            count = self.size[axis]
-            rows = block.shape[0] // count
-            block = self.reduce([block[k * rows : (k + 1) * rows] for k in range(count)], axis)
+            block = self.reduce(jnp.split(block, self.size[axis]), axis)
         return block
 
     def device_of(self, order):
@@ -141,15 +143,16 @@
             shape[depth - 1 - i] = self.size[axis]
             offsets = jnp.arange(self.size[axis], dtype=jnp.int32).reshape(shape)
             place[axis] = (self.own[axis] - offsets) % self.size[axis]
-        number = ((place["z"] * 2 + place["c"]) * self.size["y"] + place["y"]) * 2 + place["x"]
+        number = (place["z"] * 2 + place["c"]) * self.ctx
+        number = number + place["w"] * 4 + place["y"] * 2 + place["x"]
         return number.reshape(-1)
 
     def place_of(self, order):
-        count = self.dp * self.ctx
-        number = jnp.arange(count, dtype=jnp.int32)
+        number = jnp.arange(self.dp * self.ctx, dtype=jnp.int32)
         coordinate = {
             "x": number % 2,
-            "y": (number // 2) % self.size["y"],
+            "y": (number // 2) % 2,
+            "w": (number // 4) % self.size["w"],
             "c": (number // self.ctx) % 2,
             "z": number // (2 * self.ctx),
         }
@@ -160,31 +163,31 @@
         return place
 
     def ctx_relative(self):
-        y = (self.own["y"] - jnp.arange(self.size["y"], dtype=jnp.int32)) % self.size["y"]
-        x = (self.own["x"] - jnp.arange(2, dtype=jnp.int32)) % 2
-        return (y[:, None] * 2 + x[None, :]).reshape(-1)
+        return self.device_of(("x", "y", "w")) % self.ctx
+
+    def ctx_place(self):
+        number = jnp.arange(self.ctx, dtype=jnp.int32)
+        w = (self.own["w"] - number // 4) % self.size["w"]
+        return w * 4 + (lax.axis_index("ctx") ^ number) % 4
 
     def ctx_exchange(self, pieces):
-        ny = self.size["y"]
         result = [pieces[0]] + [None] * (self.ctx - 1)
         for k in range(1, self.ctx):
-            ky, kx = k // 2, k % 2
-            result[((-ky) % ny) * 2 + kx] = self.shift_ctx(pieces[k], ky, kx)
+            back = (-(k // 4)) % self.size["w"] * 4 + k % 4
+            result[back] = self.shift_ctx(pieces[k], k)
         return result
 
-    def ctx_gather(self, block):
-        half = block.shape[0] // 2
-        ny = self.size["y"]
-        first = self.ring(block[:half], "x")
-        first = self.ring(jnp.concatenate(first, axis=0), "y")
-        second = self.ring(block[half:], "y")
-        second = self.ring(jnp.concatenate(second, axis=0), "x")
-        pieces = []
-        for ky in range(ny):
-            for kx in range(2):
-                pieces.append(first[ky][kx * half : (kx + 1) * half])
-                pieces.append(second[kx][ky * half : (ky + 1) * half])
-        return jnp.concatenate(pieces, axis=0)
+
+def joined_rows(parts):
+    return parts[0] if len(parts) == 1 else jnp.concatenate(parts, axis=0)
+
+
+def plus(left, right):
+    return (left.astype(f32) + right.astype(f32)).astype(bf16)
+
+
+def tie(*values):
+    return lax.optimization_barrier(values)
 
 
 def after(value, *others):
@@ -194,12 +197,13 @@
 GROUP = 4
 
 
-def ffn_kernel(half_ff, adds, devices_ref, x_ref, *refs):
+def ffn_kernel(half_ff, parts, part_steps, sources, x_ref, *refs):
     g_refs, (m_ref, w_in, w_out) = refs[:GROUP], refs[GROUP : GROUP + 3]
     refs = refs[GROUP + 3 :]
-    if adds:
-        add_out, add_grad = refs[:2]
-    x_all, g_all, act, grad_pre, out, row_grad = refs[-6:]
+    if parts:
+        moved, refs = refs[0], refs[1:]
+    outs = refs[-max(2 * parts, 1) :]
+    x_all, g_all, act, grad_pre = refs[-len(outs) - 4 : -len(outs)]
     half_all = act.shape[1]
     count = x_ref.shape[0] // GROUP
     x_all[...] = x_ref[...]
@@ -218,53 +222,85 @@
     grad_pre[:, half_all:] = (grad_act * swished).astype(bf16)
     out_part = matmul(act[...], w_out[...])
     grad_part = matmul_right_t(grad_pre[...], w_in[...])
-    if adds:
-        out_part = out_part + add_out[...].astype(f32)
-        grad_part = grad_part + add_grad[...].astype(f32)
-    out[...] = out_part.astype(bf16)
-    row_grad[...] = grad_part.astype(bf16)
-
-
-def ffn_chunk(x, g_blocks, m, w_in, w_out, half_ff, source, place, kept, start, tokens, adds):
+    if not parts:
+        outs[0][:, :D] = out_part.astype(bf16)
+        outs[0][:, D:] = grad_part.astype(bf16)
+        return
+    out_part = (out_part + moved[:, :D].astype(f32)).astype(bf16)
+    grad_part = (grad_part + moved[:, D:].astype(f32)).astype(bf16)
+    for k in range(parts):
+
+        @pl.when(pl.program_id(0) // part_steps == k)
+        def _():
+            outs[2 * k][...] = out_part
+            outs[2 * k + 1][...] = grad_part
+
+
+def ffn_chunk(x, g_blocks, m, w_in, w_out, half_ff, sources, group, far, side, kept, moved, lean):
     half_all = w_out.shape[0]
-    count = x.shape[0] // source.shape[0]
+    tokens = m.shape[0]
+    count = tokens // sources.shape[0]
     tile = GROUP * count
     steps = x.shape[0] // tile
-    base = start // tile
-
-    def rows(width, first=0):
-        return pl.BlockSpec((tile, width), lambda i, _: (first + i, 0))
+    parts = 4 if far == 2 else 2
+    half = steps // parts
+    per_slice = 4 * half
+    base = 2 * group * per_slice + (2 * side + far % 2) * half
+
+    def second(i):
+        return (i // half) % 2
+
+    def place(i):
+        return base + i % half + second(i) * per_slice + i // (2 * half) * half
+
+    def rows(width):
+        return pl.BlockSpec((tile, width), lambda i, _: (i, 0))
+
+    def kept_rows(width):
+        return pl.BlockSpec((tile, width), lambda i, _: (i if lean else place(i), 0))
 
     def whole(value):
         return pl.BlockSpec(value.shape, lambda i, _: (0, 0), pipeline_mode=pl.Buffered(1))
 
     def g_spec(j):
-        return pl.BlockSpec((1, count, D), lambda i, s: (s[GROUP * i + j], place, 0))
-
-    operands = [source, x] + [g_blocks] * GROUP + [m, w_in, w_out]
+        def index(i, s):
+            return (s[GROUP * place(i) + j], 2 * group + second(i), 0)
+
+        return pl.BlockSpec((1, count, D), index)
+
+    operands = [sources, x] + [g_blocks] * GROUP + [m, w_in, w_out]
     in_specs = [rows(D)] + [g_spec(j) for j in range(GROUP)]
-    in_specs += [rows(1), whole(w_in), whole(w_out)]
-    if adds is not None:
-        operands += adds
-        in_specs += [rows(D)] * 2
+    in_specs += [pl.BlockSpec((tile, 1), lambda i, _: (place(i), 0)), whole(w_in), whole(w_out)]
+    out_specs = [rows(2 * D)]
+    out_shape = [jax.ShapeDtypeStruct((x.shape[0], 2 * D), bf16)]
+    if moved is not None:
+        operands.append(moved)
+        in_specs.append(rows(2 * D))
+
+        def part_spec(k):
+            return pl.BlockSpec(
+                (tile, D), lambda i, _: (jnp.clip(i - k * half, 0, half - 1), 0)
+            )
+
+        out_specs = [part_spec(k // 2) for k in range(2 * parts)]
+        out_shape = [jax.ShapeDtypeStruct((half * tile, D), bf16)] * (2 * parts)
     aliases = {}
     if kept is not None:
         aliases = {len(operands) + i: i for i in range(4)}
         operands += kept
         in_specs += [pl.BlockSpec(memory_space=pl.ANY)] * 4
     widths = (D, D, half_all, 2 * half_all)
-    out_shape = [jax.ShapeDtypeStruct((tokens, w), bf16) for w in widths]
-    out_shape += [jax.ShapeDtypeStruct(x.shape, bf16)] * 2
+    kept_count = x.shape[0] if lean else tokens
     flops = 2 * x.shape[0] * D * 6 * half_all
     result = pl.pallas_call(
-        lambda *refs: ffn_kernel(half_ff, adds is not None, *refs),
+        lambda *refs: ffn_kernel(half_ff, 0 if moved is None else parts, half, *refs),
         grid_spec=pltpu.PrefetchScalarGridSpec(
             num_scalar_prefetch=1,
             grid=(steps,),
             in_specs=in_specs,
-            out_specs=[rows(w, base) for w in widths] + [rows(D)] * 2,
+            out_specs=[kept_rows(w) for w in widths] + out_specs,
         ),
-        out_shape=out_shape,
+        out_shape=[jax.ShapeDtypeStruct((kept_count, w), bf16) for w in widths] + out_shape,
         input_output_aliases=aliases,
         compiler_params=pltpu.CompilerParams(vmem_limit_bytes=60 * 2**20),
         cost_estimate=pl.CostEstimate(
@@ -272,7 +308,7 @@
         ),
         name="ffn_chunk",
     )(*operands)
-    return result[:4], result[4], result[5]
+    return list(result[:4]), list(result[4:])
 
 
 def shards(
@@ -313,51 +349,96 @@
     up_parts = rows_d // rows_l
     scale = 1.0 / math.sqrt(NOPE + ROPE)
     rel_ctx = links.ctx_relative()
-    ctx_number = jnp.arange(ctx, dtype=jnp.int32)
-    ctx_place = ((links.own["y"] - ctx_number // 2) % links.size["y"]) * 2 + (
-        links.own["x"] - ctx_number
-    ) % 2
+    ctx_place = links.ctx_place()
 
     def columns(value, k, width):
         return lax.dynamic_slice_in_dim(value, rel_ctx[k] * width, width, 1)
 
-    hidden_row = links.ctx_gather(hidden_in)
     latent_gain = jnp.zeros((rows_d,), bf16).at[:rows_l].set(norm_latent)
     small = jnp.concatenate(
         [w_kv_down, norm_attn[:, None], norm_ffn[:, None], latent_gain[:, None]], axis=1
     )
     small = jnp.pad(small, ((0, 0), (0, -small.shape[1] % 128)))
-    small_order = ("z", "x", "y", "c")
-    small_all = links.gather(small, small_order).reshape(devices, rows_d, small.shape[1])
-    small_all = small_all[links.place_of(small_order)]
-    down_w = small_all[:, :, : LATENT + ROPE].reshape(D, LATENT + ROPE)
-    gain_attn = small_all[:, :, LATENT + ROPE].reshape(D).astype(f32)
-    gain_ffn = small_all[:, :, LATENT + ROPE + 1].reshape(D).astype(f32)
-    gain_latent = small_all[:, :rows_l, LATENT + ROPE + 2].reshape(LATENT).astype(f32)
-
+    small_cols = small.shape[1]
+    small = jnp.concatenate([small, w_out], axis=1)
     pieces = []
     for k in range(ctx):
         folded = columns(w_kv_up, k, kv_cols).reshape(rows_l, up_parts, up_fold)
         folded = folded.transpose(1, 0, 2).reshape(rows_d, up_fold)
         pieces.append(jnp.concatenate([columns(w_query, k, q_cols), folded], axis=1))
-    heads_w = jnp.concatenate(links.ctx_exchange(pieces), axis=0)
-    heads_w = links.gather(heads_w, ("z", "c")).reshape(devices, rows_d, q_cols + up_fold)
-    heads_place = links.place_of(("x", "y", "z", "c"))
+    hidden_parts = links.ctx_exchange([hidden_in] * ctx)
+    step, *received = tie(links.shift(small, "z"), *links.ctx_exchange(pieces))
+    heads_w = joined_rows(received)
+    small_parts, heads_parts = [small, step], [heads_w]
+    for i in range(links.size["z"] - 1):
+        pair = [links.shift(heads_parts[-1], "z")]
+        if i < links.size["z"] - 2:
+            pair.append(links.shift(small_parts[-1], "z"))
+        else:
+            small_all = links.gather(joined_rows(small_parts), ("w",))
+            small_all = small_all.reshape(-1, 2, rows_d // 2, small.shape[1])
+            small_a = small_all[:, 0].reshape(-1, small.shape[1])
+            small_b = small_all[:, 1].reshape(-1, small.shape[1])
+            pair += [links.shift(small_a, "x"), links.shift(small_b, "y")]
+        pair = list(tie(*pair))
+        if i < links.size["z"] - 2:
+            small_parts.append(pair[1])
+        if i == 0:
+            w_shared_in, _ = tie(w_shared_in, pair[0])
+        if i == links.size["z"] - 3:
+            pair[0], *hidden_parts = tie(pair[0], *hidden_parts)
+            hidden_row = joined_rows(hidden_parts)
+        heads_parts.append(pair[0])
+    small_a, small_b = joined_rows([small_a, pair[1]]), joined_rows([small_b, pair[2]])
+    heads_w = joined_rows(heads_parts)
+    heads_c = links.shift(heads_w, "c")
+    last_a, last_b = small_a[:, small_cols:], small_b[:, small_cols:]
+    small_a, small_b = small_a[:, :small_cols], small_b[:, :small_cols]
+    shared_pieces = jnp.concatenate(
+        [
+            w_shared_in[:, :SHARED_FF].reshape(rows_d, devices, half_sh),
+            w_shared_in[:, SHARED_FF:].reshape(rows_d, devices, half_sh),
+        ],
+        axis=2,
+    ).transpose(1, 0, 2)
+    shared_w = lax.all_to_all(shared_pieces, BOTH, split_axis=0, concat_axis=0, tiled=True)
+    far_a, far_b, shared_w = tie(links.shift(small_a, "y"), links.shift(small_b, "x"), shared_w)
+    small_all = joined_rows([small_a, far_a, small_b, far_b])
+    small_all = joined_rows([small_all, links.shift(small_all, "c")])
+    heads_w = joined_rows([heads_w, heads_c]).reshape(devices, rows_d, q_cols + up_fold)
+    blocks = devices // 2
+    place_a = links.place_of(("z", "w", "x", "y", "c"))
+    place_b = links.place_of(("z", "w", "y", "x", "c"))
+    take_a = (place_a // blocks) * 2 * blocks + place_a % blocks
+    take_b = (place_b // blocks) * 2 * blocks + blocks + place_b % blocks
+    take = jnp.stack([take_a, take_b], axis=1).reshape(-1)
+    small_all = small_all.reshape(2 * devices, rows_d // 2, small_cols)[take]
+    small_all = small_all.reshape(devices, rows_d, small_cols)
+    down_w = small_all[:, :, : LATENT + ROPE].reshape(D, LATENT + ROPE)
+    gain_attn = small_all[:, :, LATENT + ROPE].reshape(D).astype(f32)
+    gain_ffn = small_all[:, :, LATENT + ROPE + 1].reshape(D).astype(f32)
+    gain_latent = small_all[:, :rows_l, LATENT + ROPE + 2].reshape(LATENT).astype(f32)
+
+    heads_place = links.place_of(("x", "y", "w", "z", "c"))
     heads_w = heads_w[heads_place]
     query_w = heads_w[:, :, :q_cols].reshape(D, q_cols)
     up_w = heads_w[:, :, q_cols:].reshape(devices, up_parts, rows_l, up_fold)
     up_w = up_w.transpose(0, 2, 1, 3).reshape(LATENT, kv_cols)
 
-    experts = devices // 2
-    expert_number = jnp.arange(experts, dtype=jnp.int32)[:, None, None]
-    gate_matrix = jnp.sum(
-        jnp.where(routes.T[None] == expert_number, gates.T[None], 0.0), axis=1
-    )
-    m_all = lax.all_to_all(
-        jnp.repeat(gate_matrix, 2, axis=0), BOTH, split_axis=0, concat_axis=0, tiled=True
-    )
-    out_w = lax.all_gather(after(w_out, heads_w, hidden_row), BOTH, axis=0, tiled=True)
-    g_all = lax.all_gather(after(cotangent, out_w), BOTH, axis=0, tiled=True)
+    orders = (
+        ("z", "w", "x", "y"),
+        ("z", "w", "y", "x"),
+        ("y", "z", "w", "x"),
+        ("x", "z", "w", "y"),
+    )
+    slices = len(orders)
+    count = tok // slices
+    tokens = devices * tok
+    source_list = [links.device_of(order + ("c",)) for order in orders]
+    sources = jnp.concatenate(source_list)
+    m_place = jnp.concatenate([d * slices + i for i, d in enumerate(source_list)])
+    hidden_row, query_w, up_w, down_w = tie(hidden_row, query_w, up_w, down_w)
+    g_all = lax.all_gather(after(cotangent, far_a), BOTH, axis=0, tiled=True)
     g_blocks = g_all.reshape(devices, tok, D)
 
     inputs_row = hidden_row.astype(f32)
@@ -384,6 +465,11 @@
     latent = (raw_latent * inverse_latent * gain_latent).astype(bf16)
     key_rope = rotate(compressed[:, LATENT:], cosine, sine_part).astype(bf16)
     keyval = matmul(latent, up_w).astype(bf16).reshape(row, heads, NOPE + VDIM)
+    last_a, last_b = tie(last_a, last_b, far_a)[:2]
+    last_y, last_x, keyval = tie(links.shift(last_a, "y"), links.shift(last_b, "x"), keyval)
+    out_w = joined_rows([last_a, last_y, last_b, last_x])
+    out_w = joined_rows([out_w, links.shift(out_w, "c")])
+    out_w = out_w.reshape(2 * devices, rows_d // 2, D)[take].reshape(D, D)
     keyval = keyval.transpose(1, 0, 2)
     key = jnp.concatenate(
         [keyval[..., :NOPE], jnp.broadcast_to(key_rope[None], (heads, row, ROPE))], axis=-1
@@ -409,14 +495,30 @@
     inverse_ffn = rms_inverse(middle)
     ffn_in = (middle * inverse_ffn * gain_ffn).astype(bf16)
 
-    shared_pieces = jnp.concatenate(
-        [
-            w_shared_in[:, :SHARED_FF].reshape(rows_d, devices, half_sh),
-            w_shared_in[:, SHARED_FF:].reshape(rows_d, devices, half_sh),
-        ],
-        axis=2,
-    ).transpose(1, 0, 2)
-    shared_w = lax.all_to_all(shared_pieces, BOTH, split_axis=0, concat_axis=0, tiled=True)
+    cut = [ffn_in[i * count : (i + 1) * count] for i in range(slices)]
+
+    def halved(parts):
+        both = [jnp.split(part, 2) for part in parts]
+        return [joined_rows([pair[i] for pair in both]) for i in range(2)]
+
+    held = joined_rows(cut[:2])
+    near_y, near_x, first, shared_w, w_expert_in, routes, gates = tie(
+        links.shift(cut[2], "y"),
+        links.shift(cut[3], "x"),
+        links.shift(held, "z"),
+        shared_w,
+        w_expert_in,
+        routes,
+        gates,
+    )
+    experts = devices // 2
+    expert_number = jnp.arange(experts, dtype=jnp.int32)[:, None, None]
+    gate_matrix = jnp.sum(
+        jnp.where(routes.T[None] == expert_number, gates.T[None], 0.0), axis=1
+    )
+    m_all = lax.all_to_all(
+        jnp.repeat(gate_matrix, 2, axis=0), BOTH, split_axis=0, concat_axis=0, tiled=True
+    )
     shared_w = shared_w.reshape(D, 2 * half_sh)
     pad = half_all - half_ff - half_sh
     w_in = jnp.concatenate(
@@ -431,81 +533,190 @@
     w_back = jnp.concatenate(
         [w_expert_out[0], jnp.pad(w_shared_out, ((0, pad), (0, 0)))], axis=0
     )
-
-    most_rows = 3 * tok // 8
-    paths = (
-        (("y", "z", "x"), 0, most_rows),
-        (("z", "x", "y"), most_rows, most_rows),
-        (("x", "y", "z"), 2 * most_rows, tok - 2 * most_rows),
-    )
-    tokens = devices * tok
-    x_own, x_sib = [], []
-    for order, start, count in paths:
-        x_own.append(links.gather(ffn_in[start : start + count], order))
-    for x in x_own:
-        x_sib.append(links.shift(x, "c", 1))
-    region = [0] * 6
-    for i in range(1, 6):
-        region[i] = region[i - 1] + x_own[(i - 1) // 2].shape[0]
+    m = m_all.reshape(devices * slices, count)[m_place].reshape(tokens, 1)
+    ring_a = [held, first]
+    while len(ring_a) < links.size["z"]:
+        ring_a.append(links.shift(ring_a[-1], "z"))
+    held = links.gather(joined_rows(ring_a), ("w",)) if links.size["w"] > 1 else None
+    slice_0, slice_1 = halved(jnp.split(held, ctx // 4 * links.size["z"]) if held is not None else ring_a)
+    held = joined_rows([cut[2], near_y, cut[3], near_x])
+    held, slice_0, slice_1, w_in, w_back, m = tie(held, slice_0, slice_1, w_in, w_back, m)
+    ring_b = [held]
+    moved_0, moved_1, step = tie(
+        links.shift(slice_0, "x"), links.shift(slice_1, "y"), links.shift(held, "z")
+    )
+    ring_b.append(step)
+    near_a = [joined_rows([slice_0, moved_0]), joined_rows([slice_1, moved_1])]
+    far_a = [links.shift(near_a[0], "y"), links.shift(near_a[1], "x")]
+    near_a_rows = joined_rows(near_a)
+    near_a_sib = links.shift(near_a_rows, "c")
+
+    lean = devices > 32
     kept = None
-    moved, outs, row_grads = [None] * 3, [None] * 3, [None] * 3
-
-    def ffn(i, side, kept, adds):
-        order, start, count = paths[i]
-        source = links.device_of(order + ("c",)).reshape(2, -1)[side]
-        m = m_all[source][:, start : start + count].reshape(-1, 1)
-        return ffn_chunk(
-            (x_own, x_sib)[side][i],
+    done, moved = {}, {}
+
+    def ffn(rows, name, side):
+        kept_now, parts = ffn_chunk(
+            rows,
             g_blocks,
             m,
             w_in,
             w_back,
             half_ff,
-            source,
-            start // count,
-            kept,
-            region[2 * i + side],
-            tokens,
-            adds,
+            sources,
+            "ab".index(name[0]),
+            ("n", "f", "").index(name[1:]),
+            side,
+            None if lean else kept,
+            moved.get(name) if side == 0 else None,
+            lean,
         )
-
-    for i, side in ((0, 1), (1, 1), (0, 0), (2, 1), (1, 0), (2, 0)):
         if side == 1:
-            kept, out, grad = ffn(i, 1, kept, None)
-            moved[i] = [links.shift(out, "c", -1), links.shift(grad, "c", -1)]
-        else:
-            kept, out, grad = ffn(i, 0, kept, moved[i])
-            row_grads[i] = links.scatter_sum(grad, paths[i][0])
-            outs[i] = links.scatter_sum(out, paths[i][0])
-    ffn_out = jnp.concatenate(outs, axis=0).astype(f32)
-    grad_ffn = jnp.concatenate(row_grads, axis=0).astype(f32)
-    mixed = (middle + ffn_out).astype(bf16)
-    x_all, g_kept, act_all, grad_pre_all = kept
-    query_w_all = lax.all_gather(after(w_query, moved[2][0]), BOTH, axis=0, tiled=True)
-    grad_w_in = matmul_left_t(x_all, grad_pre_all)
-    grad_w_back = matmul_left_t(act_all, g_kept)
-    grad_w_expert_in = jnp.concatenate(
-        [grad_w_in[:, :half_ff], grad_w_in[:, half_all : half_all + half_ff]], axis=1
-    )
+            moved[name] = links.shift(parts[0], "c", -1)
+        done[name, side] = parts
+        if lean:
+            sums = [
+                matmul_left_t(kept_now[0], kept_now[3]),
+                matmul_left_t(kept_now[2], kept_now[1]),
+            ]
+            return sums if kept is None else [a + b for a, b in zip(kept, sums)]
+        return kept_now
+
+    near_a_sib, step = tie(near_a_sib, links.shift(ring_b[-1], "z"))
+    ring_b.append(step)
+    step = links.shift(ring_b[-1], "z")
+    kept = ffn(near_a_sib, "an", 1)
+    step, *far_a = tie(step, *far_a, done["an", 1][0])[:3]
+    far_a_rows = joined_rows(far_a)
+    far_a_sib = links.shift(far_a_rows, "c")
+    ring_b.append(step)
+    far_a_sib, ring_b[-1] = tie(far_a_sib, ring_b[-1])
+    while len(ring_b) < links.size["z"]:
+        ring_b.append(links.shift(ring_b[-1], "z"))
+    held = links.gather(joined_rows(ring_b), ("w",)) if links.size["w"] > 1 else None
+    near_b = halved(jnp.split(held, ctx // 4 * links.size["z"]) if held is not None else ring_b)
+    far_b = [links.shift(near_b[0], "x"), links.shift(near_b[1], "y")]
+    kept = ffn(far_a_sib, "af", 1)
+    kept = ffn(near_a_rows, "an", 0)
+    far_a_rows, *far_b = tie(far_a_rows, *far_b, done["an", 0][0])[:3]
+    rows_b = joined_rows([*near_b, *far_b])
+    sib_b = links.shift(rows_b, "c")
+    kept = ffn(far_a_rows, "af", 0)
+
+    def add_far(moved_rows, near):
+        return [plus(m_rows, n_rows) for m_rows, n_rows in zip(moved_rows, near)]
+
+    def split_far(rows):
+        pairs = [jnp.split(r, 2) for r in rows]
+        return [p[0] for p in pairs], [p[1] for p in pairs]
+
+    def z_parts(rows):
+        if links.size["w"] > 1:
+            rows = [links.scatter_sum(r, ("w",)) for r in rows]
+        return [joined_rows(p) for p in zip(*[jnp.split(r, links.size["z"]) for r in rows])]
+
+    def last_b(total):
+        n0, f0, n1, f1 = jnp.split(total, 4)
+        return plus(links.shift(f0, "y", -1), n0), plus(links.shift(f1, "x", -1), n1)
+
+    far = done["af", 0][1::2]
+    a_far = [links.shift(far[0], "y", -1), links.shift(far[1], "x", -1)]
+    query_w_all = lax.all_gather(after(w_query, sib_b), BOTH, axis=0, tiled=True)
+    kept = ffn(sib_b, "b", 1)
+    a_far = tie(*a_far, done["b", 1][0])[:2]
+    a_near = add_far(a_far, done["an", 0][1::2])
+    rows_b, heads_out, *a_near = tie(rows_b, heads_out, *a_near)
+    a_near, far = split_far(a_near)
+    a_far = [links.shift(far[0], "x", -1), links.shift(far[1], "y", -1)]
+    heads_half = [heads_out[: tok // 2], heads_out[tok // 2 :]]
+    heads_far = [links.shift(heads_half[0], "x"), links.shift(heads_half[1], "y")]
+    kept = ffn(rows_b, "b", 0)
+    *a_far, heads_far[0], heads_far[1] = tie(*a_far, *heads_far, done["b", 0][0])[:4]
+    done["bn", 0], done["bf", 0] = done["b", 0][:4], done["b", 0][4:]
+    heads_half = [joined_rows(p) for p in zip(heads_half, heads_far)]
+    far = done["bf", 0][1::2]
+    b_far = [links.shift(far[0], "x", -1), links.shift(far[1], "y", -1)]
+    a_parts = z_parts(add_far(a_far, a_near))
+    heads_far = [links.shift(heads_half[0], "y"), links.shift(heads_half[1], "x")]
+    a_sum = links.shift(a_parts[-1], "z", -1)
+    out_far = [done["af", 0][0], done["af", 0][2]]
+    out_far_b = [done["bf", 0][0], done["bf", 0][2]]
+    if lean:
+        grad_w_in, grad_w_back = kept
+        a_sum = plus(a_sum, a_parts[-2])
+        for part in a_parts[-3::-1]:
+            a_sum = plus(links.shift(a_sum, "z", -1), part)
+        out_far = [links.shift(p, axis, -1) for p, axis in zip(out_far, "yx")]
+        out_far_b = [links.shift(p, axis, -1) for p, axis in zip(out_far_b, "xy")]
+        b_parts = z_parts(add_far(b_far, done["bn", 0][1::2]))
+        b_sum = b_parts[-1]
+        for part in b_parts[-2:0:-1]:
+            b_sum = plus(links.shift(b_sum, "z", -1), part)
+    else:
+        x_all, g_kept, act_all, grad_pre_all = kept
+        grad_w_top = matmul_left_t(x_all[:, : D // 2], grad_pre_all)
+        *b_far, a_sum, heads_far[0], heads_far[1], _ = tie(*b_far, a_sum, *heads_far, grad_w_top)
+        b_parts = z_parts(add_far(b_far, done["bn", 0][1::2]))
+        a_sum = plus(a_sum, a_parts[-2])
+        x_all, a_sum, out_far[0], out_far[1], *b_parts = tie(x_all, a_sum, *out_far, *b_parts)
+        out_far = [links.shift(p, axis, -1) for p, axis in zip(out_far, "yx")]
+        a_next = links.shift(a_sum, "z", -1)
+        b_next = links.shift(b_parts[-1], "z", -1)
+        grad_w_end = matmul_left_t(x_all[:, D // 2 :], grad_pre_all)
+        a_next, b_next, _ = tie(a_next, b_next, grad_w_end)
+        for part in a_parts[-3:0:-1]:
+            a_sum = plus(a_next, part)
+            a_next = links.shift(a_sum, "z", -1)
+        b_sum = plus(b_next, b_parts[-2])
+        act_all, a_sum, b_sum = tie(act_all, a_sum, b_sum)
+        b_next = links.shift(b_sum, "z", -1)
+        out_far_b = [links.shift(p, axis, -1) for p, axis in zip(out_far_b, "xy")]
+        grad_w_back = matmul_left_t(act_all, g_kept)
+        a_next, b_next, *out_far, _ = tie(a_next, b_next, *out_far, grad_w_back)
+        a_sum = plus(a_next, a_parts[0])
+        b_sum = plus(b_next, b_parts[-3])
+        for part in b_parts[-4:0:-1]:
+            b_sum = plus(links.shift(b_sum, "z", -1), part)
+        grad_w_top, grad_w_end, grad_w_back, b_sum = tie(
+            grad_w_top, grad_w_end, grad_w_back, b_sum
+        )
+    out_near, out_far = split_far(add_far(out_far, [done["an", 0][0], done["an", 0][2]]))
+    out_far = [links.shift(p, axis, -1) for p, axis in zip(out_far, "xy")]
+    out_near_b = add_far(out_far_b, [done["bn", 0][0], done["bn", 0][2]])
+    b_sum = plus(links.shift(b_sum, "z", -1), b_parts[0])
+    grad_ffn = joined_rows([a_sum, *last_b(b_sum)])
+    out_far[0], out_far[1], out_near_b[0], out_near_b[1], grad_ffn = tie(
+        *out_far, *out_near_b, grad_ffn
+    )
+    grad_ffn = grad_ffn.astype(f32)
+
+    def output_steps():
+        parts = [
+            joined_rows(p)
+            for p in zip(z_parts(add_far(out_far, out_near)), z_parts(out_near_b))
+        ]
+        total = parts[-1]
+        for part in parts[-2::-1]:
+            moved_total = links.shift(total, "z", -1)
+            yield [moved_total]
+            total = plus(moved_total, part)
+        rows = total.shape[0] // 3
+        yield [joined_rows([total[:rows], *last_b(total[rows:])])]
+
+    out_steps = output_steps()
+    out_now = next(out_steps)
+    def pick(value, start, count):
+        return jnp.concatenate(
+            [value[:, start : start + count], value[:, half_all + start : half_all + start + count]],
+            axis=1,
+        )
+
+    blocks_in = [grad_w_in] if lean else [grad_w_top, grad_w_end]
+    grad_w_expert_in = joined_rows([pick(v, 0, half_ff) for v in blocks_in])
     grad_w_expert_out = grad_w_back[:half_ff]
     grad_w_shared_out = grad_w_back[half_ff : half_ff + half_sh]
-    grad_shared = jnp.concatenate(
-        [
-            grad_w_in[:, half_ff : half_ff + half_sh],
-            grad_w_in[:, half_all + half_ff : half_all + half_ff + half_sh],
-        ],
-        axis=1,
-    ).reshape(devices, rows_d, 2 * half_sh)
-    grad_shared = lax.all_to_all(grad_shared, BOTH, split_axis=0, concat_axis=0, tiled=True)
-    grad_shared = grad_shared.transpose(1, 0, 2)
-    grad_w_shared_in = jnp.concatenate(
-        [
-            grad_shared[:, :, :half_sh].reshape(rows_d, SHARED_FF),
-            grad_shared[:, :, half_sh:].reshape(rows_d, SHARED_FF),
-        ],
-        axis=1,
-    )
-
+    grad_shared = joined_rows([pick(v, half_ff, half_sh) for v in blocks_in])
+    grad_shared = grad_shared.reshape(devices, rows_d, 2 * half_sh)
     grad_out = cotangent.astype(f32)
     grad_middle_part, grad_norm_ffn = rms_backward(middle, inverse_ffn, gain_ffn, grad_ffn)
     grad_middle = grad_out + grad_middle_part
@@ -518,9 +729,27 @@
         for k in range(ctx)
     ]
     arrived = jnp.concatenate(links.ctx_exchange(pieces), axis=0)
+    arrived, grad_shared, *out_now = tie(arrived, grad_shared, *out_now)
+    grad_shared = lax.all_to_all(grad_shared, BOTH, split_axis=0, concat_axis=0, tiled=True)
+    grad_shared = grad_shared.transpose(1, 0, 2)
+    grad_w_shared_in = jnp.concatenate(
+        [
+            grad_shared[:, :, :half_sh].reshape(rows_d, SHARED_FF),
+            grad_shared[:, :, half_sh:].reshape(rows_d, SHARED_FF),
+        ],
+        axis=1,
+    )
+    out_now = next(out_steps)
     grad_heads = arrived[:, :v_cols].reshape(row, heads, VDIM).transpose(1, 0, 2)
     grad_attended_cols = arrived[:, v_cols:]
-    heads_out_row = links.ctx_gather(heads_out)
+    quarter = tok // 2
+    parts = [heads_half[0][:quarter], heads_half[1][:quarter]]
+    parts += [heads_half[0][quarter:], heads_far[1][:quarter]]
+    parts += [heads_far[0][:quarter], heads_half[1][quarter:]]
+    parts += [heads_far[0][quarter:], heads_far[1][quarter:]]
+    heads_out_row = joined_rows(parts)
+    if links.size["w"] > 1:
+        heads_out_row = links.gather(heads_out_row, ("w",))
 
     soft = jnp.exp(masked_scores() - log_total)
     grad_values = jnp.einsum(
@@ -529,6 +758,8 @@
     grad_probs = jnp.einsum("hqd,hkd->hqk", grad_heads, value, preferred_element_type=f32)
     row_delta = jnp.sum(soft * grad_probs, axis=-1, keepdims=True)
     grad_raw = (soft * (grad_probs - row_delta) * scale).astype(bf16)
+    grad_raw, grad_values, *out_now = tie(grad_raw, grad_values, *out_now)
+    out_now = next(out_steps)
     grad_query = jnp.einsum("hqk,hkd->qhd", grad_raw, key, preferred_element_type=f32)
     grad_key = jnp.einsum("hqk,hqd->khd", grad_raw, query, preferred_element_type=f32)
     grad_key_rope = jnp.sum(grad_key[..., NOPE:], axis=1)
@@ -536,10 +767,12 @@
         [grad_key[..., :NOPE], grad_values.transpose(1, 0, 2)], axis=-1
     )
     grad_keyval = grad_keyval.astype(bf16).reshape(row, kv_cols)
+    grad_keyval, *out_now = tie(grad_keyval, *out_now)
+    mixed = (middle + list(out_steps)[-1][0].astype(f32)).astype(bf16)
     grad_w_up = matmul_left_t(latent, grad_keyval)
     grad_latent = matmul_right_t(grad_keyval, up_w)
     grad_low = jnp.concatenate([grad_latent, grad_key_rope], axis=1).astype(bf16)
-    grad_low = links.scatter_sum(grad_low, ("x", "y")).astype(f32)
+    grad_low = links.scatter_sum(grad_low, ("x", "y", "w")).astype(f32)
     grad_query_raw = jnp.concatenate(
         [
             grad_query[..., :NOPE],
@@ -568,17 +801,28 @@
     )
     grad_in = grad_middle + grad_input_part
 
-    z_rel = (links.own["z"] - jnp.arange(links.size["z"], dtype=jnp.int32)) % links.size["z"]
-    c_rel = (links.own["c"] - jnp.arange(2, dtype=jnp.int32)) % 2
-    dp_rel = (c_rel[:, None] + 2 * z_rel[None, :]).reshape(-1)
-
     def to_owners(value):
-        count = value.shape[1]
-        value = value.astype(bf16).reshape(links.dp, ctx * count, -1)[dp_rel]
-        value = links.scatter_sum(value.reshape(devices * count, -1), ("z", "c"))
-        value = value.reshape(ctx, count, -1)[rel_ctx]
-        value = jnp.stack(links.ctx_exchange([value[k] for k in range(ctx)]))[ctx_place]
-        return value.astype(f32)
+        count, size = value.shape[1], links.size["z"]
+        value = value.astype(bf16).reshape(size, 2, ctx * count, -1)
+
+        def core(c):
+            return lax.dynamic_index_in_dim(value, c, 1, keepdims=False)
+
+        total = plus(links.shift(core(1 - links.own["c"]), "c"), core(links.own["c"]))
+
+        def part(k):
+            return lax.dynamic_index_in_dim(
+                total, (links.own["z"] - k) % size, 0, keepdims=False
+            )
+
+        summed = part(size - 1)
+        for k in range(size - 2, -1, -1):
+            summed = plus(links.shift(summed, "z", -1), part(k))
+        summed = summed.reshape(ctx, count, -1)
+        pieces = [
+            lax.dynamic_index_in_dim(summed, rel_ctx[k], 0, keepdims=False) for k in range(ctx)
+        ]
+        return jnp.stack(links.ctx_exchange(pieces))[ctx_place].astype(f32)
 
     def joined(value):
         return value.transpose(1, 0, 2).reshape(value.shape[1], -1)

time: 1990 us -> 1400 us (0.70)
  waiting for transfers between devices: 874 us -> 335 us
  local copies, waits for them, and re-layouts: 274 us -> 228 us
  matrix products: 260 us -> 217 us
    ppermute x86 -> x78, waiting for transfers between devices: 744 us -> 291 us  [shift(): return lax.ppermute(value, name, pairs)]
    all_gather x3 -> x2, waiting for transfers between devices: 77.6 us -> 0.01 us  [the longest x1 0.01 us: shards(): g_all = lax.all_gather(after(cotangent, far_a), BOTH, axis=0, tiled=True)]
    slice x43 -> x8, local copies, waits for them, and re-layouts: 45.8 us -> 10.3 us  [the longest x4 7.44 us: pick(): value[:, start:start + count]]
    dot_general x1, matrix products: 28.8 us -> 2.35 us  [shards(): jnp.einsum('hqk,hqd->khd', grad_raw, query, preferred_element_type=f32)]
    concatenate x12 -> x32, other arithmetic: 10.3 us -> 34.9 us  [the longest x25 31.8 us: joined_rows(): return parts[0] if len(parts) == 1 else jnp.concatenate(parts, axis=0)]
    dot_general x1, matrix products: 27.5 us -> 5.26 us  [shards(): jnp.einsum('hqk,hkd->qhd', grad_raw, key, preferred_element_type=f32)]
    split x0 -> x22, local copies, waits for them, and re-layouts: none -> 21.4 us  [the longest x7 10.8 us: halved(): both = [jnp.split(part, 2) for part in parts]]
    ppermute x24 -> x27, waiting for transfers between devices: 52.9 us -> 44.7 us  [shift_ctx(): return lax.ppermute(value, 'ctx', pairs)]
  transfers between devices with their start and end apart: 116 -> 110, of which waited for: 47 -> 48; matrix products, arithmetic and copies ran while one was open for 32% -> 41% of each run, Pallas kernels for 13% -> 15%
where the time goes in v2:
time: 1400 us; the launch traced here: 1390 us
  waiting for transfers between devices  335 us (24%)
  Pallas kernels  265 us (19%)
  local copies, waits for them, and re-layouts  228 us (16%)
  matrix products  217 us (16%)
  other arithmetic  156 us (11%)
  starting transfers between devices  156 us (11%)
  between operations  34.7 us (2%)
    ppermute x78, waiting for transfers between devices, shift(): return lax.ppermute(value, name, pairs)  291 us
    pallas_call x6, Pallas kernels, ffn_chunk(): pl.pallas_call(lambda *refs: ffn_kernel(half_ff, 0 if moved is None else...  265 us
    dot_general x7, matrix products, matmul_left_t(): lax.dot_general(left, right, (((0,), (0,)), ((), ())), preferred_element_...  129 us
    ppermute x78, starting transfers between devices, shift(): return lax.ppermute(value, name, pairs)  106 us
    unnamed x359, local copies, waits for them, and re-layouts  62.2 us
    convert_element_type x36, other arithmetic, plus(): return (left.astype(f32) + right.astype(f32)).astype(bf16)  52.9 us
    ppermute x27, waiting for transfers between devices, shift_ctx(): return lax.ppermute(value, 'ctx', pairs)  44.7 us
    ppermute x27, starting transfers between devices, shift_ctx(): return lax.ppermute(value, 'ctx', pairs)  33.3 us
  transfers between devices with their start and end apart: 110, of which 48 were waited for; matrix products, arithmetic and copies ran while one was open for 41% of the time, Pallas kernels for 15%

profile of v2, /device:TPU:0, one launch (start us, length us, event | category | flops | bytes accessed | tf_op | source)
XLA Modules:
  0.0 1393.1 jit_solution(9508234320049557901)
XLA Ops:
  41.4 14.4 %collective-permute-done.5 = bf16[64,2688]{1,0:T(8,128)(2,1)} collective-permute-done((bf16[64,2688]{1,0:T(8,128)(2,1)S(1)}, bf16[64,2688]{1,0:T(8,128)(2,1)}, u32[]{:S(2)}, u32[]{:S(2)}) %collective-permute-start.5) | collective-permute-done | bytes 344096 | tf_op jit(solution)/shard_map/ppermute | solution.py:108
  65.4 14.7 %collective-permute-done.7 = bf16[64,2688]{1,0:T(8,128)(2,1)} collective-permute-done((bf16[64,2688]{1,0:T(8,128)(2,1)}, bf16[64,2688]{1,0:T(8,128)(2,1)}, u32[]{:S(2)}, u32[]{:S(2)}) %collective-permute-start.7) | collective-permute-done | bytes 344096 | tf_op jit(solution)/shard_map/ppermute | solution.py:108
  83.0 4.5 collective-permute-done.9
  87.5 7.2 collective-permute-done.10
  94.9 11.1 collective-permute-done.11
  113.1 6.8 collective-permute-done.14
  139.5 3.9 pad_maximum_fusion.2
  162.0 5.0 gather_fusion
  175.1 4.9 collective-permute-done.16
  181.8 4.3 fusion.126
  186.3 4.1 pad_maximum_fusion.3
  192.4 7.8 fusion.161
  200.2 8.2 fusion.8
  208.5 7.6 fusion.47
  227.0 9.9 collective-permute-done.21
  237.7 5.2 constant_dynamic-update-slice_fusion.20
  242.9 9.3 gather_fusion.4
  252.2 5.9 multiply_reduce_fusion.1
  264.5 9.6 collective-permute-done.24
  274.7 11.4 collective-permute-done.26
  295.1 9.7 all-to-all-start.1
  306.6 13.7 collective-permute-done.27
  320.3 9.6 collective-permute-start.28
  334.4 11.9 concatenate.292.refs_7_
  348.3 4.1 collective-permute-done.28
  357.9 20.0 %collective-permute-done.29 = bf16[256,2048]{1,0:T(8,128)(2,1)S(1)} collective-permute-done((bf16[256,2048]{1,0:T(8,128)(2,1)S(1)}, bf16[256,2048]{1,0:T(8,128)(2,1)S(1)}, u32[]{:S(2)}, u32[]{:S(2)}) %collective-permute-start.29) | collective-permute-done | bytes 1048608 | tf_op jit(solution)/shard_map/ppermute | solution.py:108
  394.0 17.6 %collective-permute-done.33 = bf16[256,2048]{1,0:T(8,128)(2,1)} collective-permute-done((bf16[256,2048]{1,0:T(8,128)(2,1)}, bf16[256,2048]{1,0:T(8,128)(2,1)}, u32[]{:S(2)}, u32[]{:S(2)}) %collective-permute-start.33) | collective-permute-done | bytes 1048608 | tf_op jit(solution)/shard_map/ppermute | solution.py:108
  411.7 33.6 %ffn_chunk.6 = (bf16[8192,2048]{1,0:T(8,128)(2,1)}, bf16[8192,2048]{1,0:T(8,128)(2,1)}, bf16[8192,896]{1,0:T(8,128)(2,1)}, bf16[8192,1792]{1,0:T(8,128)(2,1)}, bf16[1024,4096]{1,0:T(8,128)(2,1)}) custom-call(s32[128]{0:T(128)} %pad_add_fusion.1.refs_0_, bf16[1024,2048]{1,0:T(8,128)(2,1)} %collective-permute-done.32.refs_1_, ...), custom_call_target="tpu_custom_call" | custom-call | flops 22548578304 | bytes 33554432 | tf_op jit(solution)/shard_map/ffn_chunk/pallas_call | solution.py:295
  455.2 6.0 collective-permute-done.37.refs_1_
  469.7 34.1 %ffn_chunk.7 = (bf16[8192,2048]{1,0:T(8,128)(2,1)}, bf16[8192,2048]{1,0:T(8,128)(2,1)}, bf16[8192,896]{1,0:T(8,128)(2,1)}, bf16[8192,1792]{1,0:T(8,128)(2,1)}, bf16[1024,4096]{1,0:T(8,128)(2,1)}) custom-call(s32[128]{0:T(128)} %pad_add_fusion.1.refs_0_, ...), custom_call_target="tpu_custom_call", output_to_operand_aliasing={{0}: (9, {}), {1}: (10, {}), {2}: (11, {}), {3}: (12, {})} | custom-call | flops 22548578304 | bytes 33554432 | tf_op jit(solution)/shard_map/ffn_chunk/pallas_call | solution.py:295
  509.3 36.4 %ffn_chunk.8 = (bf16[8192,2048]{1,0:T(8,128)(2,1)}, bf16[8192,2048]{1,0:T(8,128)(2,1)}, bf16[8192,896]{1,0:T(8,128)(2,1)}, bf16[8192,1792]{1,0:T(8,128)(2,1)}, b...) custom-call(s32[128]{0:T(128)} %pad_add_fusion.1.refs_0_, ...), custom_call_target="tpu_custom_call", output_to_operand_aliasing={{0}: (10, {}), {1}: (11, {}), {2}: (12, {}), {3}: (13, {})} | custom-call | flops 22548578304 | bytes 33554432 | tf_op jit(solution)/shard_map/ffn_chunk/pallas_call | solution.py:295
  552.5 36.4 %ffn_chunk.9 = (bf16[8192,2048]{1,0:T(8,128)(2,1)}, bf16[8192,2048]{1,0:T(8,128)(2,1)}, bf16[8192,896]{1,0:T(8,128)(2,1)}, bf16[8192,1792]{1,0:T(8,128)(2,1)}, b...) custom-call(s32[128]{0:T(128)} %pad_add_fusion.1.refs_0_, ...), custom_call_target="tpu_custom_call", output_to_operand_aliasing={{0}: (10, {}), {1}: (11, {}), {2}: (12, {}), {3}: (13, {})} | custom-call | flops 22548578304 | bytes 33554432 | tf_op jit(solution)/shard_map/ffn_chunk/pallas_call | solution.py:295
  589.0 59.7 %ffn_chunk.10 = (bf16[8192,2048]{1,0:T(8,128)(2,1)}, bf16[8192,2048]{1,0:T(8,128)(2,1)}, bf16[8192,896]{1,0:T(8,128)(2,1)}, bf16[8192,1792]{1,0:T(8,128)(2,1)}, bf16[2048,4096]{1,0:T(8,128)(2,1)}) custom-call(s32[128]{0:T(128)} %pad_add_fusion.1.refs_0_, ...), custom_call_target="tpu_custom_call", output_to_operand_aliasing={{0}: (9, {}), {1}: (10, {}), {2}: (11, {}), {3}: (12, {})} | custom-call | flops 45097156608 | bytes 67108864 | tf_op jit(solution)/shard_map/ffn_chunk/pallas_call | solution.py:295
  666.2 30.8 %collective-permute-done.42 = bf16[512,2048]{1,0:T(8,128)(2,1)S(1)} collective-permute-done((bf16[512,2048]{1,0:T(8,128)(2,1)}, bf16[512,2048]{1,0:T(8,128)(2,1)S(1)}, u32[]{:S(2)}, u32[]{:S(2)}) %collective-permute-start.42) | collective-permute-done | bytes 2097184 | tf_op jit(solution)/shard_map/ppermute | solution.py:108
  712.3 65.1 %ffn_chunk.11 = (bf16[8192,2048]{1,0:T(8,128)(2,1)}, bf16[8192,2048]{1,0:T(8,128)(2,1)}, bf16[8192,896]{1,0:T(8,128)(2,1)}, bf16[8192,1792]{1,0:T(8,128)(2,1)}, ...) custom-call(s32[128]{0:T(128)} %pad_add_fusion.1.refs_0_, ...), custom_call_target="tpu_custom_call", output_to_operand_aliasing={{0}: (10, {}), {1}: (11, {}), {2}: (12, {}), {3}: (13, {})} | custom-call | flops 45097156608 | bytes 67108864 | tf_op jit(solution)/shard_map/ffn_chunk/pallas_call | solution.py:295
  784.5 3.9 collective-permute-start.52
  793.4 39.6 %fusion.4 = f32[1024,1792]{1,0:T(8,128)} fusion(bf16[8192,1792]{1,0:T(8,128)(2,1)} %get-tuple-element.270, bf16[8192,2048]{1,0:T(8,128)(2,1)} %get-tuple-element.280), kind=kOutput, calls=%fused_computation.17 | convolution fusion | flops 30064771072 | bytes 53477376 | tf_op jit(solution)/shard_map/dot_general | solution.py:31
  835.8 25.2 %collective-permute-done.53 = bf16[256,2048]{0,1:T(8,128)(2,1)S(1)} collective-permute-done((bf16[256,2048]{0,1:T(8,128)(2,1)S(1)}, bf16[256,2048]{0,1:T(8,128)(2,1)S(1)}, u32[]{:S(2)}, u32[]{:S(2)}) %collective-permute-start.53) | collective-permute-done | bytes 1048608 | tf_op jit(solution)/shard_map/ppermute | solution.py:108
  872.2 39.2 %fusion.2 = f32[1024,1792]{1,0:T(8,128)} fusion(bf16[8192,1792]{1,0:T(8,128)(2,1)} %get-tuple-element.270, bf16[8192,2048]{1,0:T(8,128)(2,1)} %get-tuple-element.280), kind=kOutput, calls=%fused_computation.15 | convolution fusion | flops 30064771072 | bytes 53477376 | tf_op jit(solution)/shard_map/dot_general | solution.py:31
  934.3 35.8 %fusion.162 = f32[896,2048]{1,0:T(8,128)} fusion(bf16[8192,896]{1,0:T(8,128)(2,1)S(1)} %bitcast.309, bf16[8192,2048]{1,0:T(8,128)(2,1)} %get-tuple-element.289), kind=kOutput, calls=%fused_computation.511 | convolution fusion | flops 30064771072 | bytes 55574528 | tf_op jit(solution)/shard_map/dot_general | solution.py:31
  972.6 6.0 slice_bitcast_fusion
  994.9 14.7 %fusion.11 = f32[1,2048,1408]{2,1,0:T(8,128)} fusion(f32[1024,704]{1,0:T(8,128)S(1)} %get-tuple-element.399, f32[1024,704]{1,0:T(8,128)S(1)} %get-tuple-element.398, f32[1024,704]{1,0:T(8,128)S(1)} %get-tuple-element.397, f32[1024,704]{1,0:T(8,128)S(1)} %get-tuple-element.396), kind=kLoop, calls=%fused_computation.26 | loop fusion | flops 8650752 | bytes 23068672 | tf_op jit(solution)/shard_map/broadcast_in_dim | solution.py:873
  1027.3 4.4 collective-permute-start.68
  1046.6 6.1 collective-permute-done.75
  1052.7 5.5 collective-permute-done.74
  1060.6 4.2 add_convert_fusion.10
  1072.9 19.9 %multiply_convert_fusion = bf16[4,1024,1024]{1,2,0:T(8,128)(2,1)} fusion(f32[4,1024,1024]{1,2,0:T(8,128)} %get-tuple-element.558, f32[4,1024]{1,0:T(4,128)S(1)} %copy-done.119, bf16[4,1024,256]{1,2,0:T(8,128)(2,1)} %bitcast.368, bf16[1024,1024]{1,0:T(8,128)(2,1)} %copy-done.22), kind=kOutput, calls=%fused_computation.11 | convolution fusion | flops 2176848896 | bytes 46170112 | tf_op jit(solution)/shard_map/sub | solution.py:760
  1097.0 9.1 fusion.15
  1118.6 5.3 convolution_bitcast_fusion.1
  1127.9 22.1 %collective-permute-done.100 = bf16[256,512]{1,0:T(8,128)(2,1)S(1)} collective-permute-done((bf16[256,512]{1,0:T(8,128)(2,1)S(1)}, bf16[256,512]{1,0:T(8,128)(2,1)S(1)}, u32[]{:S(2)}, u32[]{:S(2)}) %collective-permute-start.100) | collective-permute-done | bytes 262176 | tf_op jit(solution)/shard_map/ppermute | solution.py:108
  1150.0 4.4 collective-permute-start.101
  1154.5 5.6 convolution_convert_fusion
  1162.5 28.7 %collective-permute-done.101 = bf16[256,512]{1,0:T(8,128)(2,1)S(1)} collective-permute-done((bf16[256,512]{1,0:T(8,128)(2,1)S(1)}, bf16[256,512]{1,0:T(8,128)(2,1)S(1)}, u32[]{:S(2)}, u32[]{:S(2)}) %collective-permute-start.101) | collective-permute-done | bytes 262176 | tf_op jit(solution)/shard_map/ppermute | solution.py:108
  1201.5 4.0 copy.222
  1239.2 11.2 collective-permute-done.76
  1267.3 4.1 fusion.122
  1271.4 11.6 fusion.38
  1291.5 4.5 convolution_convert_fusion.3
  1302.3 4.2 reshape.1854
  1312.3 5.5 collective-permute-start.85
  1320.7 8.1 collective-permute-done.85
  1337.0 9.2 collective-permute-done.92
  1361.9 4.3 collective-permute-start.94
  1366.2 5.0 fusion.35
  (846 shorter events, 462.4 us)
Async XLA Ops:
  11.6 23.0 %collective-permute-start = (bf16[64,2688]{1,0:T(8,128)(2,1)S(1)}, bf16[64,2688]{1,0:T(8,128)(2,1)S(1)}, u32[]{:S(2)}, u32[]{:S(2)}) collective-permute-start(bf16[64,2688]{1,0:T(8,128)(2,1)S(1)} %pad_maximum_fusion.36), channel_id=1, source_target_pairs={{0,8},{4,12},{8,16},{12,20},{16,24},{20,28},{24,0},{28,4},{1,9},{5... | collective-permute-start | bytes 1032200 | tf_op jit(solution)/shard_map/ppermute | solution.py:108
  34.7 21.1 %collective-permute-start.4 = (bf16[256,1024]{1,0:T(8,128)(2,1)S(1)}, bf16[256,1024]{1,0:T(8,128)(2,1)}, u32[]{:S(2)}, u32[]{:S(2)}) collective-permute-start(bf16[256,1024]{1,0:T(8,128)(2,1)S(1)} %pad_maximum_fusion.30), channel_id=1, source_target_pairs={{0,8},{4,12},{8,16},{12,20},{16,24},{20,28},{24,0},{28,4},{1,9},{5... | collective-permute-start | bytes 1572872 | tf_op jit(solution)/shard_map/ppermute | solution.py:108
  37.9 45.1 %collective-permute-start.8 = (bf16[256,2048]{1,0:T(8,128)(2,1)S(1)}, bf16[256,2048]{1,0:T(8,128)(2,1)}, u32[]{:S(2)}, u32[]{:S(2)}) collective-permute-start(bf16[256,2048]{1,0:T(8,128)(2,1)S(1)} %copy-done.13), channel_id=1, source_target_pairs={{0,1},{1,0},{2,3},{3,2},{4,5},{5,4},{6,7},{7,6},{8,9},{9,8},{10,11... | collective-permute-start | bytes 3145736 | tf_op jit(solution)/shard_map/ppermute | solution.py:114
  38.4 49.1 %collective-permute-start.9 = (bf16[256,2048]{1,0:T(8,128)(2,1)S(1)}, bf16[256,2048]{1,0:T(8,128)(2,1)}, u32[]{:S(2)}, u32[]{:S(2)}) collective-permute-start(bf16[256,2048]{1,0:T(8,128)(2,1)S(1)} %copy-done.13), channel_id=1, source_target_pairs={{0,2},{1,3},{2,0},{3,1},{4,6},{5,7},{6,4},{7,5},{8,10},{9,11},{10,... | collective-permute-start | bytes 3145736 | tf_op jit(solution)/shard_map/ppermute | solution.py:114
  39.4 55.3 %collective-permute-start.10 = (bf16[256,2048]{1,0:T(8,128)(2,1)S(1)}, bf16[256,2048]{1,0:T(8,128)(2,1)}, u32[]{:S(2)}, u32[]{:S(2)}) collective-permute-start(bf16[256,2048]{1,0:T(8,128)(2,1)S(1)} %copy-done.13), channel_id=1, source_target_pairs={{0,3},{1,2},{2,1},{3,0},{4,7},{5,6},{6,5},{7,4},{8,11},{9,10},{10,... | collective-permute-start | bytes 3145736 | tf_op jit(solution)/shard_map/ppermute | solution.py:114
  55.7 24.4 %collective-permute-start.6 = (bf16[256,1024]{1,0:T(8,128)(2,1)}, bf16[256,1024]{1,0:T(8,128)(2,1)}, u32[]{:S(2)}, u32[]{:S(2)}) collective-permute-start(bf16[256,1024]{1,0:T(8,128)(2,1)} %collective-permute-done.4), channel_id=1, source_target_pairs={{0,8},{4,12},{8,16},{12,20},{16,24},{20,28},{24,0},{28,4},{1,9},{5... | collective-permute-start | bytes 1572872 | tf_op jit(solution)/shard_map/ppermute | solution.py:108
  55.7 24.4 %collective-permute-start.7 = (bf16[64,2688]{1,0:T(8,128)(2,1)}, bf16[64,2688]{1,0:T(8,128)(2,1)}, u32[]{:S(2)}, u32[]{:S(2)}) collective-permute-start(bf16[64,2688]{1,0:T(8,128)(2,1)} %collective-permute-done.5), channel_id=1, source_target_pairs={{0,8},{4,12},{8,16},{12,20},{16,24},{20,28},{24,0},{28,4},{1,9},{5... | collective-permute-start | bytes 1032200 | tf_op jit(solution)/shard_map/ppermute | solution.py:108
  61.7 51.4 %all-to-all-start = ((bf16[32,64,176]{2,1,0:T(8,128)(2,1)}), bf16[32,64,176]{2,1,0:T(8,128)(2,1)S(1)}, u32[]{:S(2)}, u32[]{:S(2)}) async-start(bf16[32,64,176]{2,1,0:T(8,128)(2,1)} %maximum_bitcast_fusion.1), calls=%async_computation | async-start | bytes 2097152 | tf_op jit(solution)/shard_map/all_to_all | solution.py:404
  65.4 346.3 %all-gather.3.cloned.1.call-start = ((), (), s32[]{:S(2)}) async-start(), calls=%async_computation.3 | async-start | bytes 34603008 | tf_op jit(solution)/shard_map/all_gather | solution.py:441
  81.5 28.0 %collective-permute-start.12 = (bf16[128,2688]{1,0:T(8,128)(2,1)S(1)}, bf16[128,2688]{1,0:T(8,128)(2,1)S(1)}, u32[]{:S(2)}, u32[]{:S(2)}) collective-permute-start(bf16[128,2688]{1,0:T(8,128)(2,1)S(1)} %bitcast.340), channel_id=1, source_target_pairs={{0,1},{1,0},{2,3},{3,2},{4,5},{5,4},{6,7},{7,6},{8,9},{9,8},{10,11... | collective-permute-start | bytes 2064392 | tf_op jit(solution)/shard_map/ppermute | solution.py:108
  82.4 27.1 %collective-permute-start.13 = (bf16[128,2688]{1,0:T(8,128)(2,1)S(1)}, bf16[128,2688]{1,0:T(8,128)(2,1)S(1)}, u32[]{:S(2)}, u32[]{:S(2)}) collective-permute-start(bf16[128,2688]{1,0:T(8,128)(2,1)S(1)} %bitcast.337), channel_id=1, source_target_pairs={{0,2},{1,3},{2,0},{3,1},{4,6},{5,7},{6,4},{7,5},{8,10},{9,11},{10,... | collective-permute-start | bytes 2064392 | tf_op jit(solution)/shard_map/ppermute | solution.py:108
  137.5 21.4 %collective-permute-start.18 = (bf16[1024,1024]{1,0:T(8,128)(2,1)}, bf16[1024,1024]{1,0:T(8,128)(2,1)}, u32[]{:S(2)}, u32[]{:S(2)}) collective-permute-start(bf16[1024,1024]{1,0:T(8,128)(2,1)} %get-tuple-element.510), channel_id=1, source_target_pairs={{0,4},{4,0},{8,12},{12,8},{16,20},{20,16},{24,28},{28,24},{1,5},{5... | collective-permute-start | bytes 6291464 | tf_op jit(solution)/shard_map/ppermute | solution.py:108
  145.7 34.2 %collective-permute-start.16 = (bf16[256,2048]{1,0:T(8,128)(2,1)}, bf16[256,2048]{1,0:T(8,128)(2,1)}, u32[]{:S(2)}, u32[]{:S(2)}) collective-permute-start(bf16[256,2048]{1,0:T(8,128)(2,1)} %fusion.50), channel_id=1, source_target_pairs={{0,2},{1,3},{2,0},{3,1},{4,6},{5,7},{6,4},{7,5},{8,10},{9,11},{10,... | collective-permute-start | bytes 3145736 | tf_op jit(solution)/shard_map/ppermute | solution.py:108
  146.7 35.0 %collective-permute-start.17 = (bf16[256,2048]{1,0:T(8,128)(2,1)}, bf16[256,2048]{1,0:T(8,128)(2,1)}, u32[]{:S(2)}, u32[]{:S(2)}) collective-permute-start(bf16[256,2048]{1,0:T(8,128)(2,1)} %fusion.49), channel_id=1, source_target_pairs={{0,1},{1,0},{2,3},{3,2},{4,5},{5,4},{6,7},{7,6},{8,9},{9,8},{10,11... | collective-permute-start | bytes 3145736 | tf_op jit(solution)/shard_map/ppermute | solution.py:108
  190.4 47.3 %collective-permute-start.23 = (bf16[1024,2048]{1,0:T(8,128)(2,1)}, bf16[1024,2048]{1,0:T(8,128)(2,1)}, u32[]{:S(2)}, u32[]{:S(2)}) collective-permute-start(bf16[1024,2048]{1,0:T(8,128)(2,1)} %pad_maximum_fusion.3), channel_id=1, source_target_pairs={{0,4},{4,0},{8,12},{12,8},{16,20},{20,16},{24,28},{28,24},{1,5},{5... | collective-permute-start | bytes 12582920 | tf_op jit(solution)/shard_map/ppermute | solution.py:108
  258.5 27.6 %collective-permute-start.26 = (bf16[128,2048]{1,0:T(8,128)(2,1)S(1)}, bf16[128,2048]{1,0:T(8,128)(2,1)}, u32[]{:S(2)}, u32[]{:S(2)}) collective-permute-start(bf16[128,2048]{1,0:T(8,128)(2,1)S(1)} %concatenate.344), channel_id=1, source_target_pairs={{0,8},{4,12},{8,16},{12,20},{16,24},{20,28},{24,0},{28,4},{1,9},{5... | collective-permute-start | bytes 1572872 | tf_op jit(solution)/shard_map/ppermute | solution.py:108
  286.1 34.2 %collective-permute-start.27 = (bf16[128,2048]{1,0:T(8,128)(2,1)}, bf16[128,2048]{1,0:T(8,128)(2,1)}, u32[]{:S(2)}, u32[]{:S(2)}) collective-permute-start(bf16[128,2048]{1,0:T(8,128)(2,1)} %collective-permute-done.26), channel_id=1, source_target_pairs={{0,8},{4,12},{8,16},{12,20},{16,24},{20,28},{24,0},{28,4},{1,9},{5... | collective-permute-start | bytes 1572872 | tf_op jit(solution)/shard_map/ppermute | solution.py:108
  295.1 51.1 %all-to-all-start.1 = ((f32[32,1,256]{2,1,0:T(1,128)}), f32[32,1,256]{2,1,0:T(1,128)S(1)}, u32[]{:S(2)}, u32[]{:S(2)}) async-start(f32[32,1,256]{2,1,0:T(1,128)} %all_to_all.13), calls=%async_computation.1 | async-start | bytes 65536 | tf_op jit(solution)/shard_map/all_to_all | solution.py:519
  304.9 966.6 %all-gather.5.cloned.1.call-start = ((), (), s32[]{:S(2)}) async-start(), calls=%async_computation.4 | async-start | bytes 12976128 | tf_op jit(solution)/shard_map/all_gather | solution.py:624
  320.3 32.2 %collective-permute-start.28 = (bf16[128,2048]{1,0:T(8,128)(2,1)}, bf16[128,2048]{1,0:T(8,128)(2,1)}, u32[]{:S(2)}, u32[]{:S(2)}) collective-permute-start(bf16[128,2048]{1,0:T(8,128)(2,1)} %collective-permute-done.27), channel_id=1, source_target_pairs={{0,8},{4,12},{8,16},{12,20},{16,24},{20,28},{24,0},{28,4},{1,9},{5... | collective-permute-start | bytes 1572872 | tf_op jit(solution)/shard_map/ppermute | solution.py:108
  353.8 24.0 %collective-permute-start.29 = (bf16[256,2048]{1,0:T(8,128)(2,1)S(1)}, bf16[256,2048]{1,0:T(8,128)(2,1)S(1)}, u32[]{:S(2)}, u32[]{:S(2)}) collective-permute-start(bf16[256,2048]{1,0:T(8,128)(2,1)S(1)} %pad_maximum_fusion.20), channel_id=1, source_target_pairs={{0,1},{1,0},{2,3},{3,2},{4,5},{5,4},{6,7},{7,6},{8,9},{9,8},{10,11... | collective-permute-start | bytes 3145736 | tf_op jit(solution)/shard_map/ppermute | solution.py:108
  355.3 23.0 %collective-permute-start.30 = (bf16[256,2048]{1,0:T(8,128)(2,1)S(1)}, bf16[256,2048]{1,0:T(8,128)(2,1)S(1)}, u32[]{:S(2)}, u32[]{:S(2)}) collective-permute-start(bf16[256,2048]{1,0:T(8,128)(2,1)S(1)} %pad_maximum_fusion.21), channel_id=1, source_target_pairs={{0,2},{1,3},{2,0},{3,1},{4,6},{5,7},{6,4},{7,5},{8,10},{9,11},{10,... | collective-permute-start | bytes 3145736 | tf_op jit(solution)/shard_map/ppermute | solution.py:108
  356.8 24.1 %collective-permute-start.31 = (bf16[256,2048]{1,0:T(8,128)(2,1)S(1)}, bf16[256,2048]{1,0:T(8,128)(2,1)}, u32[]{:S(2)}, u32[]{:S(2)}) collective-permute-start(bf16[256,2048]{1,0:T(8,128)(2,1)S(1)} %copy-done.18), channel_id=1, source_target_pairs={{0,8},{4,12},{8,16},{12,20},{16,24},{20,28},{24,0},{28,4},{1,9},{5... | collective-permute-start | bytes 3145736 | tf_op jit(solution)/shard_map/ppermute | solution.py:108
  384.0 27.7 %collective-permute-start.32 = (bf16[1024,2048]{1,0:T(8,128)(2,1)}, bf16[1024,2048]{1,0:T(8,128)(2,1)}, u32[]{:S(2)}, u32[]{:S(2)}) collective-permute-start(bf16[1024,2048]{1,0:T(8,128)(2,1)} %constant_dynamic-update-slice_fusion.25.refs_1_), channel_id=1, source_target_pairs={{0,4},{4,0},{8,12},{12,8},{16,20},{20,16},{24,28},{28,24},{1,5},{5... | collective-permute-start | bytes 12582920 | tf_op jit(solution)/shard_map/ppermute | solution.py:108
  384.0 27.7 %collective-permute-start.33 = (bf16[256,2048]{1,0:T(8,128)(2,1)}, bf16[256,2048]{1,0:T(8,128)(2,1)}, u32[]{:S(2)}, u32[]{:S(2)}) collective-permute-start(bf16[256,2048]{1,0:T(8,128)(2,1)} %collective-permute-done.31), channel_id=1, source_target_pairs={{0,8},{4,12},{8,16},{12,20},{16,24},{20,28},{24,0},{28,4},{1,9},{5... | collective-permute-start | bytes 3145736 | tf_op jit(solution)/shard_map/ppermute | solution.py:108
  390.1 55.2 %collective-permute-start.35 = (bf16[512,2048]{1,0:T(8,128)(2,1)}, bf16[512,2048]{1,0:T(8,128)(2,1)}, u32[]{:S(2)}, u32[]{:S(2)}) collective-permute-start(bf16[512,2048]{1,0:T(8,128)(2,1)} %pad_maximum_fusion.4), channel_id=1, source_target_pairs={{0,2},{1,3},{2,0},{3,1},{4,6},{5,7},{6,4},{7,5},{8,10},{9,11},{10,... | collective-permute-start | bytes 6291464 | tf_op jit(solution)/shard_map/ppermute | solution.py:108
  392.8 52.5 %collective-permute-start.36 = (bf16[512,2048]{1,0:T(8,128)(2,1)}, bf16[512,2048]{1,0:T(8,128)(2,1)}, u32[]{:S(2)}, u32[]{:S(2)}) collective-permute-start(bf16[512,2048]{1,0:T(8,128)(2,1)} %pad_maximum_fusion.5), channel_id=1, source_target_pairs={{0,1},{1,0},{2,3},{3,2},{4,5},{5,4},{6,7},{7,6},{8,9},{9,8},{10,11... | collective-permute-start | bytes 6291464 | tf_op jit(solution)/shard_map/ppermute | solution.py:108
  411.7 33.7 %collective-permute-start.34 = (bf16[256,2048]{1,0:T(8,128)(2,1)}, bf16[256,2048]{1,0:T(8,128)(2,1)S(1)}, u32[]{:S(2)}, u32[]{:S(2)}) collective-permute-start(bf16[256,2048]{1,0:T(8,128)(2,1)} %collective-permute-done.33), channel_id=1, source_target_pairs={{0,8},{4,12},{8,16},{12,20},{16,24},{20,28},{24,0},{28,4},{1,9},{5... | collective-permute-start | bytes 3145736 | tf_op jit(solution)/shard_map/ppermute | solution.py:108
  448.9 60.4 %collective-permute-start.40 = (bf16[1024,4096]{1,0:T(8,128)(2,1)}, bf16[1024,4096]{1,0:T(8,128)(2,1)}, u32[]{:S(2)}, u32[]{:S(2)}) collective-permute-start(bf16[1024,4096]{1,0:T(8,128)(2,1)} %get-tuple-element.220), channel_id=1, source_target_pairs={{0,4},{4,0},{8,12},{12,8},{16,20},{20,16},{24,28},{28,24},{1,5},{5... | collective-permute-start | bytes 25165832 | tf_op jit(solution)/shard_map/ppermute | solution.py:108
  465.8 79.9 %collective-permute-start.38 = (bf16[512,2048]{1,0:T(8,128)(2,1)}, bf16[512,2048]{1,0:T(8,128)(2,1)}, u32[]{:S(2)}, u32[]{:S(2)}) collective-permute-start(bf16[512,2048]{1,0:T(8,128)(2,1)} %pad_maximum_fusion.6), channel_id=1, source_target_pairs={{0,1},{1,0},{2,3},{3,2},{4,5},{5,4},{6,7},{7,6},{8,9},{9,8},{10,11... | collective-permute-start | bytes 6291464 | tf_op jit(solution)/shard_map/ppermute | solution.py:108
  468.7 77.0 %collective-permute-start.39 = (bf16[512,2048]{1,0:T(8,128)(2,1)}, bf16[512,2048]{1,0:T(8,128)(2,1)}, u32[]{:S(2)}, u32[]{:S(2)}) collective-permute-start(bf16[512,2048]{1,0:T(8,128)(2,1)} %pad_maximum_fusion.7), channel_id=1, source_target_pairs={{0,2},{1,3},{2,0},{3,1},{4,6},{5,7},{6,4},{7,5},{8,10},{9,11},{10,... | collective-permute-start | bytes 6291464 | tf_op jit(solution)/shard_map/ppermute | solution.py:108
  503.8 48.8 %collective-permute-start.41 = (bf16[1024,4096]{1,0:T(8,128)(2,1)}, bf16[1024,4096]{1,0:T(8,128)(2,1)}, u32[]{:S(2)}, u32[]{:S(2)}) collective-permute-start(bf16[1024,4096]{1,0:T(8,128)(2,1)} %get-tuple-element.238), channel_id=1, source_target_pairs={{0,4},{4,0},{8,12},{12,8},{16,20},{20,16},{24,28},{28,24},{1,5},{5... | collective-permute-start | bytes 25165832 | tf_op jit(solution)/shard_map/ppermute | solution.py:108
  552.1 36.9 %collective-permute-start.44 = (bf16[2048,2048]{1,0:T(8,128)(2,1)}, bf16[2048,2048]{1,0:T(8,128)(2,1)}, u32[]{:S(2)}, u32[]{:S(2)}) collective-permute-start(bf16[2048,2048]{1,0:T(8,128)(2,1)} %constant_dynamic-update-slice_fusion.31.refs_1_), channel_id=1, source_target_pairs={{0,4},{4,0},{8,12},{12,8},{16,20},{20,16},{24,28},{28,24},{1,5},{5... | collective-permute-start | bytes 25165832 | tf_op jit(solution)/shard_map/ppermute | solution.py:108
  648.7 63.6 %collective-permute-start.45 = (bf16[2048,4096]{1,0:T(8,128)(2,1)}, bf16[2048,4096]{1,0:T(8,128)(2,1)}, u32[]{:S(2)}, u32[]{:S(2)}) collective-permute-start(bf16[2048,4096]{1,0:T(8,128)(2,1)} %get-tuple-element.249), channel_id=1, source_target_pairs={{0,4},{4,0},{8,12},{12,8},{16,20},{20,16},{24,28},{28,24},{1,5},{5... | collective-permute-start | bytes 50331656 | tf_op jit(solution)/shard_map/ppermute | solution.py:108
  648.8 48.2 %collective-permute-start.42 = (bf16[512,2048]{1,0:T(8,128)(2,1)}, bf16[512,2048]{1,0:T(8,128)(2,1)S(1)}, u32[]{:S(2)}, u32[]{:S(2)}) collective-permute-start(bf16[512,2048]{1,0:T(8,128)(2,1)} %get-tuple-element.243), channel_id=1, source_target_pairs={{0,2},{1,3},{2,0},{3,1},{4,6},{5,7},{6,4},{7,5},{8,10},{9,11},{10,... | collective-permute-start | bytes 6291464 | tf_op jit(solution)/shard_map/ppermute | solution.py:108
  649.8 48.0 %collective-permute-start.43 = (bf16[512,2048]{1,0:T(8,128)(2,1)}, bf16[512,2048]{1,0:T(8,128)(2,1)}, u32[]{:S(2)}, u32[]{:S(2)}) collective-permute-start(bf16[512,2048]{1,0:T(8,128)(2,1)} %get-tuple-element.244), channel_id=1, source_target_pairs={{0,1},{1,0},{2,3},{3,2},{4,5},{5,4},{6,7},{7,6},{8,9},{9,8},{10,11... | collective-permute-start | bytes 6291464 | tf_op jit(solution)/shard_map/ppermute | solution.py:108
  705.0 74.1 %collective-permute-start.48 = (bf16[256,2048]{1,0:T(8,128)(2,1)}, bf16[256,2048]{1,0:T(8,128)(2,1)}, u32[]{:S(2)}, u32[]{:S(2)}) collective-permute-start(bf16[256,2048]{1,0:T(8,128)(2,1)} %split.212), channel_id=1, source_target_pairs={{0,1},{1,0},{2,3},{3,2},{4,5},{5,4},{6,7},{7,6},{8,9},{9,8},{10,11... | collective-permute-start | bytes 3145736 | tf_op jit(solution)/shard_map/ppermute | solution.py:108
  706.8 72.3 %collective-permute-start.49 = (bf16[256,2048]{1,0:T(8,128)(2,1)}, bf16[256,2048]{1,0:T(8,128)(2,1)}, u32[]{:S(2)}, u32[]{:S(2)}) collective-permute-start(bf16[256,2048]{1,0:T(8,128)(2,1)} %split.213), channel_id=1, source_target_pairs={{0,2},{1,3},{2,0},{3,1},{4,6},{5,7},{6,4},{7,5},{8,10},{9,11},{10,... | collective-permute-start | bytes 3145736 | tf_op jit(solution)/shard_map/ppermute | solution.py:108
  708.7 69.5 %collective-permute-start.50 = (bf16[128,2048]{0,1:T(8,128)(2,1)}, bf16[128,2048]{0,1:T(8,128)(2,1)}, u32[]{:S(2)}, u32[]{:S(2)}) collective-permute-start(bf16[128,2048]{0,1:T(8,128)(2,1)} %get-tuple-element.471), channel_id=1, source_target_pairs={{0,1},{1,0},{2,3},{3,2},{4,5},{5,4},{6,7},{7,6},{8,9},{9,8},{10,11... | collective-permute-start | bytes 1572872 | tf_op jit(solution)/shard_map/ppermute | solution.py:108
  710.1 69.0 %collective-permute-start.51 = (bf16[128,2048]{0,1:T(8,128)(2,1)}, bf16[128,2048]{0,1:T(8,128)(2,1)}, u32[]{:S(2)}, u32[]{:S(2)}) collective-permute-start(bf16[128,2048]{0,1:T(8,128)(2,1)} %get-tuple-element.470), channel_id=1, source_target_pairs={{0,2},{1,3},{2,0},{3,1},{4,6},{5,7},{6,4},{7,5},{8,10},{9,11},{10,... | collective-permute-start | bytes 1572872 | tf_op jit(solution)/shard_map/ppermute | solution.py:108
  777.4 84.4 %collective-permute-start.46 = (bf16[512,2048]{1,0:T(8,128)(2,1)}, bf16[512,2048]{1,0:T(8,128)(2,1)S(1)}, u32[]{:S(2)}, u32[]{:S(2)}) collective-permute-start(bf16[512,2048]{1,0:T(8,128)(2,1)} %get-tuple-element.260), channel_id=1, source_target_pairs={{0,1},{1,0},{2,3},{3,2},{4,5},{5,4},{6,7},{7,6},{8,9},{9,8},{10,11... | collective-permute-start | bytes 6291464 | tf_op jit(solution)/shard_map/ppermute | solution.py:108
  778.3 83.4 %collective-permute-start.47 = (bf16[512,2048]{1,0:T(8,128)(2,1)}, bf16[512,2048]{1,0:T(8,128)(2,1)S(1)}, u32[]{:S(2)}, u32[]{:S(2)}) collective-permute-start(bf16[512,2048]{1,0:T(8,128)(2,1)} %get-tuple-element.261), channel_id=1, source_target_pairs={{0,2},{1,3},{2,0},{3,1},{4,6},{5,7},{6,4},{7,5},{8,10},{9,11},{10,... | collective-permute-start | bytes 6291464 | tf_op jit(solution)/shard_map/ppermute | solution.py:108
  784.5 50.5 %collective-permute-start.52 = (bf16[128,2048]{1,0:T(8,128)(2,1)S(1)}, bf16[128,2048]{1,0:T(8,128)(2,1)S(1)}, u32[]{:S(2)}, u32[]{:S(2)}) collective-permute-start(bf16[128,2048]{1,0:T(8,128)(2,1)S(1)} %pad_maximum_fusion.31), channel_id=1, source_target_pairs={{0,24},{4,28},{8,0},{12,4},{16,8},{20,12},{24,16},{28,20},{1,25},{... | collective-permute-start | bytes 1572872 | tf_op jit(solution)/shard_map/ppermute | solution.py:108
  789.7 71.3 %collective-permute-start.53 = (bf16[256,2048]{0,1:T(8,128)(2,1)S(1)}, bf16[256,2048]{0,1:T(8,128)(2,1)S(1)}, u32[]{:S(2)}, u32[]{:S(2)}) collective-permute-start(bf16[256,2048]{0,1:T(8,128)(2,1)S(1)} %pad_maximum_fusion.22), channel_id=1, source_target_pairs={{0,2},{1,3},{2,0},{3,1},{4,6},{5,7},{6,4},{7,5},{8,10},{9,11},{10,... | collective-permute-start | bytes 3145736 | tf_op jit(solution)/shard_map/ppermute | solution.py:108
  792.2 69.5 %collective-permute-start.54 = (bf16[256,2048]{0,1:T(8,128)(2,1)S(1)}, bf16[256,2048]{0,1:T(8,128)(2,1)S(1)}, u32[]{:S(2)}, u32[]{:S(2)}) collective-permute-start(bf16[256,2048]{0,1:T(8,128)(2,1)S(1)} %pad_maximum_fusion.23), channel_id=1, source_target_pairs={{0,1},{1,0},{2,3},{3,2},{4,5},{5,4},{6,7},{7,6},{8,9},{9,8},{10,11... | collective-permute-start | bytes 3145736 | tf_op jit(solution)/shard_map/ppermute | solution.py:108
  834.9 81.8 %collective-permute-start.63 = (bf16[512,2048]{1,0:T(8,128)(2,1)}, bf16[512,2048]{1,0:T(8,128)(2,1)S(1)}, u32[]{:S(2)}, u32[]{:S(2)}) collective-permute-start(bf16[512,2048]{1,0:T(8,128)(2,1)} %get-tuple-element.293), channel_id=1, source_target_pairs={{0,1},{1,0},{2,3},{3,2},{4,5},{5,4},{6,7},{7,6},{8,9},{9,8},{10,11... | collective-permute-start | bytes 6291464 | tf_op jit(solution)/shard_map/ppermute | solution.py:108
  861.0 61.0 %collective-permute-start.64 = (bf16[512,2048]{1,0:T(8,128)(2,1)}, bf16[512,2048]{1,0:T(8,128)(2,1)}, u32[]{:S(2)}, u32[]{:S(2)}) collective-permute-start(bf16[512,2048]{1,0:T(8,128)(2,1)} %get-tuple-element.294), channel_id=1, source_target_pairs={{0,2},{1,3},{2,0},{3,1},{4,6},{5,7},{6,4},{7,5},{8,10},{9,11},{10,... | collective-permute-start | bytes 6291464 | tf_op jit(solution)/shard_map/ppermute | solution.py:108
  868.5 59.8 %collective-permute-start.55 = (bf16[128,2048]{1,0:T(8,128)(2,1)}, bf16[128,2048]{1,0:T(8,128)(2,1)}, u32[]{:S(2)}, u32[]{:S(2)}) collective-permute-start(bf16[128,2048]{1,0:T(8,128)(2,1)} %add_convert_fusion.22), channel_id=1, source_target_pairs={{0,24},{4,28},{8,0},{12,4},{16,8},{20,12},{24,16},{28,20},{1,25},{... | collective-permute-start | bytes 1572872 | tf_op jit(solution)/shard_map/ppermute | solution.py:108
  871.9 56.4 %collective-permute-start.56 = (bf16[256,2048]{1,0:T(8,128)(2,1)}, bf16[256,2048]{1,0:T(8,128)(2,1)}, u32[]{:S(2)}, u32[]{:S(2)}) collective-permute-start(bf16[256,2048]{1,0:T(8,128)(2,1)} %pad_maximum_fusion.27), channel_id=1, source_target_pairs={{0,24},{4,28},{8,0},{12,4},{16,8},{20,12},{24,16},{28,20},{1,25},{... | collective-permute-start | bytes 3145736 | tf_op jit(solution)/shard_map/ppermute | solution.py:108
  911.5 58.6 %collective-permute-start.59 = (bf16[512,2048]{1,0:T(8,128)(2,1)}, bf16[512,2048]{1,0:T(8,128)(2,1)}, u32[]{:S(2)}, u32[]{:S(2)}) collective-permute-start(bf16[512,2048]{1,0:T(8,128)(2,1)} %get-tuple-element.286), channel_id=1, source_target_pairs={{0,2},{1,3},{2,0},{3,1},{4,6},{5,7},{6,4},{7,5},{8,10},{9,11},{10,... | collective-permute-start | bytes 6291464 | tf_op jit(solution)/shard_map/ppermute | solution.py:108
  918.1 52.0 %collective-permute-start.60 = (bf16[512,2048]{1,0:T(8,128)(2,1)}, bf16[512,2048]{1,0:T(8,128)(2,1)}, u32[]{:S(2)}, u32[]{:S(2)}) collective-permute-start(bf16[512,2048]{1,0:T(8,128)(2,1)} %get-tuple-element.287), channel_id=1, source_target_pairs={{0,1},{1,0},{2,3},{3,2},{4,5},{5,4},{6,7},{7,6},{8,9},{9,8},{10,11... | collective-permute-start | bytes 6291464 | tf_op jit(solution)/shard_map/ppermute | solution.py:108
  930.3 39.8 %collective-permute-start.57 = (bf16[128,2048]{1,0:T(8,128)(2,1)}, bf16[128,2048]{1,0:T(8,128)(2,1)S(1)}, u32[]{:S(2)}, u32[]{:S(2)}) collective-permute-start(bf16[128,2048]{1,0:T(8,128)(2,1)} %add_convert_fusion.21), channel_id=1, source_target_pairs={{0,24},{4,28},{8,0},{12,4},{16,8},{20,12},{24,16},{28,20},{1,25},{... | collective-permute-start | bytes 1572872 | tf_op jit(solution)/shard_map/ppermute | solution.py:108
  933.7 36.4 %collective-permute-start.58 = (bf16[256,2048]{1,0:T(8,128)(2,1)}, bf16[256,2048]{1,0:T(8,128)(2,1)S(1)}, u32[]{:S(2)}, u32[]{:S(2)}) collective-permute-start(bf16[256,2048]{1,0:T(8,128)(2,1)} %add_convert_fusion.16), channel_id=1, source_target_pairs={{0,24},{4,28},{8,0},{12,4},{16,8},{20,12},{24,16},{28,20},{1,25},{... | collective-permute-start | bytes 3145736 | tf_op jit(solution)/shard_map/ppermute | solution.py:108
  982.1 36.5 %collective-permute-start.61 = (bf16[256,2048]{1,0:T(8,128)(2,1)}, bf16[256,2048]{1,0:T(8,128)(2,1)}, u32[]{:S(2)}, u32[]{:S(2)}) collective-permute-start(bf16[256,2048]{1,0:T(8,128)(2,1)} %split.282), channel_id=1, source_target_pairs={{0,1},{1,0},{2,3},{3,2},{4,5},{5,4},{6,7},{7,6},{8,9},{9,8},{10,11... | collective-permute-start | bytes 3145736 | tf_op jit(solution)/shard_map/ppermute | solution.py:108
  986.6 32.0 %collective-permute-start.62 = (bf16[256,2048]{1,0:T(8,128)(2,1)}, bf16[256,2048]{1,0:T(8,128)(2,1)}, u32[]{:S(2)}, u32[]{:S(2)}) collective-permute-start(bf16[256,2048]{1,0:T(8,128)(2,1)} %split.283), channel_id=1, source_target_pairs={{0,2},{1,3},{2,0},{3,1},{4,6},{5,7},{6,4},{7,5},{8,10},{9,11},{10,... | collective-permute-start | bytes 3145736 | tf_op jit(solution)/shard_map/ppermute | solution.py:108
  987.2 22.8 %collective-permute-start.65 = (bf16[256,2048]{1,0:T(8,128)(2,1)S(1)}, bf16[256,2048]{1,0:T(8,128)(2,1)S(1)}, u32[]{:S(2)}, u32[]{:S(2)}) collective-permute-start(bf16[256,2048]{1,0:T(8,128)(2,1)S(1)} %add_convert_fusion.15), channel_id=1, source_target_pairs={{0,24},{4,28},{8,0},{12,4},{16,8},{20,12},{24,16},{28,20},{1,25},{... | collective-permute-start | bytes 3145736 | tf_op jit(solution)/shard_map/ppermute | solution.py:108
  1027.3 33.3 %collective-permute-start.68 = (bf16[384,2048]{1,0:T(8,128)(2,1)}, bf16[384,2048]{1,0:T(8,128)(2,1)}, u32[]{:S(2)}, u32[]{:S(2)}) collective-permute-start(bf16[384,2048]{1,0:T(8,128)(2,1)} %pad_maximum_fusion.11), channel_id=1, source_target_pairs={{0,24},{4,28},{8,0},{12,4},{16,8},{20,12},{24,16},{28,20},{1,25},{... | collective-permute-start | bytes 4718600 | tf_op jit(solution)/shard_map/ppermute | solution.py:108
  1064.8 49.8 %collective-permute-start.69 = (bf16[384,2048]{1,0:T(8,128)(2,1)}, bf16[384,2048]{1,0:T(8,128)(2,1)}, u32[]{:S(2)}, u32[]{:S(2)}) collective-permute-start(bf16[384,2048]{1,0:T(8,128)(2,1)} %add_convert_fusion.10), channel_id=1, source_target_pairs={{0,24},{4,28},{8,0},{12,4},{16,8},{20,12},{24,16},{28,20},{1,25},{... | collective-permute-start | bytes 4718600 | tf_op jit(solution)/shard_map/ppermute | solution.py:108
  1106.1 114.8 %all-to-all-start.2 = ((f32[32,64,176]{2,1,0:T(8,128)}), f32[32,64,176]{2,1,0:T(8,128)}, u32[]{:S(2)}, u32[]{:S(2)}) async-start(f32[32,64,176]{2,1,0:T(8,128)} %bitcast.330), calls=%async_computation.2 | async-start | bytes 4194304 | tf_op jit(solution)/shard_map/all_to_all | solution.py:733
  1111.0 39.0 %collective-permute-start.100 = (bf16[256,512]{1,0:T(8,128)(2,1)S(1)}, bf16[256,512]{1,0:T(8,128)(2,1)S(1)}, u32[]{:S(2)}, u32[]{:S(2)}) collective-permute-start(bf16[256,512]{1,0:T(8,128)(2,1)S(1)} %fusion.70), channel_id=1, source_target_pairs={{0,24},{4,28},{8,0},{12,4},{16,8},{20,12},{24,16},{28,20},{1,25},{... | collective-permute-start | bytes 786440 | tf_op jit(solution)/shard_map/ppermute | solution.py:108
  1118.1 115.7 %collective-permute-start.70 = (bf16[384,2048]{1,0:T(8,128)(2,1)}, bf16[384,2048]{1,0:T(8,128)(2,1)}, u32[]{:S(2)}, u32[]{:S(2)}) collective-permute-start(bf16[384,2048]{1,0:T(8,128)(2,1)} %add_convert_fusion.9), channel_id=1, source_target_pairs={{0,24},{4,28},{8,0},{12,4},{16,8},{20,12},{24,16},{28,20},{1,25},{... | collective-permute-start | bytes 4718600 | tf_op jit(solution)/shard_map/ppermute | solution.py:108
  1125.5 89.4 %collective-permute-start.80 = (bf16[256,768]{0,1:T(8,128)(2,1)}, bf16[256,768]{0,1:T(8,128)(2,1)}, u32[]{:S(2)}, u32[]{:S(2)}) collective-permute-start(bf16[256,768]{0,1:T(8,128)(2,1)} %bitcast.69), channel_id=1, source_target_pairs={{0,3},{1,2},{2,1},{3,0},{4,7},{5,6},{6,5},{7,4},{8,11},{9,10},{10,... | collective-permute-start | bytes 1179656 | tf_op jit(solution)/shard_map/ppermute | solution.py:114
  1150.0 41.1 %collective-permute-start.101 = (bf16[256,512]{1,0:T(8,128)(2,1)S(1)}, bf16[256,512]{1,0:T(8,128)(2,1)S(1)}, u32[]{:S(2)}, u32[]{:S(2)}) collective-permute-start(bf16[256,512]{1,0:T(8,128)(2,1)S(1)} %fusion.69), channel_id=1, source_target_pairs={{0,24},{4,28},{8,0},{12,4},{16,8},{20,12},{24,16},{28,20},{1,25},{... | collective-permute-start | bytes 786440 | tf_op jit(solution)/shard_map/ppermute | solution.py:108
  1261.8 67.1 %collective-permute-start.91 = (bf16[4,256,1024]{2,1,0:T(8,128)(2,1)}, bf16[4,256,1024]{2,1,0:T(8,128)(2,1)}, u32[]{:S(2)}, u32[]{:S(2)}) collective-permute-start(bf16[4,256,1024]{2,1,0:T(8,128)(2,1)} %fusion.42), channel_id=1, source_target_pairs={{0,4},{4,0},{8,12},{12,8},{16,20},{20,16},{24,28},{28,24},{1,5},{5... | collective-permute-start | bytes 6291464 | tf_op jit(solution)/shard_map/ppermute | solution.py:108
  (208 other events, 2950.3 us)
Sparse Core Ops, SparseCore 0:
  121.4 231.5 all-gather.2
  711.3 114.5 all-gather.4

commit v3 on v2

--- a/solution.py
+++ b/solution.py
@@ -88,14 +88,21 @@
         self.dp = lax.axis_size("dp")
         self.ctx = lax.axis_size("ctx")
         self.size = {"z": self.dp // 2, "c": 2, "w": self.ctx // 4, "y": 2, "x": 2}
-        dp, ctx = lax.axis_index("dp"), lax.axis_index("ctx")
+        dp = lax.axis_index("dp").astype(jnp.uint32)
+        self.place = ctx = lax.axis_index("ctx").astype(jnp.uint32)
         self.own = {
-            "z": dp // 2,
-            "c": dp % 2,
-            "w": ctx // 4,
-            "y": (ctx // 2) % 2,
-            "x": ctx % 2,
+            "z": dp >> 1,
+            "c": dp & 1,
+            "w": ctx >> 2,
+            "y": (ctx >> 1) & 1,
+            "x": ctx & 1,
         }
+
+    def minus(self, axis, steps):
+        return (self.own[axis] - steps) & (self.size[axis] - 1)
+
+    def ctx_at(self, k):
+        return self.minus("w", jnp.uint32(k // 4)) * 4 + ((self.place ^ jnp.uint32(k)) & 3)
 
     def shift(self, value, axis, by=1):
         name, count = ("dp", self.dp) if axis in "zc" else ("ctx", self.ctx)
@@ -141,34 +148,30 @@
         for i, axis in enumerate(order):
             shape = [1] * depth
             shape[depth - 1 - i] = self.size[axis]
-            offsets = jnp.arange(self.size[axis], dtype=jnp.int32).reshape(shape)
-            place[axis] = (self.own[axis] - offsets) % self.size[axis]
+            place[axis] = self.minus(
+                axis, jnp.arange(self.size[axis], dtype=jnp.uint32).reshape(shape)
+            )
         number = (place["z"] * 2 + place["c"]) * self.ctx
         number = number + place["w"] * 4 + place["y"] * 2 + place["x"]
         return number.reshape(-1)
 
     def place_of(self, order):
-        number = jnp.arange(self.dp * self.ctx, dtype=jnp.int32)
+        number = jnp.arange(self.dp * self.ctx, dtype=jnp.uint32)
         coordinate = {
-            "x": number % 2,
-            "y": (number // 2) % 2,
-            "w": (number // 4) % self.size["w"],
-            "c": (number // self.ctx) % 2,
+            "x": number & 1,
+            "y": (number >> 1) & 1,
+            "w": (number >> 2) & (self.size["w"] - 1),
+            "c": (number // self.ctx) & 1,
             "z": number // (2 * self.ctx),
         }
         place = jnp.zeros_like(number)
         for axis in order[::-1]:
-            steps = (self.own[axis] - coordinate[axis]) % self.size[axis]
-            place = place * self.size[axis] + steps
+            place = place * self.size[axis] + self.minus(axis, coordinate[axis])
         return place
 
-    def ctx_relative(self):
-        return self.device_of(("x", "y", "w")) % self.ctx
-
     def ctx_place(self):
-        number = jnp.arange(self.ctx, dtype=jnp.int32)
-        w = (self.own["w"] - number // 4) % self.size["w"]
-        return w * 4 + (lax.axis_index("ctx") ^ number) % 4
+        number = jnp.arange(self.ctx, dtype=jnp.uint32)
+        return self.minus("w", number >> 2) * 4 + ((self.place ^ number) & 3)
 
     def ctx_exchange(self, pieces):
         result = [pieces[0]] + [None] * (self.ctx - 1)
@@ -334,7 +337,6 @@
     row = segments.shape[0]
     ctx = links.ctx
     devices = links.dp * ctx
-    me = lax.axis_index("dp") * ctx + lax.axis_index("ctx")
     half_ff = EXPERT_FF // 2
     half_sh = w_shared_out.shape[0]
     half_all = -(-(half_ff + half_sh) // 128) * 128
@@ -348,7 +350,7 @@
     up_fold = rows_l * kv_cols // rows_d
     up_parts = rows_d // rows_l
     scale = 1.0 / math.sqrt(NOPE + ROPE)
-    rel_ctx = links.ctx_relative()
+    rel_ctx = [links.ctx_at(k) for k in range(ctx)]
     ctx_place = links.ctx_place()
 
     def columns(value, k, width):
@@ -435,7 +437,7 @@
     count = tok // slices
     tokens = devices * tok
     source_list = [links.device_of(order + ("c",)) for order in orders]
-    sources = jnp.concatenate(source_list)
+    sources = jnp.concatenate(source_list).astype(jnp.int32)
     m_place = jnp.concatenate([d * slices + i for i, d in enumerate(source_list)])
     hidden_row, query_w, up_w, down_w = tie(hidden_row, query_w, up_w, down_w)
     g_all = lax.all_gather(after(cotangent, far_a), BOTH, axis=0, tiled=True)
@@ -444,8 +446,10 @@
     inputs_row = hidden_row.astype(f32)
     inverse_row = rms_inverse(inputs_row)
     normed_row = (inputs_row * inverse_row * gain_attn).astype(bf16)
-    positions = (rel_ctx[:, None] * tok + jnp.arange(tok, dtype=jnp.int32)[None, :]).reshape(-1)
-    row_segments = segments.reshape(ctx, tok)[rel_ctx].reshape(-1)
+    rel_numbers = jnp.stack(rel_ctx)
+    positions = rel_numbers.astype(jnp.int32)[:, None] * tok
+    positions = (positions + jnp.arange(tok, dtype=jnp.int32)[None, :]).reshape(-1)
+    row_segments = segments.reshape(ctx, tok)[rel_numbers].reshape(-1)
     allowed = (positions[None, :] <= positions[:, None]) & (
         row_segments[None, :] == row_segments[:, None]
     )
@@ -502,6 +506,7 @@
         return [joined_rows([pair[i] for pair in both]) for i in range(2)]
 
     held = joined_rows(cut[:2])
+    heads_half = [heads_out[: tok // 2], heads_out[tok // 2 :]]
     near_y, near_x, first, shared_w, w_expert_in, routes, gates = tie(
         links.shift(cut[2], "y"),
         links.shift(cut[3], "x"),
@@ -535,8 +540,13 @@
     )
     m = m_all.reshape(devices * slices, count)[m_place].reshape(tokens, 1)
     ring_a = [held, first]
+    heads_far = [links.shift(heads_half[0], "x"), links.shift(heads_half[1], "y")]
     while len(ring_a) < links.size["z"]:
-        ring_a.append(links.shift(ring_a[-1], "z"))
+        step, *heads_far = tie(links.shift(ring_a[-1], "z"), *heads_far)
+        if len(ring_a) == 2:
+            heads_half = [joined_rows(p) for p in zip(heads_half, heads_far)]
+            heads_far = [links.shift(heads_half[0], "y"), links.shift(heads_half[1], "x")]
+        ring_a.append(step)
     held = links.gather(joined_rows(ring_a), ("w",)) if links.size["w"] > 1 else None
     slice_0, slice_1 = halved(jnp.split(held, ctx // 4 * links.size["z"]) if held is not None else ring_a)
     held = joined_rows([cut[2], near_y, cut[3], near_x])
@@ -597,11 +607,10 @@
     near_b = halved(jnp.split(held, ctx // 4 * links.size["z"]) if held is not None else ring_b)
     far_b = [links.shift(near_b[0], "x"), links.shift(near_b[1], "y")]
     kept = ffn(far_a_sib, "af", 1)
-    kept = ffn(near_a_rows, "an", 0)
-    far_a_rows, *far_b = tie(far_a_rows, *far_b, done["an", 0][0])[:3]
+    kept = ffn(far_a_rows, "af", 0)
+    near_a_rows, *far_b = tie(near_a_rows, *far_b, done["af", 0][0])[:3]
     rows_b = joined_rows([*near_b, *far_b])
     sib_b = links.shift(rows_b, "c")
-    kept = ffn(far_a_rows, "af", 0)
 
     def add_far(moved_rows, near):
         return [plus(m_rows, n_rows) for m_rows, n_rows in zip(moved_rows, near)]
@@ -621,72 +630,79 @@
 
     far = done["af", 0][1::2]
     a_far = [links.shift(far[0], "y", -1), links.shift(far[1], "x", -1)]
+    kept = ffn(near_a_rows, "an", 0)
+    a_far = tie(*a_far, done["an", 0][0])[:2]
+    a_near = add_far(a_far, done["an", 0][1::2])
+    sib_b, *a_near = tie(sib_b, *a_near)
+    a_near, far = split_far(a_near)
+    a_far = [links.shift(far[0], "x", -1), links.shift(far[1], "y", -1)]
     query_w_all = lax.all_gather(after(w_query, sib_b), BOTH, axis=0, tiled=True)
     kept = ffn(sib_b, "b", 1)
     a_far = tie(*a_far, done["b", 1][0])[:2]
-    a_near = add_far(a_far, done["an", 0][1::2])
-    rows_b, heads_out, *a_near = tie(rows_b, heads_out, *a_near)
-    a_near, far = split_far(a_near)
-    a_far = [links.shift(far[0], "x", -1), links.shift(far[1], "y", -1)]
-    heads_half = [heads_out[: tok // 2], heads_out[tok // 2 :]]
-    heads_far = [links.shift(heads_half[0], "x"), links.shift(heads_half[1], "y")]
+    a_parts = z_parts(add_far(a_far, a_near))
+    rows_b, *a_parts = tie(rows_b, *a_parts)
+    a_sum = links.shift(a_parts[-1], "z", -1)
     kept = ffn(rows_b, "b", 0)
-    *a_far, heads_far[0], heads_far[1] = tie(*a_far, *heads_far, done["b", 0][0])[:4]
+    a_sum = after(a_sum, done["b", 0][0])
     done["bn", 0], done["bf", 0] = done["b", 0][:4], done["b", 0][4:]
-    heads_half = [joined_rows(p) for p in zip(heads_half, heads_far)]
     far = done["bf", 0][1::2]
     b_far = [links.shift(far[0], "x", -1), links.shift(far[1], "y", -1)]
-    a_parts = z_parts(add_far(a_far, a_near))
-    heads_far = [links.shift(heads_half[0], "y"), links.shift(heads_half[1], "x")]
-    a_sum = links.shift(a_parts[-1], "z", -1)
     out_far = [done["af", 0][0], done["af", 0][2]]
     out_far_b = [done["bf", 0][0], done["bf", 0][2]]
+
+    def send_outputs(far_rows, far_rows_b):
+        near_rows, far_rows = split_far(add_far(far_rows, [done["an", 0][0], done["an", 0][2]]))
+        return near_rows, [
+            links.shift(joined_rows(pair), axis, -1)
+            for pair, axis in zip(zip(far_rows, far_rows_b), "xy")
+        ]
+
     if lean:
         grad_w_in, grad_w_back = kept
         a_sum = plus(a_sum, a_parts[-2])
         for part in a_parts[-3::-1]:
             a_sum = plus(links.shift(a_sum, "z", -1), part)
         out_far = [links.shift(p, axis, -1) for p, axis in zip(out_far, "yx")]
-        out_far_b = [links.shift(p, axis, -1) for p, axis in zip(out_far_b, "xy")]
+        out_near, out_sent = send_outputs(out_far, out_far_b)
         b_parts = z_parts(add_far(b_far, done["bn", 0][1::2]))
         b_sum = b_parts[-1]
         for part in b_parts[-2:0:-1]:
             b_sum = plus(links.shift(b_sum, "z", -1), part)
     else:
         x_all, g_kept, act_all, grad_pre_all = kept
+        a_sum = plus(a_sum, a_parts[-2])
+        x_all, a_sum = tie(x_all, a_sum)
+        a_next = links.shift(a_sum, "z", -1)
         grad_w_top = matmul_left_t(x_all[:, : D // 2], grad_pre_all)
-        *b_far, a_sum, heads_far[0], heads_far[1], _ = tie(*b_far, a_sum, *heads_far, grad_w_top)
+        *b_far, a_next, _ = tie(*b_far, a_next, grad_w_top)
         b_parts = z_parts(add_far(b_far, done["bn", 0][1::2]))
-        a_sum = plus(a_sum, a_parts[-2])
+        a_sum = plus(a_next, a_parts[-3])
         x_all, a_sum, out_far[0], out_far[1], *b_parts = tie(x_all, a_sum, *out_far, *b_parts)
         out_far = [links.shift(p, axis, -1) for p, axis in zip(out_far, "yx")]
         a_next = links.shift(a_sum, "z", -1)
         b_next = links.shift(b_parts[-1], "z", -1)
         grad_w_end = matmul_left_t(x_all[:, D // 2 :], grad_pre_all)
         a_next, b_next, _ = tie(a_next, b_next, grad_w_end)
-        for part in a_parts[-3:0:-1]:
-            a_sum = plus(a_next, part)
-            a_next = links.shift(a_sum, "z", -1)
+        a_sum = plus(a_next, a_parts[-4])
         b_sum = plus(b_next, b_parts[-2])
-        act_all, a_sum, b_sum = tie(act_all, a_sum, b_sum)
+        act_all, a_sum, b_sum, *out_all = tie(act_all, a_sum, b_sum, *out_far, *out_far_b)
+        out_near, out_sent = send_outputs(out_all[:2], out_all[2:])
         b_next = links.shift(b_sum, "z", -1)
-        out_far_b = [links.shift(p, axis, -1) for p, axis in zip(out_far_b, "xy")]
         grad_w_back = matmul_left_t(act_all, g_kept)
-        a_next, b_next, *out_far, _ = tie(a_next, b_next, *out_far, grad_w_back)
-        a_sum = plus(a_next, a_parts[0])
+        b_next, _ = tie(b_next, grad_w_back)
         b_sum = plus(b_next, b_parts[-3])
         for part in b_parts[-4:0:-1]:
             b_sum = plus(links.shift(b_sum, "z", -1), part)
         grad_w_top, grad_w_end, grad_w_back, b_sum = tie(
             grad_w_top, grad_w_end, grad_w_back, b_sum
         )
-    out_near, out_far = split_far(add_far(out_far, [done["an", 0][0], done["an", 0][2]]))
-    out_far = [links.shift(p, axis, -1) for p, axis in zip(out_far, "xy")]
-    out_near_b = add_far(out_far_b, [done["bn", 0][0], done["bn", 0][2]])
     b_sum = plus(links.shift(b_sum, "z", -1), b_parts[0])
     grad_ffn = joined_rows([a_sum, *last_b(b_sum)])
-    out_far[0], out_far[1], out_near_b[0], out_near_b[1], grad_ffn = tie(
-        *out_far, *out_near_b, grad_ffn
+    out_sent[0], out_sent[1], grad_ffn = tie(*out_sent, grad_ffn)
+    out_split = out_near[0].shape[0]
+    out_far = [p[:out_split] for p in out_sent]
+    out_near_b = add_far(
+        [p[out_split:] for p in out_sent], [done["bn", 0][0], done["bn", 0][2]]
     )
     grad_ffn = grad_ffn.astype(f32)
 
@@ -717,6 +733,38 @@
     grad_w_shared_out = grad_w_back[half_ff : half_ff + half_sh]
     grad_shared = joined_rows([pick(v, half_ff, half_sh) for v in blocks_in])
     grad_shared = grad_shared.reshape(devices, rows_d, 2 * half_sh)
+    def owner_steps(value, direct):
+        count, size = value.shape[1], links.size["z"]
+        value = value.reshape(size, 2, ctx * count, -1)
+
+        def core(c):
+            return lax.dynamic_index_in_dim(value, c, 1, keepdims=False)
+
+        moved_core = links.shift(core(links.own["c"] ^ 1), "c")
+        (moved_core,) = yield [moved_core]
+        total = plus(moved_core, core(links.own["c"]))
+        parts = [
+            lax.dynamic_index_in_dim(total, links.minus("z", jnp.uint32(k)), 0, keepdims=False)
+            for k in range(size)
+        ]
+        if direct:
+            back = [links.shift(parts[k], "z", -k) for k in range(1, size)]
+            back = yield back
+            summed = sum([p.astype(f32) for p in back], parts[0].astype(f32)).astype(bf16)
+        else:
+            summed = parts[-1]
+            for part in parts[-2::-1]:
+                moved_sum = links.shift(summed, "z", -1)
+                (moved_sum,) = yield [moved_sum]
+                summed = plus(moved_sum, part)
+        summed = summed.reshape(ctx, count, -1)
+        pieces = [
+            lax.dynamic_index_in_dim(summed, rel_ctx[k], 0, keepdims=False) for k in range(ctx)
+        ]
+        pieces = links.ctx_exchange(pieces)
+        received = yield pieces[1:]
+        yield jnp.stack([pieces[0], *received])[ctx_place].astype(f32)
+
     grad_out = cotangent.astype(f32)
     grad_middle_part, grad_norm_ffn = rms_backward(middle, inverse_ffn, gain_ffn, grad_ffn)
     grad_middle = grad_out + grad_middle_part
@@ -767,12 +815,9 @@
         [grad_key[..., :NOPE], grad_values.transpose(1, 0, 2)], axis=-1
     )
     grad_keyval = grad_keyval.astype(bf16).reshape(row, kv_cols)
-    grad_keyval, *out_now = tie(grad_keyval, *out_now)
-    mixed = (middle + list(out_steps)[-1][0].astype(f32)).astype(bf16)
     grad_w_up = matmul_left_t(latent, grad_keyval)
     grad_latent = matmul_right_t(grad_keyval, up_w)
     grad_low = jnp.concatenate([grad_latent, grad_key_rope], axis=1).astype(bf16)
-    grad_low = links.scatter_sum(grad_low, ("x", "y", "w")).astype(f32)
     grad_query_raw = jnp.concatenate(
         [
             grad_query[..., :NOPE],
@@ -781,7 +826,30 @@
         axis=-1,
     )
     grad_query_raw = grad_query_raw.astype(bf16).reshape(ctx, tok, q_cols)
-    query_back = jnp.stack(links.ctx_exchange([grad_query_raw[k] for k in range(ctx)]))
+    query_back = links.ctx_exchange([grad_query_raw[k] for k in range(ctx)])
+    grad_low, *query_back = tie(grad_low, *query_back)
+    query_back = jnp.stack(query_back)
+    grad_out_cols = matmul_left_t(heads_out_row, grad_attended_cols)
+    grad_w_q = matmul_left_t(normed_row, grad_query_raw.reshape(row, q_cols))
+    grad_w_up = grad_w_up.astype(bf16).reshape(devices, rows_l, up_parts, up_fold)
+    grad_w_up = grad_w_up.transpose(0, 2, 1, 3).reshape(devices, rows_d, up_fold)
+    heads_owned = owner_steps(
+        jnp.concatenate(
+            [
+                grad_w_q.astype(bf16).reshape(devices, rows_d, q_cols),
+                grad_w_up,
+                grad_out_cols.astype(bf16).reshape(devices, rows_d, D // ctx),
+            ],
+            axis=2,
+        ),
+        False,
+    )
+    heads_moved = next(heads_owned)
+    low_parts = links.ctx_exchange(list(grad_low.reshape(ctx, tok, -1)))
+    *low_parts, out_now[0], heads_moved[0] = tie(*low_parts, *out_now, *heads_moved)
+    heads_moved = heads_owned.send(heads_moved)
+    grad_low = sum(p.astype(f32) for p in low_parts)
+    mixed = (middle + list(out_steps)[-1][0].astype(f32)).astype(bf16)
     query_back = query_back[ctx_place].transpose(1, 0, 2).reshape(tok, ctx * q_cols)
     grad_compressed_latent, grad_norm_latent = rms_backward(
         raw_latent[:tok], inverse_latent[:tok], gain_latent, grad_low[:, :LATENT]
@@ -796,50 +864,15 @@
     grad_normed = matmul_right_t(grad_compressed, down_w) + matmul_right_t(
         query_back, query_w_all
     )
+    grad_normed, heads_moved[0] = tie(grad_normed, *heads_moved)
+    heads_moved = heads_owned.send(heads_moved)
     grad_input_part, grad_norm_attn = rms_backward(
         inputs, inverse_row[:tok], gain_attn, grad_normed
     )
     grad_in = grad_middle + grad_input_part
 
-    def to_owners(value):
-        count, size = value.shape[1], links.size["z"]
-        value = value.astype(bf16).reshape(size, 2, ctx * count, -1)
-
-        def core(c):
-            return lax.dynamic_index_in_dim(value, c, 1, keepdims=False)
-
-        total = plus(links.shift(core(1 - links.own["c"]), "c"), core(links.own["c"]))
-
-        def part(k):
-            return lax.dynamic_index_in_dim(
-                total, (links.own["z"] - k) % size, 0, keepdims=False
-            )
-
-        summed = part(size - 1)
-        for k in range(size - 2, -1, -1):
-            summed = plus(links.shift(summed, "z", -1), part(k))
-        summed = summed.reshape(ctx, count, -1)
-        pieces = [
-            lax.dynamic_index_in_dim(summed, rel_ctx[k], 0, keepdims=False) for k in range(ctx)
-        ]
-        return jnp.stack(links.ctx_exchange(pieces))[ctx_place].astype(f32)
-
     def joined(value):
         return value.transpose(1, 0, 2).reshape(value.shape[1], -1)
-
-    grad_out_cols = matmul_left_t(heads_out_row, grad_attended_cols)
-    grad_w_out = joined(to_owners(grad_out_cols.reshape(devices, rows_d, D // ctx)))
-    grad_w_q = matmul_left_t(normed_row, grad_query_raw.reshape(row, q_cols))
-    grad_w_up = grad_w_up.astype(bf16).reshape(devices, rows_l, up_parts, up_fold)
-    grad_w_up = grad_w_up.transpose(0, 2, 1, 3).reshape(devices, rows_d, up_fold)
-    heads_grads = to_owners(
-        jnp.concatenate(
-            [grad_w_q.astype(bf16).reshape(devices, rows_d, q_cols), grad_w_up], axis=2
-        )
-    )
-    grad_w_query = joined(heads_grads[:, :, :q_cols])
-    grad_w_kv_up = heads_grads[:, :, q_cols:].reshape(ctx, up_parts, rows_l, up_fold)
-    grad_w_kv_up = grad_w_kv_up.transpose(2, 0, 1, 3).reshape(rows_l, ctx * kv_cols)
 
     compressed_cols = jnp.concatenate(
         links.ctx_exchange([columns(grad_compressed, k, dn_cols) for k in range(ctx)]), axis=0
@@ -853,9 +886,26 @@
         axis=1,
     )
     vectors = jnp.pad(vectors, ((0, 0), (0, 13), (0, 0))).astype(bf16)
-    last_grads = to_owners(
-        jnp.concatenate([grad_w_down.reshape(devices, rows_d, dn_cols), vectors], axis=1)
-    )
+    last_owned = owner_steps(
+        jnp.concatenate([grad_w_down.reshape(devices, rows_d, dn_cols), vectors], axis=1), True
+    )
+    last_moved = next(last_owned)
+    last_moved[0], heads_moved[0] = tie(*last_moved, *heads_moved)
+    heads_moved = heads_owned.send(heads_moved)
+    last_moved = last_owned.send(last_moved)
+
+    def finish(steps, received):
+        for received in iter(lambda: steps.send(received), None):
+            if not isinstance(received, list):
+                return received
+
+    heads_grads = finish(heads_owned, heads_moved)
+    last_grads = finish(last_owned, last_moved)
+    grad_w_query = joined(heads_grads[:, :, :q_cols])
+    grad_w_out = joined(heads_grads[:, :, q_cols + up_fold :])
+    grad_w_kv_up = heads_grads[:, :, q_cols : q_cols + up_fold]
+    grad_w_kv_up = grad_w_kv_up.reshape(ctx, up_parts, rows_l, up_fold)
+    grad_w_kv_up = grad_w_kv_up.transpose(2, 0, 1, 3).reshape(rows_l, ctx * kv_cols)
     grad_w_kv_down = joined(last_grads[:, :rows_d])
     vector_sums = jnp.sum(last_grads[:, rows_d : rows_d + 3], axis=0)
     return (

time: 1400 us -> 1290 us (0.921)
  waiting for transfers between devices: 335 us -> 258 us
  starting transfers between devices: 156 us -> 125 us
  between operations: 34.7 us -> 16.8 us
    ppermute x78 -> x70, waiting for transfers between devices: 291 us -> 216 us  [shift(): return lax.ppermute(value, name, pairs)]
    ppermute x78 -> x70, starting transfers between devices: 106 us -> 78.3 us  [shift(): return lax.ppermute(value, name, pairs)]
    convert_element_type x36 -> x28, other arithmetic: 52.9 us -> 46.3 us  [plus(): return (left.astype(f32) + right.astype(f32)).astype(bf16)]
    unnamed x359 -> x301, local copies, waits for them, and re-layouts: 62.2 us -> 64.4 us
    concatenate x25 -> x30, other arithmetic: 31.8 us -> 31.7 us  [joined_rows(): return parts[0] if len(parts) == 1 else jnp.concatenate(parts, axis=0)]
  transfers between devices with their start and end apart: 110 -> 102, of which waited for: 48 -> 47; matrix products, arithmetic and copies ran while one was open for 41% -> 45% of each run, Pallas kernels for 15% -> 14%
where the time goes in v3:
time: 1290 us; the launch traced here: 1270 us
  Pallas kernels  266 us (21%)
  waiting for transfers between devices  258 us (20%)
  local copies, waits for them, and re-layouts  229 us (18%)
  matrix products  222 us (17%)
  other arithmetic  154 us (12%)
  starting transfers between devices  125 us (10%)
  between operations  16.8 us (1%)
    pallas_call x6, Pallas kernels, ffn_chunk(): pl.pallas_call(lambda *refs: ffn_kernel(half_ff, 0 if moved is None else...  266 us
    ppermute x70, waiting for transfers between devices, shift(): return lax.ppermute(value, name, pairs)  216 us
    dot_general x7, matrix products, matmul_left_t(): lax.dot_general(left, right, (((0,), (0,)), ((), ())), preferred_element_...  133 us
    ppermute x70, starting transfers between devices, shift(): return lax.ppermute(value, name, pairs)  78.3 us
    unnamed x301, local copies, waits for them, and re-layouts  64.4 us
    convert_element_type x28, other arithmetic, plus(): return (left.astype(f32) + right.astype(f32)).astype(bf16)  46.3 us
    ppermute x27, waiting for transfers between devices, shift_ctx(): return lax.ppermute(value, 'ctx', pairs)  41.5 us
    ppermute x27, starting transfers between devices, shift_ctx(): return lax.ppermute(value, 'ctx', pairs)  32 us
  transfers between devices with their start and end apart: 102, of which 47 were waited for; matrix products, arithmetic and copies ran while one was open for 45% of the time, Pallas kernels for 14%

profile of v3, /device:TPU:0, one launch (start us, length us, event | category | flops | bytes accessed | tf_op | source)
XLA Modules:
  0.0 1270.0 jit_solution(12179008139709109253)
XLA Ops:
  21.7 4.3 collective-permute-done.2
  32.8 14.5 %collective-permute-done.5 = bf16[64,2688]{1,0:T(8,128)(2,1)} collective-permute-done((bf16[64,2688]{1,0:T(8,128)(2,1)S(1)}, bf16[64,2688]{1,0:T(8,128)(2,1)}, u32[]{:S(2)}, u32[]{:S(2)}) %collective-permute-start.5) | collective-permute-done | bytes 344096 | tf_op jit(solution)/shard_map/ppermute | solution.py:115
  54.2 5.0 all-to-all-start
  59.3 12.2 collective-permute-done.7
  75.7 7.9 collective-permute-done.9
  86.7 10.5 collective-permute-done.11
  104.5 5.8 collective-permute-done.14
  130.0 3.9 pad_maximum_fusion.3
  143.1 4.1 gather_fusion.1
  153.8 5.0 gather_fusion
  168.9 4.3 fusion.93
  173.4 3.8 pad_maximum_fusion.4
  179.2 7.8 fusion.128
  187.0 8.2 fusion.8
  195.3 7.6 fusion.45
  213.1 8.6 collective-permute-done.21
  222.8 4.9 constant_dynamic-update-slice_fusion.20
  227.7 9.1 gather_fusion.4
  236.8 6.0 multiply_reduce_fusion.1
  249.6 9.5 collective-permute-done.24
  261.0 9.9 collective-permute-done.26
  270.9 7.1 collective-permute-start.27
  282.2 5.8 all-to-all-start.1
  289.7 12.7 collective-permute-done.27
  315.8 12.0 concatenate.299.refs_7_
  329.9 9.4 collective-permute-done.30
  345.3 18.6 %collective-permute-done.33 = bf16[256,2048]{1,0:T(8,128)(2,1)S(1)} collective-permute-done((bf16[256,2048]{1,0:T(8,128)(2,1)S(1)}, bf16[256,2048]{1,0:T(8,128)(2,1)S(1)}, u32[]{:S(2)}, u32[]{:S(2)}) %collective-permute-start.33) | collective-permute-done | bytes 1048608 | tf_op jit(solution)/shard_map/ppermute | solution.py:115
  364.0 5.4 collective-permute-done.35
  381.9 18.3 %collective-permute-done.37 = bf16[256,2048]{1,0:T(8,128)(2,1)} collective-permute-done((bf16[256,2048]{1,0:T(8,128)(2,1)}, bf16[256,2048]{1,0:T(8,128)(2,1)}, u32[]{:S(2)}, u32[]{:S(2)}) %collective-permute-start.37) | collective-permute-done | bytes 1048608 | tf_op jit(solution)/shard_map/ppermute | solution.py:115
  400.2 33.6 %ffn_chunk.6 = (bf16[8192,2048]{1,0:T(8,128)(2,1)}, bf16[8192,2048]{1,0:T(8,128)(2,1)}, bf16[8192,896]{1,0:T(8,128)(2,1)}, bf16[8192,1792]{1,0:T(8,128)(2,1)}, bf16[1024,4096]{1,0:T(8,128)(2,1)}) custom-call(s32[128]{0:T(128)} %add_convert_fusion.31.refs_0_, bf16[1024,2048]{1,0:T(8,128)(2,1)} %collective-permute-done.36.refs_1_, ...), custom_call_target="tpu_custom_call" | custom-call | flops 22548578304 | bytes 33554432 | tf_op jit(solution)/shard_map/ffn_chunk/pallas_call | solution.py:298
  439.3 7.2 collective-permute-done.41.refs_1_
  448.5 33.8 %ffn_chunk.7 = (bf16[8192,2048]{1,0:T(8,128)(2,1)}, bf16[8192,2048]{1,0:T(8,128)(2,1)}, bf16[8192,896]{1,0:T(8,128)(2,1)}, bf16[8192,1792]{1,0:T(8,128)(2,1)}, bf16[1024,4096]{1,0:T(8,128)(2,1)}) custom-call(s32[128]{0:T(128)} %add_convert_fusion.31.refs_0_, ...), custom_call_target="tpu_custom_call", output_to_operand_aliasing={{0}: (9, {}), {1}: (10, {}), {2}: (11, {}), {3}: (12, {})} | custom-call | flops 22548578304 | bytes 33554432 | tf_op jit(solution)/shard_map/ffn_chunk/pallas_call | solution.py:298
  497.9 36.3 %ffn_chunk.8 = (bf16[8192,2048]{1,0:T(8,128)(2,1)}, bf16[8192,2048]{1,0:T(8,128)(2,1)}, bf16[8192,896]{1,0:T(8,128)(2,1)}, bf16[8192,1792]{1,0:T(8,128)(2,1)}, b...) custom-call(s32[128]{0:T(128)} %add_convert_fusion.31.refs_0_, ...), custom_call_target="tpu_custom_call", output_to_operand_aliasing={{0}: (10, {}), {1}: (11, {}), {2}: (12, {}), {3}: (13, {})} | custom-call | flops 22548578304 | bytes 33554432 | tf_op jit(solution)/shard_map/ffn_chunk/pallas_call | solution.py:298
  534.3 4.4 collective-permute-done.42
  538.6 5.1 collective-permute-done.43
  552.2 36.7 %ffn_chunk.9 = (bf16[8192,2048]{1,0:T(8,128)(2,1)}, bf16[8192,2048]{1,0:T(8,128)(2,1)}, bf16[8192,896]{1,0:T(8,128)(2,1)}, bf16[8192,1792]{1,0:T(8,128)(2,1)}, b...) custom-call(s32[128]{0:T(128)} %add_convert_fusion.31.refs_0_, ...), custom_call_target="tpu_custom_call", output_to_operand_aliasing={{0}: (10, {}), {1}: (11, {}), {2}: (12, {}), {3}: (13, {})} | custom-call | flops 22548578304 | bytes 33554432 | tf_op jit(solution)/shard_map/ffn_chunk/pallas_call | solution.py:298
  588.9 9.4 collective-permute-done.46
  602.8 3.7 add_convert_fusion.6
  606.5 59.7 %ffn_chunk.10 = (bf16[8192,2048]{1,0:T(8,128)(2,1)}, bf16[8192,2048]{1,0:T(8,128)(2,1)}, bf16[8192,896]{1,0:T(8,128)(2,1)}, bf16[8192,1792]{1,0:T(8,128)(2,1)}, bf16[2048,4096]{1,0:T(8,128)(2,1)}) custom-call(s32[128]{0:T(128)} %add_convert_fusion.31.refs_0_, ...), custom_call_target="tpu_custom_call", output_to_operand_aliasing={{0}: (9, {}), {1}: (10, {}), {2}: (11, {}), {3}: (12, {})} | custom-call | flops 45097156608 | bytes 67108864 | tf_op jit(solution)/shard_map/ffn_chunk/pallas_call | solution.py:298
  689.2 19.6 %collective-permute-done.49 = bf16[256,2048]{1,0:T(8,128)(2,1)S(1)} collective-permute-done((bf16[256,2048]{1,0:T(8,128)(2,1)}, bf16[256,2048]{1,0:T(8,128)(2,1)S(1)}, u32[]{:S(2)}, u32[]{:S(2)}) %collective-permute-start.49) | collective-permute-done | bytes 1048608 | tf_op jit(solution)/shard_map/ppermute | solution.py:115
  714.4 3.8 collective-permute-start.52
  718.3 65.4 %ffn_chunk.11 = (bf16[8192,2048]{1,0:T(8,128)(2,1)}, bf16[8192,2048]{1,0:T(8,128)(2,1)}, bf16[8192,896]{1,0:T(8,128)(2,1)}, bf16[8192,1792]{1,0:T(8,128)(2,1)}, ...) custom-call(s32[128]{0:T(128)} %add_convert_fusion.31.refs_0_, ...), custom_call_target="tpu_custom_call", output_to_operand_aliasing={{0}: (10, {}), {1}: (11, {}), {2}: (12, {}), {3}: (13, {})} | custom-call | flops 45097156608 | bytes 67108864 | tf_op jit(solution)/shard_map/ffn_chunk/pallas_call | solution.py:298
  785.7 39.7 %fusion.4 = f32[1024,1792]{1,0:T(8,128)} fusion(bf16[8192,1792]{1,0:T(8,128)(2,1)} %get-tuple-element.302, bf16[8192,2048]{1,0:T(8,128)(2,1)} %get-tuple-element.312), kind=kOutput, calls=%fused_computation.16 | convolution fusion | flops 30064771072 | bytes 53477376 | tf_op jit(solution)/shard_map/dot_general | solution.py:31
  825.4 5.6 collective-permute-done.53
  839.0 39.5 %fusion.2 = f32[1024,1792]{1,0:T(8,128)} fusion(bf16[8192,1792]{1,0:T(8,128)(2,1)} %get-tuple-element.302, bf16[8192,2048]{1,0:T(8,128)(2,1)} %get-tuple-element.312), kind=kOutput, calls=%fused_computation.14 | convolution fusion | flops 30064771072 | bytes 53477376 | tf_op jit(solution)/shard_map/dot_general | solution.py:31
  895.3 36.0 %fusion.129 = f32[896,2048]{1,0:T(8,128)} fusion(bf16[8192,896]{1,0:T(8,128)(2,1)S(1)} %bitcast.284, bf16[8192,2048]{1,0:T(8,128)(2,1)} %get-tuple-element.328), kind=kOutput, calls=%fused_computation.415 | convolution fusion | flops 30064771072 | bytes 55574528 | tf_op jit(solution)/shard_map/dot_general | solution.py:31
  946.4 14.4 %fusion.11 = f32[1,2048,1408]{2,1,0:T(8,128)} fusion(f32[1024,704]{1,0:T(8,128)S(1)} %get-tuple-element.442, f32[1024,704]{1,0:T(8,128)S(1)} %get-tuple-element.441, f32[1024,704]{1,0:T(8,128)S(1)} %get-tuple-element.440, f32[1024,704]{1,0:T(8,128)S(1)} %get-tuple-element.439), kind=kLoop, calls=%fused_computation.25 | loop fusion | flops 8650752 | bytes 23068672 | tf_op jit(solution)/shard_map/broadcast_in_dim | solution.py:923
  999.9 5.6 collective-permute-done.73
  1005.5 5.5 collective-permute-done.72
  1020.9 4.0 all-to-all-start.2
  1024.9 6.3 convolution_convert_fusion.1
  1031.2 9.1 fusion.15
  1040.4 19.7 %multiply_convert_fusion = bf16[4,1024,1024]{1,2,0:T(8,128)(2,1)} fusion(f32[4,1024,1024]{1,2,0:T(8,128)} %get-tuple-element.600, f32[4,1024]{1,0:T(4,128)S(1)} %copy-done.100, bf16[4,1024,256]{1,2,0:T(8,128)(2,1)} %bitcast.337, bf16[1024,1024]{1,0:T(8,128)(2,1)} %pad_maximum_fusion.11), kind=kOutput, calls=%fused_computation.10 | convolution fusion | flops 2176848896 | bytes 46170112 | tf_op jit(solution)/shard_map/sub | solution.py:808
  1060.4 6.1 convolution_bitcast_fusion
  1071.7 4.2 copy.225
  1075.9 5.7 convolution_bitcast_fusion.1
  1101.0 6.6 convolution_convert_fusion
  1107.7 3.9 pad_maximum_fusion.2
  1127.6 9.9 fusion.130
  1173.5 5.0 convolution_add_fusion
  1198.1 4.0 reshape.1051
  1210.5 10.8 collective-permute-done.86
  1221.6 4.9 collective-permute-start.88
  1239.0 5.2 fusion.35
  (757 shorter events, 441.0 us)
Async XLA Ops:
  29.3 46.5 %collective-permute-start.8 = (bf16[256,2048]{1,0:T(8,128)(2,1)S(1)}, bf16[256,2048]{1,0:T(8,128)(2,1)}, u32[]{:S(2)}, u32[]{:S(2)}) collective-permute-start(bf16[256,2048]{1,0:T(8,128)(2,1)S(1)} %copy-done.5), channel_id=1, source_target_pairs={{0,1},{1,0},{2,3},{3,2},{4,5},{5,4},{6,7},{7,6},{8,9},{9,8},{10,11... | collective-permute-start | bytes 3145736 | tf_op jit(solution)/shard_map/ppermute | solution.py:121
  30.1 53.5 %collective-permute-start.9 = (bf16[256,2048]{1,0:T(8,128)(2,1)S(1)}, bf16[256,2048]{1,0:T(8,128)(2,1)}, u32[]{:S(2)}, u32[]{:S(2)}) collective-permute-start(bf16[256,2048]{1,0:T(8,128)(2,1)S(1)} %copy-done.5), channel_id=1, source_target_pairs={{0,2},{1,3},{2,0},{3,1},{4,6},{5,7},{6,4},{7,5},{8,10},{9,11},{10,... | collective-permute-start | bytes 3145736 | tf_op jit(solution)/shard_map/ppermute | solution.py:121
  31.1 54.8 %collective-permute-start.10 = (bf16[256,2048]{1,0:T(8,128)(2,1)S(1)}, bf16[256,2048]{1,0:T(8,128)(2,1)}, u32[]{:S(2)}, u32[]{:S(2)}) collective-permute-start(bf16[256,2048]{1,0:T(8,128)(2,1)S(1)} %copy-done.5), channel_id=1, source_target_pairs={{0,3},{1,2},{2,1},{3,0},{4,7},{5,6},{6,5},{7,4},{8,11},{9,10},{10,... | collective-permute-start | bytes 3145736 | tf_op jit(solution)/shard_map/ppermute | solution.py:121
  47.3 24.2 %collective-permute-start.6 = (bf16[256,1024]{1,0:T(8,128)(2,1)}, bf16[256,1024]{1,0:T(8,128)(2,1)}, u32[]{:S(2)}, u32[]{:S(2)}) collective-permute-start(bf16[256,1024]{1,0:T(8,128)(2,1)} %collective-permute-done.4), channel_id=1, source_target_pairs={{0,8},{4,12},{8,16},{12,20},{16,24},{20,28},{24,0},{28,4},{1,9},{5... | collective-permute-start | bytes 1572872 | tf_op jit(solution)/shard_map/ppermute | solution.py:115
  47.4 24.2 %collective-permute-start.7 = (bf16[64,2688]{1,0:T(8,128)(2,1)}, bf16[64,2688]{1,0:T(8,128)(2,1)}, u32[]{:S(2)}, u32[]{:S(2)}) collective-permute-start(bf16[64,2688]{1,0:T(8,128)(2,1)} %collective-permute-done.5), channel_id=1, source_target_pairs={{0,8},{4,12},{8,16},{12,20},{16,24},{20,28},{24,0},{28,4},{1,9},{5... | collective-permute-start | bytes 1032200 | tf_op jit(solution)/shard_map/ppermute | solution.py:115
  54.2 50.3 %all-to-all-start = ((bf16[32,64,176]{2,1,0:T(8,128)(2,1)}), bf16[32,64,176]{2,1,0:T(8,128)(2,1)S(1)}, u32[]{:S(2)}, u32[]{:S(2)}) async-start(bf16[32,64,176]{2,1,0:T(8,128)(2,1)} %maximum_bitcast_fusion.1), calls=%async_computation | async-start | bytes 2097152 | tf_op jit(solution)/shard_map/all_to_all | solution.py:406
  59.2 341.0 %all-gather.3.cloned.1.call-start = ((), (), s32[]{:S(2)}) async-start(), calls=%async_computation.3 | async-start | bytes 34603008 | tf_op jit(solution)/shard_map/all_gather | solution.py:443
  72.8 27.2 %collective-permute-start.12 = (bf16[128,2688]{1,0:T(8,128)(2,1)S(1)}, bf16[128,2688]{1,0:T(8,128)(2,1)S(1)}, u32[]{:S(2)}, u32[]{:S(2)}) collective-permute-start(bf16[128,2688]{1,0:T(8,128)(2,1)S(1)} %bitcast.308), channel_id=1, source_target_pairs={{0,1},{1,0},{2,3},{3,2},{4,5},{5,4},{6,7},{7,6},{8,9},{9,8},{10,11... | collective-permute-start | bytes 2064392 | tf_op jit(solution)/shard_map/ppermute | solution.py:115
  74.9 26.3 %collective-permute-start.13 = (bf16[128,2688]{1,0:T(8,128)(2,1)S(1)}, bf16[128,2688]{1,0:T(8,128)(2,1)S(1)}, u32[]{:S(2)}, u32[]{:S(2)}) collective-permute-start(bf16[128,2688]{1,0:T(8,128)(2,1)S(1)} %bitcast.305), channel_id=1, source_target_pairs={{0,2},{1,3},{2,0},{3,1},{4,6},{5,7},{6,4},{7,5},{8,10},{9,11},{10,... | collective-permute-start | bytes 2064392 | tf_op jit(solution)/shard_map/ppermute | solution.py:115
  128.2 22.5 %collective-permute-start.18 = (bf16[1024,1024]{1,0:T(8,128)(2,1)}, bf16[1024,1024]{1,0:T(8,128)(2,1)}, u32[]{:S(2)}, u32[]{:S(2)}) collective-permute-start(bf16[1024,1024]{1,0:T(8,128)(2,1)} %get-tuple-element.557), channel_id=1, source_target_pairs={{0,4},{4,0},{8,12},{12,8},{16,20},{20,16},{24,28},{28,24},{1,5},{5... | collective-permute-start | bytes 6291464 | tf_op jit(solution)/shard_map/ppermute | solution.py:115
  134.2 33.4 %collective-permute-start.16 = (bf16[256,2048]{1,0:T(8,128)(2,1)S(1)}, bf16[256,2048]{1,0:T(8,128)(2,1)}, u32[]{:S(2)}, u32[]{:S(2)}) collective-permute-start(bf16[256,2048]{1,0:T(8,128)(2,1)S(1)} %fusion.48), channel_id=1, source_target_pairs={{0,2},{1,3},{2,0},{3,1},{4,6},{5,7},{6,4},{7,5},{8,10},{9,11},{10,... | collective-permute-start | bytes 3145736 | tf_op jit(solution)/shard_map/ppermute | solution.py:115
  134.9 32.6 %collective-permute-start.17 = (bf16[256,2048]{1,0:T(8,128)(2,1)S(1)}, bf16[256,2048]{1,0:T(8,128)(2,1)}, u32[]{:S(2)}, u32[]{:S(2)}) collective-permute-start(bf16[256,2048]{1,0:T(8,128)(2,1)S(1)} %fusion.47), channel_id=1, source_target_pairs={{0,1},{1,0},{2,3},{3,2},{4,5},{5,4},{6,7},{7,6},{8,9},{9,8},{10,11... | collective-permute-start | bytes 3145736 | tf_op jit(solution)/shard_map/ppermute | solution.py:115
  177.2 45.7 %collective-permute-start.23 = (bf16[1024,2048]{1,0:T(8,128)(2,1)}, bf16[1024,2048]{1,0:T(8,128)(2,1)}, u32[]{:S(2)}, u32[]{:S(2)}) collective-permute-start(bf16[1024,2048]{1,0:T(8,128)(2,1)} %pad_maximum_fusion.4), channel_id=1, source_target_pairs={{0,4},{4,0},{8,12},{12,8},{16,20},{20,16},{24,28},{28,24},{1,5},{5... | collective-permute-start | bytes 12582920 | tf_op jit(solution)/shard_map/ppermute | solution.py:115
  243.1 27.8 %collective-permute-start.26 = (bf16[128,2048]{1,0:T(8,128)(2,1)S(1)}, bf16[128,2048]{1,0:T(8,128)(2,1)}, u32[]{:S(2)}, u32[]{:S(2)}) collective-permute-start(bf16[128,2048]{1,0:T(8,128)(2,1)S(1)} %concatenate.352), channel_id=1, source_target_pairs={{0,8},{4,12},{8,16},{12,20},{16,24},{20,28},{24,0},{28,4},{1,9},{5... | collective-permute-start | bytes 1572872 | tf_op jit(solution)/shard_map/ppermute | solution.py:115
  247.4 42.2 %collective-permute-start.28 = (bf16[128,2048]{0,1:T(8,128)(2,1)}, bf16[128,2048]{0,1:T(8,128)(2,1)}, u32[]{:S(2)}, u32[]{:S(2)}) collective-permute-start(bf16[128,2048]{0,1:T(8,128)(2,1)} %bitcast.51), channel_id=1, source_target_pairs={{0,1},{1,0},{2,3},{3,2},{4,5},{5,4},{6,7},{7,6},{8,9},{9,8},{10,11... | collective-permute-start | bytes 1572872 | tf_op jit(solution)/shard_map/ppermute | solution.py:115
  249.4 40.2 %collective-permute-start.29 = (bf16[128,2048]{0,1:T(8,128)(2,1)}, bf16[128,2048]{0,1:T(8,128)(2,1)}, u32[]{:S(2)}, u32[]{:S(2)}) collective-permute-start(bf16[128,2048]{0,1:T(8,128)(2,1)} %bitcast.52), channel_id=1, source_target_pairs={{0,2},{1,3},{2,0},{3,1},{4,6},{5,7},{6,4},{7,5},{8,10},{9,11},{10,... | collective-permute-start | bytes 1572872 | tf_op jit(solution)/shard_map/ppermute | solution.py:115
  270.9 31.4 %collective-permute-start.27 = (bf16[128,2048]{1,0:T(8,128)(2,1)}, bf16[128,2048]{1,0:T(8,128)(2,1)}, u32[]{:S(2)}, u32[]{:S(2)}) collective-permute-start(bf16[128,2048]{1,0:T(8,128)(2,1)} %collective-permute-done.26), channel_id=1, source_target_pairs={{0,8},{4,12},{8,16},{12,20},{16,24},{20,28},{24,0},{28,4},{1,9},{5... | collective-permute-start | bytes 1572872 | tf_op jit(solution)/shard_map/ppermute | solution.py:115
  282.2 45.6 %all-to-all-start.1 = ((f32[32,1,256]{2,1,0:T(1,128)}), f32[32,1,256]{2,1,0:T(1,128)S(1)}, u32[]{:S(2)}, u32[]{:S(2)}) async-start(f32[32,1,256]{2,1,0:T(1,128)} %all_to_all.13), calls=%async_computation.1 | async-start | bytes 65536 | tf_op jit(solution)/shard_map/all_to_all | solution.py:524
  288.0 839.6 %all-gather.5.cloned.1.call-start = ((), (), s32[]{:S(2)}) async-start(), calls=%async_computation.4 | async-start | bytes 12976128 | tf_op jit(solution)/shard_map/all_gather | solution.py:639
  304.6 34.6 %collective-permute-start.31 = (bf16[256,2048]{0,1:T(8,128)(2,1)}, bf16[256,2048]{0,1:T(8,128)(2,1)}, u32[]{:S(2)}, u32[]{:S(2)}) collective-permute-start(bf16[256,2048]{0,1:T(8,128)(2,1)} %pad_maximum_fusion.24), channel_id=1, source_target_pairs={{0,2},{1,3},{2,0},{3,1},{4,6},{5,7},{6,4},{7,5},{8,10},{9,11},{10,... | collective-permute-start | bytes 3145736 | tf_op jit(solution)/shard_map/ppermute | solution.py:115
  308.4 30.9 %collective-permute-start.32 = (bf16[256,2048]{0,1:T(8,128)(2,1)}, bf16[256,2048]{0,1:T(8,128)(2,1)}, u32[]{:S(2)}, u32[]{:S(2)}) collective-permute-start(bf16[256,2048]{0,1:T(8,128)(2,1)} %pad_maximum_fusion.25), channel_id=1, source_target_pairs={{0,1},{1,0},{2,3},{3,2},{4,5},{5,4},{6,7},{7,6},{8,9},{9,8},{10,11... | collective-permute-start | bytes 3145736 | tf_op jit(solution)/shard_map/ppermute | solution.py:115
  312.1 27.1 %collective-permute-start.30 = (bf16[128,2048]{1,0:T(8,128)(2,1)}, bf16[128,2048]{1,0:T(8,128)(2,1)}, u32[]{:S(2)}, u32[]{:S(2)}) collective-permute-start(bf16[128,2048]{1,0:T(8,128)(2,1)} %collective-permute-done.27), channel_id=1, source_target_pairs={{0,8},{4,12},{8,16},{12,20},{16,24},{20,28},{24,0},{28,4},{1,9},{5... | collective-permute-start | bytes 1572872 | tf_op jit(solution)/shard_map/ppermute | solution.py:115
  341.6 22.3 %collective-permute-start.33 = (bf16[256,2048]{1,0:T(8,128)(2,1)S(1)}, bf16[256,2048]{1,0:T(8,128)(2,1)S(1)}, u32[]{:S(2)}, u32[]{:S(2)}) collective-permute-start(bf16[256,2048]{1,0:T(8,128)(2,1)S(1)} %pad_maximum_fusion.26), channel_id=1, source_target_pairs={{0,1},{1,0},{2,3},{3,2},{4,5},{5,4},{6,7},{7,6},{8,9},{9,8},{10,11... | collective-permute-start | bytes 3145736 | tf_op jit(solution)/shard_map/ppermute | solution.py:115
  341.9 22.1 %collective-permute-start.34 = (bf16[256,2048]{1,0:T(8,128)(2,1)S(1)}, bf16[256,2048]{1,0:T(8,128)(2,1)S(1)}, u32[]{:S(2)}, u32[]{:S(2)}) collective-permute-start(bf16[256,2048]{1,0:T(8,128)(2,1)S(1)} %pad_maximum_fusion.27), channel_id=1, source_target_pairs={{0,2},{1,3},{2,0},{3,1},{4,6},{5,7},{6,4},{7,5},{8,10},{9,11},{10,... | collective-permute-start | bytes 3145736 | tf_op jit(solution)/shard_map/ppermute | solution.py:115
  342.3 27.1 %collective-permute-start.35 = (bf16[256,2048]{1,0:T(8,128)(2,1)S(1)}, bf16[256,2048]{1,0:T(8,128)(2,1)}, u32[]{:S(2)}, u32[]{:S(2)}) collective-permute-start(bf16[256,2048]{1,0:T(8,128)(2,1)S(1)} %copy-done.11), channel_id=1, source_target_pairs={{0,8},{4,12},{8,16},{12,20},{16,24},{20,28},{24,0},{28,4},{1,9},{5... | collective-permute-start | bytes 3145736 | tf_op jit(solution)/shard_map/ppermute | solution.py:115
  372.5 27.7 %collective-permute-start.36 = (bf16[1024,2048]{1,0:T(8,128)(2,1)}, bf16[1024,2048]{1,0:T(8,128)(2,1)}, u32[]{:S(2)}, u32[]{:S(2)}) collective-permute-start(bf16[1024,2048]{1,0:T(8,128)(2,1)} %constant_dynamic-update-slice_fusion.25.refs_1_), channel_id=1, source_target_pairs={{0,4},{4,0},{8,12},{12,8},{16,20},{20,16},{24,28},{28,24},{1,5},{5... | collective-permute-start | bytes 12582920 | tf_op jit(solution)/shard_map/ppermute | solution.py:115
  372.5 27.7 %collective-permute-start.37 = (bf16[256,2048]{1,0:T(8,128)(2,1)}, bf16[256,2048]{1,0:T(8,128)(2,1)}, u32[]{:S(2)}, u32[]{:S(2)}) collective-permute-start(bf16[256,2048]{1,0:T(8,128)(2,1)} %collective-permute-done.35), channel_id=1, source_target_pairs={{0,8},{4,12},{8,16},{12,20},{16,24},{20,28},{24,0},{28,4},{1,9},{5... | collective-permute-start | bytes 3145736 | tf_op jit(solution)/shard_map/ppermute | solution.py:115
  378.7 55.1 %collective-permute-start.39 = (bf16[512,2048]{1,0:T(8,128)(2,1)}, bf16[512,2048]{1,0:T(8,128)(2,1)}, u32[]{:S(2)}, u32[]{:S(2)}) collective-permute-start(bf16[512,2048]{1,0:T(8,128)(2,1)} %pad_maximum_fusion.7), channel_id=1, source_target_pairs={{0,2},{1,3},{2,0},{3,1},{4,6},{5,7},{6,4},{7,5},{8,10},{9,11},{10,... | collective-permute-start | bytes 6291464 | tf_op jit(solution)/shard_map/ppermute | solution.py:115
  381.1 52.8 %collective-permute-start.40 = (bf16[512,2048]{1,0:T(8,128)(2,1)}, bf16[512,2048]{1,0:T(8,128)(2,1)}, u32[]{:S(2)}, u32[]{:S(2)}) collective-permute-start(bf16[512,2048]{1,0:T(8,128)(2,1)} %pad_maximum_fusion.8), channel_id=1, source_target_pairs={{0,1},{1,0},{2,3},{3,2},{4,5},{5,4},{6,7},{7,6},{8,9},{9,8},{10,11... | collective-permute-start | bytes 6291464 | tf_op jit(solution)/shard_map/ppermute | solution.py:115
  400.2 33.6 %collective-permute-start.38 = (bf16[256,2048]{1,0:T(8,128)(2,1)}, bf16[256,2048]{1,0:T(8,128)(2,1)S(1)}, u32[]{:S(2)}, u32[]{:S(2)}) collective-permute-start(bf16[256,2048]{1,0:T(8,128)(2,1)} %collective-permute-done.37), channel_id=1, source_target_pairs={{0,8},{4,12},{8,16},{12,20},{16,24},{20,28},{24,0},{28,4},{1,9},{5... | collective-permute-start | bytes 3145736 | tf_op jit(solution)/shard_map/ppermute | solution.py:115
  487.8 64.4 %collective-permute-start.48 = (bf16[1024,4096]{1,0:T(8,128)(2,1)}, bf16[1024,4096]{1,0:T(8,128)(2,1)}, u32[]{:S(2)}, u32[]{:S(2)}) collective-permute-start(bf16[1024,4096]{1,0:T(8,128)(2,1)} %get-tuple-element.247), channel_id=1, source_target_pairs={{0,4},{4,0},{8,12},{12,8},{16,20},{20,16},{24,28},{28,24},{1,5},{5... | collective-permute-start | bytes 25165832 | tf_op jit(solution)/shard_map/ppermute | solution.py:115
  490.6 48.0 %collective-permute-start.42 = (bf16[512,2048]{1,0:T(8,128)(2,1)}, bf16[512,2048]{1,0:T(8,128)(2,1)}, u32[]{:S(2)}, u32[]{:S(2)}) collective-permute-start(bf16[512,2048]{1,0:T(8,128)(2,1)} %pad_maximum_fusion.9), channel_id=1, source_target_pairs={{0,1},{1,0},{2,3},{3,2},{4,5},{5,4},{6,7},{7,6},{8,9},{9,8},{10,11... | collective-permute-start | bytes 6291464 | tf_op jit(solution)/shard_map/ppermute | solution.py:115
  496.1 47.6 %collective-permute-start.43 = (bf16[512,2048]{1,0:T(8,128)(2,1)S(1)}, bf16[512,2048]{1,0:T(8,128)(2,1)}, u32[]{:S(2)}, u32[]{:S(2)}) collective-permute-start(bf16[512,2048]{1,0:T(8,128)(2,1)S(1)} %pad_maximum_fusion.10), channel_id=1, source_target_pairs={{0,2},{1,3},{2,0},{3,1},{4,6},{5,7},{6,4},{7,5},{8,10},{9,11},{10,... | collective-permute-start | bytes 6291464 | tf_op jit(solution)/shard_map/ppermute | solution.py:115
  550.0 56.4 %collective-permute-start.45 = (bf16[2048,2048]{1,0:T(8,128)(2,1)}, bf16[2048,2048]{1,0:T(8,128)(2,1)}, u32[]{:S(2)}, u32[]{:S(2)}) collective-permute-start(bf16[2048,2048]{1,0:T(8,128)(2,1)} %constant_dynamic-update-slice_fusion.31.refs_1_), channel_id=1, source_target_pairs={{0,4},{4,0},{8,12},{12,8},{16,20},{20,16},{24,28},{28,24},{1,5},{5... | collective-permute-start | bytes 25165832 | tf_op jit(solution)/shard_map/ppermute | solution.py:115
  550.0 48.3 %collective-permute-start.46 = (bf16[512,2048]{1,0:T(8,128)(2,1)}, bf16[512,2048]{1,0:T(8,128)(2,1)S(1)}, u32[]{:S(2)}, u32[]{:S(2)}) collective-permute-start(bf16[512,2048]{1,0:T(8,128)(2,1)} %get-tuple-element.265), channel_id=1, source_target_pairs={{0,2},{1,3},{2,0},{3,1},{4,6},{5,7},{6,4},{7,5},{8,10},{9,11},{10,... | collective-permute-start | bytes 6291464 | tf_op jit(solution)/shard_map/ppermute | solution.py:115
  551.0 48.1 %collective-permute-start.47 = (bf16[512,2048]{1,0:T(8,128)(2,1)}, bf16[512,2048]{1,0:T(8,128)(2,1)}, u32[]{:S(2)}, u32[]{:S(2)}) collective-permute-start(bf16[512,2048]{1,0:T(8,128)(2,1)} %get-tuple-element.266), channel_id=1, source_target_pairs={{0,1},{1,0},{2,3},{3,2},{4,5},{5,4},{6,7},{7,6},{8,9},{9,8},{10,11... | collective-permute-start | bytes 6291464 | tf_op jit(solution)/shard_map/ppermute | solution.py:115
  666.2 52.1 %collective-permute-start.51 = (bf16[2048,4096]{1,0:T(8,128)(2,1)}, bf16[2048,4096]{1,0:T(8,128)(2,1)}, u32[]{:S(2)}, u32[]{:S(2)}) collective-permute-start(bf16[2048,4096]{1,0:T(8,128)(2,1)} %get-tuple-element.284), channel_id=1, source_target_pairs={{0,4},{4,0},{8,12},{12,8},{16,20},{20,16},{24,28},{28,24},{1,5},{5... | collective-permute-start | bytes 50331656 | tf_op jit(solution)/shard_map/ppermute | solution.py:115
  680.2 28.6 %collective-permute-start.49 = (bf16[256,2048]{1,0:T(8,128)(2,1)}, bf16[256,2048]{1,0:T(8,128)(2,1)S(1)}, u32[]{:S(2)}, u32[]{:S(2)}) collective-permute-start(bf16[256,2048]{1,0:T(8,128)(2,1)} %split.200), channel_id=1, source_target_pairs={{0,1},{1,0},{2,3},{3,2},{4,5},{5,4},{6,7},{7,6},{8,9},{9,8},{10,11... | collective-permute-start | bytes 3145736 | tf_op jit(solution)/shard_map/ppermute | solution.py:115
  682.5 28.4 %collective-permute-start.50 = (bf16[256,2048]{1,0:T(8,128)(2,1)}, bf16[256,2048]{1,0:T(8,128)(2,1)}, u32[]{:S(2)}, u32[]{:S(2)}) collective-permute-start(bf16[256,2048]{1,0:T(8,128)(2,1)} %split.201), channel_id=1, source_target_pairs={{0,2},{1,3},{2,0},{3,1},{4,6},{5,7},{6,4},{7,5},{8,10},{9,11},{10,... | collective-permute-start | bytes 3145736 | tf_op jit(solution)/shard_map/ppermute | solution.py:115
  714.4 69.3 %collective-permute-start.52 = (bf16[128,2048]{1,0:T(8,128)(2,1)S(1)}, bf16[128,2048]{1,0:T(8,128)(2,1)S(1)}, u32[]{:S(2)}, u32[]{:S(2)}) collective-permute-start(bf16[128,2048]{1,0:T(8,128)(2,1)S(1)} %pad_maximum_fusion.38), channel_id=1, source_target_pairs={{0,24},{4,28},{8,0},{12,4},{16,8},{20,12},{24,16},{28,20},{1,25},{... | collective-permute-start | bytes 1572872 | tf_op jit(solution)/shard_map/ppermute | solution.py:115
  783.8 47.2 %collective-permute-start.53 = (bf16[512,2048]{1,0:T(8,128)(2,1)}, bf16[512,2048]{1,0:T(8,128)(2,1)S(1)}, u32[]{:S(2)}, u32[]{:S(2)}) collective-permute-start(bf16[512,2048]{1,0:T(8,128)(2,1)} %get-tuple-element.299), channel_id=1, source_target_pairs={{0,1},{1,0},{2,3},{3,2},{4,5},{5,4},{6,7},{7,6},{8,9},{9,8},{10,11... | collective-permute-start | bytes 6291464 | tf_op jit(solution)/shard_map/ppermute | solution.py:115
  784.8 46.7 %collective-permute-start.54 = (bf16[512,2048]{1,0:T(8,128)(2,1)}, bf16[512,2048]{1,0:T(8,128)(2,1)S(1)}, u32[]{:S(2)}, u32[]{:S(2)}) collective-permute-start(bf16[512,2048]{1,0:T(8,128)(2,1)} %get-tuple-element.300), channel_id=1, source_target_pairs={{0,2},{1,3},{2,0},{3,1},{4,6},{5,7},{6,4},{7,5},{8,10},{9,11},{10,... | collective-permute-start | bytes 6291464 | tf_op jit(solution)/shard_map/ppermute | solution.py:115
  785.7 39.7 %collective-permute-start.55 = (bf16[128,2048]{1,0:T(8,128)(2,1)S(1)}, bf16[128,2048]{1,0:T(8,128)(2,1)S(1)}, u32[]{:S(2)}, u32[]{:S(2)}) collective-permute-start(bf16[128,2048]{1,0:T(8,128)(2,1)S(1)} %add_convert_fusion.21), channel_id=1, source_target_pairs={{0,24},{4,28},{8,0},{12,4},{16,8},{20,12},{24,16},{28,20},{1,25},{... | collective-permute-start | bytes 1572872 | tf_op jit(solution)/shard_map/ppermute | solution.py:115
  835.5 43.0 %collective-permute-start.56 = (bf16[128,2048]{1,0:T(8,128)(2,1)S(1)}, bf16[128,2048]{1,0:T(8,128)(2,1)S(1)}, u32[]{:S(2)}, u32[]{:S(2)}) collective-permute-start(bf16[128,2048]{1,0:T(8,128)(2,1)S(1)} %add_convert_fusion.20), channel_id=1, source_target_pairs={{0,24},{4,28},{8,0},{12,4},{16,8},{20,12},{24,16},{28,20},{1,25},{... | collective-permute-start | bytes 1572872 | tf_op jit(solution)/shard_map/ppermute | solution.py:115
  835.6 42.9 %collective-permute-start.57 = (bf16[256,2048]{1,0:T(8,128)(2,1)S(1)}, bf16[256,2048]{1,0:T(8,128)(2,1)S(1)}, u32[]{:S(2)}, u32[]{:S(2)}) collective-permute-start(bf16[256,2048]{1,0:T(8,128)(2,1)S(1)} %pad_maximum_fusion.31), channel_id=1, source_target_pairs={{0,24},{4,28},{8,0},{12,4},{16,8},{20,12},{24,16},{28,20},{1,25},{... | collective-permute-start | bytes 3145736 | tf_op jit(solution)/shard_map/ppermute | solution.py:115
  836.8 45.6 %collective-permute-start.58 = (bf16[512,2048]{1,0:T(8,128)(2,1)S(1)}, bf16[512,2048]{1,0:T(8,128)(2,1)S(1)}, u32[]{:S(2)}, u32[]{:S(2)}) collective-permute-start(bf16[512,2048]{1,0:T(8,128)(2,1)S(1)} %copy-done.117), channel_id=1, source_target_pairs={{0,2},{1,3},{2,0},{3,1},{4,6},{5,7},{6,4},{7,5},{8,10},{9,11},{10,... | collective-permute-start | bytes 6291464 | tf_op jit(solution)/shard_map/ppermute | solution.py:115
  837.7 45.3 %collective-permute-start.59 = (bf16[512,2048]{1,0:T(8,128)(2,1)S(1)}, bf16[512,2048]{1,0:T(8,128)(2,1)S(1)}, u32[]{:S(2)}, u32[]{:S(2)}) collective-permute-start(bf16[512,2048]{1,0:T(8,128)(2,1)S(1)} %copy-done.116), channel_id=1, source_target_pairs={{0,1},{1,0},{2,3},{3,2},{4,5},{5,4},{6,7},{7,6},{8,9},{9,8},{10,11... | collective-permute-start | bytes 6291464 | tf_op jit(solution)/shard_map/ppermute | solution.py:115
  887.8 81.0 %collective-permute-start.60 = (bf16[768,2048]{1,0:T(8,128)(2,1)}, bf16[768,2048]{1,0:T(8,128)(2,1)}, u32[]{:S(2)}, u32[]{:S(2)}) collective-permute-start(bf16[768,2048]{1,0:T(8,128)(2,1)} %pad_maximum_fusion.5), channel_id=1, source_target_pairs={{0,1},{1,0},{2,3},{3,2},{4,5},{5,4},{6,7},{7,6},{8,9},{9,8},{10,11... | collective-permute-start | bytes 9437192 | tf_op jit(solution)/shard_map/ppermute | solution.py:115
  893.9 75.0 %collective-permute-start.61 = (bf16[768,2048]{1,0:T(8,128)(2,1)}, bf16[768,2048]{1,0:T(8,128)(2,1)}, u32[]{:S(2)}, u32[]{:S(2)}) collective-permute-start(bf16[768,2048]{1,0:T(8,128)(2,1)} %pad_maximum_fusion.6), channel_id=1, source_target_pairs={{0,2},{1,3},{2,0},{3,1},{4,6},{5,7},{6,4},{7,5},{8,10},{9,11},{10,... | collective-permute-start | bytes 9437192 | tf_op jit(solution)/shard_map/ppermute | solution.py:115
  895.0 36.3 %collective-permute-start.62 = (bf16[256,2048]{1,0:T(8,128)(2,1)S(1)}, bf16[256,2048]{1,0:T(8,128)(2,1)}, u32[]{:S(2)}, u32[]{:S(2)}) collective-permute-start(bf16[256,2048]{1,0:T(8,128)(2,1)S(1)} %add_convert_fusion.16), channel_id=1, source_target_pairs={{0,24},{4,28},{8,0},{12,4},{16,8},{20,12},{24,16},{28,20},{1,25},{... | collective-permute-start | bytes 3145736 | tf_op jit(solution)/shard_map/ppermute | solution.py:115
  933.1 27.8 %collective-permute-start.63 = (bf16[256,2048]{1,0:T(8,128)(2,1)S(1)}, bf16[256,2048]{1,0:T(8,128)(2,1)S(1)}, u32[]{:S(2)}, u32[]{:S(2)}) collective-permute-start(bf16[256,2048]{1,0:T(8,128)(2,1)S(1)} %add_convert_fusion.15), channel_id=1, source_target_pairs={{0,24},{4,28},{8,0},{12,4},{16,8},{20,12},{24,16},{28,20},{1,25},{... | collective-permute-start | bytes 3145736 | tf_op jit(solution)/shard_map/ppermute | solution.py:115
  983.7 31.7 %collective-permute-start.66 = (bf16[384,2048]{1,0:T(8,128)(2,1)}, bf16[384,2048]{1,0:T(8,128)(2,1)}, u32[]{:S(2)}, u32[]{:S(2)}) collective-permute-start(bf16[384,2048]{1,0:T(8,128)(2,1)} %pad_maximum_fusion.14), channel_id=1, source_target_pairs={{0,24},{4,28},{8,0},{12,4},{16,8},{20,12},{24,16},{28,20},{1,25},{... | collective-permute-start | bytes 4718600 | tf_op jit(solution)/shard_map/ppermute | solution.py:115
  1018.6 41.9 %collective-permute-start.67 = (bf16[384,2048]{1,0:T(8,128)(2,1)}, bf16[384,2048]{1,0:T(8,128)(2,1)}, u32[]{:S(2)}, u32[]{:S(2)}) collective-permute-start(bf16[384,2048]{1,0:T(8,128)(2,1)} %add_convert_fusion.10), channel_id=1, source_target_pairs={{0,24},{4,28},{8,0},{12,4},{16,8},{20,12},{24,16},{28,20},{1,25},{... | collective-permute-start | bytes 4718600 | tf_op jit(solution)/shard_map/ppermute | solution.py:115
  1020.9 116.6 %all-to-all-start.2 = ((f32[32,64,176]{2,1,0:T(8,128)}), f32[32,64,176]{2,1,0:T(8,128)}, u32[]{:S(2)}, u32[]{:S(2)}) async-start(f32[32,64,176]{2,1,0:T(8,128)} %bitcast.300), calls=%async_computation.2 | async-start | bytes 4194304 | tf_op jit(solution)/shard_map/all_to_all | solution.py:781
  1084.4 32.8 %collective-permute-start.74 = (bf16[256,768]{0,1:T(8,128)(2,1)}, bf16[256,768]{0,1:T(8,128)(2,1)}, u32[]{:S(2)}, u32[]{:S(2)}) collective-permute-start(bf16[256,768]{0,1:T(8,128)(2,1)} %bitcast.71), channel_id=1, source_target_pairs={{0,1},{1,0},{2,3},{3,2},{4,5},{5,4},{6,7},{7,6},{8,9},{9,8},{10,11... | collective-permute-start | bytes 1179656 | tf_op jit(solution)/shard_map/ppermute | solution.py:121
  1085.9 31.2 %collective-permute-start.75 = (bf16[256,768]{0,1:T(8,128)(2,1)}, bf16[256,768]{0,1:T(8,128)(2,1)}, u32[]{:S(2)}, u32[]{:S(2)}) collective-permute-start(bf16[256,768]{0,1:T(8,128)(2,1)} %bitcast.72), channel_id=1, source_target_pairs={{0,2},{1,3},{2,0},{3,1},{4,6},{5,7},{6,4},{7,5},{8,10},{9,11},{10,... | collective-permute-start | bytes 1179656 | tf_op jit(solution)/shard_map/ppermute | solution.py:121
  1087.4 29.7 %collective-permute-start.76 = (bf16[256,768]{0,1:T(8,128)(2,1)}, bf16[256,768]{0,1:T(8,128)(2,1)}, u32[]{:S(2)}, u32[]{:S(2)}) collective-permute-start(bf16[256,768]{0,1:T(8,128)(2,1)} %bitcast.73), channel_id=1, source_target_pairs={{0,3},{1,2},{2,1},{3,0},{4,7},{5,6},{6,5},{7,4},{8,11},{9,10},{10,... | collective-permute-start | bytes 1179656 | tf_op jit(solution)/shard_map/ppermute | solution.py:121
  1091.1 62.0 %collective-permute-start.68 = (bf16[384,2048]{1,0:T(8,128)(2,1)}, bf16[384,2048]{1,0:T(8,128)(2,1)}, u32[]{:S(2)}, u32[]{:S(2)}) collective-permute-start(bf16[384,2048]{1,0:T(8,128)(2,1)} %add_convert_fusion.9), channel_id=1, source_target_pairs={{0,24},{4,28},{8,0},{12,4},{16,8},{20,12},{24,16},{28,20},{1,25},{... | collective-permute-start | bytes 4718600 | tf_op jit(solution)/shard_map/ppermute | solution.py:115
  1115.7 43.2 %collective-permute-start.80 = (bf16[4,256,1536]{2,1,0:T(8,128)(2,1)}, bf16[4,256,1536]{2,1,0:T(8,128)(2,1)}, u32[]{:S(2)}, u32[]{:S(2)}) collective-permute-start(bf16[4,256,1536]{2,1,0:T(8,128)(2,1)} %dynamic-slice_bitcast_fusion), channel_id=1, source_target_pairs={{0,4},{4,0},{8,12},{12,8},{16,20},{20,16},{24,28},{28,24},{1,5},{5... | collective-permute-start | bytes 9437192 | tf_op jit(solution)/shard_map/ppermute | solution.py:115
  1124.1 34.8 %collective-permute-start.77 = (bf16[256,576]{0,1:T(8,128)(2,1)}, bf16[256,576]{0,1:T(8,128)(2,1)}, u32[]{:S(2)}, u32[]{:S(2)}) collective-permute-start(bf16[256,576]{0,1:T(8,128)(2,1)} %get-tuple-element.487), channel_id=1, source_target_pairs={{0,1},{1,0},{2,3},{3,2},{4,5},{5,4},{6,7},{7,6},{8,9},{9,8},{10,11... | collective-permute-start | bytes 884744 | tf_op jit(solution)/shard_map/ppermute | solution.py:121
  1125.6 33.3 %collective-permute-start.78 = (bf16[256,576]{0,1:T(8,128)(2,1)}, bf16[256,576]{0,1:T(8,128)(2,1)}, u32[]{:S(2)}, u32[]{:S(2)}) collective-permute-start(bf16[256,576]{0,1:T(8,128)(2,1)} %get-tuple-element.486), channel_id=1, source_target_pairs={{0,2},{1,3},{2,0},{3,1},{4,6},{5,7},{6,4},{7,5},{8,10},{9,11},{10,... | collective-permute-start | bytes 884744 | tf_op jit(solution)/shard_map/ppermute | solution.py:121
  1127.1 31.8 %collective-permute-start.79 = (bf16[256,576]{0,1:T(8,128)(2,1)}, bf16[256,576]{0,1:T(8,128)(2,1)}, u32[]{:S(2)}, u32[]{:S(2)}) collective-permute-start(bf16[256,576]{0,1:T(8,128)(2,1)} %get-tuple-element.485), channel_id=1, source_target_pairs={{0,3},{1,2},{2,1},{3,0},{4,7},{5,6},{6,5},{7,4},{8,11},{9,10},{10,... | collective-permute-start | bytes 884744 | tf_op jit(solution)/shard_map/ppermute | solution.py:121
  1157.4 50.5 %collective-permute-start.69 = (bf16[64,2048]{1,0:T(8,128)(2,1)}, bf16[64,2048]{1,0:T(8,128)(2,1)}, u32[]{:S(2)}, u32[]{:S(2)}) collective-permute-start(bf16[64,2048]{1,0:T(8,128)(2,1)} %get-tuple-element.481), channel_id=1, source_target_pairs={{0,2},{1,3},{2,0},{3,1},{4,6},{5,7},{6,4},{7,5},{8,10},{9,11},{10,... | collective-permute-start | bytes 786440 | tf_op jit(solution)/shard_map/ppermute | solution.py:115
  1178.5 29.4 %collective-permute-start.70 = (bf16[64,2048]{1,0:T(8,128)(2,1)}, bf16[64,2048]{1,0:T(8,128)(2,1)}, u32[]{:S(2)}, u32[]{:S(2)}) collective-permute-start(bf16[64,2048]{1,0:T(8,128)(2,1)} %get-tuple-element.482), channel_id=1, source_target_pairs={{0,1},{1,0},{2,3},{3,2},{4,5},{5,4},{6,7},{7,6},{8,9},{9,8},{10,11... | collective-permute-start | bytes 786440 | tf_op jit(solution)/shard_map/ppermute | solution.py:115
  (170 other events, 2036.1 us)
Sparse Core Ops, SparseCore 0:
  112.4 233.4 all-gather.2
  689.3 107.7 all-gather.4

commit v4 on v3

--- a/solution.py
+++ b/solution.py
@@ -638,12 +638,10 @@
     a_far = [links.shift(far[0], "x", -1), links.shift(far[1], "y", -1)]
     query_w_all = lax.all_gather(after(w_query, sib_b), BOTH, axis=0, tiled=True)
     kept = ffn(sib_b, "b", 1)
-    a_far = tie(*a_far, done["b", 1][0])[:2]
+    kept = ffn(rows_b, "b", 0)
+    a_far = tie(*a_far, done["b", 0][0])[:2]
     a_parts = z_parts(add_far(a_far, a_near))
-    rows_b, *a_parts = tie(rows_b, *a_parts)
     a_sum = links.shift(a_parts[-1], "z", -1)
-    kept = ffn(rows_b, "b", 0)
-    a_sum = after(a_sum, done["b", 0][0])
     done["bn", 0], done["bf", 0] = done["b", 0][:4], done["b", 0][4:]
     far = done["bf", 0][1::2]
     b_far = [links.shift(far[0], "x", -1), links.shift(far[1], "y", -1)]
@@ -670,26 +668,25 @@
             b_sum = plus(links.shift(b_sum, "z", -1), part)
     else:
         x_all, g_kept, act_all, grad_pre_all = kept
+        grad_w_top = matmul_left_t(x_all[:, : D // 2], grad_pre_all)
+        *b_far, a_sum, _ = tie(*b_far, a_sum, grad_w_top)
+        b_parts = z_parts(add_far(b_far, done["bn", 0][1::2]))
         a_sum = plus(a_sum, a_parts[-2])
-        x_all, a_sum = tie(x_all, a_sum)
-        a_next = links.shift(a_sum, "z", -1)
-        grad_w_top = matmul_left_t(x_all[:, : D // 2], grad_pre_all)
-        *b_far, a_next, _ = tie(*b_far, a_next, grad_w_top)
-        b_parts = z_parts(add_far(b_far, done["bn", 0][1::2]))
-        a_sum = plus(a_next, a_parts[-3])
         x_all, a_sum, out_far[0], out_far[1], *b_parts = tie(x_all, a_sum, *out_far, *b_parts)
         out_far = [links.shift(p, axis, -1) for p, axis in zip(out_far, "yx")]
         a_next = links.shift(a_sum, "z", -1)
         b_next = links.shift(b_parts[-1], "z", -1)
         grad_w_end = matmul_left_t(x_all[:, D // 2 :], grad_pre_all)
         a_next, b_next, _ = tie(a_next, b_next, grad_w_end)
-        a_sum = plus(a_next, a_parts[-4])
+        a_sum = plus(a_next, a_parts[-3])
         b_sum = plus(b_next, b_parts[-2])
         act_all, a_sum, b_sum, *out_all = tie(act_all, a_sum, b_sum, *out_far, *out_far_b)
         out_near, out_sent = send_outputs(out_all[:2], out_all[2:])
         b_next = links.shift(b_sum, "z", -1)
+        a_next = links.shift(a_sum, "z", -1)
         grad_w_back = matmul_left_t(act_all, g_kept)
-        b_next, _ = tie(b_next, grad_w_back)
+        a_next, b_next, _ = tie(a_next, b_next, grad_w_back)
+        a_sum = plus(a_next, a_parts[-4])
         b_sum = plus(b_next, b_parts[-3])
         for part in b_parts[-4:0:-1]:
             b_sum = plus(links.shift(b_sum, "z", -1), part)

time: 1290 us -> 1280 us (level)
    ppermute x70, waiting for transfers between devices: 216 us -> 203 us  [shift(): return lax.ppermute(value, name, pairs)]
    unnamed x301 -> x305, local copies, waits for them, and re-layouts: 64.4 us -> 59.2 us
    concatenate x30 -> x27, other arithmetic: 31.7 us -> 30.9 us  [joined_rows(): return parts[0] if len(parts) == 1 else jnp.concatenate(parts, axis=0)]
  transfers between devices with their start and end apart: 102 -> 102, of which waited for: 47 -> 44; matrix products, arithmetic and copies ran while one was open for 45% -> 45% of each run, Pallas kernels for 14% -> 14%
where the time goes in v4:
time: 1280 us; the launch traced here: 1260 us
  Pallas kernels  266 us (21%)
  waiting for transfers between devices  246 us (19%)
  local copies, waits for them, and re-layouts  222 us (17%)
  matrix products  222 us (17%)
  other arithmetic  155 us (12%)
  starting transfers between devices  129 us (10%)
  between operations  16.9 us (1%)
    pallas_call x6, Pallas kernels, ffn_chunk(): pl.pallas_call(lambda *refs: ffn_kernel(half_ff, 0 if moved is None else...  266 us
    ppermute x70, waiting for transfers between devices, shift(): return lax.ppermute(value, name, pairs)  203 us
    dot_general x7, matrix products, matmul_left_t(): lax.dot_general(left, right, (((0,), (0,)), ((), ())), preferred_element_...  132 us
    ppermute x70, starting transfers between devices, shift(): return lax.ppermute(value, name, pairs)  82.7 us
    unnamed x305, local copies, waits for them, and re-layouts  59.2 us
    convert_element_type x28, other arithmetic, plus(): return (left.astype(f32) + right.astype(f32)).astype(bf16)  47.6 us
    ppermute x27, waiting for transfers between devices, shift_ctx(): return lax.ppermute(value, 'ctx', pairs)  42.9 us
    ppermute x27, starting transfers between devices, shift_ctx(): return lax.ppermute(value, 'ctx', pairs)  32 us
  transfers between devices with their start and end apart: 102, of which 44 were waited for; matrix products, arithmetic and copies ran while one was open for 45% of the time, Pallas kernels for 14%

profile of v4, /device:TPU:0, one launch (start us, length us, event | category | flops | bytes accessed | tf_op | source)
XLA Modules:
  0.0 1256.6 jit_solution(7328110051711293252)
XLA Ops:
  21.7 4.3 collective-permute-done.2
  32.8 14.5 %collective-permute-done.5 = bf16[64,2688]{1,0:T(8,128)(2,1)} collective-permute-done((bf16[64,2688]{1,0:T(8,128)(2,1)S(1)}, bf16[64,2688]{1,0:T(8,128)(2,1)}, u32[]{:S(2)}, u32[]{:S(2)}) %collective-permute-start.5) | collective-permute-done | bytes 344096 | tf_op jit(solution)/shard_map/ppermute | solution.py:115
  54.2 5.0 all-to-all-start
  59.3 12.2 collective-permute-done.7
  75.7 7.9 collective-permute-done.9
  86.7 10.5 collective-permute-done.11
  104.5 5.8 collective-permute-done.14
  130.0 3.9 pad_maximum_fusion.3
  143.1 4.1 gather_fusion.1
  153.8 4.9 gather_fusion
  168.9 4.3 fusion.93
  173.3 3.8 pad_maximum_fusion.4
  179.1 7.8 fusion.128
  187.0 8.2 fusion.8
  195.2 7.6 fusion.45
  213.1 8.6 collective-permute-done.21
  222.8 4.8 constant_dynamic-update-slice_fusion.20
  227.6 9.1 gather_fusion.4
  236.7 6.0 multiply_reduce_fusion.1
  249.5 9.5 collective-permute-done.24
  261.0 9.8 collective-permute-done.26
  270.8 7.2 collective-permute-start.27
  282.2 5.8 all-to-all-start.1
  289.7 12.6 %collective-permute-done.27 = bf16[128,2048]{1,0:T(8,128)(2,1)} collective-permute-done((bf16[128,2048]{1,0:T(8,128)(2,1)}, bf16[128,2048]{1,0:T(8,128)(2,1)}, u32[]{:S(2)}, u32[]{:S(2)}) %collective-permute-start.27) | collective-permute-done | bytes 524320 | tf_op jit(solution)/shard_map/ppermute | solution.py:115
  315.9 12.0 concatenate.299.refs_7_
  330.0 9.4 collective-permute-done.30
  345.3 18.8 %collective-permute-done.33 = bf16[256,2048]{1,0:T(8,128)(2,1)S(1)} collective-permute-done((bf16[256,2048]{1,0:T(8,128)(2,1)S(1)}, bf16[256,2048]{1,0:T(8,128)(2,1)S(1)}, u32[]{:S(2)}, u32[]{:S(2)}) %collective-permute-start.33) | collective-permute-done | bytes 1048608 | tf_op jit(solution)/shard_map/ppermute | solution.py:115
  364.3 5.2 collective-permute-done.35
  381.8 18.5 %collective-permute-done.37 = bf16[256,2048]{1,0:T(8,128)(2,1)} collective-permute-done((bf16[256,2048]{1,0:T(8,128)(2,1)}, bf16[256,2048]{1,0:T(8,128)(2,1)}, u32[]{:S(2)}, u32[]{:S(2)}) %collective-permute-start.37) | collective-permute-done | bytes 1048608 | tf_op jit(solution)/shard_map/ppermute | solution.py:115
  400.4 33.6 %ffn_chunk.6 = (bf16[8192,2048]{1,0:T(8,128)(2,1)}, bf16[8192,2048]{1,0:T(8,128)(2,1)}, bf16[8192,896]{1,0:T(8,128)(2,1)}, bf16[8192,1792]{1,0:T(8,128)(2,1)}, bf16[1024,4096]{1,0:T(8,128)(2,1)}) custom-call(s32[128]{0:T(128)} %add_convert_fusion.31.refs_0_, bf16[1024,2048]{1,0:T(8,128)(2,1)} %collective-permute-done.36.refs_1_, ...), custom_call_target="tpu_custom_call" | custom-call | flops 22548578304 | bytes 33554432 | tf_op jit(solution)/shard_map/ffn_chunk/pallas_call | solution.py:298
  439.4 7.2 collective-permute-done.41.refs_1_
  448.6 33.8 %ffn_chunk.7 = (bf16[8192,2048]{1,0:T(8,128)(2,1)}, bf16[8192,2048]{1,0:T(8,128)(2,1)}, bf16[8192,896]{1,0:T(8,128)(2,1)}, bf16[8192,1792]{1,0:T(8,128)(2,1)}, bf16[1024,4096]{1,0:T(8,128)(2,1)}) custom-call(s32[128]{0:T(128)} %add_convert_fusion.31.refs_0_, ...), custom_call_target="tpu_custom_call", output_to_operand_aliasing={{0}: (9, {}), {1}: (10, {}), {2}: (11, {}), {3}: (12, {})} | custom-call | flops 22548578304 | bytes 33554432 | tf_op jit(solution)/shard_map/ffn_chunk/pallas_call | solution.py:298
  497.9 36.4 %ffn_chunk.8 = (bf16[8192,2048]{1,0:T(8,128)(2,1)}, bf16[8192,2048]{1,0:T(8,128)(2,1)}, bf16[8192,896]{1,0:T(8,128)(2,1)}, bf16[8192,1792]{1,0:T(8,128)(2,1)}, b...) custom-call(s32[128]{0:T(128)} %add_convert_fusion.31.refs_0_, ...), custom_call_target="tpu_custom_call", output_to_operand_aliasing={{0}: (10, {}), {1}: (11, {}), {2}: (12, {}), {3}: (13, {})} | custom-call | flops 22548578304 | bytes 33554432 | tf_op jit(solution)/shard_map/ffn_chunk/pallas_call | solution.py:298
  534.4 4.5 collective-permute-done.42
  538.9 5.1 collective-permute-done.43
  552.2 36.8 %ffn_chunk.9 = (bf16[8192,2048]{1,0:T(8,128)(2,1)}, bf16[8192,2048]{1,0:T(8,128)(2,1)}, bf16[8192,896]{1,0:T(8,128)(2,1)}, bf16[8192,1792]{1,0:T(8,128)(2,1)}, b...) custom-call(s32[128]{0:T(128)} %add_convert_fusion.31.refs_0_, ...), custom_call_target="tpu_custom_call", output_to_operand_aliasing={{0}: (10, {}), {1}: (11, {}), {2}: (12, {}), {3}: (13, {})} | custom-call | flops 22548578304 | bytes 33554432 | tf_op jit(solution)/shard_map/ffn_chunk/pallas_call | solution.py:298
  589.0 9.5 collective-permute-done.46
  606.7 59.8 %ffn_chunk.10 = (bf16[8192,2048]{1,0:T(8,128)(2,1)}, bf16[8192,2048]{1,0:T(8,128)(2,1)}, bf16[8192,896]{1,0:T(8,128)(2,1)}, bf16[8192,1792]{1,0:T(8,128)(2,1)}, bf16[2048,4096]{1,0:T(8,128)(2,1)}) custom-call(s32[128]{0:T(128)} %add_convert_fusion.31.refs_0_, ...), custom_call_target="tpu_custom_call", output_to_operand_aliasing={{0}: (9, {}), {1}: (10, {}), {2}: (11, {}), {3}: (12, {})} | custom-call | flops 45097156608 | bytes 67108864 | tf_op jit(solution)/shard_map/ffn_chunk/pallas_call | solution.py:298
  683.8 8.2 collective-permute-done.49.refs_9_
  692.0 65.4 %ffn_chunk.11 = (bf16[8192,2048]{1,0:T(8,128)(2,1)}, bf16[8192,2048]{1,0:T(8,128)(2,1)}, bf16[8192,896]{1,0:T(8,128)(2,1)}, bf16[8192,1792]{1,0:T(8,128)(2,1)}, ...) custom-call(s32[128]{0:T(128)} %add_convert_fusion.31.refs_0_, ...), custom_call_target="tpu_custom_call", output_to_operand_aliasing={{0}: (10, {}), {1}: (11, {}), {2}: (12, {}), {3}: (13, {})} | custom-call | flops 45097156608 | bytes 67108864 | tf_op jit(solution)/shard_map/ffn_chunk/pallas_call | solution.py:298
  763.0 4.0 collective-permute-start.54
  766.9 39.6 %fusion.4 = f32[1024,1792]{1,0:T(8,128)} fusion(bf16[8192,1792]{1,0:T(8,128)(2,1)} %get-tuple-element.289, bf16[8192,2048]{1,0:T(8,128)(2,1)} %get-tuple-element.298), kind=kOutput, calls=%fused_computation.16 | convolution fusion | flops 30064771072 | bytes 53477376 | tf_op jit(solution)/shard_map/dot_general | solution.py:31
  806.5 4.1 collective-permute-done.50
  820.6 39.2 %fusion.2 = f32[1024,1792]{1,0:T(8,128)} fusion(bf16[8192,1792]{1,0:T(8,128)(2,1)} %get-tuple-element.289, bf16[8192,2048]{1,0:T(8,128)(2,1)} %get-tuple-element.298), kind=kOutput, calls=%fused_computation.14 | convolution fusion | flops 30064771072 | bytes 53477376 | tf_op jit(solution)/shard_map/dot_general | solution.py:31
  861.1 4.2 collective-permute-done.57
  880.0 36.0 %fusion.129 = f32[896,2048]{1,0:T(8,128)} fusion(bf16[8192,896]{1,0:T(8,128)(2,1)S(1)} %bitcast.284, bf16[8192,2048]{1,0:T(8,128)(2,1)} %get-tuple-element.314), kind=kOutput, calls=%fused_computation.412 | convolution fusion | flops 30064771072 | bytes 55574528 | tf_op jit(solution)/shard_map/dot_general | solution.py:31
  930.8 14.5 %fusion.11 = f32[1,2048,1408]{2,1,0:T(8,128)} fusion(f32[1024,704]{1,0:T(8,128)S(1)} %get-tuple-element.428, f32[1024,704]{1,0:T(8,128)S(1)} %get-tuple-element.427, f32[1024,704]{1,0:T(8,128)S(1)} %get-tuple-element.426, f32[1024,704]{1,0:T(8,128)S(1)} %get-tuple-element.425), kind=kLoop, calls=%fused_computation.25 | loop fusion | flops 8650752 | bytes 23068672 | tf_op jit(solution)/shard_map/broadcast_in_dim | solution.py:920
  985.2 6.3 collective-permute-done.73
  991.5 6.2 collective-permute-done.72
  1011.3 6.3 convolution_convert_fusion.1
  1017.6 9.1 fusion.15
  1026.8 19.8 %multiply_convert_fusion = bf16[4,1024,1024]{1,2,0:T(8,128)(2,1)} fusion(f32[4,1024,1024]{1,2,0:T(8,128)} %get-tuple-element.586, f32[4,1024]{1,0:T(4,128)S(1)} %copy-done.100, bf16[4,1024,256]{1,2,0:T(8,128)(2,1)} %bitcast.339, bf16[1024,1024]{1,0:T(8,128)(2,1)} %pad_maximum_fusion.11), kind=kOutput, calls=%fused_computation.10 | convolution fusion | flops 2176848896 | bytes 46170112 | tf_op jit(solution)/shard_map/sub | solution.py:805
  1046.6 6.1 convolution_bitcast_fusion
  1057.9 4.2 copy.225
  1062.2 5.7 convolution_bitcast_fusion.1
  1077.4 3.7 collective-permute-start.68
  1087.5 6.6 convolution_convert_fusion
  1094.2 4.1 pad_maximum_fusion.2
  1114.3 9.9 fusion.130
  1159.9 5.0 convolution_add_fusion
  1184.6 4.0 reshape.1051
  1197.0 10.8 collective-permute-done.86
  1208.1 4.8 collective-permute-start.88
  1225.5 5.2 fusion.35
  (759 shorter events, 437.7 us)
Async XLA Ops:
  29.3 46.5 %collective-permute-start.8 = (bf16[256,2048]{1,0:T(8,128)(2,1)S(1)}, bf16[256,2048]{1,0:T(8,128)(2,1)}, u32[]{:S(2)}, u32[]{:S(2)}) collective-permute-start(bf16[256,2048]{1,0:T(8,128)(2,1)S(1)} %copy-done.5), channel_id=1, source_target_pairs={{0,1},{1,0},{2,3},{3,2},{4,5},{5,4},{6,7},{7,6},{8,9},{9,8},{10,11... | collective-permute-start | bytes 3145736 | tf_op jit(solution)/shard_map/ppermute | solution.py:121
  30.1 53.5 %collective-permute-start.9 = (bf16[256,2048]{1,0:T(8,128)(2,1)S(1)}, bf16[256,2048]{1,0:T(8,128)(2,1)}, u32[]{:S(2)}, u32[]{:S(2)}) collective-permute-start(bf16[256,2048]{1,0:T(8,128)(2,1)S(1)} %copy-done.5), channel_id=1, source_target_pairs={{0,2},{1,3},{2,0},{3,1},{4,6},{5,7},{6,4},{7,5},{8,10},{9,11},{10,... | collective-permute-start | bytes 3145736 | tf_op jit(solution)/shard_map/ppermute | solution.py:121
  31.1 54.8 %collective-permute-start.10 = (bf16[256,2048]{1,0:T(8,128)(2,1)S(1)}, bf16[256,2048]{1,0:T(8,128)(2,1)}, u32[]{:S(2)}, u32[]{:S(2)}) collective-permute-start(bf16[256,2048]{1,0:T(8,128)(2,1)S(1)} %copy-done.5), channel_id=1, source_target_pairs={{0,3},{1,2},{2,1},{3,0},{4,7},{5,6},{6,5},{7,4},{8,11},{9,10},{10,... | collective-permute-start | bytes 3145736 | tf_op jit(solution)/shard_map/ppermute | solution.py:121
  47.3 24.2 %collective-permute-start.6 = (bf16[256,1024]{1,0:T(8,128)(2,1)}, bf16[256,1024]{1,0:T(8,128)(2,1)}, u32[]{:S(2)}, u32[]{:S(2)}) collective-permute-start(bf16[256,1024]{1,0:T(8,128)(2,1)} %collective-permute-done.4), channel_id=1, source_target_pairs={{0,8},{4,12},{8,16},{12,20},{16,24},{20,28},{24,0},{28,4},{1,9},{5... | collective-permute-start | bytes 1572872 | tf_op jit(solution)/shard_map/ppermute | solution.py:115
  47.4 24.2 %collective-permute-start.7 = (bf16[64,2688]{1,0:T(8,128)(2,1)}, bf16[64,2688]{1,0:T(8,128)(2,1)}, u32[]{:S(2)}, u32[]{:S(2)}) collective-permute-start(bf16[64,2688]{1,0:T(8,128)(2,1)} %collective-permute-done.5), channel_id=1, source_target_pairs={{0,8},{4,12},{8,16},{12,20},{16,24},{20,28},{24,0},{28,4},{1,9},{5... | collective-permute-start | bytes 1032200 | tf_op jit(solution)/shard_map/ppermute | solution.py:115
  54.2 50.3 %all-to-all-start = ((bf16[32,64,176]{2,1,0:T(8,128)(2,1)}), bf16[32,64,176]{2,1,0:T(8,128)(2,1)S(1)}, u32[]{:S(2)}, u32[]{:S(2)}) async-start(bf16[32,64,176]{2,1,0:T(8,128)(2,1)} %maximum_bitcast_fusion.1), calls=%async_computation | async-start | bytes 2097152 | tf_op jit(solution)/shard_map/all_to_all | solution.py:406
  59.2 341.1 %all-gather.3.cloned.1.call-start = ((), (), s32[]{:S(2)}) async-start(), calls=%async_computation.3 | async-start | bytes 34603008 | tf_op jit(solution)/shard_map/all_gather | solution.py:443
  72.8 27.2 %collective-permute-start.12 = (bf16[128,2688]{1,0:T(8,128)(2,1)S(1)}, bf16[128,2688]{1,0:T(8,128)(2,1)S(1)}, u32[]{:S(2)}, u32[]{:S(2)}) collective-permute-start(bf16[128,2688]{1,0:T(8,128)(2,1)S(1)} %bitcast.310), channel_id=1, source_target_pairs={{0,1},{1,0},{2,3},{3,2},{4,5},{5,4},{6,7},{7,6},{8,9},{9,8},{10,11... | collective-permute-start | bytes 2064392 | tf_op jit(solution)/shard_map/ppermute | solution.py:115
  74.9 26.3 %collective-permute-start.13 = (bf16[128,2688]{1,0:T(8,128)(2,1)S(1)}, bf16[128,2688]{1,0:T(8,128)(2,1)S(1)}, u32[]{:S(2)}, u32[]{:S(2)}) collective-permute-start(bf16[128,2688]{1,0:T(8,128)(2,1)S(1)} %bitcast.307), channel_id=1, source_target_pairs={{0,2},{1,3},{2,0},{3,1},{4,6},{5,7},{6,4},{7,5},{8,10},{9,11},{10,... | collective-permute-start | bytes 2064392 | tf_op jit(solution)/shard_map/ppermute | solution.py:115
  128.2 22.5 %collective-permute-start.18 = (bf16[1024,1024]{1,0:T(8,128)(2,1)}, bf16[1024,1024]{1,0:T(8,128)(2,1)}, u32[]{:S(2)}, u32[]{:S(2)}) collective-permute-start(bf16[1024,1024]{1,0:T(8,128)(2,1)} %get-tuple-element.543), channel_id=1, source_target_pairs={{0,4},{4,0},{8,12},{12,8},{16,20},{20,16},{24,28},{28,24},{1,5},{5... | collective-permute-start | bytes 6291464 | tf_op jit(solution)/shard_map/ppermute | solution.py:115
  134.2 33.3 %collective-permute-start.16 = (bf16[256,2048]{1,0:T(8,128)(2,1)S(1)}, bf16[256,2048]{1,0:T(8,128)(2,1)}, u32[]{:S(2)}, u32[]{:S(2)}) collective-permute-start(bf16[256,2048]{1,0:T(8,128)(2,1)S(1)} %fusion.48), channel_id=1, source_target_pairs={{0,2},{1,3},{2,0},{3,1},{4,6},{5,7},{6,4},{7,5},{8,10},{9,11},{10,... | collective-permute-start | bytes 3145736 | tf_op jit(solution)/shard_map/ppermute | solution.py:115
  134.9 32.6 %collective-permute-start.17 = (bf16[256,2048]{1,0:T(8,128)(2,1)S(1)}, bf16[256,2048]{1,0:T(8,128)(2,1)}, u32[]{:S(2)}, u32[]{:S(2)}) collective-permute-start(bf16[256,2048]{1,0:T(8,128)(2,1)S(1)} %fusion.47), channel_id=1, source_target_pairs={{0,1},{1,0},{2,3},{3,2},{4,5},{5,4},{6,7},{7,6},{8,9},{9,8},{10,11... | collective-permute-start | bytes 3145736 | tf_op jit(solution)/shard_map/ppermute | solution.py:115
  177.2 45.6 %collective-permute-start.23 = (bf16[1024,2048]{1,0:T(8,128)(2,1)}, bf16[1024,2048]{1,0:T(8,128)(2,1)}, u32[]{:S(2)}, u32[]{:S(2)}) collective-permute-start(bf16[1024,2048]{1,0:T(8,128)(2,1)} %pad_maximum_fusion.4), channel_id=1, source_target_pairs={{0,4},{4,0},{8,12},{12,8},{16,20},{20,16},{24,28},{28,24},{1,5},{5... | collective-permute-start | bytes 12582920 | tf_op jit(solution)/shard_map/ppermute | solution.py:115
  243.0 27.8 %collective-permute-start.26 = (bf16[128,2048]{1,0:T(8,128)(2,1)S(1)}, bf16[128,2048]{1,0:T(8,128)(2,1)}, u32[]{:S(2)}, u32[]{:S(2)}) collective-permute-start(bf16[128,2048]{1,0:T(8,128)(2,1)S(1)} %concatenate.352), channel_id=1, source_target_pairs={{0,8},{4,12},{8,16},{12,20},{16,24},{20,28},{24,0},{28,4},{1,9},{5... | collective-permute-start | bytes 1572872 | tf_op jit(solution)/shard_map/ppermute | solution.py:115
  247.4 42.3 %collective-permute-start.28 = (bf16[128,2048]{0,1:T(8,128)(2,1)}, bf16[128,2048]{0,1:T(8,128)(2,1)}, u32[]{:S(2)}, u32[]{:S(2)}) collective-permute-start(bf16[128,2048]{0,1:T(8,128)(2,1)} %bitcast.51), channel_id=1, source_target_pairs={{0,1},{1,0},{2,3},{3,2},{4,5},{5,4},{6,7},{7,6},{8,9},{9,8},{10,11... | collective-permute-start | bytes 1572872 | tf_op jit(solution)/shard_map/ppermute | solution.py:115
  249.4 40.2 %collective-permute-start.29 = (bf16[128,2048]{0,1:T(8,128)(2,1)}, bf16[128,2048]{0,1:T(8,128)(2,1)}, u32[]{:S(2)}, u32[]{:S(2)}) collective-permute-start(bf16[128,2048]{0,1:T(8,128)(2,1)} %bitcast.52), channel_id=1, source_target_pairs={{0,2},{1,3},{2,0},{3,1},{4,6},{5,7},{6,4},{7,5},{8,10},{9,11},{10,... | collective-permute-start | bytes 1572872 | tf_op jit(solution)/shard_map/ppermute | solution.py:115
  270.8 31.5 %collective-permute-start.27 = (bf16[128,2048]{1,0:T(8,128)(2,1)}, bf16[128,2048]{1,0:T(8,128)(2,1)}, u32[]{:S(2)}, u32[]{:S(2)}) collective-permute-start(bf16[128,2048]{1,0:T(8,128)(2,1)} %collective-permute-done.26), channel_id=1, source_target_pairs={{0,8},{4,12},{8,16},{12,20},{16,24},{20,28},{24,0},{28,4},{1,9},{5... | collective-permute-start | bytes 1572872 | tf_op jit(solution)/shard_map/ppermute | solution.py:115
  282.2 45.7 %all-to-all-start.1 = ((f32[32,1,256]{2,1,0:T(1,128)}), f32[32,1,256]{2,1,0:T(1,128)S(1)}, u32[]{:S(2)}, u32[]{:S(2)}) async-start(f32[32,1,256]{2,1,0:T(1,128)} %all_to_all.13), calls=%async_computation.1 | async-start | bytes 65536 | tf_op jit(solution)/shard_map/all_to_all | solution.py:524
  288.0 826.3 %all-gather.5.cloned.1.call-start = ((), (), s32[]{:S(2)}) async-start(), calls=%async_computation.4 | async-start | bytes 12976128 | tf_op jit(solution)/shard_map/all_gather | solution.py:639
  304.6 34.9 %collective-permute-start.31 = (bf16[256,2048]{0,1:T(8,128)(2,1)}, bf16[256,2048]{0,1:T(8,128)(2,1)}, u32[]{:S(2)}, u32[]{:S(2)}) collective-permute-start(bf16[256,2048]{0,1:T(8,128)(2,1)} %pad_maximum_fusion.24), channel_id=1, source_target_pairs={{0,2},{1,3},{2,0},{3,1},{4,6},{5,7},{6,4},{7,5},{8,10},{9,11},{10,... | collective-permute-start | bytes 3145736 | tf_op jit(solution)/shard_map/ppermute | solution.py:115
  308.4 31.1 %collective-permute-start.32 = (bf16[256,2048]{0,1:T(8,128)(2,1)}, bf16[256,2048]{0,1:T(8,128)(2,1)}, u32[]{:S(2)}, u32[]{:S(2)}) collective-permute-start(bf16[256,2048]{0,1:T(8,128)(2,1)} %pad_maximum_fusion.25), channel_id=1, source_target_pairs={{0,1},{1,0},{2,3},{3,2},{4,5},{5,4},{6,7},{7,6},{8,9},{9,8},{10,11... | collective-permute-start | bytes 3145736 | tf_op jit(solution)/shard_map/ppermute | solution.py:115
  312.3 27.2 %collective-permute-start.30 = (bf16[128,2048]{1,0:T(8,128)(2,1)}, bf16[128,2048]{1,0:T(8,128)(2,1)}, u32[]{:S(2)}, u32[]{:S(2)}) collective-permute-start(bf16[128,2048]{1,0:T(8,128)(2,1)} %collective-permute-done.27), channel_id=1, source_target_pairs={{0,8},{4,12},{8,16},{12,20},{16,24},{20,28},{24,0},{28,4},{1,9},{5... | collective-permute-start | bytes 1572872 | tf_op jit(solution)/shard_map/ppermute | solution.py:115
  341.8 22.4 %collective-permute-start.33 = (bf16[256,2048]{1,0:T(8,128)(2,1)S(1)}, bf16[256,2048]{1,0:T(8,128)(2,1)S(1)}, u32[]{:S(2)}, u32[]{:S(2)}) collective-permute-start(bf16[256,2048]{1,0:T(8,128)(2,1)S(1)} %pad_maximum_fusion.26), channel_id=1, source_target_pairs={{0,1},{1,0},{2,3},{3,2},{4,5},{5,4},{6,7},{7,6},{8,9},{9,8},{10,11... | collective-permute-start | bytes 3145736 | tf_op jit(solution)/shard_map/ppermute | solution.py:115
  342.0 22.3 %collective-permute-start.34 = (bf16[256,2048]{1,0:T(8,128)(2,1)S(1)}, bf16[256,2048]{1,0:T(8,128)(2,1)S(1)}, u32[]{:S(2)}, u32[]{:S(2)}) collective-permute-start(bf16[256,2048]{1,0:T(8,128)(2,1)S(1)} %pad_maximum_fusion.27), channel_id=1, source_target_pairs={{0,2},{1,3},{2,0},{3,1},{4,6},{5,7},{6,4},{7,5},{8,10},{9,11},{10,... | collective-permute-start | bytes 3145736 | tf_op jit(solution)/shard_map/ppermute | solution.py:115
  342.4 27.1 %collective-permute-start.35 = (bf16[256,2048]{1,0:T(8,128)(2,1)S(1)}, bf16[256,2048]{1,0:T(8,128)(2,1)}, u32[]{:S(2)}, u32[]{:S(2)}) collective-permute-start(bf16[256,2048]{1,0:T(8,128)(2,1)S(1)} %copy-done.11), channel_id=1, source_target_pairs={{0,8},{4,12},{8,16},{12,20},{16,24},{20,28},{24,0},{28,4},{1,9},{5... | collective-permute-start | bytes 3145736 | tf_op jit(solution)/shard_map/ppermute | solution.py:115
  372.6 27.7 %collective-permute-start.36 = (bf16[1024,2048]{1,0:T(8,128)(2,1)}, bf16[1024,2048]{1,0:T(8,128)(2,1)}, u32[]{:S(2)}, u32[]{:S(2)}) collective-permute-start(bf16[1024,2048]{1,0:T(8,128)(2,1)} %constant_dynamic-update-slice_fusion.25.refs_1_), channel_id=1, source_target_pairs={{0,4},{4,0},{8,12},{12,8},{16,20},{20,16},{24,28},{28,24},{1,5},{5... | collective-permute-start | bytes 12582920 | tf_op jit(solution)/shard_map/ppermute | solution.py:115
  372.6 27.7 %collective-permute-start.37 = (bf16[256,2048]{1,0:T(8,128)(2,1)}, bf16[256,2048]{1,0:T(8,128)(2,1)}, u32[]{:S(2)}, u32[]{:S(2)}) collective-permute-start(bf16[256,2048]{1,0:T(8,128)(2,1)} %collective-permute-done.35), channel_id=1, source_target_pairs={{0,8},{4,12},{8,16},{12,20},{16,24},{20,28},{24,0},{28,4},{1,9},{5... | collective-permute-start | bytes 3145736 | tf_op jit(solution)/shard_map/ppermute | solution.py:115
  378.8 55.2 %collective-permute-start.39 = (bf16[512,2048]{1,0:T(8,128)(2,1)}, bf16[512,2048]{1,0:T(8,128)(2,1)}, u32[]{:S(2)}, u32[]{:S(2)}) collective-permute-start(bf16[512,2048]{1,0:T(8,128)(2,1)} %pad_maximum_fusion.7), channel_id=1, source_target_pairs={{0,2},{1,3},{2,0},{3,1},{4,6},{5,7},{6,4},{7,5},{8,10},{9,11},{10,... | collective-permute-start | bytes 6291464 | tf_op jit(solution)/shard_map/ppermute | solution.py:115
  381.1 52.8 %collective-permute-start.40 = (bf16[512,2048]{1,0:T(8,128)(2,1)}, bf16[512,2048]{1,0:T(8,128)(2,1)}, u32[]{:S(2)}, u32[]{:S(2)}) collective-permute-start(bf16[512,2048]{1,0:T(8,128)(2,1)} %pad_maximum_fusion.8), channel_id=1, source_target_pairs={{0,1},{1,0},{2,3},{3,2},{4,5},{5,4},{6,7},{7,6},{8,9},{9,8},{10,11... | collective-permute-start | bytes 6291464 | tf_op jit(solution)/shard_map/ppermute | solution.py:115
  400.3 33.6 %collective-permute-start.38 = (bf16[256,2048]{1,0:T(8,128)(2,1)}, bf16[256,2048]{1,0:T(8,128)(2,1)S(1)}, u32[]{:S(2)}, u32[]{:S(2)}) collective-permute-start(bf16[256,2048]{1,0:T(8,128)(2,1)} %collective-permute-done.37), channel_id=1, source_target_pairs={{0,8},{4,12},{8,16},{12,20},{16,24},{20,28},{24,0},{28,4},{1,9},{5... | collective-permute-start | bytes 3145736 | tf_op jit(solution)/shard_map/ppermute | solution.py:115
  488.0 64.2 %collective-permute-start.48 = (bf16[1024,4096]{1,0:T(8,128)(2,1)}, bf16[1024,4096]{1,0:T(8,128)(2,1)}, u32[]{:S(2)}, u32[]{:S(2)}) collective-permute-start(bf16[1024,4096]{1,0:T(8,128)(2,1)} %get-tuple-element.240), channel_id=1, source_target_pairs={{0,4},{4,0},{8,12},{12,8},{16,20},{20,16},{24,28},{28,24},{1,5},{5... | collective-permute-start | bytes 25165832 | tf_op jit(solution)/shard_map/ppermute | solution.py:115
  490.9 48.0 %collective-permute-start.42 = (bf16[512,2048]{1,0:T(8,128)(2,1)}, bf16[512,2048]{1,0:T(8,128)(2,1)}, u32[]{:S(2)}, u32[]{:S(2)}) collective-permute-start(bf16[512,2048]{1,0:T(8,128)(2,1)} %pad_maximum_fusion.9), channel_id=1, source_target_pairs={{0,1},{1,0},{2,3},{3,2},{4,5},{5,4},{6,7},{7,6},{8,9},{9,8},{10,11... | collective-permute-start | bytes 6291464 | tf_op jit(solution)/shard_map/ppermute | solution.py:115
  496.3 47.6 %collective-permute-start.43 = (bf16[512,2048]{1,0:T(8,128)(2,1)S(1)}, bf16[512,2048]{1,0:T(8,128)(2,1)}, u32[]{:S(2)}, u32[]{:S(2)}) collective-permute-start(bf16[512,2048]{1,0:T(8,128)(2,1)S(1)} %pad_maximum_fusion.10), channel_id=1, source_target_pairs={{0,2},{1,3},{2,0},{3,1},{4,6},{5,7},{6,4},{7,5},{8,10},{9,11},{10,... | collective-permute-start | bytes 6291464 | tf_op jit(solution)/shard_map/ppermute | solution.py:115
  550.3 56.4 %collective-permute-start.45 = (bf16[2048,2048]{1,0:T(8,128)(2,1)}, bf16[2048,2048]{1,0:T(8,128)(2,1)}, u32[]{:S(2)}, u32[]{:S(2)}) collective-permute-start(bf16[2048,2048]{1,0:T(8,128)(2,1)} %constant_dynamic-update-slice_fusion.31.refs_1_), channel_id=1, source_target_pairs={{0,4},{4,0},{8,12},{12,8},{16,20},{20,16},{24,28},{28,24},{1,5},{5... | collective-permute-start | bytes 25165832 | tf_op jit(solution)/shard_map/ppermute | solution.py:115
  550.3 48.3 %collective-permute-start.46 = (bf16[512,2048]{1,0:T(8,128)(2,1)}, bf16[512,2048]{1,0:T(8,128)(2,1)S(1)}, u32[]{:S(2)}, u32[]{:S(2)}) collective-permute-start(bf16[512,2048]{1,0:T(8,128)(2,1)} %get-tuple-element.258), channel_id=1, source_target_pairs={{0,2},{1,3},{2,0},{3,1},{4,6},{5,7},{6,4},{7,5},{8,10},{9,11},{10,... | collective-permute-start | bytes 6291464 | tf_op jit(solution)/shard_map/ppermute | solution.py:115
  550.9 48.1 %collective-permute-start.47 = (bf16[512,2048]{1,0:T(8,128)(2,1)}, bf16[512,2048]{1,0:T(8,128)(2,1)}, u32[]{:S(2)}, u32[]{:S(2)}) collective-permute-start(bf16[512,2048]{1,0:T(8,128)(2,1)} %get-tuple-element.259), channel_id=1, source_target_pairs={{0,1},{1,0},{2,3},{3,2},{4,5},{5,4},{6,7},{7,6},{8,9},{9,8},{10,11... | collective-permute-start | bytes 6291464 | tf_op jit(solution)/shard_map/ppermute | solution.py:115
  666.5 25.6 %collective-permute-start.49 = (bf16[2048,4096]{1,0:T(8,128)(2,1)}, bf16[2048,4096]{1,0:T(8,128)(2,1)}, u32[]{:S(2)}, u32[]{:S(2)}) collective-permute-start(bf16[2048,4096]{1,0:T(8,128)(2,1)} %get-tuple-element.275), channel_id=1, source_target_pairs={{0,4},{4,0},{8,12},{12,8},{16,20},{20,16},{24,28},{28,24},{1,5},{5... | collective-permute-start | bytes 50331656 | tf_op jit(solution)/shard_map/ppermute | solution.py:115
  680.8 78.9 %collective-permute-start.52 = (bf16[256,2048]{1,0:T(8,128)(2,1)}, bf16[256,2048]{1,0:T(8,128)(2,1)S(1)}, u32[]{:S(2)}, u32[]{:S(2)}) collective-permute-start(bf16[256,2048]{1,0:T(8,128)(2,1)} %split.200), channel_id=1, source_target_pairs={{0,1},{1,0},{2,3},{3,2},{4,5},{5,4},{6,7},{7,6},{8,9},{9,8},{10,11... | collective-permute-start | bytes 3145736 | tf_op jit(solution)/shard_map/ppermute | solution.py:115
  683.1 76.6 %collective-permute-start.53 = (bf16[256,2048]{1,0:T(8,128)(2,1)}, bf16[256,2048]{1,0:T(8,128)(2,1)}, u32[]{:S(2)}, u32[]{:S(2)}) collective-permute-start(bf16[256,2048]{1,0:T(8,128)(2,1)} %split.201), channel_id=1, source_target_pairs={{0,2},{1,3},{2,0},{3,1},{4,6},{5,7},{6,4},{7,5},{8,10},{9,11},{10,... | collective-permute-start | bytes 3145736 | tf_op jit(solution)/shard_map/ppermute | solution.py:115
  757.4 53.1 %collective-permute-start.50 = (bf16[512,2048]{1,0:T(8,128)(2,1)}, bf16[512,2048]{1,0:T(8,128)(2,1)S(1)}, u32[]{:S(2)}, u32[]{:S(2)}) collective-permute-start(bf16[512,2048]{1,0:T(8,128)(2,1)} %get-tuple-element.282), channel_id=1, source_target_pairs={{0,1},{1,0},{2,3},{3,2},{4,5},{5,4},{6,7},{7,6},{8,9},{9,8},{10,11... | collective-permute-start | bytes 6291464 | tf_op jit(solution)/shard_map/ppermute | solution.py:115
  758.8 51.8 %collective-permute-start.51 = (bf16[512,2048]{1,0:T(8,128)(2,1)}, bf16[512,2048]{1,0:T(8,128)(2,1)S(1)}, u32[]{:S(2)}, u32[]{:S(2)}) collective-permute-start(bf16[512,2048]{1,0:T(8,128)(2,1)} %get-tuple-element.283), channel_id=1, source_target_pairs={{0,2},{1,3},{2,0},{3,1},{4,6},{5,7},{6,4},{7,5},{8,10},{9,11},{10,... | collective-permute-start | bytes 6291464 | tf_op jit(solution)/shard_map/ppermute | solution.py:115
  763.0 43.6 %collective-permute-start.54 = (bf16[128,2048]{1,0:T(8,128)(2,1)S(1)}, bf16[128,2048]{1,0:T(8,128)(2,1)S(1)}, u32[]{:S(2)}, u32[]{:S(2)}) collective-permute-start(bf16[128,2048]{1,0:T(8,128)(2,1)S(1)} %pad_maximum_fusion.35), channel_id=1, source_target_pairs={{0,24},{4,28},{8,0},{12,4},{16,8},{20,12},{24,16},{28,20},{1,25},{... | collective-permute-start | bytes 1572872 | tf_op jit(solution)/shard_map/ppermute | solution.py:115
  814.6 45.2 %collective-permute-start.55 = (bf16[128,2048]{1,0:T(8,128)(2,1)S(1)}, bf16[128,2048]{1,0:T(8,128)(2,1)S(1)}, u32[]{:S(2)}, u32[]{:S(2)}) collective-permute-start(bf16[128,2048]{1,0:T(8,128)(2,1)S(1)} %add_convert_fusion.21), channel_id=1, source_target_pairs={{0,24},{4,28},{8,0},{12,4},{16,8},{20,12},{24,16},{28,20},{1,25},{... | collective-permute-start | bytes 1572872 | tf_op jit(solution)/shard_map/ppermute | solution.py:115
  818.0 41.8 %collective-permute-start.56 = (bf16[256,2048]{1,0:T(8,128)(2,1)S(1)}, bf16[256,2048]{1,0:T(8,128)(2,1)S(1)}, u32[]{:S(2)}, u32[]{:S(2)}) collective-permute-start(bf16[256,2048]{1,0:T(8,128)(2,1)S(1)} %pad_maximum_fusion.31), channel_id=1, source_target_pairs={{0,24},{4,28},{8,0},{12,4},{16,8},{20,12},{24,16},{28,20},{1,25},{... | collective-permute-start | bytes 3145736 | tf_op jit(solution)/shard_map/ppermute | solution.py:115
  818.5 46.8 %collective-permute-start.57 = (bf16[512,2048]{1,0:T(8,128)(2,1)S(1)}, bf16[512,2048]{1,0:T(8,128)(2,1)S(1)}, u32[]{:S(2)}, u32[]{:S(2)}) collective-permute-start(bf16[512,2048]{1,0:T(8,128)(2,1)S(1)} %copy-done.117), channel_id=1, source_target_pairs={{0,2},{1,3},{2,0},{3,1},{4,6},{5,7},{6,4},{7,5},{8,10},{9,11},{10,... | collective-permute-start | bytes 6291464 | tf_op jit(solution)/shard_map/ppermute | solution.py:115
  820.0 46.5 %collective-permute-start.58 = (bf16[512,2048]{1,0:T(8,128)(2,1)S(1)}, bf16[512,2048]{1,0:T(8,128)(2,1)S(1)}, u32[]{:S(2)}, u32[]{:S(2)}) collective-permute-start(bf16[512,2048]{1,0:T(8,128)(2,1)S(1)} %copy-done.116), channel_id=1, source_target_pairs={{0,1},{1,0},{2,3},{3,2},{4,5},{5,4},{6,7},{7,6},{8,9},{9,8},{10,11... | collective-permute-start | bytes 6291464 | tf_op jit(solution)/shard_map/ppermute | solution.py:115
  871.3 82.4 %collective-permute-start.59 = (bf16[768,2048]{1,0:T(8,128)(2,1)}, bf16[768,2048]{1,0:T(8,128)(2,1)}, u32[]{:S(2)}, u32[]{:S(2)}) collective-permute-start(bf16[768,2048]{1,0:T(8,128)(2,1)} %pad_maximum_fusion.5), channel_id=1, source_target_pairs={{0,1},{1,0},{2,3},{3,2},{4,5},{5,4},{6,7},{7,6},{8,9},{9,8},{10,11... | collective-permute-start | bytes 9437192 | tf_op jit(solution)/shard_map/ppermute | solution.py:115
  877.3 76.5 %collective-permute-start.60 = (bf16[768,2048]{1,0:T(8,128)(2,1)}, bf16[768,2048]{1,0:T(8,128)(2,1)}, u32[]{:S(2)}, u32[]{:S(2)}) collective-permute-start(bf16[768,2048]{1,0:T(8,128)(2,1)} %pad_maximum_fusion.6), channel_id=1, source_target_pairs={{0,2},{1,3},{2,0},{3,1},{4,6},{5,7},{6,4},{7,5},{8,10},{9,11},{10,... | collective-permute-start | bytes 9437192 | tf_op jit(solution)/shard_map/ppermute | solution.py:115
  878.0 38.0 %collective-permute-start.61 = (bf16[128,2048]{1,0:T(8,128)(2,1)}, bf16[128,2048]{1,0:T(8,128)(2,1)}, u32[]{:S(2)}, u32[]{:S(2)}) collective-permute-start(bf16[128,2048]{1,0:T(8,128)(2,1)} %add_convert_fusion.20), channel_id=1, source_target_pairs={{0,24},{4,28},{8,0},{12,4},{16,8},{20,12},{24,16},{28,20},{1,25},{... | collective-permute-start | bytes 1572872 | tf_op jit(solution)/shard_map/ppermute | solution.py:115
  879.4 36.6 %collective-permute-start.62 = (bf16[256,2048]{1,0:T(8,128)(2,1)S(1)}, bf16[256,2048]{1,0:T(8,128)(2,1)}, u32[]{:S(2)}, u32[]{:S(2)}) collective-permute-start(bf16[256,2048]{1,0:T(8,128)(2,1)S(1)} %add_convert_fusion.16), channel_id=1, source_target_pairs={{0,24},{4,28},{8,0},{12,4},{16,8},{20,12},{24,16},{28,20},{1,25},{... | collective-permute-start | bytes 3145736 | tf_op jit(solution)/shard_map/ppermute | solution.py:115
  917.8 27.4 %collective-permute-start.63 = (bf16[256,2048]{1,0:T(8,128)(2,1)S(1)}, bf16[256,2048]{1,0:T(8,128)(2,1)S(1)}, u32[]{:S(2)}, u32[]{:S(2)}) collective-permute-start(bf16[256,2048]{1,0:T(8,128)(2,1)S(1)} %add_convert_fusion.15), channel_id=1, source_target_pairs={{0,24},{4,28},{8,0},{12,4},{16,8},{20,12},{24,16},{28,20},{1,25},{... | collective-permute-start | bytes 3145736 | tf_op jit(solution)/shard_map/ppermute | solution.py:115
  968.6 32.6 %collective-permute-start.66 = (bf16[384,2048]{1,0:T(8,128)(2,1)}, bf16[384,2048]{1,0:T(8,128)(2,1)}, u32[]{:S(2)}, u32[]{:S(2)}) collective-permute-start(bf16[384,2048]{1,0:T(8,128)(2,1)} %pad_maximum_fusion.14), channel_id=1, source_target_pairs={{0,24},{4,28},{8,0},{12,4},{16,8},{20,12},{24,16},{28,20},{1,25},{... | collective-permute-start | bytes 4718600 | tf_op jit(solution)/shard_map/ppermute | solution.py:115
  1004.4 42.2 %collective-permute-start.67 = (bf16[384,2048]{1,0:T(8,128)(2,1)}, bf16[384,2048]{1,0:T(8,128)(2,1)}, u32[]{:S(2)}, u32[]{:S(2)}) collective-permute-start(bf16[384,2048]{1,0:T(8,128)(2,1)} %add_convert_fusion.10), channel_id=1, source_target_pairs={{0,24},{4,28},{8,0},{12,4},{16,8},{20,12},{24,16},{28,20},{1,25},{... | collective-permute-start | bytes 4718600 | tf_op jit(solution)/shard_map/ppermute | solution.py:115
  1007.6 116.6 %all-to-all-start.2 = ((f32[32,64,176]{2,1,0:T(8,128)}), f32[32,64,176]{2,1,0:T(8,128)}, u32[]{:S(2)}, u32[]{:S(2)}) async-start(f32[32,64,176]{2,1,0:T(8,128)} %bitcast.300), calls=%async_computation.2 | async-start | bytes 4194304 | tf_op jit(solution)/shard_map/all_to_all | solution.py:778
  1070.6 33.2 %collective-permute-start.74 = (bf16[256,768]{0,1:T(8,128)(2,1)}, bf16[256,768]{0,1:T(8,128)(2,1)}, u32[]{:S(2)}, u32[]{:S(2)}) collective-permute-start(bf16[256,768]{0,1:T(8,128)(2,1)} %bitcast.71), channel_id=1, source_target_pairs={{0,1},{1,0},{2,3},{3,2},{4,5},{5,4},{6,7},{7,6},{8,9},{9,8},{10,11... | collective-permute-start | bytes 1179656 | tf_op jit(solution)/shard_map/ppermute | solution.py:121
  1072.4 31.4 %collective-permute-start.75 = (bf16[256,768]{0,1:T(8,128)(2,1)}, bf16[256,768]{0,1:T(8,128)(2,1)}, u32[]{:S(2)}, u32[]{:S(2)}) collective-permute-start(bf16[256,768]{0,1:T(8,128)(2,1)} %bitcast.72), channel_id=1, source_target_pairs={{0,2},{1,3},{2,0},{3,1},{4,6},{5,7},{6,4},{7,5},{8,10},{9,11},{10,... | collective-permute-start | bytes 1179656 | tf_op jit(solution)/shard_map/ppermute | solution.py:121
  1073.9 29.9 %collective-permute-start.76 = (bf16[256,768]{0,1:T(8,128)(2,1)}, bf16[256,768]{0,1:T(8,128)(2,1)}, u32[]{:S(2)}, u32[]{:S(2)}) collective-permute-start(bf16[256,768]{0,1:T(8,128)(2,1)} %bitcast.73), channel_id=1, source_target_pairs={{0,3},{1,2},{2,1},{3,0},{4,7},{5,6},{6,5},{7,4},{8,11},{9,10},{10,... | collective-permute-start | bytes 1179656 | tf_op jit(solution)/shard_map/ppermute | solution.py:121
  1077.4 62.5 %collective-permute-start.68 = (bf16[384,2048]{1,0:T(8,128)(2,1)}, bf16[384,2048]{1,0:T(8,128)(2,1)}, u32[]{:S(2)}, u32[]{:S(2)}) collective-permute-start(bf16[384,2048]{1,0:T(8,128)(2,1)} %add_convert_fusion.9), channel_id=1, source_target_pairs={{0,24},{4,28},{8,0},{12,4},{16,8},{20,12},{24,16},{28,20},{1,25},{... | collective-permute-start | bytes 4718600 | tf_op jit(solution)/shard_map/ppermute | solution.py:115
  1102.5 43.2 %collective-permute-start.80 = (bf16[4,256,1536]{2,1,0:T(8,128)(2,1)}, bf16[4,256,1536]{2,1,0:T(8,128)(2,1)}, u32[]{:S(2)}, u32[]{:S(2)}) collective-permute-start(bf16[4,256,1536]{2,1,0:T(8,128)(2,1)} %dynamic-slice_bitcast_fusion), channel_id=1, source_target_pairs={{0,4},{4,0},{8,12},{12,8},{16,20},{20,16},{24,28},{28,24},{1,5},{5... | collective-permute-start | bytes 9437192 | tf_op jit(solution)/shard_map/ppermute | solution.py:115
  1110.8 34.8 %collective-permute-start.77 = (bf16[256,576]{0,1:T(8,128)(2,1)}, bf16[256,576]{0,1:T(8,128)(2,1)}, u32[]{:S(2)}, u32[]{:S(2)}) collective-permute-start(bf16[256,576]{0,1:T(8,128)(2,1)} %get-tuple-element.473), channel_id=1, source_target_pairs={{0,1},{1,0},{2,3},{3,2},{4,5},{5,4},{6,7},{7,6},{8,9},{9,8},{10,11... | collective-permute-start | bytes 884744 | tf_op jit(solution)/shard_map/ppermute | solution.py:121
  1112.3 33.3 %collective-permute-start.78 = (bf16[256,576]{0,1:T(8,128)(2,1)}, bf16[256,576]{0,1:T(8,128)(2,1)}, u32[]{:S(2)}, u32[]{:S(2)}) collective-permute-start(bf16[256,576]{0,1:T(8,128)(2,1)} %get-tuple-element.472), channel_id=1, source_target_pairs={{0,2},{1,3},{2,0},{3,1},{4,6},{5,7},{6,4},{7,5},{8,10},{9,11},{10,... | collective-permute-start | bytes 884744 | tf_op jit(solution)/shard_map/ppermute | solution.py:121
  1113.8 31.8 %collective-permute-start.79 = (bf16[256,576]{0,1:T(8,128)(2,1)}, bf16[256,576]{0,1:T(8,128)(2,1)}, u32[]{:S(2)}, u32[]{:S(2)}) collective-permute-start(bf16[256,576]{0,1:T(8,128)(2,1)} %get-tuple-element.471), channel_id=1, source_target_pairs={{0,3},{1,2},{2,1},{3,0},{4,7},{5,6},{6,5},{7,4},{8,11},{9,10},{10,... | collective-permute-start | bytes 884744 | tf_op jit(solution)/shard_map/ppermute | solution.py:121
  1144.1 50.3 %collective-permute-start.69 = (bf16[64,2048]{1,0:T(8,128)(2,1)}, bf16[64,2048]{1,0:T(8,128)(2,1)}, u32[]{:S(2)}, u32[]{:S(2)}) collective-permute-start(bf16[64,2048]{1,0:T(8,128)(2,1)} %get-tuple-element.467), channel_id=1, source_target_pairs={{0,2},{1,3},{2,0},{3,1},{4,6},{5,7},{6,4},{7,5},{8,10},{9,11},{10,... | collective-permute-start | bytes 786440 | tf_op jit(solution)/shard_map/ppermute | solution.py:115
  1165.0 29.5 %collective-permute-start.70 = (bf16[64,2048]{1,0:T(8,128)(2,1)}, bf16[64,2048]{1,0:T(8,128)(2,1)}, u32[]{:S(2)}, u32[]{:S(2)}) collective-permute-start(bf16[64,2048]{1,0:T(8,128)(2,1)} %get-tuple-element.468), channel_id=1, source_target_pairs={{0,1},{1,0},{2,3},{3,2},{4,5},{5,4},{6,7},{7,6},{8,9},{9,8},{10,11... | collective-permute-start | bytes 786440 | tf_op jit(solution)/shard_map/ppermute | solution.py:115
  (172 other events, 2030.2 us)
Sparse Core Ops, SparseCore 0:
  112.4 233.4 all-gather.2
  683.9 108.0 all-gather.4

commit v5 on v4

--- a/solution.py
+++ b/solution.py
@@ -439,7 +439,6 @@
     source_list = [links.device_of(order + ("c",)) for order in orders]
     sources = jnp.concatenate(source_list).astype(jnp.int32)
     m_place = jnp.concatenate([d * slices + i for i, d in enumerate(source_list)])
-    hidden_row, query_w, up_w, down_w = tie(hidden_row, query_w, up_w, down_w)
     g_all = lax.all_gather(after(cotangent, far_a), BOTH, axis=0, tiled=True)
     g_blocks = g_all.reshape(devices, tok, D)
 

time: 1280 us -> 1280 us (level)
    ppermute x70, waiting for transfers between devices: 203 us -> 186 us  [shift(): return lax.ppermute(value, name, pairs)]
    concatenate x27 -> x26, other arithmetic: 30.9 us -> 27.4 us  [joined_rows(): return parts[0] if len(parts) == 1 else jnp.concatenate(parts, axis=0)]
    unnamed x305 -> x335, local copies, waits for them, and re-layouts: 59.2 us -> 60.8 us
  transfers between devices with their start and end apart: 102 -> 102, of which waited for: 44 -> 44; matrix products, arithmetic and copies ran while one was open for 45% -> 46% of each run, Pallas kernels for 14% -> 14%
where the time goes in v5:
time: 1280 us; the launch traced here: 1260 us
  Pallas kernels  266 us (21%)
  waiting for transfers between devices  238 us (19%)
  local copies, waits for them, and re-layouts  225 us (18%)
  matrix products  223 us (17%)
  other arithmetic  159 us (12%)
  starting transfers between devices  131 us (10%)
  between operations  17 us (1%)
    pallas_call x6, Pallas kernels, ffn_chunk(): pl.pallas_call(lambda *refs: ffn_kernel(half_ff, 0 if moved is None else...  266 us
    ppermute x70, waiting for transfers between devices, shift(): return lax.ppermute(value, name, pairs)  186 us
    dot_general x7, matrix products, matmul_left_t(): lax.dot_general(left, right, (((0,), (0,)), ((), ())), preferred_element_...  131 us
    ppermute x70, starting transfers between devices, shift(): return lax.ppermute(value, name, pairs)  86.2 us
    unnamed x335, local copies, waits for them, and re-layouts  60.8 us
    ppermute x27, waiting for transfers between devices, shift_ctx(): return lax.ppermute(value, 'ctx', pairs)  51.2 us
    convert_element_type x28, other arithmetic, plus(): return (left.astype(f32) + right.astype(f32)).astype(bf16)  47.9 us
    ppermute x27, starting transfers between devices, shift_ctx(): return lax.ppermute(value, 'ctx', pairs)  32.1 us
  transfers between devices with their start and end apart: 102, of which 44 were waited for; matrix products, arithmetic and copies ran while one was open for 46% of the time, Pallas kernels for 14%

profile of v5, /device:TPU:0, one launch (start us, length us, event | category | flops | bytes accessed | tf_op | source)
XLA Modules:
  0.0 1260.1 jit_solution(5684518402292202475)
XLA Ops:
  21.7 4.3 collective-permute-done.2
  32.8 14.5 %collective-permute-done.5 = bf16[64,2688]{1,0:T(8,128)(2,1)} collective-permute-done((bf16[64,2688]{1,0:T(8,128)(2,1)S(1)}, bf16[64,2688]{1,0:T(8,128)(2,1)}, u32[]{:S(2)}, u32[]{:S(2)}) %collective-permute-start.5) | collective-permute-done | bytes 344096 | tf_op jit(solution)/shard_map/ppermute | solution.py:115
  55.8 5.2 all-to-all-start
  61.0 8.9 collective-permute-done.7
  75.2 8.6 collective-permute-done.9
  87.0 10.4 collective-permute-done.11
  104.5 5.8 collective-permute-done.14
  144.0 4.1 gather_fusion
  163.2 5.1 gather_fusion.1
  168.4 4.0 slice.430
  177.9 4.7 copy.220
  182.5 6.2 fusion.22
  189.0 3.8 pad_maximum_fusion.4
  193.1 8.2 fusion.124
  201.3 8.1 fusion.8
  209.5 9.0 fusion.47
  227.9 6.5 collective-permute-done.22
  234.3 4.7 collective-permute-done.21
  239.0 6.3 collective-permute-done.20
  246.1 4.8 constant_dynamic-update-slice_fusion.20
  250.9 9.3 gather_fusion.4
  260.1 6.0 multiply_reduce_fusion.1
  272.9 9.5 collective-permute-done.24
  283.2 4.3 collective-permute-done.26
  291.7 4.3 all-to-all-start.1
  297.7 6.5 collective-permute-done.28
  316.9 11.8 concatenate.298.refs_7_
  330.9 9.2 collective-permute-done.30
  344.8 7.2 collective-permute-start.35
  353.1 12.9 %collective-permute-done.33 = bf16[256,2048]{1,0:T(8,128)(2,1)S(1)} collective-permute-done((bf16[256,2048]{1,0:T(8,128)(2,1)S(1)}, bf16[256,2048]{1,0:T(8,128)(2,1)S(1)}, u32[]{:S(2)}, u32[]{:S(2)}) %collective-permute-start.33) | collective-permute-done | bytes 1048608 | tf_op jit(solution)/shard_map/ppermute | solution.py:115
  367.3 9.9 collective-permute-done.35
  390.5 17.6 %collective-permute-done.37 = bf16[256,2048]{1,0:T(8,128)(2,1)} collective-permute-done((bf16[256,2048]{1,0:T(8,128)(2,1)}, bf16[256,2048]{1,0:T(8,128)(2,1)}, u32[]{:S(2)}, u32[]{:S(2)}) %collective-permute-start.37) | collective-permute-done | bytes 1048608 | tf_op jit(solution)/shard_map/ppermute | solution.py:115
  408.2 33.6 %ffn_chunk.6 = (bf16[8192,2048]{1,0:T(8,128)(2,1)}, bf16[8192,2048]{1,0:T(8,128)(2,1)}, bf16[8192,896]{1,0:T(8,128)(2,1)}, bf16[8192,1792]{1,0:T(8,128)(2,1)}, bf16[1024,4096]{1,0:T(8,128)(2,1)}) custom-call(s32[128]{0:T(128)} %add_convert_fusion.31.refs_0_, bf16[1024,2048]{1,0:T(8,128)(2,1)} %collective-permute-done.36.refs_1_, ...), custom_call_target="tpu_custom_call" | custom-call | flops 22548578304 | bytes 33554432 | tf_op jit(solution)/shard_map/ffn_chunk/pallas_call | solution.py:298
  447.4 7.2 collective-permute-done.41.refs_1_
  456.5 34.0 %ffn_chunk.7 = (bf16[8192,2048]{1,0:T(8,128)(2,1)}, bf16[8192,2048]{1,0:T(8,128)(2,1)}, bf16[8192,896]{1,0:T(8,128)(2,1)}, bf16[8192,1792]{1,0:T(8,128)(2,1)}, bf16[1024,4096]{1,0:T(8,128)(2,1)}) custom-call(s32[128]{0:T(128)} %add_convert_fusion.31.refs_0_, ...), custom_call_target="tpu_custom_call", output_to_operand_aliasing={{0}: (9, {}), {1}: (10, {}), {2}: (11, {}), {3}: (12, {})} | custom-call | flops 22548578304 | bytes 33554432 | tf_op jit(solution)/shard_map/ffn_chunk/pallas_call | solution.py:298
  506.8 36.4 %ffn_chunk.8 = (bf16[8192,2048]{1,0:T(8,128)(2,1)}, bf16[8192,2048]{1,0:T(8,128)(2,1)}, bf16[8192,896]{1,0:T(8,128)(2,1)}, bf16[8192,1792]{1,0:T(8,128)(2,1)}, b...) custom-call(s32[128]{0:T(128)} %add_convert_fusion.31.refs_0_, ...), custom_call_target="tpu_custom_call", output_to_operand_aliasing={{0}: (10, {}), {1}: (11, {}), {2}: (12, {}), {3}: (13, {})} | custom-call | flops 22548578304 | bytes 33554432 | tf_op jit(solution)/shard_map/ffn_chunk/pallas_call | solution.py:298
  546.9 5.8 collective-permute-done.43
  560.8 36.7 %ffn_chunk.9 = (bf16[8192,2048]{1,0:T(8,128)(2,1)}, bf16[8192,2048]{1,0:T(8,128)(2,1)}, bf16[8192,896]{1,0:T(8,128)(2,1)}, bf16[8192,1792]{1,0:T(8,128)(2,1)}, b...) custom-call(s32[128]{0:T(128)} %add_convert_fusion.31.refs_0_, ...), custom_call_target="tpu_custom_call", output_to_operand_aliasing={{0}: (10, {}), {1}: (11, {}), {2}: (12, {}), {3}: (13, {})} | custom-call | flops 22548578304 | bytes 33554432 | tf_op jit(solution)/shard_map/ffn_chunk/pallas_call | solution.py:298
  597.6 9.7 collective-permute-done.46
  615.4 60.1 %ffn_chunk.10 = (bf16[8192,2048]{1,0:T(8,128)(2,1)}, bf16[8192,2048]{1,0:T(8,128)(2,1)}, bf16[8192,896]{1,0:T(8,128)(2,1)}, bf16[8192,1792]{1,0:T(8,128)(2,1)}, bf16[2048,4096]{1,0:T(8,128)(2,1)}) custom-call(s32[128]{0:T(128)} %add_convert_fusion.31.refs_0_, ...), custom_call_target="tpu_custom_call", output_to_operand_aliasing={{0}: (9, {}), {1}: (10, {}), {2}: (11, {}), {3}: (12, {})} | custom-call | flops 45097156608 | bytes 67108864 | tf_op jit(solution)/shard_map/ffn_chunk/pallas_call | solution.py:298
  692.7 8.4 collective-permute-done.49.refs_9_
  701.1 65.4 %ffn_chunk.11 = (bf16[8192,2048]{1,0:T(8,128)(2,1)}, bf16[8192,2048]{1,0:T(8,128)(2,1)}, bf16[8192,896]{1,0:T(8,128)(2,1)}, bf16[8192,1792]{1,0:T(8,128)(2,1)}, ...) custom-call(s32[128]{0:T(128)} %add_convert_fusion.31.refs_0_, ...), custom_call_target="tpu_custom_call", output_to_operand_aliasing={{0}: (10, {}), {1}: (11, {}), {2}: (12, {}), {3}: (13, {})} | custom-call | flops 45097156608 | bytes 67108864 | tf_op jit(solution)/shard_map/ffn_chunk/pallas_call | solution.py:298
  775.5 39.3 %fusion.4 = f32[1024,1792]{1,0:T(8,128)} fusion(bf16[8192,1792]{1,0:T(8,128)(2,1)} %get-tuple-element.281, bf16[8192,2048]{1,0:T(8,128)(2,1)} %get-tuple-element.290), kind=kOutput, calls=%fused_computation.16 | convolution fusion | flops 30064771072 | bytes 53477376 | tf_op jit(solution)/shard_map/dot_general | solution.py:31
  814.8 4.9 collective-permute-done.50
  829.6 39.3 %fusion.2 = f32[1024,1792]{1,0:T(8,128)} fusion(bf16[8192,1792]{1,0:T(8,128)(2,1)} %get-tuple-element.281, bf16[8192,2048]{1,0:T(8,128)(2,1)} %get-tuple-element.290), kind=kOutput, calls=%fused_computation.14 | convolution fusion | flops 30064771072 | bytes 53477376 | tf_op jit(solution)/shard_map/dot_general | solution.py:31
  870.2 4.2 collective-permute-done.57
  889.0 36.3 %fusion.126 = f32[896,2048]{1,0:T(8,128)} fusion(bf16[8192,896]{1,0:T(8,128)(2,1)S(1)} %bitcast.289, bf16[8192,2048]{1,0:T(8,128)(2,1)} %get-tuple-element.306), kind=kOutput, calls=%fused_computation.411 | convolution fusion | flops 30064771072 | bytes 55574528 | tf_op jit(solution)/shard_map/dot_general | solution.py:31
  940.1 14.4 %fusion.11 = f32[1,2048,1408]{2,1,0:T(8,128)} fusion(f32[1024,704]{1,0:T(8,128)S(1)} %get-tuple-element.420, f32[1024,704]{1,0:T(8,128)S(1)} %get-tuple-element.419, f32[1024,704]{1,0:T(8,128)S(1)} %get-tuple-element.418, f32[1024,704]{1,0:T(8,128)S(1)} %get-tuple-element.417), kind=kLoop, calls=%fused_computation.25 | loop fusion | flops 8650752 | bytes 23068672 | tf_op jit(solution)/shard_map/broadcast_in_dim | solution.py:919
  993.6 7.0 collective-permute-done.73
  1000.5 5.6 collective-permute-done.72
  1019.7 6.3 convolution_convert_fusion.1
  1026.1 9.1 fusion.15
  1035.2 19.8 %multiply_convert_fusion = bf16[4,1024,1024]{1,2,0:T(8,128)(2,1)} fusion(f32[4,1024,1024]{1,2,0:T(8,128)} %get-tuple-element.578, f32[4,1024]{1,0:T(4,128)S(1)} %copy-done.105, bf16[4,1024,256]{1,2,0:T(8,128)(2,1)} %bitcast.341, bf16[1024,1024]{1,0:T(8,128)(2,1)} %pad_maximum_fusion.11), kind=kOutput, calls=%fused_computation.10 | convolution fusion | flops 2176848896 | bytes 46170112 | tf_op jit(solution)/shard_map/sub | solution.py:804
  1055.0 5.8 convolution_bitcast_fusion
  1064.7 4.5 copy.232
  1069.3 5.4 convolution_bitcast_fusion.1
  1092.3 6.4 convolution_convert_fusion
  1118.6 9.9 fusion.127
  1162.0 4.7 convolution_add_fusion
  1185.4 4.0 reshape.1056
  1189.4 4.3 collective-permute-start.86
  1200.5 10.5 collective-permute-done.86
  1211.3 4.8 collective-permute-start.88
  1228.8 5.2 fusion.37
  (789 shorter events, 452.6 us)
Async XLA Ops:
  29.4 45.8 %collective-permute-start.8 = (bf16[256,2048]{1,0:T(8,128)(2,1)S(1)}, bf16[256,2048]{1,0:T(8,128)(2,1)S(1)}, u32[]{:S(2)}, u32[]{:S(2)}) collective-permute-start(bf16[256,2048]{1,0:T(8,128)(2,1)S(1)} %copy-done.2), channel_id=1, source_target_pairs={{0,1},{1,0},{2,3},{3,2},{4,5},{5,4},{6,7},{7,6},{8,9},{9,8},{10,11... | collective-permute-start | bytes 3145736 | tf_op jit(solution)/shard_map/ppermute | solution.py:121
  30.2 53.6 %collective-permute-start.9 = (bf16[256,2048]{1,0:T(8,128)(2,1)S(1)}, bf16[256,2048]{1,0:T(8,128)(2,1)}, u32[]{:S(2)}, u32[]{:S(2)}) collective-permute-start(bf16[256,2048]{1,0:T(8,128)(2,1)S(1)} %copy-done.2), channel_id=1, source_target_pairs={{0,2},{1,3},{2,0},{3,1},{4,6},{5,7},{6,4},{7,5},{8,10},{9,11},{10,... | collective-permute-start | bytes 3145736 | tf_op jit(solution)/shard_map/ppermute | solution.py:121
  31.2 54.7 %collective-permute-start.10 = (bf16[256,2048]{1,0:T(8,128)(2,1)S(1)}, bf16[256,2048]{1,0:T(8,128)(2,1)}, u32[]{:S(2)}, u32[]{:S(2)}) collective-permute-start(bf16[256,2048]{1,0:T(8,128)(2,1)S(1)} %copy-done.2), channel_id=1, source_target_pairs={{0,3},{1,2},{2,1},{3,0},{4,7},{5,6},{6,5},{7,4},{8,11},{9,10},{10,... | collective-permute-start | bytes 3145736 | tf_op jit(solution)/shard_map/ppermute | solution.py:121
  47.3 22.6 %collective-permute-start.6 = (bf16[256,1024]{1,0:T(8,128)(2,1)}, bf16[256,1024]{1,0:T(8,128)(2,1)}, u32[]{:S(2)}, u32[]{:S(2)}) collective-permute-start(bf16[256,1024]{1,0:T(8,128)(2,1)} %collective-permute-done.4), channel_id=1, source_target_pairs={{0,8},{4,12},{8,16},{12,20},{16,24},{20,28},{24,0},{28,4},{1,9},{5... | collective-permute-start | bytes 1572872 | tf_op jit(solution)/shard_map/ppermute | solution.py:115
  47.3 22.6 %collective-permute-start.7 = (bf16[64,2688]{1,0:T(8,128)(2,1)}, bf16[64,2688]{1,0:T(8,128)(2,1)}, u32[]{:S(2)}, u32[]{:S(2)}) collective-permute-start(bf16[64,2688]{1,0:T(8,128)(2,1)} %collective-permute-done.5), channel_id=1, source_target_pairs={{0,8},{4,12},{8,16},{12,20},{16,24},{20,28},{24,0},{28,4},{1,9},{5... | collective-permute-start | bytes 1032200 | tf_op jit(solution)/shard_map/ppermute | solution.py:115
  55.8 48.7 %all-to-all-start = ((bf16[32,64,176]{2,1,0:T(8,128)(2,1)}), bf16[32,64,176]{2,1,0:T(8,128)(2,1)}, u32[]{:S(2)}, u32[]{:S(2)}) async-start(bf16[32,64,176]{2,1,0:T(8,128)(2,1)} %maximum_bitcast_fusion.1), calls=%async_computation | async-start | bytes 2097152 | tf_op jit(solution)/shard_map/all_to_all | solution.py:406
  61.0 347.3 %all-gather.3.cloned.1.call-start = ((), (), s32[]{:S(2)}) async-start(), calls=%async_computation.3 | async-start | bytes 34603008 | tf_op jit(solution)/shard_map/all_gather | solution.py:442
  71.3 29.0 %collective-permute-start.12 = (bf16[128,2688]{1,0:T(8,128)(2,1)S(1)}, bf16[128,2688]{1,0:T(8,128)(2,1)S(1)}, u32[]{:S(2)}, u32[]{:S(2)}) collective-permute-start(bf16[128,2688]{1,0:T(8,128)(2,1)S(1)} %bitcast.315), channel_id=1, source_target_pairs={{0,1},{1,0},{2,3},{3,2},{4,5},{5,4},{6,7},{7,6},{8,9},{9,8},{10,11... | collective-permute-start | bytes 2064392 | tf_op jit(solution)/shard_map/ppermute | solution.py:115
  75.0 26.3 %collective-permute-start.13 = (bf16[128,2688]{1,0:T(8,128)(2,1)S(1)}, bf16[128,2688]{1,0:T(8,128)(2,1)S(1)}, u32[]{:S(2)}, u32[]{:S(2)}) collective-permute-start(bf16[128,2688]{1,0:T(8,128)(2,1)S(1)} %bitcast.312), channel_id=1, source_target_pairs={{0,2},{1,3},{2,0},{3,1},{4,6},{5,7},{6,4},{7,5},{8,10},{9,11},{10,... | collective-permute-start | bytes 2064392 | tf_op jit(solution)/shard_map/ppermute | solution.py:115
  134.5 25.7 %collective-permute-start.19 = (bf16[1024,1024]{1,0:T(8,128)(2,1)}, bf16[1024,1024]{1,0:T(8,128)(2,1)}, u32[]{:S(2)}, u32[]{:S(2)}) collective-permute-start(bf16[1024,1024]{1,0:T(8,128)(2,1)} %get-tuple-element.535), channel_id=1, source_target_pairs={{0,4},{4,0},{8,12},{12,8},{16,20},{20,16},{24,28},{28,24},{1,5},{5... | collective-permute-start | bytes 6291464 | tf_op jit(solution)/shard_map/ppermute | solution.py:115
  135.2 40.3 %collective-permute-start.16 = (bf16[256,2048]{1,0:T(8,128)(2,1)S(1)}, bf16[256,2048]{1,0:T(8,128)(2,1)}, u32[]{:S(2)}, u32[]{:S(2)}) collective-permute-start(bf16[256,2048]{1,0:T(8,128)(2,1)S(1)} %fusion.50), channel_id=1, source_target_pairs={{0,2},{1,3},{2,0},{3,1},{4,6},{5,7},{6,4},{7,5},{8,10},{9,11},{10,... | collective-permute-start | bytes 3145736 | tf_op jit(solution)/shard_map/ppermute | solution.py:115
  135.8 39.7 %collective-permute-start.17 = (bf16[256,2048]{1,0:T(8,128)(2,1)S(1)}, bf16[256,2048]{1,0:T(8,128)(2,1)}, u32[]{:S(2)}, u32[]{:S(2)}) collective-permute-start(bf16[256,2048]{1,0:T(8,128)(2,1)S(1)} %fusion.49), channel_id=1, source_target_pairs={{0,1},{1,0},{2,3},{3,2},{4,5},{5,4},{6,7},{7,6},{8,9},{9,8},{10,11... | collective-permute-start | bytes 3145736 | tf_op jit(solution)/shard_map/ppermute | solution.py:115
  192.8 53.3 %collective-permute-start.23 = (bf16[1024,2048]{1,0:T(8,128)(2,1)}, bf16[1024,2048]{1,0:T(8,128)(2,1)}, u32[]{:S(2)}, u32[]{:S(2)}) collective-permute-start(bf16[1024,2048]{1,0:T(8,128)(2,1)} %pad_maximum_fusion.4), channel_id=1, source_target_pairs={{0,4},{4,0},{8,12},{12,8},{16,20},{20,16},{24,28},{28,24},{1,5},{5... | collective-permute-start | bytes 12582920 | tf_op jit(solution)/shard_map/ppermute | solution.py:115
  220.0 25.3 %collective-permute-start.20 = (bf16[256,512]{0,1:T(8,128)(2,1)S(1)}, bf16[256,512]{0,1:T(8,128)(2,1)S(1)}, u32[]{:S(2)}, u32[]{:S(2)}) collective-permute-start(bf16[256,512]{0,1:T(8,128)(2,1)S(1)} %bitcast.345), channel_id=1, source_target_pairs={{0,1},{1,0},{2,3},{3,2},{4,5},{5,4},{6,7},{7,6},{8,9},{9,8},{10,11... | collective-permute-start | bytes 786440 | tf_op jit(solution)/shard_map/ppermute | solution.py:121
  269.6 34.6 %collective-permute-start.28 = (bf16[128,2048]{0,1:T(8,128)(2,1)}, bf16[128,2048]{0,1:T(8,128)(2,1)}, u32[]{:S(2)}, u32[]{:S(2)}) collective-permute-start(bf16[128,2048]{0,1:T(8,128)(2,1)} %bitcast.53), channel_id=1, source_target_pairs={{0,1},{1,0},{2,3},{3,2},{4,5},{5,4},{6,7},{7,6},{8,9},{9,8},{10,11... | collective-permute-start | bytes 1572872 | tf_op jit(solution)/shard_map/ppermute | solution.py:115
  271.6 32.5 %collective-permute-start.29 = (bf16[128,2048]{0,1:T(8,128)(2,1)}, bf16[128,2048]{0,1:T(8,128)(2,1)}, u32[]{:S(2)}, u32[]{:S(2)}) collective-permute-start(bf16[128,2048]{0,1:T(8,128)(2,1)} %bitcast.54), channel_id=1, source_target_pairs={{0,2},{1,3},{2,0},{3,1},{4,6},{5,7},{6,4},{7,5},{8,10},{9,11},{10,... | collective-permute-start | bytes 1572872 | tf_op jit(solution)/shard_map/ppermute | solution.py:115
  291.7 37.0 %all-to-all-start.1 = ((f32[32,1,256]{2,1,0:T(1,128)}), f32[32,1,256]{2,1,0:T(1,128)S(1)}, u32[]{:S(2)}, u32[]{:S(2)}) async-start(f32[32,1,256]{2,1,0:T(1,128)} %all_to_all.13), calls=%async_computation.1 | async-start | bytes 65536 | tf_op jit(solution)/shard_map/all_to_all | solution.py:523
  295.9 822.7 %all-gather.5.cloned.1.call-start = ((), (), s32[]{:S(2)}) async-start(), calls=%async_computation.4 | async-start | bytes 12976128 | tf_op jit(solution)/shard_map/all_gather | solution.py:638
  306.7 33.4 %collective-permute-start.31 = (bf16[256,2048]{0,1:T(8,128)(2,1)}, bf16[256,2048]{0,1:T(8,128)(2,1)}, u32[]{:S(2)}, u32[]{:S(2)}) collective-permute-start(bf16[256,2048]{0,1:T(8,128)(2,1)} %pad_maximum_fusion.23), channel_id=1, source_target_pairs={{0,2},{1,3},{2,0},{3,1},{4,6},{5,7},{6,4},{7,5},{8,10},{9,11},{10,... | collective-permute-start | bytes 3145736 | tf_op jit(solution)/shard_map/ppermute | solution.py:115
  310.5 29.6 %collective-permute-start.32 = (bf16[256,2048]{0,1:T(8,128)(2,1)}, bf16[256,2048]{0,1:T(8,128)(2,1)}, u32[]{:S(2)}, u32[]{:S(2)}) collective-permute-start(bf16[256,2048]{0,1:T(8,128)(2,1)} %pad_maximum_fusion.24), channel_id=1, source_target_pairs={{0,1},{1,0},{2,3},{3,2},{4,5},{5,4},{6,7},{7,6},{8,9},{9,8},{10,11... | collective-permute-start | bytes 3145736 | tf_op jit(solution)/shard_map/ppermute | solution.py:115
  312.6 27.6 %collective-permute-start.30 = (bf16[128,2048]{1,0:T(8,128)(2,1)}, bf16[128,2048]{1,0:T(8,128)(2,1)}, u32[]{:S(2)}, u32[]{:S(2)}) collective-permute-start(bf16[128,2048]{1,0:T(8,128)(2,1)} %collective-permute-done.27), channel_id=1, source_target_pairs={{0,8},{4,12},{8,16},{12,20},{16,24},{20,28},{24,0},{28,4},{1,9},{5... | collective-permute-start | bytes 1572872 | tf_op jit(solution)/shard_map/ppermute | solution.py:115
  342.5 23.5 %collective-permute-start.33 = (bf16[256,2048]{1,0:T(8,128)(2,1)S(1)}, bf16[256,2048]{1,0:T(8,128)(2,1)S(1)}, u32[]{:S(2)}, u32[]{:S(2)}) collective-permute-start(bf16[256,2048]{1,0:T(8,128)(2,1)S(1)} %pad_maximum_fusion.25), channel_id=1, source_target_pairs={{0,1},{1,0},{2,3},{3,2},{4,5},{5,4},{6,7},{7,6},{8,9},{9,8},{10,11... | collective-permute-start | bytes 3145736 | tf_op jit(solution)/shard_map/ppermute | solution.py:115
  344.3 23.0 %collective-permute-start.34 = (bf16[256,2048]{1,0:T(8,128)(2,1)S(1)}, bf16[256,2048]{1,0:T(8,128)(2,1)S(1)}, u32[]{:S(2)}, u32[]{:S(2)}) collective-permute-start(bf16[256,2048]{1,0:T(8,128)(2,1)S(1)} %pad_maximum_fusion.26), channel_id=1, source_target_pairs={{0,2},{1,3},{2,0},{3,1},{4,6},{5,7},{6,4},{7,5},{8,10},{9,11},{10,... | collective-permute-start | bytes 3145736 | tf_op jit(solution)/shard_map/ppermute | solution.py:115
  344.8 32.4 %collective-permute-start.35 = (bf16[256,2048]{1,0:T(8,128)(2,1)S(1)}, bf16[256,2048]{1,0:T(8,128)(2,1)}, u32[]{:S(2)}, u32[]{:S(2)}) collective-permute-start(bf16[256,2048]{1,0:T(8,128)(2,1)S(1)} %copy-done.11), channel_id=1, source_target_pairs={{0,8},{4,12},{8,16},{12,20},{16,24},{20,28},{24,0},{28,4},{1,9},{5... | collective-permute-start | bytes 3145736 | tf_op jit(solution)/shard_map/ppermute | solution.py:115
  380.4 27.7 %collective-permute-start.36 = (bf16[1024,2048]{1,0:T(8,128)(2,1)}, bf16[1024,2048]{1,0:T(8,128)(2,1)}, u32[]{:S(2)}, u32[]{:S(2)}) collective-permute-start(bf16[1024,2048]{1,0:T(8,128)(2,1)} %constant_dynamic-update-slice_fusion.25.refs_1_), channel_id=1, source_target_pairs={{0,4},{4,0},{8,12},{12,8},{16,20},{20,16},{24,28},{28,24},{1,5},{5... | collective-permute-start | bytes 12582920 | tf_op jit(solution)/shard_map/ppermute | solution.py:115
  380.4 27.7 %collective-permute-start.37 = (bf16[256,2048]{1,0:T(8,128)(2,1)}, bf16[256,2048]{1,0:T(8,128)(2,1)}, u32[]{:S(2)}, u32[]{:S(2)}) collective-permute-start(bf16[256,2048]{1,0:T(8,128)(2,1)} %collective-permute-done.35), channel_id=1, source_target_pairs={{0,8},{4,12},{8,16},{12,20},{16,24},{20,28},{24,0},{28,4},{1,9},{5... | collective-permute-start | bytes 3145736 | tf_op jit(solution)/shard_map/ppermute | solution.py:115
  386.6 55.3 %collective-permute-start.39 = (bf16[512,2048]{1,0:T(8,128)(2,1)}, bf16[512,2048]{1,0:T(8,128)(2,1)}, u32[]{:S(2)}, u32[]{:S(2)}) collective-permute-start(bf16[512,2048]{1,0:T(8,128)(2,1)} %pad_maximum_fusion.7), channel_id=1, source_target_pairs={{0,2},{1,3},{2,0},{3,1},{4,6},{5,7},{6,4},{7,5},{8,10},{9,11},{10,... | collective-permute-start | bytes 6291464 | tf_op jit(solution)/shard_map/ppermute | solution.py:115
  389.3 52.6 %collective-permute-start.40 = (bf16[512,2048]{1,0:T(8,128)(2,1)}, bf16[512,2048]{1,0:T(8,128)(2,1)}, u32[]{:S(2)}, u32[]{:S(2)}) collective-permute-start(bf16[512,2048]{1,0:T(8,128)(2,1)} %pad_maximum_fusion.8), channel_id=1, source_target_pairs={{0,1},{1,0},{2,3},{3,2},{4,5},{5,4},{6,7},{7,6},{8,9},{9,8},{10,11... | collective-permute-start | bytes 6291464 | tf_op jit(solution)/shard_map/ppermute | solution.py:115
  408.1 33.8 %collective-permute-start.38 = (bf16[256,2048]{1,0:T(8,128)(2,1)}, bf16[256,2048]{1,0:T(8,128)(2,1)S(1)}, u32[]{:S(2)}, u32[]{:S(2)}) collective-permute-start(bf16[256,2048]{1,0:T(8,128)(2,1)} %collective-permute-done.37), channel_id=1, source_target_pairs={{0,8},{4,12},{8,16},{12,20},{16,24},{20,28},{24,0},{28,4},{1,9},{5... | collective-permute-start | bytes 3145736 | tf_op jit(solution)/shard_map/ppermute | solution.py:115
  496.0 64.8 %collective-permute-start.48 = (bf16[1024,4096]{1,0:T(8,128)(2,1)}, bf16[1024,4096]{1,0:T(8,128)(2,1)}, u32[]{:S(2)}, u32[]{:S(2)}) collective-permute-start(bf16[1024,4096]{1,0:T(8,128)(2,1)} %get-tuple-element.232), channel_id=1, source_target_pairs={{0,4},{4,0},{8,12},{12,8},{16,20},{20,16},{24,28},{28,24},{1,5},{5... | collective-permute-start | bytes 25165832 | tf_op jit(solution)/shard_map/ppermute | solution.py:115
  498.9 48.0 %collective-permute-start.42 = (bf16[512,2048]{1,0:T(8,128)(2,1)}, bf16[512,2048]{1,0:T(8,128)(2,1)}, u32[]{:S(2)}, u32[]{:S(2)}) collective-permute-start(bf16[512,2048]{1,0:T(8,128)(2,1)} %pad_maximum_fusion.9), channel_id=1, source_target_pairs={{0,1},{1,0},{2,3},{3,2},{4,5},{5,4},{6,7},{7,6},{8,9},{9,8},{10,11... | collective-permute-start | bytes 6291464 | tf_op jit(solution)/shard_map/ppermute | solution.py:115
  505.1 47.6 %collective-permute-start.43 = (bf16[512,2048]{1,0:T(8,128)(2,1)S(1)}, bf16[512,2048]{1,0:T(8,128)(2,1)}, u32[]{:S(2)}, u32[]{:S(2)}) collective-permute-start(bf16[512,2048]{1,0:T(8,128)(2,1)S(1)} %pad_maximum_fusion.10), channel_id=1, source_target_pairs={{0,2},{1,3},{2,0},{3,1},{4,6},{5,7},{6,4},{7,5},{8,10},{9,11},{10,... | collective-permute-start | bytes 6291464 | tf_op jit(solution)/shard_map/ppermute | solution.py:115
  559.0 56.4 %collective-permute-start.45 = (bf16[2048,2048]{1,0:T(8,128)(2,1)}, bf16[2048,2048]{1,0:T(8,128)(2,1)}, u32[]{:S(2)}, u32[]{:S(2)}) collective-permute-start(bf16[2048,2048]{1,0:T(8,128)(2,1)} %constant_dynamic-update-slice_fusion.31.refs_1_), channel_id=1, source_target_pairs={{0,4},{4,0},{8,12},{12,8},{16,20},{20,16},{24,28},{28,24},{1,5},{5... | collective-permute-start | bytes 25165832 | tf_op jit(solution)/shard_map/ppermute | solution.py:115
  559.0 48.3 %collective-permute-start.46 = (bf16[512,2048]{1,0:T(8,128)(2,1)}, bf16[512,2048]{1,0:T(8,128)(2,1)S(1)}, u32[]{:S(2)}, u32[]{:S(2)}) collective-permute-start(bf16[512,2048]{1,0:T(8,128)(2,1)} %get-tuple-element.250), channel_id=1, source_target_pairs={{0,2},{1,3},{2,0},{3,1},{4,6},{5,7},{6,4},{7,5},{8,10},{9,11},{10,... | collective-permute-start | bytes 6291464 | tf_op jit(solution)/shard_map/ppermute | solution.py:115
  559.8 48.1 %collective-permute-start.47 = (bf16[512,2048]{1,0:T(8,128)(2,1)}, bf16[512,2048]{1,0:T(8,128)(2,1)}, u32[]{:S(2)}, u32[]{:S(2)}) collective-permute-start(bf16[512,2048]{1,0:T(8,128)(2,1)} %get-tuple-element.251), channel_id=1, source_target_pairs={{0,1},{1,0},{2,3},{3,2},{4,5},{5,4},{6,7},{7,6},{8,9},{9,8},{10,11... | collective-permute-start | bytes 6291464 | tf_op jit(solution)/shard_map/ppermute | solution.py:115
  675.5 25.6 %collective-permute-start.49 = (bf16[2048,4096]{1,0:T(8,128)(2,1)}, bf16[2048,4096]{1,0:T(8,128)(2,1)}, u32[]{:S(2)}, u32[]{:S(2)}) collective-permute-start(bf16[2048,4096]{1,0:T(8,128)(2,1)} %get-tuple-element.267), channel_id=1, source_target_pairs={{0,4},{4,0},{8,12},{12,8},{16,20},{20,16},{24,28},{28,24},{1,5},{5... | collective-permute-start | bytes 50331656 | tf_op jit(solution)/shard_map/ppermute | solution.py:115
  689.8 78.7 %collective-permute-start.52 = (bf16[256,2048]{1,0:T(8,128)(2,1)}, bf16[256,2048]{1,0:T(8,128)(2,1)S(1)}, u32[]{:S(2)}, u32[]{:S(2)}) collective-permute-start(bf16[256,2048]{1,0:T(8,128)(2,1)} %split.200), channel_id=1, source_target_pairs={{0,1},{1,0},{2,3},{3,2},{4,5},{5,4},{6,7},{7,6},{8,9},{9,8},{10,11... | collective-permute-start | bytes 3145736 | tf_op jit(solution)/shard_map/ppermute | solution.py:115
  691.4 77.1 %collective-permute-start.53 = (bf16[256,2048]{1,0:T(8,128)(2,1)}, bf16[256,2048]{1,0:T(8,128)(2,1)}, u32[]{:S(2)}, u32[]{:S(2)}) collective-permute-start(bf16[256,2048]{1,0:T(8,128)(2,1)} %split.201), channel_id=1, source_target_pairs={{0,2},{1,3},{2,0},{3,1},{4,6},{5,7},{6,4},{7,5},{8,10},{9,11},{10,... | collective-permute-start | bytes 3145736 | tf_op jit(solution)/shard_map/ppermute | solution.py:115
  766.5 53.2 %collective-permute-start.50 = (bf16[512,2048]{1,0:T(8,128)(2,1)}, bf16[512,2048]{1,0:T(8,128)(2,1)S(1)}, u32[]{:S(2)}, u32[]{:S(2)}) collective-permute-start(bf16[512,2048]{1,0:T(8,128)(2,1)} %get-tuple-element.274), channel_id=1, source_target_pairs={{0,1},{1,0},{2,3},{3,2},{4,5},{5,4},{6,7},{7,6},{8,9},{9,8},{10,11... | collective-permute-start | bytes 6291464 | tf_op jit(solution)/shard_map/ppermute | solution.py:115
  767.2 52.5 %collective-permute-start.51 = (bf16[512,2048]{1,0:T(8,128)(2,1)}, bf16[512,2048]{1,0:T(8,128)(2,1)S(1)}, u32[]{:S(2)}, u32[]{:S(2)}) collective-permute-start(bf16[512,2048]{1,0:T(8,128)(2,1)} %get-tuple-element.275), channel_id=1, source_target_pairs={{0,2},{1,3},{2,0},{3,1},{4,6},{5,7},{6,4},{7,5},{8,10},{9,11},{10,... | collective-permute-start | bytes 6291464 | tf_op jit(solution)/shard_map/ppermute | solution.py:115
  771.8 43.0 %collective-permute-start.54 = (bf16[128,2048]{1,0:T(8,128)(2,1)S(1)}, bf16[128,2048]{1,0:T(8,128)(2,1)S(1)}, u32[]{:S(2)}, u32[]{:S(2)}) collective-permute-start(bf16[128,2048]{1,0:T(8,128)(2,1)S(1)} %pad_maximum_fusion.34), channel_id=1, source_target_pairs={{0,24},{4,28},{8,0},{12,4},{16,8},{20,12},{24,16},{28,20},{1,25},{... | collective-permute-start | bytes 1572872 | tf_op jit(solution)/shard_map/ppermute | solution.py:115
  823.7 45.2 %collective-permute-start.55 = (bf16[128,2048]{1,0:T(8,128)(2,1)S(1)}, bf16[128,2048]{1,0:T(8,128)(2,1)S(1)}, u32[]{:S(2)}, u32[]{:S(2)}) collective-permute-start(bf16[128,2048]{1,0:T(8,128)(2,1)S(1)} %add_convert_fusion.21), channel_id=1, source_target_pairs={{0,24},{4,28},{8,0},{12,4},{16,8},{20,12},{24,16},{28,20},{1,25},{... | collective-permute-start | bytes 1572872 | tf_op jit(solution)/shard_map/ppermute | solution.py:115
  827.0 41.8 %collective-permute-start.56 = (bf16[256,2048]{1,0:T(8,128)(2,1)S(1)}, bf16[256,2048]{1,0:T(8,128)(2,1)S(1)}, u32[]{:S(2)}, u32[]{:S(2)}) collective-permute-start(bf16[256,2048]{1,0:T(8,128)(2,1)S(1)} %pad_maximum_fusion.30), channel_id=1, source_target_pairs={{0,24},{4,28},{8,0},{12,4},{16,8},{20,12},{24,16},{28,20},{1,25},{... | collective-permute-start | bytes 3145736 | tf_op jit(solution)/shard_map/ppermute | solution.py:115
  827.6 46.8 %collective-permute-start.57 = (bf16[512,2048]{1,0:T(8,128)(2,1)S(1)}, bf16[512,2048]{1,0:T(8,128)(2,1)S(1)}, u32[]{:S(2)}, u32[]{:S(2)}) collective-permute-start(bf16[512,2048]{1,0:T(8,128)(2,1)S(1)} %copy-done.132), channel_id=1, source_target_pairs={{0,2},{1,3},{2,0},{3,1},{4,6},{5,7},{6,4},{7,5},{8,10},{9,11},{10,... | collective-permute-start | bytes 6291464 | tf_op jit(solution)/shard_map/ppermute | solution.py:115
  829.0 46.5 %collective-permute-start.58 = (bf16[512,2048]{1,0:T(8,128)(2,1)S(1)}, bf16[512,2048]{1,0:T(8,128)(2,1)S(1)}, u32[]{:S(2)}, u32[]{:S(2)}) collective-permute-start(bf16[512,2048]{1,0:T(8,128)(2,1)S(1)} %copy-done.131), channel_id=1, source_target_pairs={{0,1},{1,0},{2,3},{3,2},{4,5},{5,4},{6,7},{7,6},{8,9},{9,8},{10,11... | collective-permute-start | bytes 6291464 | tf_op jit(solution)/shard_map/ppermute | solution.py:115
  880.4 82.5 %collective-permute-start.59 = (bf16[768,2048]{1,0:T(8,128)(2,1)}, bf16[768,2048]{1,0:T(8,128)(2,1)}, u32[]{:S(2)}, u32[]{:S(2)}) collective-permute-start(bf16[768,2048]{1,0:T(8,128)(2,1)} %pad_maximum_fusion.5), channel_id=1, source_target_pairs={{0,1},{1,0},{2,3},{3,2},{4,5},{5,4},{6,7},{7,6},{8,9},{9,8},{10,11... | collective-permute-start | bytes 9437192 | tf_op jit(solution)/shard_map/ppermute | solution.py:115
  886.4 76.6 %collective-permute-start.60 = (bf16[768,2048]{1,0:T(8,128)(2,1)}, bf16[768,2048]{1,0:T(8,128)(2,1)}, u32[]{:S(2)}, u32[]{:S(2)}) collective-permute-start(bf16[768,2048]{1,0:T(8,128)(2,1)} %pad_maximum_fusion.6), channel_id=1, source_target_pairs={{0,2},{1,3},{2,0},{3,1},{4,6},{5,7},{6,4},{7,5},{8,10},{9,11},{10,... | collective-permute-start | bytes 9437192 | tf_op jit(solution)/shard_map/ppermute | solution.py:115
  887.1 38.3 %collective-permute-start.61 = (bf16[128,2048]{1,0:T(8,128)(2,1)}, bf16[128,2048]{1,0:T(8,128)(2,1)}, u32[]{:S(2)}, u32[]{:S(2)}) collective-permute-start(bf16[128,2048]{1,0:T(8,128)(2,1)} %add_convert_fusion.20), channel_id=1, source_target_pairs={{0,24},{4,28},{8,0},{12,4},{16,8},{20,12},{24,16},{28,20},{1,25},{... | collective-permute-start | bytes 1572872 | tf_op jit(solution)/shard_map/ppermute | solution.py:115
  888.5 36.9 %collective-permute-start.62 = (bf16[256,2048]{1,0:T(8,128)(2,1)S(1)}, bf16[256,2048]{1,0:T(8,128)(2,1)}, u32[]{:S(2)}, u32[]{:S(2)}) collective-permute-start(bf16[256,2048]{1,0:T(8,128)(2,1)S(1)} %add_convert_fusion.16), channel_id=1, source_target_pairs={{0,24},{4,28},{8,0},{12,4},{16,8},{20,12},{24,16},{28,20},{1,25},{... | collective-permute-start | bytes 3145736 | tf_op jit(solution)/shard_map/ppermute | solution.py:115
  927.1 27.3 %collective-permute-start.63 = (bf16[256,2048]{1,0:T(8,128)(2,1)S(1)}, bf16[256,2048]{1,0:T(8,128)(2,1)S(1)}, u32[]{:S(2)}, u32[]{:S(2)}) collective-permute-start(bf16[256,2048]{1,0:T(8,128)(2,1)S(1)} %add_convert_fusion.15), channel_id=1, source_target_pairs={{0,24},{4,28},{8,0},{12,4},{16,8},{20,12},{24,16},{28,20},{1,25},{... | collective-permute-start | bytes 3145736 | tf_op jit(solution)/shard_map/ppermute | solution.py:115
  977.9 32.3 %collective-permute-start.66 = (bf16[384,2048]{1,0:T(8,128)(2,1)}, bf16[384,2048]{1,0:T(8,128)(2,1)}, u32[]{:S(2)}, u32[]{:S(2)}) collective-permute-start(bf16[384,2048]{1,0:T(8,128)(2,1)} %pad_maximum_fusion.13), channel_id=1, source_target_pairs={{0,24},{4,28},{8,0},{12,4},{16,8},{20,12},{24,16},{28,20},{1,25},{... | collective-permute-start | bytes 4718600 | tf_op jit(solution)/shard_map/ppermute | solution.py:115
  1013.4 41.7 %collective-permute-start.67 = (bf16[384,2048]{1,0:T(8,128)(2,1)}, bf16[384,2048]{1,0:T(8,128)(2,1)}, u32[]{:S(2)}, u32[]{:S(2)}) collective-permute-start(bf16[384,2048]{1,0:T(8,128)(2,1)} %add_convert_fusion.10), channel_id=1, source_target_pairs={{0,24},{4,28},{8,0},{12,4},{16,8},{20,12},{24,16},{28,20},{1,25},{... | collective-permute-start | bytes 4718600 | tf_op jit(solution)/shard_map/ppermute | solution.py:115
  1016.0 112.5 %all-to-all-start.2 = ((f32[32,64,176]{2,1,0:T(8,128)}), f32[32,64,176]{2,1,0:T(8,128)}, u32[]{:S(2)}, u32[]{:S(2)}) async-start(f32[32,64,176]{2,1,0:T(8,128)} %bitcast.305), calls=%async_computation.2 | async-start | bytes 4194304 | tf_op jit(solution)/shard_map/all_to_all | solution.py:777
  1077.4 30.7 %collective-permute-start.74 = (bf16[256,768]{0,1:T(8,128)(2,1)}, bf16[256,768]{0,1:T(8,128)(2,1)}, u32[]{:S(2)}, u32[]{:S(2)}) collective-permute-start(bf16[256,768]{0,1:T(8,128)(2,1)} %bitcast.73), channel_id=1, source_target_pairs={{0,1},{1,0},{2,3},{3,2},{4,5},{5,4},{6,7},{7,6},{8,9},{9,8},{10,11... | collective-permute-start | bytes 1179656 | tf_op jit(solution)/shard_map/ppermute | solution.py:121
  1079.3 28.9 %collective-permute-start.75 = (bf16[256,768]{0,1:T(8,128)(2,1)}, bf16[256,768]{0,1:T(8,128)(2,1)}, u32[]{:S(2)}, u32[]{:S(2)}) collective-permute-start(bf16[256,768]{0,1:T(8,128)(2,1)} %bitcast.74), channel_id=1, source_target_pairs={{0,2},{1,3},{2,0},{3,1},{4,6},{5,7},{6,4},{7,5},{8,10},{9,11},{10,... | collective-permute-start | bytes 1179656 | tf_op jit(solution)/shard_map/ppermute | solution.py:121
  1080.8 27.4 %collective-permute-start.76 = (bf16[256,768]{0,1:T(8,128)(2,1)}, bf16[256,768]{0,1:T(8,128)(2,1)}, u32[]{:S(2)}, u32[]{:S(2)}) collective-permute-start(bf16[256,768]{0,1:T(8,128)(2,1)} %bitcast.75), channel_id=1, source_target_pairs={{0,3},{1,2},{2,1},{3,0},{4,7},{5,6},{6,5},{7,4},{8,11},{9,10},{10,... | collective-permute-start | bytes 1179656 | tf_op jit(solution)/shard_map/ppermute | solution.py:121
  1084.2 55.6 %collective-permute-start.68 = (bf16[384,2048]{1,0:T(8,128)(2,1)}, bf16[384,2048]{1,0:T(8,128)(2,1)}, u32[]{:S(2)}, u32[]{:S(2)}) collective-permute-start(bf16[384,2048]{1,0:T(8,128)(2,1)} %add_convert_fusion.9), channel_id=1, source_target_pairs={{0,24},{4,28},{8,0},{12,4},{16,8},{20,12},{24,16},{28,20},{1,25},{... | collective-permute-start | bytes 4718600 | tf_op jit(solution)/shard_map/ppermute | solution.py:115
  1106.7 38.8 %collective-permute-start.80 = (bf16[4,256,1536]{2,1,0:T(8,128)(2,1)}, bf16[4,256,1536]{2,1,0:T(8,128)(2,1)}, u32[]{:S(2)}, u32[]{:S(2)}) collective-permute-start(bf16[4,256,1536]{2,1,0:T(8,128)(2,1)} %dynamic-slice_bitcast_fusion), channel_id=1, source_target_pairs={{0,4},{4,0},{8,12},{12,8},{16,20},{20,16},{24,28},{28,24},{1,5},{5... | collective-permute-start | bytes 9437192 | tf_op jit(solution)/shard_map/ppermute | solution.py:115
  1115.1 30.4 %collective-permute-start.77 = (bf16[256,576]{0,1:T(8,128)(2,1)}, bf16[256,576]{0,1:T(8,128)(2,1)}, u32[]{:S(2)}, u32[]{:S(2)}) collective-permute-start(bf16[256,576]{0,1:T(8,128)(2,1)} %get-tuple-element.465), channel_id=1, source_target_pairs={{0,1},{1,0},{2,3},{3,2},{4,5},{5,4},{6,7},{7,6},{8,9},{9,8},{10,11... | collective-permute-start | bytes 884744 | tf_op jit(solution)/shard_map/ppermute | solution.py:121
  1116.6 29.0 %collective-permute-start.78 = (bf16[256,576]{0,1:T(8,128)(2,1)}, bf16[256,576]{0,1:T(8,128)(2,1)}, u32[]{:S(2)}, u32[]{:S(2)}) collective-permute-start(bf16[256,576]{0,1:T(8,128)(2,1)} %get-tuple-element.464), channel_id=1, source_target_pairs={{0,2},{1,3},{2,0},{3,1},{4,6},{5,7},{6,4},{7,5},{8,10},{9,11},{10,... | collective-permute-start | bytes 884744 | tf_op jit(solution)/shard_map/ppermute | solution.py:121
  1118.1 27.5 %collective-permute-start.79 = (bf16[256,576]{0,1:T(8,128)(2,1)}, bf16[256,576]{0,1:T(8,128)(2,1)}, u32[]{:S(2)}, u32[]{:S(2)}) collective-permute-start(bf16[256,576]{0,1:T(8,128)(2,1)} %get-tuple-element.463), channel_id=1, source_target_pairs={{0,3},{1,2},{2,1},{3,0},{4,7},{5,6},{6,5},{7,4},{8,11},{9,10},{10,... | collective-permute-start | bytes 884744 | tf_op jit(solution)/shard_map/ppermute | solution.py:121
  1144.1 53.1 %collective-permute-start.69 = (bf16[64,2048]{1,0:T(8,128)(2,1)}, bf16[64,2048]{1,0:T(8,128)(2,1)S(1)}, u32[]{:S(2)}, u32[]{:S(2)}) collective-permute-start(bf16[64,2048]{1,0:T(8,128)(2,1)} %get-tuple-element.459), channel_id=1, source_target_pairs={{0,2},{1,3},{2,0},{3,1},{4,6},{5,7},{6,4},{7,5},{8,10},{9,11},{10,... | collective-permute-start | bytes 786440 | tf_op jit(solution)/shard_map/ppermute | solution.py:115
  1166.7 31.2 %collective-permute-start.70 = (bf16[64,2048]{1,0:T(8,128)(2,1)}, bf16[64,2048]{1,0:T(8,128)(2,1)}, u32[]{:S(2)}, u32[]{:S(2)}) collective-permute-start(bf16[64,2048]{1,0:T(8,128)(2,1)} %get-tuple-element.460), channel_id=1, source_target_pairs={{0,1},{1,0},{2,3},{3,2},{4,5},{5,4},{6,7},{7,6},{8,9},{9,8},{10,11... | collective-permute-start | bytes 786440 | tf_op jit(solution)/shard_map/ppermute | solution.py:115
  1189.4 21.7 %collective-permute-start.86 = (bf16[256,1536]{1,0:T(8,128)(2,1)}, bf16[256,1536]{1,0:T(8,128)(2,1)S(1)}, u32[]{:S(2)}, u32[]{:S(2)}) collective-permute-start(bf16[256,1536]{1,0:T(8,128)(2,1)} %fusion.45), channel_id=1, source_target_pairs={{0,24},{4,28},{8,0},{12,4},{16,8},{20,12},{24,16},{28,20},{1,25},{... | collective-permute-start | bytes 2359304 | tf_op jit(solution)/shard_map/ppermute | solution.py:115
  (186 other events, 2203.5 us)
Sparse Core Ops, SparseCore 0:
  112.5 240.1 all-gather.2
  692.8 108.5 all-gather.4
